TPU v7x, 32 devices: a whole 2x2x4 slice. The times are simulated.
32 devices in a mesh: blk: 4 (over z), rows: 8 (over y, x, core).
Axes of the slice: x: 2, y: 2, z: 4, core: 2. Of those that a mesh axis runs over, the one named last changes fastest.
Arguments:
- embeddings: bfloat16 [16384, 768], P(('blk', 'rows')), as said below
- centroids: bfloat16 [8192, 768], P('blk'), as said below
- log_mix: float32 [8192], P('blk'), may hold values from -1.5 to 3.7
Outputs:
- new_centroids: float32 [8192, 768], P('blk')
- new_weights: float32 [8192], P('blk')
Inputs may be any that keep to these rules, and one draw needn't show every extreme that they name: `embeddings`: real vectors of no fixed length. `centroids`: real vectors of no fixed length.
All inputs are finite; a program needn't handle non-finite values.
Results may differ from a plain program's by a relative error of at most 0.0024.
Values may be sent and summed in bfloat16 or wider, within the bound.
No kernel may reach another device: no remote copies, remote signals or barrier semaphores. Data moves between devices by JAX's collectives and lax.ppermute only.
A program may use at most 64 MiB of HBM per device.

v0:
```python
import math

import jax
import jax.numpy as jnp
from jax import lax
from jax.sharding import PartitionSpec as P

K = 8192


concentration = 32.0


def to_unit(values):
    values = values.astype(jnp.float32)
    return (values * lax.rsqrt(jnp.sum(values * values, axis=-1, keepdims=True) + 1e-06)).astype(
        jnp.bfloat16
    )


def finish(weighted, masses, factor):
    new_centroids = weighted * lax.rsqrt(
        jnp.sum(weighted * weighted, axis=1, keepdims=True) + 1e-06
    )
    return (new_centroids, masses * factor)


def local(embeddings, centroids, log_mix):
    centroid_units = to_unit(centroids)
    row_units = to_unit(embeddings)
    gathered = lax.all_gather(row_units, "blk", axis=0, tiled=True)
    row_total = gathered.shape[0]
    block_rows = math.gcd(row_total, 512)
    grouped = gathered.reshape(row_total // block_rows, block_rows, gathered.shape[1])

    def exponents(row_block):
        cosines = lax.dot_general(
            row_block, centroid_units, (((1,), (1,)), ((), ())), preferred_element_type=jnp.float32
        )
        return jnp.exp(log_mix[None, :] + concentration * (cosines - 1.0))

    def add_block(carried, resp, row_block):
        weighted = carried[0] + lax.dot_general(
            resp, row_block, (((0,), (0,)), ((), ())), preferred_element_type=jnp.float32
        )
        masses = carried[1] + jnp.sum(resp.astype(jnp.float32), axis=0)
        return (weighted, masses)

    local_centroids = centroids.shape[0]
    start_state = (
        jnp.zeros((local_centroids, centroids.shape[1]), jnp.float32),
        jnp.zeros((local_centroids,), jnp.float32),
    )
    partial_sums = lax.map(lambda row_block: jnp.sum(exponents(row_block), axis=1), grouped)
    totals = lax.psum(partial_sums, "blk")

    def accumulate(carried, element):
        row_block, block_totals = element
        resp = (exponents(row_block) / block_totals[:, None]).astype(jnp.bfloat16)
        return (add_block(carried, resp, row_block), None)

    (weighted, masses), _ = lax.scan(accumulate, start_state, (grouped, totals))
    factor = K / (row_total * lax.axis_size("rows"))
    summed, summed_masses = lax.psum((weighted, masses), "rows")
    return finish(summed, summed_masses, factor)


def solution(mesh):
    return jax.shard_map(
        local,
        mesh=mesh,
        in_specs=(P(("blk", "rows"), None), P("blk", None), P("blk")),
        out_specs=(P("blk", None), P("blk")),
        check_vma=False,
    )
```

profile of v0, /device:TPU:0, one launch (start us, length us, event | category | flops | bytes accessed | tf_op | source)
XLA Modules:
  0.0 269.0 jit_solution(14953942261130785813)
XLA Ops:
  7.2 0.0 all-gather.2.cloned.1.call-start
  7.2 1.5 fusion.11
  8.7 2.2 fusion.12
  11.0 0.0 all-reduce.2.cloned.1.call-start
  11.1 0.7 fusion.9
  11.8 2.3 fusion.10
  14.1 63.3 %all-gather.2.cloned.1.call-done = bf16[2048,768]{1,0:T(8,128)(2,1)} async-done(((bf16[512,768]{1,0:T(8,128)(2,1)}), bf16[2048,768]{1,0:T(8,128)(2,1)}) %all-gather.2.cloned.1.call-update) | async-done | bytes 3145744 | tf_op jit(solution)/shard_map/all_gather | solution.py:31
  77.3 17.0 %while.27 = (s32[]{:T(128)}, f32[4,512]{1,0:T(4,128)S(1)}, f32[2048]{0:T(1024)S(1)}, bf16[4,512,768]{2,1,0:T(8,128)(2,1)}, bf16[2048,768]{1,0:T(8,128)(2,1)}, /*index=5*/s32[]{:T(128)}, s32[]{:T(128)}) while((s32[]{:T(128)}, f32[4,512]{1,0:T(4,128)S(1)}, f32[2048]{0:T(1024)S(1)}, bf16[4,512,768]{2,1,0:T(8,128)(2,1)}, ...), condition=%wide.region_4.5_spmd, body=%wide.region_2.4_spmd.sunk | while | flops 1614806528 | bytes 3946589 | solution.py:54
  77.3 4.2 %exponential_reduce_fusion.2 = f32[512]{0:T(512)S(1)} fusion(bf16[2048,768]{1,0:T(8,128)(2,1)} %get-tuple-element.306, f32[2048]{0:T(1024)S(1)} %get-tuple-element.304, bf16[4,512,768]{2,1,0:T(8,128)(2,1)} %get-tuple-element.305, s32[]{:T(128)S(6)} %copy.8), kind=kOutput, calls=%fused_computation.clone.1 | convolution fusion | flops 1614806528 | bytes 3942404 | tf_op jit(solution)/shard_map/while/body/eval_jaxpr/dot_general | solution.py:37
  81.6 4.2 %exponential_reduce_fusion.2 = f32[512]{0:T(512)S(1)} fusion(bf16[2048,768]{1,0:T(8,128)(2,1)} %get-tuple-element.306, f32[2048]{0:T(1024)S(1)} %get-tuple-element.304, bf16[4,512,768]{2,1,0:T(8,128)(2,1)} %get-tuple-element.305, s32[]{:T(128)S(6)} %copy.8), kind=kOutput, calls=%fused_computation.clone.1 | convolution fusion | flops 1614806528 | bytes 3942404 | tf_op jit(solution)/shard_map/while/body/eval_jaxpr/dot_general | solution.py:37
  85.8 4.2 %exponential_reduce_fusion.2 = f32[512]{0:T(512)S(1)} fusion(bf16[2048,768]{1,0:T(8,128)(2,1)} %get-tuple-element.306, f32[2048]{0:T(1024)S(1)} %get-tuple-element.304, bf16[4,512,768]{2,1,0:T(8,128)(2,1)} %get-tuple-element.305, s32[]{:T(128)S(6)} %copy.8), kind=kOutput, calls=%fused_computation.clone.1 | convolution fusion | flops 1614806528 | bytes 3942404 | tf_op jit(solution)/shard_map/while/body/eval_jaxpr/dot_general | solution.py:37
  90.1 4.2 %exponential_reduce_fusion.2 = f32[512]{0:T(512)S(1)} fusion(bf16[2048,768]{1,0:T(8,128)(2,1)} %get-tuple-element.306, f32[2048]{0:T(1024)S(1)} %get-tuple-element.304, bf16[4,512,768]{2,1,0:T(8,128)(2,1)} %get-tuple-element.305, s32[]{:T(128)S(6)} %copy.8), kind=kOutput, calls=%fused_computation.clone.1 | convolution fusion | flops 1614806528 | bytes 3942404 | tf_op jit(solution)/shard_map/while/body/eval_jaxpr/dot_general | solution.py:37
  94.3 9.2 %psum.21 = f32[4,512]{1,0:T(4,128)S(1)} all-reduce(f32[4,512]{1,0:T(4,128)S(1)} %get-tuple-element.157), channel_id=1, replica_groups=mesh['blk'=4,'rows'=8] {'blk'}, use_global_device_ids=true, to_apply=%region_5.6 | all-reduce | flops 2048 | bytes 16384 | tf_op jit(solution)/shard_map/psum | solution.py:55
  103.6 47.5 %while.28 = (s32[]{:T(128)}, f32[2048,768]{1,0:T(8,128)}, f32[2048]{0:T(1024)S(1)}, f32[2048]{0:T(1024)S(1)}, bf16[4,512,768]{2,1,0:T(8,128)(2,1)}, /*index=5*/b...) while((s32[]{:T(128)}, f32[2048,768]{1,0:T(8,128)}, f32[2048]{0:T(1024)S(1)}, ...), condition=%wide.region_8.9_spmd.clone, body=%wide.region_6.8_spmd.clone.sunk | while | flops 3231713280 | bytes 65583300 | solution.py:62
  103.6 4.5 %convert_reduce_fusion.2 = (f32[2048]{0:T(1024)S(1)}, bf16[512,2048]{1,0:T(8,128)(2,1)S(1)}) fusion(f32[512]{0:T(512)S(1)} %bitcast.36, bf16[2048,768]{1,0:T(8,128)(2,1)} %get-tuple-element.332, bf16[4,512,768]{2,1,0:T(8,128)(2,1)} %get-tuple-element.331, s32[]{:T(128)S(6)} %copy.15, f32[2048]{0:T(1024)S(1)} %get-tuple-element.330), kind=kOutput, calls=%fused_computation.5.clone.1 | convolution fusion | flops 1617950720 | bytes 6047748 | tf_op jit(solution)/shard_map/while/body/eval_jaxpr/dot_general | solution.py:37
  108.1 4.6 %select_add_fusion.4 = f32[2048,768]{1,0:T(8,128)S(1)} fusion(f32[2048,768]{1,0:T(8,128)S(1)} %bitcast.33, bf16[512,2048]{1,0:T(8,128)(2,1)S(1)} %get-tuple-element.286, pred[]{:T(512)S(6)} %compare.3, bf16[4,512,768]{2,1,0:T(8,128)(2,1)} %get-tuple-element.331, s32[]{:T(128)S(6)} %copy.15), kind=kOutput, calls=%fused_computation.4.clone.1 | convolution fusion | flops 1613758464 | bytes 15466501 | tf_op jit(solution)/shard_map/while/body/eval_jaxpr/dot_general | solution.py:43
  112.8 2.7 %copy-done = f32[2048,768]{1,0:T(8,128)} copy-done((f32[2048,768]{1,0:T(8,128)}, f32[2048,768]{1,0:T(8,128)S(1)}, u32[]{:S(2)}) %copy-start) | copy-done | bytes 6291480 | tf_op jit(solution)/shard_map/while
  115.5 4.5 %convert_reduce_fusion.2 = (f32[2048]{0:T(1024)S(1)}, bf16[512,2048]{1,0:T(8,128)(2,1)S(1)}) fusion(f32[512]{0:T(512)S(1)} %bitcast.36, bf16[2048,768]{1,0:T(8,128)(2,1)} %get-tuple-element.332, bf16[4,512,768]{2,1,0:T(8,128)(2,1)} %get-tuple-element.331, s32[]{:T(128)S(6)} %copy.15, f32[2048]{0:T(1024)S(1)} %get-tuple-element.330), kind=kOutput, calls=%fused_computation.5.clone.1 | convolution fusion | flops 1617950720 | bytes 6047748 | tf_op jit(solution)/shard_map/while/body/eval_jaxpr/dot_general | solution.py:37
  120.0 4.6 %select_add_fusion.4 = f32[2048,768]{1,0:T(8,128)S(1)} fusion(f32[2048,768]{1,0:T(8,128)S(1)} %bitcast.33, bf16[512,2048]{1,0:T(8,128)(2,1)S(1)} %get-tuple-element.286, pred[]{:T(512)S(6)} %compare.3, bf16[4,512,768]{2,1,0:T(8,128)(2,1)} %get-tuple-element.331, s32[]{:T(128)S(6)} %copy.15), kind=kOutput, calls=%fused_computation.4.clone.1 | convolution fusion | flops 1613758464 | bytes 15466501 | tf_op jit(solution)/shard_map/while/body/eval_jaxpr/dot_general | solution.py:43
  124.6 2.7 %copy-done = f32[2048,768]{1,0:T(8,128)} copy-done((f32[2048,768]{1,0:T(8,128)}, f32[2048,768]{1,0:T(8,128)S(1)}, u32[]{:S(2)}) %copy-start) | copy-done | bytes 6291480 | tf_op jit(solution)/shard_map/while
  127.3 4.5 %convert_reduce_fusion.2 = (f32[2048]{0:T(1024)S(1)}, bf16[512,2048]{1,0:T(8,128)(2,1)S(1)}) fusion(f32[512]{0:T(512)S(1)} %bitcast.36, bf16[2048,768]{1,0:T(8,128)(2,1)} %get-tuple-element.332, bf16[4,512,768]{2,1,0:T(8,128)(2,1)} %get-tuple-element.331, s32[]{:T(128)S(6)} %copy.15, f32[2048]{0:T(1024)S(1)} %get-tuple-element.330), kind=kOutput, calls=%fused_computation.5.clone.1 | convolution fusion | flops 1617950720 | bytes 6047748 | tf_op jit(solution)/shard_map/while/body/eval_jaxpr/dot_general | solution.py:37
  131.9 4.6 %select_add_fusion.4 = f32[2048,768]{1,0:T(8,128)S(1)} fusion(f32[2048,768]{1,0:T(8,128)S(1)} %bitcast.33, bf16[512,2048]{1,0:T(8,128)(2,1)S(1)} %get-tuple-element.286, pred[]{:T(512)S(6)} %compare.3, bf16[4,512,768]{2,1,0:T(8,128)(2,1)} %get-tuple-element.331, s32[]{:T(128)S(6)} %copy.15), kind=kOutput, calls=%fused_computation.4.clone.1 | convolution fusion | flops 1613758464 | bytes 15466501 | tf_op jit(solution)/shard_map/while/body/eval_jaxpr/dot_general | solution.py:43
  136.5 2.7 %copy-done = f32[2048,768]{1,0:T(8,128)} copy-done((f32[2048,768]{1,0:T(8,128)}, f32[2048,768]{1,0:T(8,128)S(1)}, u32[]{:S(2)}) %copy-start) | copy-done | bytes 6291480 | tf_op jit(solution)/shard_map/while
  139.2 4.5 %convert_reduce_fusion.2 = (f32[2048]{0:T(1024)S(1)}, bf16[512,2048]{1,0:T(8,128)(2,1)S(1)}) fusion(f32[512]{0:T(512)S(1)} %bitcast.36, bf16[2048,768]{1,0:T(8,128)(2,1)} %get-tuple-element.332, bf16[4,512,768]{2,1,0:T(8,128)(2,1)} %get-tuple-element.331, s32[]{:T(128)S(6)} %copy.15, f32[2048]{0:T(1024)S(1)} %get-tuple-element.330), kind=kOutput, calls=%fused_computation.5.clone.1 | convolution fusion | flops 1617950720 | bytes 6047748 | tf_op jit(solution)/shard_map/while/body/eval_jaxpr/dot_general | solution.py:37
  143.7 4.6 %select_add_fusion.4 = f32[2048,768]{1,0:T(8,128)S(1)} fusion(f32[2048,768]{1,0:T(8,128)S(1)} %bitcast.33, bf16[512,2048]{1,0:T(8,128)(2,1)S(1)} %get-tuple-element.286, pred[]{:T(512)S(6)} %compare.3, bf16[4,512,768]{2,1,0:T(8,128)(2,1)} %get-tuple-element.331, s32[]{:T(128)S(6)} %copy.15), kind=kOutput, calls=%fused_computation.4.clone.1 | convolution fusion | flops 1613758464 | bytes 15466501 | tf_op jit(solution)/shard_map/while/body/eval_jaxpr/dot_general | solution.py:43
  148.3 2.7 %copy-done = f32[2048,768]{1,0:T(8,128)} copy-done((f32[2048,768]{1,0:T(8,128)}, f32[2048,768]{1,0:T(8,128)S(1)}, u32[]{:S(2)}) %copy-start) | copy-done | bytes 6291480 | tf_op jit(solution)/shard_map/while
  151.0 12.7 %psum.23 = f32[2048]{0:T(1024)S(1)} all-reduce(f32[2048]{0:T(1024)S(1)} %get-tuple-element.159), channel_id=1, replica_groups=mesh['blk'=4,'rows'=8] {'rows'}, use_global_device_ids=true, to_apply=%region_11.12 | all-reduce | flops 2048 | bytes 16384 | tf_op jit(solution)/shard_map/psum | solution.py:64
  163.8 0.6 broadcast_multiply_fusion.1
  164.4 90.0 %all-reduce.2.cloned.1.call-done = f32[2048,768]{1,0:T(8,128)} async-done(((f32[2048,768]{1,0:T(8,128)}), f32[2048,768]{1,0:T(8,128)}) %all-reduce.2.cloned.1.call-update) | async-done | bytes 6291472 | tf_op jit(solution)/shard_map/psum | solution.py:64
  254.4 3.4 %multiply_reduce_fusion = f32[2048]{0:T(1024)S(1)} fusion(f32[2048,768]{1,0:T(8,128)} %all-reduce.2.cloned.1.call-done), kind=kLoop, calls=%fused_computation.19 | loop fusion | flops 3143680 | bytes 6299648 | tf_op jit(solution)/shard_map/reduce_sum | solution.py:23
  257.8 1.2 copy-done.1
  259.0 3.2 %broadcast_multiply_fusion = f32[2048,768]{1,0:T(8,128)} fusion(f32[2048,768]{1,0:T(8,128)S(1)} %copy-done.1, f32[2048]{0:T(1024)S(1)} %add_rsqrt_fusion), kind=kLoop, calls=%fused_computation.20 | loop fusion | flops 1572864 | bytes 12591104 | tf_op jit(solution)/shard_map/mul | solution.py:22
  (49 shorter events, 0.4 us)
Async XLA Ops:
  7.2 3.9 %copy-start.2 = (bf16[2048,768]{1,0:T(8,128)(2,1)S(1)}, bf16[2048,768]{1,0:T(8,128)(2,1)}, u32[]{:S(2)}) copy-start(bf16[2048,768]{1,0:T(8,128)(2,1)} %param.8) | copy-start | bytes 9437188
  7.2 70.2 %all-gather.2.cloned.1.call-start = ((), (), s32[]{:S(2)}) async-start(), calls=%async_computation | async-start | bytes 3932160 | tf_op jit(solution)/shard_map/all_gather | solution.py:31
  11.0 243.4 %all-reduce.2.cloned.1.call-start = ((), (), s32[]{:S(2)}) async-start(), calls=%async_computation.1 | async-start | bytes 12582912 | tf_op jit(solution)/shard_map/psum | solution.py:64
  11.1 66.3 %copy-start.3 = (f32[2048]{0:T(1024)S(1)}, f32[2048]{0:T(1024)}, u32[]{:S(2)}) copy-start(f32[2048]{0:T(1024)} %param.9) | copy-start | bytes 24580
  103.6 4.5 %slice-start = ((s8[6291456]{0:T(1024)(128)(4,1)}), s8[4194304]{0:T(1024)(128)(4,1)S(1)}, s32[]{:S(2)}) async-start(s8[6291456]{0:T(1024)(128)(4,1)} %bitcast.32), calls=%async_computation.2 | async-start | bytes 8388608 | tf_op jit(solution)/shard_map/while
  103.6 4.5 %slice-start.1 = ((s8[6291456]{0:T(1024)(128)(4,1)}), s8[2097152]{0:T(1024)(128)(4,1)S(1)}, s32[]{:S(2)}) async-start(s8[6291456]{0:T(1024)(128)(4,1)} %bitcast.32), calls=%async_computation.3 | async-start | bytes 4194304 | tf_op jit(solution)/shard_map/while
  112.7 2.7 %copy-start = (f32[2048,768]{1,0:T(8,128)}, f32[2048,768]{1,0:T(8,128)S(1)}, u32[]{:S(2)}) copy-start(f32[2048,768]{1,0:T(8,128)S(1)} %select_add_fusion.4) | copy-start | bytes 18874372 | tf_op jit(solution)/shard_map/while
  115.5 4.5 %slice-start = ((s8[6291456]{0:T(1024)(128)(4,1)}), s8[4194304]{0:T(1024)(128)(4,1)S(1)}, s32[]{:S(2)}) async-start(s8[6291456]{0:T(1024)(128)(4,1)} %bitcast.32), calls=%async_computation.2 | async-start | bytes 8388608 | tf_op jit(solution)/shard_map/while
  115.5 4.5 %slice-start.1 = ((s8[6291456]{0:T(1024)(128)(4,1)}), s8[2097152]{0:T(1024)(128)(4,1)S(1)}, s32[]{:S(2)}) async-start(s8[6291456]{0:T(1024)(128)(4,1)} %bitcast.32), calls=%async_computation.3 | async-start | bytes 4194304 | tf_op jit(solution)/shard_map/while
  124.6 2.7 %copy-start = (f32[2048,768]{1,0:T(8,128)}, f32[2048,768]{1,0:T(8,128)S(1)}, u32[]{:S(2)}) copy-start(f32[2048,768]{1,0:T(8,128)S(1)} %select_add_fusion.4) | copy-start | bytes 18874372 | tf_op jit(solution)/shard_map/while
  127.3 4.5 %slice-start = ((s8[6291456]{0:T(1024)(128)(4,1)}), s8[4194304]{0:T(1024)(128)(4,1)S(1)}, s32[]{:S(2)}) async-start(s8[6291456]{0:T(1024)(128)(4,1)} %bitcast.32), calls=%async_computation.2 | async-start | bytes 8388608 | tf_op jit(solution)/shard_map/while
  127.3 4.5 %slice-start.1 = ((s8[6291456]{0:T(1024)(128)(4,1)}), s8[2097152]{0:T(1024)(128)(4,1)S(1)}, s32[]{:S(2)}) async-start(s8[6291456]{0:T(1024)(128)(4,1)} %bitcast.32), calls=%async_computation.3 | async-start | bytes 4194304 | tf_op jit(solution)/shard_map/while
  136.5 2.7 %copy-start = (f32[2048,768]{1,0:T(8,128)}, f32[2048,768]{1,0:T(8,128)S(1)}, u32[]{:S(2)}) copy-start(f32[2048,768]{1,0:T(8,128)S(1)} %select_add_fusion.4) | copy-start | bytes 18874372 | tf_op jit(solution)/shard_map/while
  139.2 4.5 %slice-start = ((s8[6291456]{0:T(1024)(128)(4,1)}), s8[4194304]{0:T(1024)(128)(4,1)S(1)}, s32[]{:S(2)}) async-start(s8[6291456]{0:T(1024)(128)(4,1)} %bitcast.32), calls=%async_computation.2 | async-start | bytes 8388608 | tf_op jit(solution)/shard_map/while
  139.2 4.5 %slice-start.1 = ((s8[6291456]{0:T(1024)(128)(4,1)}), s8[2097152]{0:T(1024)(128)(4,1)S(1)}, s32[]{:S(2)}) async-start(s8[6291456]{0:T(1024)(128)(4,1)} %bitcast.32), calls=%async_computation.3 | async-start | bytes 4194304 | tf_op jit(solution)/shard_map/while
  148.3 2.7 %copy-start = (f32[2048,768]{1,0:T(8,128)}, f32[2048,768]{1,0:T(8,128)S(1)}, u32[]{:S(2)}) copy-start(f32[2048,768]{1,0:T(8,128)S(1)} %select_add_fusion.4) | copy-start | bytes 18874372 | tf_op jit(solution)/shard_map/while
  254.4 4.6 %copy-start.1 = (f32[2048,768]{1,0:T(8,128)S(1)}, f32[2048,768]{1,0:T(8,128)}, u32[]{:S(2)}) copy-start(f32[2048,768]{1,0:T(8,128)} %all-reduce.2.cloned.1.call-done) | copy-start | bytes 18874372
Sparse Core Ops, SparseCore 0:
  11.1 66.1 all-gather.1
  151.2 103.1 all-reduce.1
where the time goes:
time: 269 us
  waiting for transfers between devices  153 us (57%)
  matrix products  53 us (20%)
  blocking collectives  22 us (8%)
  between operations  14.1 us (5%)
  other arithmetic  13.9 us (5%)
  local copies, waits for them, and re-layouts  12.2 us (5%)
    psum x1, waiting for transfers between devices, local(): summed, summed_masses = lax.psum((weighted, masses), 'rows')  90 us
    all_gather x1, waiting for transfers between devices, local(): gathered = lax.all_gather(row_units, 'blk', axis=0, tiled=True)  63.3 us
    dot_general x8, matrix products, exponents(): lax.dot_general(row_block, centroid_units, (((1,), (1,)), ((), ())), pref...  34.6 us
    dot_general x4, matrix products, add_block(): lax.dot_general(resp, row_block, (((0,), (0,)), ((), ())), preferred_elem...  18.4 us
    psum x1, blocking collectives, local(): summed, summed_masses = lax.psum((weighted, masses), 'rows')  12.7 us
    while x24, local copies, waits for them, and re-layouts  10.8 us
    psum x1, blocking collectives, local(): totals = lax.psum(partial_sums, 'blk')  9.24 us
  transfers between devices with their start and end apart: 2, of which 2 were waited for; matrix products, arithmetic and copies ran while one was open for 1% of the time, Pallas kernels for 0%

commit v1 on v0

v1 whole, which is shorter than its diff:
```python
import functools
import math

import jax
import jax.numpy as jnp
from jax import lax
from jax.experimental import pallas as pl
from jax.experimental.pallas import tpu as pltpu
from jax.sharding import PartitionSpec as P

concentration = 32.0
LOG2E = math.log2(math.e)
LANES = 128
VMEM_LIMIT = 48 * 1024 * 1024


def to_unit(values):
    values = values.astype(jnp.float32)
    return (values * lax.rsqrt(jnp.sum(values * values, axis=-1, keepdims=True) + 1e-06)).astype(
        jnp.bfloat16
    )


def arrival_plan(n):
    plan = []
    for place in range(n):
        order = [("own", 0, place)]
        for step in range(1, n):
            if place - step >= 0:
                order.append(("up", step, place - step))
            if place + step < n:
                order.append(("down", step, place + step))
        plan.append(order)
    return plan


def score_kernel(n_sources, picks, *refs):
    sources = refs[:n_sources]
    units_in, log_mix = refs[n_sources], refs[n_sources + 1]
    scores, rows_out, totals, raw, units, sem = refs[-6:]

    @pl.when(pl.program_id(0) == 0)
    def _():
        for number, source in enumerate(sources):

            @pl.when(picks[0] == number)
            def _():
                pltpu.make_async_copy(source, raw, sem).start()

        pltpu.make_async_copy(sources[0], raw, sem).wait()
        values = raw[...].astype(jnp.float32)
        square = jnp.sum(values * values, axis=-1, keepdims=True)
        unit = (values * lax.rsqrt(square + 1e-06)).astype(jnp.bfloat16)
        units[...] = unit
        rows_out[...] = unit
        totals[...] = jnp.zeros_like(totals)

    cosines = lax.dot_general(
        units_in[...], units[...], (((1,), (1,)), ((), ())), preferred_element_type=jnp.float32
    )
    offset = log_mix[...]
    repeats = cosines.shape[1] // offset.shape[1]
    if repeats > 1:
        offset = jnp.concatenate([offset] * repeats, axis=1)
    value = jnp.exp2(cosines * (concentration * LOG2E) + offset)
    scores[...] = value
    totals[0] += jnp.sum(value, axis=0, keepdims=True)


def score_block(picks, sources, centroid_units, offsets, carried, slot, n_slots):
    part, depth = sources[0].shape
    count = centroid_units.shape[0]
    tile = math.gcd(count, 512)
    shapes = (
        jax.ShapeDtypeStruct((count, n_slots * part), jnp.float32),
        jax.ShapeDtypeStruct((n_slots * part, depth), jnp.bfloat16),
        jax.ShapeDtypeStruct((n_slots, 1, part), jnp.float32),
    )
    n_sources = len(sources)
    aliases = {}
    extra = ()
    if carried is not None:
        extra = carried
        aliases = {1 + n_sources + 2 + i: i for i in range(3)}
    anywhere = pl.BlockSpec(memory_space=pl.ANY)
    return pl.pallas_call(
        functools.partial(score_kernel, n_sources),
        grid_spec=pltpu.PrefetchScalarGridSpec(
            num_scalar_prefetch=1,
            grid=(count // tile,),
            in_specs=[anywhere] * n_sources
            + [
                pl.BlockSpec((tile, depth), lambda t, s: (t, 0)),
                pl.BlockSpec((tile, offsets.shape[1]), lambda t, s: (t, 0)),
            ]
            + [anywhere] * len(extra),
            out_specs=[
                pl.BlockSpec((tile, part), lambda t, s: (t, slot)),
                pl.BlockSpec((part, depth), lambda t, s: (slot, 0)),
                pl.BlockSpec((1, 1, part), lambda t, s: (s[1], 0, 0)),
            ],
            scratch_shapes=[
                pltpu.VMEM((part, depth), jnp.bfloat16),
                pltpu.VMEM((part, depth), jnp.bfloat16),
                pltpu.SemaphoreType.DMA,
            ],
        ),
        out_shape=shapes,
        input_output_aliases=aliases,
        compiler_params=pltpu.CompilerParams(vmem_limit_bytes=VMEM_LIMIT),
        cost_estimate=pl.CostEstimate(
            flops=2 * count * part * depth,
            bytes_accessed=count * part * 4 + count * depth * 2,
            transcendentals=count * part,
        ),
        name="scores",
    )(picks, *sources, centroid_units, offsets, *extra)


def sum_kernel(n_totals, n_slots, has_other, order, *refs):
    totals = refs[:n_totals]
    scores, rows = refs[n_totals], refs[n_totals + 1]
    other = refs[n_totals + 2] if has_other else None
    out, masses, inverse = refs[-3:]
    steps = pl.num_programs(0)
    part = scores.shape[1] // n_slots

    @pl.when(pl.program_id(0) == 0)
    def _():
        for slot in range(n_slots):
            place = order[steps + slot]
            total = totals[0][place]
            for more in totals[1:]:
                total = total + more[place]
            inverse[:, slot * part : (slot + 1) * part] = 1.0 / total

    resp = (scores[...] * inverse[...]).astype(jnp.bfloat16)
    weighted = lax.dot_general(
        resp, rows[...], (((1,), (0,)), ((), ())), preferred_element_type=jnp.float32
    )
    wide = resp.astype(jnp.float32)
    mass = wide[:, :LANES]
    for start in range(LANES, wide.shape[1], LANES):
        mass = mass + wide[:, start : start + LANES]
    masses[0] = jnp.sum(mass.T, axis=0, keepdims=True)
    if has_other:
        weighted = weighted + other[0].astype(jnp.float32)
    out[0] = weighted.astype(out.dtype)


def sum_blocks(blocks, slots_of, totals, scores, rows, masses, other, dtype, n_blocks):
    steps = blocks.shape[0]
    count, width = scores.shape
    depth = rows.shape[1]
    size = count // n_blocks
    n_slots = totals[0].shape[0]
    whole = lambda array: pl.BlockSpec(array.shape, lambda t, s: (0,) * array.ndim)
    inputs = [*totals, scores, rows]
    specs = [whole(array) for array in totals] + [
        pl.BlockSpec((size, width), lambda t, s: (s[t], 0)),
        whole(rows),
    ]
    if other is not None:
        inputs.append(other)
        specs.append(pl.BlockSpec((1, size, depth), lambda t, s: (t, 0, 0)))
    aliases = {}
    if masses is not None:
        aliases = {1 + len(inputs): 1}
        inputs.append(masses)
        specs.append(pl.BlockSpec(memory_space=pl.ANY))
    return pl.pallas_call(
        functools.partial(sum_kernel, len(totals), n_slots, other is not None),
        grid_spec=pltpu.PrefetchScalarGridSpec(
            num_scalar_prefetch=1,
            grid=(steps,),
            in_specs=specs,
            out_specs=[
                pl.BlockSpec((1, size, depth), lambda t, s: (t, 0, 0)),
                pl.BlockSpec((1, 1, size), lambda t, s: (s[t], 0, 0)),
            ],
            scratch_shapes=[pltpu.VMEM((1, width), jnp.float32)],
        ),
        out_shape=(
            jax.ShapeDtypeStruct((steps, size, depth), dtype),
            jax.ShapeDtypeStruct((n_blocks, 1, size), jnp.float32),
        ),
        input_output_aliases=aliases,
        compiler_params=pltpu.CompilerParams(vmem_limit_bytes=VMEM_LIMIT),
        cost_estimate=pl.CostEstimate(
            flops=2 * steps * size * width * depth,
            bytes_accessed=steps * size * (width * 4 + depth * 4) + width * depth * 2,
            transcendentals=0,
        ),
        name="sums",
    )(jnp.concatenate([blocks, slots_of]), *inputs)


def local(embeddings, centroids, log_mix):
    n_places = lax.axis_size("blk")
    n_rows = lax.axis_size("rows")
    place = lax.axis_index("blk")
    me = lax.axis_index("rows")
    held, depth = embeddings.shape
    n_parts = 2 if held % (2 * LANES) == 0 else 1
    part = held // n_parts

    moving = {}
    for number in range(n_parts):
        own = embeddings[number * part : (number + 1) * part]
        moving["own", 0, number] = own
        moving["up", 0, number] = own
        moving["down", 0, number] = own
    for step in range(1, n_places):
        for number in range(n_parts):
            moving["up", step, number] = lax.ppermute(
                moving["up", step - 1, number],
                "blk",
                [(i, i + 1) for i in range(step - 1, n_places - 1)],
            )
            moving["down", step, number] = lax.ppermute(
                moving["down", step - 1, number],
                "blk",
                [(i + 1, i) for i in range(0, n_places - step)],
            )

    centroid_units = to_unit(centroids)
    offsets = jnp.broadcast_to(
        ((log_mix - concentration) * LOG2E)[:, None], (log_mix.shape[0], LANES)
    )

    plan = arrival_plan(n_places)
    n_slots = n_places * n_parts
    carried = None
    blocks_of = []
    for turn in range(n_places):
        kinds = sorted({plan[i][turn][:2] for i in range(n_places)})
        source = jnp.array([kinds.index(plan[i][turn][:2]) for i in range(n_places)], jnp.int32)[place]
        block = jnp.array([plan[i][turn][2] for i in range(n_places)], jnp.int32)[place]
        for number in range(n_parts):
            total_slot = block * n_parts + number
            blocks_of.append(total_slot)
            carried = score_block(
                jnp.stack([source, total_slot]),
                [moving[kind + (number,)] for kind in kinds],
                centroid_units,
                offsets,
                carried,
                turn * n_parts + number,
                n_slots,
            )
    scores, rows, totals = carried
    all_totals = [totals] + [
        lax.ppermute(totals, "blk", [(i, (i + turn) % n_places) for i in range(n_places)])
        for turn in range(1, n_places)
    ]
    slots_of = jnp.stack(blocks_of).astype(jnp.int32)

    def exchange(array, distance):
        return lax.ppermute(array, "rows", [(i, i ^ distance) for i in range(n_rows)])

    def blocks(distances):
        return jnp.stack([me ^ distance for distance in distances]).astype(jnp.int32)

    far = list(range(2, n_rows, 2))
    args = (slots_of, all_totals, scores, rows)
    given, masses = sum_blocks(
        blocks([d ^ 1 for d in far]), *args, None, None, jnp.bfloat16, n_rows
    )
    taken = exchange(given, 1)
    near, masses = sum_blocks(blocks([1]), *args, masses, None, jnp.bfloat16, n_rows)
    near = exchange(near, 1)
    mine, masses = sum_blocks(blocks([0]), *args, masses, None, jnp.float32, n_rows)
    sent, masses = sum_blocks(blocks(far), *args, masses, taken, jnp.bfloat16, n_rows)
    summed = mine[0] + near[0].astype(jnp.float32)
    arrived = [exchange(sent[number], distance) for number, distance in enumerate(far)]
    for array in arrived:
        summed = summed + array.astype(jnp.float32)

    distance = 1
    while distance < n_rows:
        masses = masses + exchange(masses, distance)
        distance *= 2

    unit = summed * lax.rsqrt(jnp.sum(summed * summed, axis=1, keepdims=True) + 1e-06)
    unit = unit.astype(jnp.float16)
    size = unit.shape[0]
    pieces = {0: unit}
    for distance in far:
        pieces[distance] = exchange(unit, distance)
    for distance in [0] + far:
        pieces[distance ^ 1] = exchange(pieces[distance], 1)
    result = jnp.zeros((size * n_rows, depth), jnp.float32)
    for distance, piece in pieces.items():
        result = lax.dynamic_update_slice(
            result, piece.astype(jnp.float32), ((me ^ distance) * size, 0)
        )
    count = size * n_rows * n_places
    factor = count / (held * n_rows * n_places)
    return (result, masses.reshape(-1) * factor)


def solution(mesh):
    return jax.shard_map(
        local,
        mesh=mesh,
        in_specs=(P(("blk", "rows"), None), P("blk", None), P("blk")),
        out_specs=(P("blk", None), P("blk")),
        check_vma=False,
    )
```

time: 269 us -> 184 us (0.68)
  waiting for transfers between devices: 153 us -> 42.7 us
  Pallas kernels: 0 us -> 66.3 us
  matrix products: 53 us -> 0 us
  starting transfers between devices: 0.08 us -> 40.8 us
  blocking collectives: 22 us -> 0 us
  between operations: 14.1 us -> 3.09 us
  other arithmetic: 13.9 us -> 21 us
  local copies, waits for them, and re-layouts: 12.2 us -> 8.52 us
    psum x1 -> x0, waiting for transfers between devices: 90 us -> none  [local(): summed, summed_masses = lax.psum((weighted, masses), 'rows')]
    pallas_call x0 -> x12, Pallas kernels: none -> 66.3 us  [the longest x8 46.8 us: score_block(): pl.pallas_call(functools.partial(score_kernel, n_sources), grid_spec=pltp...]
    all_gather x1 -> x0, waiting for transfers between devices: 63.3 us -> none  [local(): gathered = lax.all_gather(row_units, 'blk', axis=0, tiled=True)]
    dot_general x12 -> x0, matrix products: 53 us -> none  [the longest x8 34.6 us: exponents(): lax.dot_general(row_block, centroid_units, (((1,), (1,)), ((), ())), pref...]
    ppermute x0 -> x30, waiting for transfers between devices: none -> 42.7 us  [the longest x15 34.1 us: exchange(): lax.ppermute(array, 'rows', [(i, i ^ distance) for i in range(n_rows)])]
    ppermute x0 -> x30, starting transfers between devices: none -> 40.8 us  [the longest x6 13.6 us: local(): lax.ppermute(moving['up', step - 1, number], 'blk', [(i, i + 1) for i in...]
    psum x2 -> x0, blocking collectives: 22 us -> none  [the longest x1 12.7 us: local(): summed, summed_masses = lax.psum((weighted, masses), 'rows')]
    while x24 -> x0, local copies, waits for them, and re-layouts: 10.8 us -> none
  transfers between devices with their start and end apart: 2 -> 30, of which waited for: 2 -> 8; matrix products, arithmetic and copies ran while one was open for 1% -> 12% of each run, Pallas kernels for 0% -> 30%
where the time goes in v1:
time: 184 us; the launch traced here: 182 us
  Pallas kernels  66.3 us (36%)
  waiting for transfers between devices  42.7 us (23%)
  starting transfers between devices  40.8 us (22%)
  other arithmetic  21 us (11%)
  local copies, waits for them, and re-layouts  8.52 us (5%)
  between operations  3.09 us (2%)
    pallas_call x8, Pallas kernels, score_block(): pl.pallas_call(functools.partial(score_kernel, n_sources), grid_spec=pltp...  46.8 us
    ppermute x15, waiting for transfers between devices, exchange(): lax.ppermute(array, 'rows', [(i, i ^ distance) for i in range(n_rows)])  34.1 us
    pallas_call x4, Pallas kernels, sum_blocks(): pl.pallas_call(functools.partial(sum_kernel, len(totals), n_slots, other...  19.5 us
    ppermute x6, starting transfers between devices, local(): lax.ppermute(moving['up', step - 1, number], 'blk', [(i, i + 1) for i in...  13.6 us
    ppermute x15, starting transfers between devices, exchange(): lax.ppermute(array, 'rows', [(i, i ^ distance) for i in range(n_rows)])  10.5 us
    ppermute x3, starting transfers between devices, local(): lax.ppermute(totals, 'blk', [(i, (i + turn) % n_places) for i in range(n_...  8.98 us
    dynamic_update_slice x8, other arithmetic, local(): lax.dynamic_update_slice(result, piece.astype(jnp.float32), ((me ^ distan...  7.8 us
    ppermute x6, starting transfers between devices, local(): lax.ppermute(moving['down', step - 1, number], 'blk', [(i + 1, i) for i i...  7.71 us
  transfers between devices with their start and end apart: 30, of which 8 were waited for; matrix products, arithmetic and copies ran while one was open for 12% of the time, Pallas kernels for 30%

profile of v1, /device:TPU:0, one launch (start us, length us, event | category | flops | bytes accessed | tf_op | source)
XLA Modules:
  0.0 182.4 jit_solution(4299378308820744290)
XLA Ops:
  1.9 1.3 collective-permute-start.6
  3.2 5.6 %collective-permute-start.9 = (bf16[256,768]{1,0:T(8,128)(2,1)S(1)}, bf16[256,768]{1,0:T(8,128)(2,1)S(1)}, u32[]{:S(2)}, u32[]{:S(2)}) collective-permute-start(bf16[256,768]{1,0:T(8,128)(2,1)S(1)} %get-tuple-element.71.refs_0_), channel_id=1, source_target_pairs={{0,8},{8,16},{16,24},{1,9},{9,17},{17,25},{2,10},{10,18},{18,26},{... | collective-permute-start | bytes 1179656 | tf_op jit(solution)/shard_map/ppermute | solution.py:215
  8.8 1.3 collective-permute-start
  10.1 5.3 %collective-permute-start.3 = (bf16[256,768]{1,0:T(8,128)(2,1)S(1)}, bf16[256,768]{1,0:T(8,128)(2,1)}, u32[]{:S(2)}, u32[]{:S(2)}) collective-permute-start(bf16[256,768]{1,0:T(8,128)(2,1)S(1)} %get-tuple-element.72.refs_0_), channel_id=1, source_target_pairs={{0,8},{8,16},{16,24},{1,9},{9,17},{17,25},{2,10},{10,18},{18,26},{... | collective-permute-start | bytes 1179656 | tf_op jit(solution)/shard_map/ppermute | solution.py:215
  15.4 2.6 %fusion = f32[2048]{0:T(1024)S(1)} fusion(bf16[2048,768]{1,0:T(8,128)(2,1)} %param.12), kind=kLoop, calls=%fused_computation.2 | loop fusion | flops 4716544 | bytes 3153920 | tf_op jit(solution)/shard_map/reduce_sum | solution.py:19
  18.0 4.1 %fusion.1.refs_1_.refs_2_.refs_3_.refs_4_ = bf16[2048,768]{1,0:T(8,128)(2,1)} fusion(bf16[2048,768]{1,0:T(8,128)(2,1)} %param.12, f32[2048]{0:T(1024)S(1)} %add_rsqrt_fusion), kind=kLoop, calls=%fused_computation.3 | loop fusion | flops 4718592 | bytes 6299648 | tf_op jit(solution)/shard_map/convert_element_type | solution.py:19
  37.4 7.0 %collective-permute-done.7.refs_1_.refs_0_ = bf16[256,768]{1,0:T(8,128)(2,1)S(1)} collective-permute-done((bf16[256,768]{1,0:T(8,128)(2,1)S(1)}, bf16[256,768]{1,0:T(8,128)(2,1)S(1)}, u32[]{:S(2)}, u32[]{:S(2)}) %collective-permute-start.7) | collective-permute-done | bytes 393248 | tf_op jit(solution)/shard_map/ppermute | solution.py:220
  46.8 5.7 %scores.8 = (f32[2048,2048]{1,0:T(8,128)}, bf16[2048,768]{1,0:T(8,128)(2,1)S(1)}, f32[8,1,256]{2,1,0:T(1,128)S(1)}) custom-call(s32[2]{0:T(128)S(1)} %pad_add_fusion.6.picks, bf16[256,768]{1,0:T(8,128)(2,1)S(1)} %get-tuple-element.71.refs_0_, bf16[2048,768]{1,0:T(8,128)(2,1)} %fusion.1.refs_1_.refs_2_.refs_3_.refs_4_, ...), custom_call_target="tpu_custom_call" | custom-call | flops 805306368 | bytes 5242880 | tf_op jit(solution)/shard_map/scores/pallas_call | solution.py:86
  55.8 5.7 %scores.9 = (f32[2048,2048]{1,0:T(8,128)}, bf16[2048,768]{1,0:T(8,128)(2,1)S(1)}, f32[8,1,256]{2,1,0:T(1,128)S(1)}) custom-call(s32[2]{0:T(128)S(1)} %pad.picks, bf16[256,768]{1,0:T(8,128)(2,1)S(1)} %copy-done.3, bf16[2048,768]{1,0:T(8,128)(2,1)} %fusion.1.refs_1_.refs_2_.refs_3_.refs_4_, ...), custom_call_target="tpu_custom_call", output_to_operand_aliasing={{0}: (4, {}), {1}: (5, {}), {2}: (6, {})} | custom-call | flops 805306368 | bytes 5242880 | tf_op jit(solution)/shard_map/scores/pallas_call | solution.py:86
  61.6 5.7 %scores.10 = (f32[2048,2048]{1,0:T(8,128)}, bf16[2048,768]{1,0:T(8,128)(2,1)S(1)}, f32[8,1,256]{2,1,0:T(1,128)S(1)}) custom-call(s32[2]{0:T(128)S(1)} %pad_add_fusion.5.picks, bf16[256,768]{1,0:T(8,128)(2,1)S(1)} %copy-done.5, bf16[256,768]{1,0:T(8,128)(2,1)S(1)} %copy-done.7, ...), custom_call_target="tpu_custom_call", output_to_operand_aliasing={{0}: (5, {}), {1}: (6, {}), {2}: (7, {})} | custom-call | flops 805306368 | bytes 5242880 | tf_op jit(solution)/shard_map/scores/pallas_call | solution.py:86
  67.3 6.6 %scores.11 = (f32[2048,2048]{1,0:T(8,128)}, bf16[2048,768]{1,0:T(8,128)(2,1)S(1)}, f32[8,1,256]{2,1,0:T(1,128)S(1)}) custom-call(s32[2]{0:T(128)S(1)} %pad_add_fusion.4.picks, bf16[256,768]{1,0:T(8,128)(2,1)} %collective-permute-done.refs_0_, ...), custom_call_target="tpu_custom_call", output_to_operand_aliasing={{0}: (5, {}), {1}: (6, {}), {2}: (7, {})} | custom-call | flops 805306368 | bytes 5242880 | tf_op jit(solution)/shard_map/scores/pallas_call | solution.py:86
  73.9 5.7 %scores.12 = (f32[2048,2048]{1,0:T(8,128)}, bf16[2048,768]{1,0:T(8,128)(2,1)S(1)}, f32[8,1,256]{2,1,0:T(1,128)S(1)}) custom-call(s32[2]{0:T(128)S(1)} %pad_add_fusion.3.picks, bf16[256,768]{1,0:T(8,128)(2,1)S(1)} %copy-done.5, ...), custom_call_target="tpu_custom_call", output_to_operand_aliasing={{0}: (6, {}), {1}: (7, {}), {2}: (8, {})} | custom-call | flops 805306368 | bytes 5242880 | tf_op jit(solution)/shard_map/scores/pallas_call | solution.py:86
  79.7 5.7 %scores.13 = (f32[2048,2048]{1,0:T(8,128)}, bf16[2048,768]{1,0:T(8,128)(2,1)S(1)}, f32[8,1,256]{2,1,0:T(1,128)S(1)}) custom-call(s32[2]{0:T(128)S(1)} %pad_add_fusion.2.picks, bf16[256,768]{1,0:T(8,128)(2,1)} %collective-permute-done.refs_0_, ...), custom_call_target="tpu_custom_call", output_to_operand_aliasing={{0}: (6, {}), {1}: (7, {}), {2}: (8, {})} | custom-call | flops 805306368 | bytes 5242880 | tf_op jit(solution)/shard_map/scores/pallas_call | solution.py:86
  85.4 5.8 %scores.14 = (f32[2048,2048]{1,0:T(8,128)}, bf16[2048,768]{1,0:T(8,128)(2,1)S(1)}, f32[8,1,256]{2,1,0:T(1,128)S(1)}) custom-call(s32[2]{0:T(128)S(1)} %pad_add_fusion.1.picks, bf16[256,768]{1,0:T(8,128)(2,1)S(1)} %collective-permute-done.7.refs_1_.refs_0_, ...), custom_call_target="tpu_custom_call", output_to_operand_aliasing={{0}: (7, {}), {1}: (8, {}), {2}: (9, {})} | custom-call | flops 805306368 | bytes 5242880 | tf_op jit(solution)/shard_map/scores/pallas_call | solution.py:86
  91.2 5.8 %scores.15 = (f32[2048,2048]{1,0:T(8,128)}, bf16[2048,768]{1,0:T(8,128)(2,1)S(1)}, f32[8,1,256]{2,1,0:T(1,128)S(1)}) custom-call(s32[2]{0:T(128)S(1)} %pad_add_fusion.picks, bf16[256,768]{1,0:T(8,128)(2,1)S(1)} %collective-permute-done.1.refs_1_.refs_0_, ...), custom_call_target="tpu_custom_call", output_to_operand_aliasing={{0}: (7, {}), {1}: (8, {}), {2}: (9, {})} | custom-call | flops 805306368 | bytes 5242880 | tf_op jit(solution)/shard_map/scores/pallas_call | solution.py:86
  97.0 3.6 %collective-permute-start.12 = (f32[8,1,256]{2,1,0:T(1,128)S(1)}, f32[8,1,256]{2,1,0:T(1,128)S(1)}, u32[]{:S(2)}, u32[]{:S(2)}) collective-permute-start(f32[8,1,256]{2,1,0:T(1,128)S(1)} %get-tuple-element.55.refs_0_), channel_id=1, source_target_pairs={{0,8},{8,16},{16,24},{24,0},{1,9},{9,17},{17,25},{25,1},{2,10},{10... | collective-permute-start | bytes 24584 | tf_op jit(solution)/shard_map/ppermute | solution.py:253
  100.6 2.5 %collective-permute-start.13 = (f32[8,1,256]{2,1,0:T(1,128)S(1)}, f32[8,1,256]{2,1,0:T(1,128)S(1)}, u32[]{:S(2)}, u32[]{:S(2)}) collective-permute-start(f32[8,1,256]{2,1,0:T(1,128)S(1)} %get-tuple-element.55.refs_0_), channel_id=1, source_target_pairs={{0,16},{8,24},{16,0},{24,8},{1,17},{9,25},{17,1},{25,9},{2,18},{10... | collective-permute-start | bytes 24584 | tf_op jit(solution)/shard_map/ppermute | solution.py:253
  103.1 2.8 %collective-permute-start.14 = (f32[8,1,256]{2,1,0:T(1,128)S(1)}, f32[8,1,256]{2,1,0:T(1,128)S(1)}, u32[]{:S(2)}, u32[]{:S(2)}) collective-permute-start(f32[8,1,256]{2,1,0:T(1,128)S(1)} %get-tuple-element.55.refs_0_), channel_id=1, source_target_pairs={{0,24},{8,0},{16,8},{24,16},{1,25},{9,1},{17,9},{25,17},{2,26},{10... | collective-permute-start | bytes 24584 | tf_op jit(solution)/shard_map/ppermute | solution.py:253
  107.3 6.6 %sums.4 = (bf16[3,256,768]{2,1,0:T(8,128)(2,1)}, f32[8,1,256]{2,1,0:T(1,128)S(1)}) custom-call(s32[11]{0:T(128)S(1)} %concatenate.18.order, f32[8,1,256]{2,1,0:T(1,128)S(1)} %get-tuple-element.55.refs_0_, f32[8,1,256]{2,1,0:T(1,128)S(1)} %collective-permute-done.12.refs_1_, f32[8,1,256]{2,1,0:T(1,128)S(1)} %collective-permute-done.13.refs_2_, ...), custom_call_target="tpu_custom_call" | custom-call | flops 2415919104 | bytes 11796480 | tf_op jit(solution)/shard_map/sums/pallas_call | solution.py:171
  114.2 3.9 %sums.5 = (bf16[1,256,768]{2,1,0:T(8,128)(2,1)}, f32[8,1,256]{2,1,0:T(1,128)S(1)}) custom-call(s32[9]{0:T(128)S(1)} %concatenate.17.order, f32[8,1,256]{2,1,0:T(1,128)S(1)} %get-tuple-element.55.refs_0_, f32[8,1,256]{2,1,0:T(1,128)S(1)} %collective-permute-done.12.refs_1_, ...), custom_call_target="tpu_custom_call", output_to_operand_aliasing={{1}: (7, {})} | custom-call | flops 805306368 | bytes 6029312 | tf_op jit(solution)/shard_map/sums/pallas_call | solution.py:171
  118.6 3.1 %sums.6 = (f32[1,256,768]{2,1,0:T(8,128)S(1)}, f32[8,1,256]{2,1,0:T(1,128)S(1)}) custom-call(s32[9]{0:T(128)S(1)} %concatenate.16.order, f32[8,1,256]{2,1,0:T(1,128)S(1)} %get-tuple-element.55.refs_0_, f32[8,1,256]{2,1,0:T(1,128)S(1)} %collective-permute-done.12.refs_1_, ...), custom_call_target="tpu_custom_call", output_to_operand_aliasing={{1}: (7, {})} | custom-call | flops 805306368 | bytes 6029312 | tf_op jit(solution)/shard_map/sums/pallas_call | solution.py:171
  121.8 5.9 %sums.7 = (bf16[3,256,768]{2,1,0:T(8,128)(2,1)S(1)}, f32[8,1,256]{2,1,0:T(1,128)S(1)}) custom-call(s32[11]{0:T(128)S(1)} %concatenate.19.order, f32[8,1,256]{2,1,0:T(1,128)S(1)} %get-tuple-element.55.refs_0_, f32[8,1,256]{2,1,0:T(1,128)S(1)} %collective-permute-done.12.refs_1_, ...), custom_call_target="tpu_custom_call", output_to_operand_aliasing={{1}: (8, {})} | custom-call | flops 2415919104 | bytes 11796480 | tf_op jit(solution)/shard_map/sums/pallas_call | solution.py:171
  127.8 1.6 collective-permute-start.17
  129.3 1.5 collective-permute-start.18
  131.3 8.5 %collective-permute-done.17 = bf16[256,768]{1,0:T(8,128)(2,1)S(1)} collective-permute-done((bf16[256,768]{1,0:T(8,128)(2,1)S(1)}, bf16[256,768]{1,0:T(8,128)(2,1)S(1)}, u32[]{:S(2)}, u32[]{:S(2)}) %collective-permute-start.17) | collective-permute-done | bytes 393248 | tf_op jit(solution)/shard_map/ppermute | solution.py:259
  139.8 8.7 %collective-permute-done.18 = bf16[256,768]{1,0:T(8,128)(2,1)S(1)} collective-permute-done((bf16[256,768]{1,0:T(8,128)(2,1)S(1)}, bf16[256,768]{1,0:T(8,128)(2,1)S(1)}, u32[]{:S(2)}, u32[]{:S(2)}) %collective-permute-start.18) | collective-permute-done | bytes 393248 | tf_op jit(solution)/shard_map/ppermute | solution.py:259
  148.5 1.6 multiply_reduce_fusion
  151.8 1.3 collective-permute-start.20
  153.9 1.4 collective-permute-start.22
  156.5 1.3 collective-permute-start.28
  157.8 12.6 %collective-permute-done.28 = f32[8,1,256]{2,1,0:T(1,128)S(1)} collective-permute-done((f32[8,1,256]{2,1,0:T(1,128)S(1)}, f32[8,1,256]{2,1,0:T(1,128)S(1)}, u32[]{:S(2)}, u32[]{:S(2)}) %collective-permute-start.28) | collective-permute-done | bytes 8224 | tf_op jit(solution)/shard_map/ppermute | solution.py:259
  171.1 3.1 %collective-permute-done.29 = f32[8,1,256]{2,1,0:T(1,128)S(1)} collective-permute-done((f32[8,1,256]{2,1,0:T(1,128)S(1)}, f32[8,1,256]{2,1,0:T(1,128)S(1)}, u32[]{:S(2)}, u32[]{:S(2)}) %collective-permute-start.29) | collective-permute-done | bytes 8224 | tf_op jit(solution)/shard_map/ppermute | solution.py:259
  (111 shorter events, 35.3 us)
Async XLA Ops:
  0.7 36.7 %copy-start.9 = (f32[2048]{0:T(1024)S(1)}, f32[2048]{0:T(1024)}, u32[]{:S(2)}) copy-start(f32[2048]{0:T(1024)} %param.13) | copy-start | bytes 24580
  1.9 44.5 %copy-start.2 = (bf16[256,768]{1,0:T(8,128)(2,1)}, bf16[256,768]{1,0:T(8,128)(2,1)S(1)}, u32[]{:S(2)}) copy-start(bf16[256,768]{1,0:T(8,128)(2,1)S(1)} %get-tuple-element.72.refs_0_) | copy-start | bytes 1179652
  1.9 29.2 %collective-permute-start.6 = (bf16[256,768]{1,0:T(8,128)(2,1)S(1)}, bf16[256,768]{1,0:T(8,128)(2,1)S(1)}, u32[]{:S(2)}, u32[]{:S(2)}) collective-permute-start(bf16[256,768]{1,0:T(8,128)(2,1)S(1)} %get-tuple-element.71.refs_0_), channel_id=1, source_target_pairs={{8,0},{16,8},{24,16},{9,1},{17,9},{25,17},{10,2},{18,10},{26,18},{... | collective-permute-start | bytes 1179656 | tf_op jit(solution)/shard_map/ppermute | solution.py:220
  3.2 30.0 %collective-permute-start.9 = (bf16[256,768]{1,0:T(8,128)(2,1)S(1)}, bf16[256,768]{1,0:T(8,128)(2,1)S(1)}, u32[]{:S(2)}, u32[]{:S(2)}) collective-permute-start(bf16[256,768]{1,0:T(8,128)(2,1)S(1)} %get-tuple-element.71.refs_0_), channel_id=1, source_target_pairs={{0,8},{8,16},{16,24},{1,9},{9,17},{17,25},{2,10},{10,18},{18,26},{... | collective-permute-start | bytes 1179656 | tf_op jit(solution)/shard_map/ppermute | solution.py:215
  8.8 26.5 %collective-permute-start = (bf16[256,768]{1,0:T(8,128)(2,1)S(1)}, bf16[256,768]{1,0:T(8,128)(2,1)}, u32[]{:S(2)}, u32[]{:S(2)}) collective-permute-start(bf16[256,768]{1,0:T(8,128)(2,1)S(1)} %get-tuple-element.72.refs_0_), channel_id=1, source_target_pairs={{8,0},{16,8},{24,16},{9,1},{17,9},{25,17},{10,2},{18,10},{26,18},{... | collective-permute-start | bytes 1179656 | tf_op jit(solution)/shard_map/ppermute | solution.py:220
  10.1 26.5 %collective-permute-start.3 = (bf16[256,768]{1,0:T(8,128)(2,1)S(1)}, bf16[256,768]{1,0:T(8,128)(2,1)}, u32[]{:S(2)}, u32[]{:S(2)}) collective-permute-start(bf16[256,768]{1,0:T(8,128)(2,1)S(1)} %get-tuple-element.72.refs_0_), channel_id=1, source_target_pairs={{0,8},{8,16},{16,24},{1,9},{9,17},{17,25},{2,10},{10,18},{18,26},{... | collective-permute-start | bytes 1179656 | tf_op jit(solution)/shard_map/ppermute | solution.py:215
  31.1 13.3 %collective-permute-start.7 = (bf16[256,768]{1,0:T(8,128)(2,1)S(1)}, bf16[256,768]{1,0:T(8,128)(2,1)S(1)}, u32[]{:S(2)}, u32[]{:S(2)}) collective-permute-start(bf16[256,768]{1,0:T(8,128)(2,1)S(1)} %collective-permute-done.6.refs_0_), channel_id=1, source_target_pairs={{8,0},{16,8},{9,1},{17,9},{10,2},{18,10},{11,3},{19,11},{12,4},{20... | collective-permute-start | bytes 1179656 | tf_op jit(solution)/shard_map/ppermute | solution.py:220
  33.2 12.5 %collective-permute-start.10 = (bf16[256,768]{1,0:T(8,128)(2,1)S(1)}, bf16[256,768]{1,0:T(8,128)(2,1)S(1)}, u32[]{:S(2)}, u32[]{:S(2)}) collective-permute-start(bf16[256,768]{1,0:T(8,128)(2,1)S(1)} %collective-permute-done.9.refs_1_), channel_id=1, source_target_pairs={{8,16},{16,24},{9,17},{17,25},{10,18},{18,26},{11,19},{19,27},{12,... | collective-permute-start | bytes 1179656 | tf_op jit(solution)/shard_map/ppermute | solution.py:215
  35.4 17.5 %collective-permute-start.1 = (bf16[256,768]{1,0:T(8,128)(2,1)}, bf16[256,768]{1,0:T(8,128)(2,1)S(1)}, u32[]{:S(2)}, u32[]{:S(2)}) collective-permute-start(bf16[256,768]{1,0:T(8,128)(2,1)} %collective-permute-done.refs_0_), channel_id=1, source_target_pairs={{8,0},{16,8},{9,1},{17,9},{10,2},{18,10},{11,3},{19,11},{12,4},{20... | collective-permute-start | bytes 1179656 | tf_op jit(solution)/shard_map/ppermute | solution.py:220
  36.6 17.5 %collective-permute-start.4 = (bf16[256,768]{1,0:T(8,128)(2,1)}, bf16[256,768]{1,0:T(8,128)(2,1)S(1)}, u32[]{:S(2)}, u32[]{:S(2)}) collective-permute-start(bf16[256,768]{1,0:T(8,128)(2,1)} %collective-permute-done.3.refs_1_), channel_id=1, source_target_pairs={{8,16},{16,24},{9,17},{17,25},{10,18},{18,26},{11,19},{19,27},{12,... | collective-permute-start | bytes 1179656 | tf_op jit(solution)/shard_map/ppermute | solution.py:215
  44.4 41.0 %collective-permute-start.8 = (bf16[256,768]{1,0:T(8,128)(2,1)S(1)}, bf16[256,768]{1,0:T(8,128)(2,1)S(1)}, u32[]{:S(2)}, u32[]{:S(2)}) collective-permute-start(bf16[256,768]{1,0:T(8,128)(2,1)S(1)} %collective-permute-done.7.refs_1_.refs_0_), channel_id=1, source_target_pairs={{8,0},{9,1},{10,2},{11,3},{12,4},{13,5},{14,6},{15,7}} | collective-permute-start | bytes 1179656 | tf_op jit(solution)/shard_map/ppermute | solution.py:220
  45.7 39.7 %collective-permute-start.11 = (bf16[256,768]{1,0:T(8,128)(2,1)S(1)}, bf16[256,768]{1,0:T(8,128)(2,1)S(1)}, u32[]{:S(2)}, u32[]{:S(2)}) collective-permute-start(bf16[256,768]{1,0:T(8,128)(2,1)S(1)} %collective-permute-done.10.refs_2_), channel_id=1, source_target_pairs={{16,24},{17,25},{18,26},{19,27},{20,28},{21,29},{22,30},{23,31}} | collective-permute-start | bytes 1179656 | tf_op jit(solution)/shard_map/ppermute | solution.py:215
  52.8 38.4 %collective-permute-start.2 = (bf16[256,768]{1,0:T(8,128)(2,1)S(1)}, bf16[256,768]{1,0:T(8,128)(2,1)S(1)}, u32[]{:S(2)}, u32[]{:S(2)}) collective-permute-start(bf16[256,768]{1,0:T(8,128)(2,1)S(1)} %collective-permute-done.1.refs_1_.refs_0_), channel_id=1, source_target_pairs={{8,0},{9,1},{10,2},{11,3},{12,4},{13,5},{14,6},{15,7}} | collective-permute-start | bytes 1179656 | tf_op jit(solution)/shard_map/ppermute | solution.py:220
  54.1 37.1 %collective-permute-start.5 = (bf16[256,768]{1,0:T(8,128)(2,1)S(1)}, bf16[256,768]{1,0:T(8,128)(2,1)S(1)}, u32[]{:S(2)}, u32[]{:S(2)}) collective-permute-start(bf16[256,768]{1,0:T(8,128)(2,1)S(1)} %collective-permute-done.4.refs_2_), channel_id=1, source_target_pairs={{16,24},{17,25},{18,26},{19,27},{20,28},{21,29},{22,30},{23,31}} | collective-permute-start | bytes 1179656 | tf_op jit(solution)/shard_map/ppermute | solution.py:215
  97.0 9.1 %collective-permute-start.12 = (f32[8,1,256]{2,1,0:T(1,128)S(1)}, f32[8,1,256]{2,1,0:T(1,128)S(1)}, u32[]{:S(2)}, u32[]{:S(2)}) collective-permute-start(f32[8,1,256]{2,1,0:T(1,128)S(1)} %get-tuple-element.55.refs_0_), channel_id=1, source_target_pairs={{0,8},{8,16},{16,24},{24,0},{1,9},{9,17},{17,25},{25,1},{2,10},{10... | collective-permute-start | bytes 24584 | tf_op jit(solution)/shard_map/ppermute | solution.py:253
  100.6 5.5 %collective-permute-start.13 = (f32[8,1,256]{2,1,0:T(1,128)S(1)}, f32[8,1,256]{2,1,0:T(1,128)S(1)}, u32[]{:S(2)}, u32[]{:S(2)}) collective-permute-start(f32[8,1,256]{2,1,0:T(1,128)S(1)} %get-tuple-element.55.refs_0_), channel_id=1, source_target_pairs={{0,16},{8,24},{16,0},{24,8},{1,17},{9,25},{17,1},{25,9},{2,18},{10... | collective-permute-start | bytes 24584 | tf_op jit(solution)/shard_map/ppermute | solution.py:253
  103.1 4.2 %collective-permute-start.14 = (f32[8,1,256]{2,1,0:T(1,128)S(1)}, f32[8,1,256]{2,1,0:T(1,128)S(1)}, u32[]{:S(2)}, u32[]{:S(2)}) collective-permute-start(f32[8,1,256]{2,1,0:T(1,128)S(1)} %get-tuple-element.55.refs_0_), channel_id=1, source_target_pairs={{0,24},{8,0},{16,8},{24,16},{1,25},{9,1},{17,9},{25,17},{2,26},{10... | collective-permute-start | bytes 24584 | tf_op jit(solution)/shard_map/ppermute | solution.py:253
  114.0 7.8 %collective-permute-start.16 = (bf16[3,256,768]{2,1,0:T(8,128)(2,1)}, bf16[3,256,768]{2,1,0:T(8,128)(2,1)}, u32[]{:S(2)}, u32[]{:S(2)}) collective-permute-start(bf16[3,256,768]{2,1,0:T(8,128)(2,1)} %get-tuple-element.62), channel_id=1, source_target_pairs={{0,1},{1,0},{2,3},{3,2},{4,5},{5,4},{6,7},{7,6},{8,9},{9,8},{10,11... | collective-permute-start | bytes 3538952 | tf_op jit(solution)/shard_map/ppermute | solution.py:259
  118.1 13.2 %collective-permute-start.15 = (bf16[1,256,768]{2,1,0:T(8,128)(2,1)}, bf16[1,256,768]{2,1,0:T(8,128)(2,1)}, u32[]{:S(2)}, u32[]{:S(2)}) collective-permute-start(bf16[1,256,768]{2,1,0:T(8,128)(2,1)} %get-tuple-element.61), channel_id=1, source_target_pairs={{0,1},{1,0},{2,3},{3,2},{4,5},{5,4},{6,7},{7,6},{8,9},{9,8},{10,11... | collective-permute-start | bytes 1179656 | tf_op jit(solution)/shard_map/ppermute | solution.py:259
  127.8 12.0 %collective-permute-start.17 = (bf16[256,768]{1,0:T(8,128)(2,1)S(1)}, bf16[256,768]{1,0:T(8,128)(2,1)S(1)}, u32[]{:S(2)}, u32[]{:S(2)}) collective-permute-start(bf16[256,768]{1,0:T(8,128)(2,1)S(1)} %get-tuple-element.68), channel_id=1, source_target_pairs={{0,2},{1,3},{2,0},{3,1},{4,6},{5,7},{6,4},{7,5},{8,10},{9,11},{10,... | collective-permute-start | bytes 1179656 | tf_op jit(solution)/shard_map/ppermute | solution.py:259
  129.3 19.2 %collective-permute-start.18 = (bf16[256,768]{1,0:T(8,128)(2,1)S(1)}, bf16[256,768]{1,0:T(8,128)(2,1)S(1)}, u32[]{:S(2)}, u32[]{:S(2)}) collective-permute-start(bf16[256,768]{1,0:T(8,128)(2,1)S(1)} %get-tuple-element.70), channel_id=1, source_target_pairs={{0,4},{1,5},{2,6},{3,7},{4,0},{5,1},{6,2},{7,3},{8,12},{9,13},{10,... | collective-permute-start | bytes 1179656 | tf_op jit(solution)/shard_map/ppermute | solution.py:259
  130.8 17.7 %collective-permute-start.19 = (bf16[256,768]{1,0:T(8,128)(2,1)S(1)}, bf16[256,768]{1,0:T(8,128)(2,1)S(1)}, u32[]{:S(2)}, u32[]{:S(2)}) collective-permute-start(bf16[256,768]{1,0:T(8,128)(2,1)S(1)} %get-tuple-element.69), channel_id=1, source_target_pairs={{0,6},{1,7},{2,4},{3,5},{4,2},{5,3},{6,0},{7,1},{8,14},{9,15},{10,... | collective-permute-start | bytes 1179656 | tf_op jit(solution)/shard_map/ppermute | solution.py:259
  151.8 23.0 %collective-permute-start.20 = (f16[256,768]{1,0:T(8,128)(2,1)S(1)}, f16[256,768]{1,0:T(8,128)(2,1)S(1)}, u32[]{:S(2)}, u32[]{:S(2)}) collective-permute-start(f16[256,768]{1,0:T(8,128)(2,1)S(1)} %get-tuple-element.67), channel_id=1, source_target_pairs={{0,2},{1,3},{2,0},{3,1},{4,6},{5,7},{6,4},{7,5},{8,10},{9,11},{10,... | collective-permute-start | bytes 1179656 | tf_op jit(solution)/shard_map/ppermute | solution.py:259
  153.1 22.2 %collective-permute-start.21 = (f16[256,768]{1,0:T(8,128)(2,1)S(1)}, f16[256,768]{1,0:T(8,128)(2,1)S(1)}, u32[]{:S(2)}, u32[]{:S(2)}) collective-permute-start(f16[256,768]{1,0:T(8,128)(2,1)S(1)} %get-tuple-element.67), channel_id=1, source_target_pairs={{0,4},{1,5},{2,6},{3,7},{4,0},{5,1},{6,2},{7,3},{8,12},{9,13},{10,... | collective-permute-start | bytes 1179656 | tf_op jit(solution)/shard_map/ppermute | solution.py:259
  153.9 21.5 %collective-permute-start.22 = (f16[256,768]{1,0:T(8,128)(2,1)S(1)}, f16[256,768]{1,0:T(8,128)(2,1)S(1)}, u32[]{:S(2)}, u32[]{:S(2)}) collective-permute-start(f16[256,768]{1,0:T(8,128)(2,1)S(1)} %get-tuple-element.67), channel_id=1, source_target_pairs={{0,6},{1,7},{2,4},{3,5},{4,2},{5,3},{6,0},{7,1},{8,14},{9,15},{10,... | collective-permute-start | bytes 1179656 | tf_op jit(solution)/shard_map/ppermute | solution.py:259
  155.3 1.2 collective-permute-start.27
  156.5 13.9 %collective-permute-start.28 = (f32[8,1,256]{2,1,0:T(1,128)S(1)}, f32[8,1,256]{2,1,0:T(1,128)S(1)}, u32[]{:S(2)}, u32[]{:S(2)}) collective-permute-start(f32[8,1,256]{2,1,0:T(1,128)S(1)} %add.119), channel_id=1, source_target_pairs={{0,2},{1,3},{2,0},{3,1},{4,6},{5,7},{6,4},{7,5},{8,10},{9,11},{10,... | collective-permute-start | bytes 24584 | tf_op jit(solution)/shard_map/ppermute | solution.py:259
  170.5 3.7 %collective-permute-start.29 = (f32[8,1,256]{2,1,0:T(1,128)S(1)}, f32[8,1,256]{2,1,0:T(1,128)S(1)}, u32[]{:S(2)}, u32[]{:S(2)}) collective-permute-start(f32[8,1,256]{2,1,0:T(1,128)S(1)} %add.120), channel_id=1, source_target_pairs={{0,4},{1,5},{2,6},{3,7},{4,0},{5,1},{6,2},{7,3},{8,12},{9,13},{10,... | collective-permute-start | bytes 24584 | tf_op jit(solution)/shard_map/ppermute | solution.py:259
  174.8 3.8 %collective-permute-start.23 = (f16[256,768]{1,0:T(8,128)(2,1)S(1)}, f16[256,768]{1,0:T(8,128)(2,1)S(1)}, u32[]{:S(2)}, u32[]{:S(2)}) collective-permute-start(f16[256,768]{1,0:T(8,128)(2,1)S(1)} %get-tuple-element.67), channel_id=1, source_target_pairs={{0,1},{1,0},{2,3},{3,2},{4,5},{5,4},{6,7},{7,6},{8,9},{9,8},{10,11... | collective-permute-start | bytes 1179656 | tf_op jit(solution)/shard_map/ppermute | solution.py:259
  174.8 4.8 %collective-permute-start.24 = (f16[256,768]{1,0:T(8,128)(2,1)S(1)}, f16[256,768]{1,0:T(8,128)(2,1)S(1)}, u32[]{:S(2)}, u32[]{:S(2)}) collective-permute-start(f16[256,768]{1,0:T(8,128)(2,1)S(1)} %collective-permute-done.20), channel_id=1, source_target_pairs={{0,1},{1,0},{2,3},{3,2},{4,5},{5,4},{6,7},{7,6},{8,9},{9,8},{10,11... | collective-permute-start | bytes 1179656 | tf_op jit(solution)/shard_map/ppermute | solution.py:259
  175.3 5.2 %collective-permute-start.25 = (f16[256,768]{1,0:T(8,128)(2,1)S(1)}, f16[256,768]{1,0:T(8,128)(2,1)S(1)}, u32[]{:S(2)}, u32[]{:S(2)}) collective-permute-start(f16[256,768]{1,0:T(8,128)(2,1)S(1)} %collective-permute-done.21), channel_id=1, source_target_pairs={{0,1},{1,0},{2,3},{3,2},{4,5},{5,4},{6,7},{7,6},{8,9},{9,8},{10,11... | collective-permute-start | bytes 1179656 | tf_op jit(solution)/shard_map/ppermute | solution.py:259
  175.4 6.0 %collective-permute-start.26 = (f16[256,768]{1,0:T(8,128)(2,1)S(1)}, f16[256,768]{1,0:T(8,128)(2,1)S(1)}, u32[]{:S(2)}, u32[]{:S(2)}) collective-permute-start(f16[256,768]{1,0:T(8,128)(2,1)S(1)} %collective-permute-done.22), channel_id=1, source_target_pairs={{0,1},{1,0},{2,3},{3,2},{4,5},{5,4},{6,7},{7,6},{8,9},{9,8},{10,11... | collective-permute-start | bytes 1179656 | tf_op jit(solution)/shard_map/ppermute | solution.py:259
  (14 other events, 193.2 us)

commit v2 on v1

v2 whole, which is shorter than its diff:
```python
import functools
import math

import jax
import jax.numpy as jnp
from jax import lax
from jax.experimental import pallas as pl
from jax.experimental.pallas import tpu as pltpu
from jax.sharding import PartitionSpec as P

concentration = 32.0
LOG2E = math.log2(math.e)
LANES = 128
CORES = 2
VMEM_LIMIT = 48 * 1024 * 1024


def to_unit(values):
    values = values.astype(jnp.float32)
    return (values * lax.rsqrt(jnp.sum(values * values, axis=-1, keepdims=True) + 1e-06)).astype(
        jnp.bfloat16
    )


def arrival_plan(n):
    orders = []
    for place in range(n):
        first = 1 if place < n // 2 else -1
        if 0 < place < n - 1:
            first = -first
        order = [place]
        for step in range(1, n):
            for way in (first, -first):
                if 0 <= place + way * step < n:
                    order.append(place + way * step)
        orders.append(order)
    moves = []
    for place in range(n):
        for slot in range(1, n):
            block = orders[place][slot]
            source = place + (1 if block > place else -1)
            moves.append((source, place, orders[source].index(block), slot))
    return orders, moves


def pick(index, values):
    result = jnp.int32(values[0])
    for number in range(1, len(values)):
        if values[number] != values[0]:
            result = jnp.where(index == number, jnp.int32(values[number]), result)
    return result


def score_kernel(n_sources, choice, ids, *refs):
    sources = refs[:n_sources]
    units_in, log_mix = refs[n_sources], refs[n_sources + 1]
    scores, rows_out, totals, raw, units, sem = refs[-6:]

    @pl.when(pl.program_id(0) == 0)
    def _():
        chosen = pick(ids[0], choice)
        for number, source in enumerate(sources):

            @pl.when(chosen == number)
            def _():
                pltpu.make_async_copy(source, raw, sem).start()

        pltpu.make_async_copy(sources[0], raw, sem).wait()
        values = raw[...].astype(jnp.float32)
        square = jnp.sum(values * values, axis=-1, keepdims=True)
        unit = (values * lax.rsqrt(square + 1e-06)).astype(jnp.bfloat16)
        units[...] = unit
        rows_out[...] = unit
        totals[...] = jnp.zeros_like(totals)

    cosines = lax.dot_general(
        units_in[...], units[...], (((1,), (1,)), ((), ())), preferred_element_type=jnp.float32
    )
    offset = log_mix[...]
    repeats = cosines.shape[1] // offset.shape[1]
    if repeats > 1:
        offset = jnp.concatenate([offset] * repeats, axis=1)
    value = jnp.exp2(cosines * (concentration * LOG2E) + offset)
    scores[...] = value
    totals[0] += jnp.sum(value, axis=0, keepdims=True)


def score_block(ids, sources, choice, blocks, who, units, offsets, carried, column, n_columns):
    part, depth = sources[0].shape
    count = units.shape[0]
    tile = math.gcd(count, 512)
    shapes = (
        jax.ShapeDtypeStruct((count, n_columns * part), jnp.float32),
        jax.ShapeDtypeStruct((n_columns * part, depth), jnp.bfloat16),
        jax.ShapeDtypeStruct((n_columns, 1, part), jnp.float32),
    )
    n_sources = len(sources)
    aliases = {}
    extra = ()
    if carried is not None:
        extra = carried
        aliases = {1 + n_sources + 2 + i: i for i in range(3)}
    anywhere = pl.BlockSpec(memory_space=pl.ANY)
    return pl.pallas_call(
        functools.partial(score_kernel, n_sources, choice),
        grid_spec=pltpu.PrefetchScalarGridSpec(
            num_scalar_prefetch=1,
            grid=(count // tile,),
            in_specs=[anywhere] * n_sources
            + [
                pl.BlockSpec((tile, depth), lambda t, s: (t, 0)),
                pl.BlockSpec((tile, offsets.shape[1]), lambda t, s: (t, 0)),
            ]
            + [anywhere] * len(extra),
            out_specs=[
                pl.BlockSpec((tile, part), lambda t, s: (t, column)),
                pl.BlockSpec((part, depth), lambda t, s: (column, 0)),
                pl.BlockSpec(
                    (1, 1, part),
                    lambda t, s: (pick(s[0], blocks) * CORES + ((s[1] % CORES) ^ who), 0, 0),
                ),
            ],
            scratch_shapes=[
                pltpu.VMEM((part, depth), jnp.bfloat16),
                pltpu.VMEM((part, depth), jnp.bfloat16),
                pltpu.SemaphoreType.DMA,
            ],
        ),
        out_shape=shapes,
        input_output_aliases=aliases,
        compiler_params=pltpu.CompilerParams(vmem_limit_bytes=VMEM_LIMIT),
        cost_estimate=pl.CostEstimate(
            flops=2 * count * part * depth,
            bytes_accessed=2 * (count * part * 4 + count * depth * 2),
            transcendentals=count * part,
        ),
        name="scores",
    )(ids, *sources, units, offsets, *extra)


def sum_kernel(orders, n_totals, ids, *refs):
    totals = refs[:n_totals]
    scores, rows, sent, mine, masses, inverse, total, mass = refs[n_totals:]
    step = pl.program_id(0)
    n_columns = inverse.shape[0]

    @pl.when(step == 0)
    def _():
        for column in range(n_columns):
            slot, who = divmod(column, CORES)
            place = pick(ids[0], [order[slot] for order in orders]) * CORES + (
                (ids[1] % CORES) ^ who
            )
            value = totals[0][place]
            for more in totals[1:]:
                value = value + more[place]
            inverse[column] = 1.0 / value
        total[...] = jnp.zeros_like(total)
        mass[...] = jnp.zeros_like(mass)

    resp = (scores[...] * inverse[step]).astype(jnp.bfloat16)
    total[...] += lax.dot_general(
        resp, rows[...], (((1,), (0,)), ((), ())), preferred_element_type=jnp.float32
    )
    wide = resp.astype(jnp.float32)
    partial = wide[:, :LANES]
    for start in range(LANES, wide.shape[1], LANES):
        partial = partial + wide[:, start : start + LANES]
    mass[...] += partial

    @pl.when(step == pl.num_programs(0) - 1)
    def _():
        size = mine.shape[0]
        quarter = ids[1] // CORES
        for number in range(total.shape[0] // size):
            block = total[number * size : (number + 1) * size, :]
            away = quarter ^ number

            @pl.when(away == 0)
            def _():
                mine[...] = block

            @pl.when(away != 0)
            def _():
                sent[away - 1] = block.astype(sent.dtype)

        masses[...] = jnp.sum(mass[...].T, axis=0, keepdims=True)


def sum_rows(ids, orders, totals, scores, rows, n_owners):
    count, width = scores.shape
    depth = rows.shape[1]
    size = count // n_owners
    n_columns, _, part = totals[0].shape
    return pl.pallas_call(
        functools.partial(sum_kernel, orders, len(totals)),
        grid_spec=pltpu.PrefetchScalarGridSpec(
            num_scalar_prefetch=1,
            grid=(n_columns,),
            in_specs=[pl.BlockSpec(totals[0].shape, lambda t, s: (0, 0, 0)) for _ in totals]
            + [
                pl.BlockSpec((count, part), lambda t, s: (0, t)),
                pl.BlockSpec((part, depth), lambda t, s: (t, 0)),
            ],
            out_specs=[
                pl.BlockSpec((n_owners - 1, size, depth), lambda t, s: (0, 0, 0)),
                pl.BlockSpec((size, depth), lambda t, s: (0, 0)),
                pl.BlockSpec((1, count), lambda t, s: (0, 0)),
            ],
            scratch_shapes=[
                pltpu.VMEM((n_columns, 1, part), jnp.float32),
                pltpu.VMEM((count, depth), jnp.float32),
                pltpu.VMEM((count, LANES), jnp.float32),
            ],
        ),
        out_shape=(
            jax.ShapeDtypeStruct((n_owners - 1, size, depth), jnp.bfloat16),
            jax.ShapeDtypeStruct((size, depth), jnp.float32),
            jax.ShapeDtypeStruct((1, count), jnp.float32),
        ),
        compiler_params=pltpu.CompilerParams(vmem_limit_bytes=VMEM_LIMIT),
        cost_estimate=pl.CostEstimate(
            flops=2 * count * width * depth,
            bytes_accessed=count * (width * 4 + depth * 4) + width * depth * 2,
            transcendentals=0,
        ),
        name="sums",
    )(ids, *totals, scores, rows)


def local(embeddings, centroids, log_mix):
    n_places = lax.axis_size("blk")
    n_rows = lax.axis_size("rows")
    n_owners = n_rows // CORES
    place = lax.axis_index("blk")
    me = lax.axis_index("rows")
    core = lax.rem(me, CORES)
    held, depth = embeddings.shape
    local_centroids = centroids.shape[0]
    half = local_centroids // CORES
    ids = jnp.stack([place, me]).astype(jnp.int32)
    orders, moves = arrival_plan(n_places)

    def exchange(array, distance):
        return lax.ppermute(array, "rows", [(i, i ^ distance) for i in range(n_rows)])

    def swap_cores(array, places):
        pairs = [
            (spot * n_rows + i, spot * n_rows + (i ^ 1)) for spot in places for i in range(n_rows)
        ]
        return lax.ppermute(array, ("blk", "rows"), pairs)

    slots = [[(embeddings, list(range(n_places)))]] + [[] for _ in range(n_places - 1)]

    def start_ready(moves):
        groups = {}
        left = []
        for move in moves:
            source, target, source_slot, slot = move
            holds = [n for n, (_, places) in enumerate(slots[source_slot]) if source in places]
            if not holds:
                left.append(move)
                continue
            turn = 0
            while any(source == s for s, _ in groups.get((slot, source_slot, holds[0], turn), [])):
                turn += 1
            groups.setdefault((slot, source_slot, holds[0], turn), []).append((source, target))
        moved = [
            (slot, lax.ppermute(slots[source_slot][hold][0], "blk", pairs), [p[1] for p in pairs])
            for (slot, source_slot, hold, _), pairs in sorted(groups.items())
        ]
        return moved, left

    def merged(candidates):
        if len(candidates) <= 2:
            return candidates
        array, held_at = candidates[0][0], list(candidates[0][1])
        for other, places in candidates[1:]:
            here = functools.reduce(jnp.logical_or, [place == spot for spot in places])
            array = jnp.where(here, other, array)
            held_at += places
        return [(array, held_at)]

    own_centroids = lax.dynamic_slice_in_dim(centroids, core * half, half, 0)
    own_mix = lax.dynamic_slice_in_dim(log_mix, core * half, half, 0)
    units = to_unit(own_centroids)
    offsets = jnp.broadcast_to(((own_mix - concentration) * LOG2E)[:, None], (half, LANES))

    n_columns = n_places * CORES
    carried = None

    def scores_of(slot, carried):
        blocks = [order[slot] for order in orders]
        swapped = [(swap_cores(array, places), places) for array, places in slots[slot]]
        for who, candidates in enumerate((slots[slot], swapped)):
            choice = [
                next(n for n, (_, places) in enumerate(candidates) if spot in places)
                for spot in range(n_places)
            ]
            carried = score_block(
                ids,
                [array for array, _ in candidates],
                choice,
                blocks,
                who,
                units,
                offsets,
                carried,
                slot * CORES + who,
                n_columns,
            )
        return carried

    for turn in range(n_places):
        while sum(len(places) for _, places in slots[turn]) < n_places:
            moved, moves = start_ready(moves)
            for slot, array, places in moved:
                slots[slot].append((array, places))
        slots[turn] = merged(slots[turn])
        moved, moves = start_ready(moves)
        carried = scores_of(turn, carried)
        if moved:
            arrays, carried = lax.optimization_barrier(([array for _, array, _ in moved], carried))
            for (slot, _, places), array in zip(moved, arrays):
                slots[slot].append((array, places))
    scores, rows, totals = carried
    totals = totals + exchange(totals, 1)
    all_totals = [totals] + [
        lax.ppermute(totals, "blk", [(i, (i + turn) % n_places) for i in range(n_places)])
        for turn in range(1, n_places)
    ]

    sent, summed, masses = sum_rows(ids, orders, all_totals, scores, rows, n_owners)
    far = [CORES * away for away in range(1, n_owners)]
    arrived = [exchange(sent[number], distance) for number, distance in enumerate(far)]
    for array in arrived:
        summed = summed + array.astype(jnp.float32)

    distance = CORES
    while distance < n_rows:
        masses = masses + exchange(masses, distance)
        distance *= 2
    masses = masses.reshape(half)
    other_masses = exchange(masses, 1)
    both = jnp.where(
        core == 0,
        jnp.concatenate([masses, other_masses]),
        jnp.concatenate([other_masses, masses]),
    )

    unit = summed * lax.rsqrt(jnp.sum(summed * summed, axis=1, keepdims=True) + 1e-06)
    unit = unit.astype(jnp.float16)
    size = unit.shape[0]
    result = jnp.zeros((local_centroids, depth), jnp.float32)
    pieces = [(0, unit)] + [(distance, exchange(unit, distance)) for distance in far]
    for distance, piece in pieces:
        for flip, array in ((0, piece), (1, exchange(piece, 1))):
            start = (core ^ flip) * half + lax.div(me ^ distance, CORES) * size
            result = lax.dynamic_update_slice(result, array.astype(jnp.float32), (start, 0))
    count = local_centroids * n_places
    factor = count / (held * n_rows * n_places)
    return (result, both * factor)


def solution(mesh):
    return jax.shard_map(
        local,
        mesh=mesh,
        in_specs=(P(("blk", "rows"), None), P("blk", None), P("blk")),
        out_specs=(P("blk", None), P("blk")),
        check_vma=False,
    )
```

time: 184 us -> 152 us (0.83)
  waiting for transfers between devices: 42.7 us -> 70.7 us
  Pallas kernels: 66.3 us -> 39.7 us
  starting transfers between devices: 40.8 us -> 26.4 us
  other arithmetic: 21 us -> 12 us
  local copies, waits for them, and re-layouts: 8.52 us -> 1.82 us
  between operations: 3.09 us -> 1 us
    ppermute x12 -> x11, waiting for transfers between devices: 7.29 us -> 34 us  [the longest x5 34 us: start_ready(): lax.ppermute(slots[source_slot][hold][0], 'blk', pairs)]
    pallas_call x12 -> x9, Pallas kernels: 66.3 us -> 39.7 us  [the longest x8 25.6 us: score_block(): pl.pallas_call(functools.partial(score_kernel, n_sources, choice), grid_s...]
    ppermute x12 -> x11, starting transfers between devices: 21.3 us -> 12.4 us  [the longest x5 6.64 us: start_ready(): lax.ppermute(slots[source_slot][hold][0], 'blk', pairs)]
    ppermute x3, starting transfers between devices: 8.98 us -> 3.87 us  [local(): lax.ppermute(totals, 'blk', [(i, (i + turn) % n_places) for i in range(n_...]
    another operation x7 -> x1, other arithmetic: 4.25 us -> 0.08 us  [local(): ids = jnp.stack([place, me]).astype(jnp.int32)]
    dynamic_slice x6 -> x0, local copies, waits for them, and re-layouts: 3.55 us -> none  [the longest x3 1.8 us: local(): jnp.array([kinds.index(plan[i][turn][:2]) for i in range(n_places)], jnp....]
    convert_element_type x1, other arithmetic: 4.13 us -> 1.73 us  [to_unit(): (values * lax.rsqrt(jnp.sum(values * values, axis=-1, keepdims=True) + 1e...]
    ppermute x15 -> x14, waiting for transfers between devices: 34.1 us -> 33.6 us  [exchange(): lax.ppermute(array, 'rows', [(i, i ^ distance) for i in range(n_rows)])]
  transfers between devices with their start and end apart: 30 -> 28, of which waited for: 8 -> 11; matrix products, arithmetic and copies ran while one was open for 12% -> 7% of each run, Pallas kernels for 30% -> 15%
where the time goes in v2:
time: 152 us
  waiting for transfers between devices  70.7 us (47%)
  Pallas kernels  39.7 us (26%)
  starting transfers between devices  26.4 us (17%)
  other arithmetic  12 us (8%)
  local copies, waits for them, and re-layouts  1.82 us (1%)
    ppermute x5, waiting for transfers between devices, start_ready(): lax.ppermute(slots[source_slot][hold][0], 'blk', pairs)  34 us
    ppermute x14, waiting for transfers between devices, exchange(): lax.ppermute(array, 'rows', [(i, i ^ distance) for i in range(n_rows)])  33.6 us
    pallas_call x8, Pallas kernels, score_block(): pl.pallas_call(functools.partial(score_kernel, n_sources, choice), grid_s...  25.6 us
    pallas_call x1, Pallas kernels, sum_rows(): pl.pallas_call(functools.partial(sum_kernel, orders, len(totals)), grid_s...  14 us
    ppermute x14, starting transfers between devices, exchange(): lax.ppermute(array, 'rows', [(i, i ^ distance) for i in range(n_rows)])  10.2 us
    dynamic_update_slice x8, other arithmetic, local(): lax.dynamic_update_slice(result, array.astype(jnp.float32), (start, 0))  6.75 us
    ppermute x5, starting transfers between devices, start_ready(): lax.ppermute(slots[source_slot][hold][0], 'blk', pairs)  6.64 us
    ppermute x6, starting transfers between devices, swap_cores(): return lax.ppermute(array, ('blk', 'rows'), pairs)  5.76 us
  transfers between devices with their start and end apart: 28, of which 11 were waited for; matrix products, arithmetic and copies ran while one was open for 7% of the time, Pallas kernels for 15%

profile of v2, /device:TPU:0, one launch (start us, length us, event | category | flops | bytes accessed | tf_op | source)
XLA Modules:
  0.0 151.5 jit_solution(14001713488883319644)
XLA Ops:
  1.1 2.7 %collective-permute-start = (bf16[512,768]{1,0:T(8,128)(2,1)}, bf16[512,768]{1,0:T(8,128)(2,1)S(1)}, u32[]{:S(2)}, u32[]{:S(2)}) collective-permute-start(bf16[512,768]{1,0:T(8,128)(2,1)} %refs_0_.1), channel_id=1, source_target_pairs={{8,0},{0,8},{24,16},{16,24},{9,1},{1,9},{25,17},{17,25},{10,2},{2,... | collective-permute-start | bytes 2359304 | tf_op jit(solution)/shard_map/ppermute | solution.py:269
  4.6 1.8 %fusion = f32[1024]{0:T(1024)S(1)} fusion(bf16[2048,768]{1,0:T(8,128)(2,1)} %param.4, s32[]{:T(128)S(6)} %select_n.36), kind=kLoop, calls=%fused_computation.2 | loop fusion | flops 2358272 | bytes 1576964 | tf_op jit(solution)/shard_map/reduce_sum | solution.py:20
  7.1 1.7 %fusion.1.refs_1_.refs_2_ = bf16[1024,768]{1,0:T(8,128)(2,1)S(1)} fusion(f32[1024]{0:T(1024)S(1)} %add_rsqrt_fusion, bf16[2048,768]{1,0:T(8,128)(2,1)} %param.4, s32[]{:T(128)S(6)} %select_n.36), kind=kLoop, calls=%fused_computation.3 | loop fusion | flops 2359296 | bytes 3149828 | tf_op jit(solution)/shard_map/convert_element_type | solution.py:20
  9.0 1.1 copy-done
  10.1 3.3 %scores.8 = (f32[1024,4096]{1,0:T(8,128)}, bf16[4096,768]{1,0:T(8,128)(2,1)}, f32[8,1,512]{2,1,0:T(1,128)S(1)}) custom-call(s32[2]{0:T(128)S(1)} %pad_add_fusion.ids, bf16[512,768]{1,0:T(8,128)(2,1)S(1)} %copy-done, bf16[1024,768]{1,0:T(8,128)(2,1)S(1)} %fusion.1.refs_1_.refs_2_, f32[1024,128]{1,0:T(8,128)S(1)} %broadcast_in_dim.5.refs_2_.refs_3_), custom_call_target="tpu_custom_call" | custom-call | flops 805306368 | bytes 7340032 | tf_op jit(solution)/shard_map/scores/pallas_call | solution.py:104
  13.5 3.2 %scores.9 = (f32[1024,4096]{1,0:T(8,128)}, bf16[4096,768]{1,0:T(8,128)(2,1)}, f32[8,1,512]{2,1,0:T(1,128)S(1)}) custom-call(s32[2]{0:T(128)S(1)} %pad_add_fusion.ids, bf16[512,768]{1,0:T(8,128)(2,1)S(1)} %collective-permute-done.2.refs_0_, bf16[1024,768]{1,0:T(8,128)(2,1)S(1)} %fusion.1.refs_1_.refs_2_, ...), custom_call_target="tpu_custom_call", output_to_operand_aliasing={{0}: (4, {}), {1}: (5, {}), {2}: (6, {})} | custom-call | flops 805306368 | bytes 7340032 | tf_op jit(solution)/shard_map/scores/pallas_call | solution.py:104
  16.7 5.5 %collective-permute-done.refs_0_ = bf16[512,768]{1,0:T(8,128)(2,1)S(1)} collective-permute-done((bf16[512,768]{1,0:T(8,128)(2,1)}, bf16[512,768]{1,0:T(8,128)(2,1)S(1)}, u32[]{:S(2)}, u32[]{:S(2)}) %collective-permute-start) | collective-permute-done | bytes 786464 | tf_op jit(solution)/shard_map/ppermute | solution.py:269
  22.1 1.3 collective-permute-start.3
  24.9 3.2 %scores.10 = (f32[1024,4096]{1,0:T(8,128)}, bf16[4096,768]{1,0:T(8,128)(2,1)}, f32[8,1,512]{2,1,0:T(1,128)S(1)}) custom-call(s32[2]{0:T(128)S(1)} %pad_add_fusion.ids, bf16[512,768]{1,0:T(8,128)(2,1)S(1)} %collective-permute-done.refs_0_, bf16[1024,768]{1,0:T(8,128)(2,1)S(1)} %fusion.1.refs_1_.refs_2_, ...), custom_call_target="tpu_custom_call", output_to_operand_aliasing={{0}: (4, {}), {1}: (5, {}), {2}: (6, {})} | custom-call | flops 805306368 | bytes 7340032 | tf_op jit(solution)/shard_map/scores/pallas_call | solution.py:104
  28.1 3.2 %scores.11 = (f32[1024,4096]{1,0:T(8,128)}, bf16[4096,768]{1,0:T(8,128)(2,1)}, f32[8,1,512]{2,1,0:T(1,128)S(1)}) custom-call(s32[2]{0:T(128)S(1)} %pad_add_fusion.ids, bf16[512,768]{1,0:T(8,128)(2,1)S(1)} %collective-permute-done.5.refs_0_, bf16[1024,768]{1,0:T(8,128)(2,1)S(1)} %fusion.1.refs_1_.refs_2_, ...), custom_call_target="tpu_custom_call", output_to_operand_aliasing={{0}: (4, {}), {1}: (5, {}), {2}: (6, {})} | custom-call | flops 805306368 | bytes 7340032 | tf_op jit(solution)/shard_map/scores/pallas_call | solution.py:104
  31.3 15.1 %collective-permute-done.3.refs_1_ = bf16[512,768]{1,0:T(8,128)(2,1)S(1)} collective-permute-done((bf16[512,768]{1,0:T(8,128)(2,1)S(1)}, bf16[512,768]{1,0:T(8,128)(2,1)S(1)}, u32[]{:S(2)}, u32[]{:S(2)}) %collective-permute-start.3) | collective-permute-done | bytes 786464 | tf_op jit(solution)/shard_map/ppermute | solution.py:269
  46.4 1.9 %collective-permute-start.9 = (bf16[512,768]{1,0:T(8,128)(2,1)S(1)}, bf16[512,768]{1,0:T(8,128)(2,1)S(1)}, u32[]{:S(2)}, u32[]{:S(2)}) collective-permute-start(bf16[512,768]{1,0:T(8,128)(2,1)S(1)} %collective-permute-done.3.refs_1_), channel_id=1, source_target_pairs={{0,1},{1,0},{2,3},{3,2},{4,5},{5,4},{6,7},{7,6},{24,25},{25,24},{2... | collective-permute-start | bytes 2359304 | tf_op jit(solution)/shard_map/ppermute | solution.py:251
  48.3 1.3 collective-permute-start.7
  50.3 3.2 %scores.12 = (f32[1024,4096]{1,0:T(8,128)}, bf16[4096,768]{1,0:T(8,128)(2,1)}, f32[8,1,512]{2,1,0:T(1,128)S(1)}) custom-call(s32[2]{0:T(128)S(1)} %pad_add_fusion.ids, bf16[512,768]{1,0:T(8,128)(2,1)S(1)} %collective-permute-done.1.refs_0_, ...), custom_call_target="tpu_custom_call", output_to_operand_aliasing={{0}: (5, {}), {1}: (6, {}), {2}: (7, {})} | custom-call | flops 805306368 | bytes 7340032 | tf_op jit(solution)/shard_map/scores/pallas_call | solution.py:104
  53.6 3.2 %scores.13 = (f32[1024,4096]{1,0:T(8,128)}, bf16[4096,768]{1,0:T(8,128)(2,1)}, f32[8,1,512]{2,1,0:T(1,128)S(1)}) custom-call(s32[2]{0:T(128)S(1)} %pad_add_fusion.ids, bf16[512,768]{1,0:T(8,128)(2,1)S(1)} %collective-permute-done.8.refs_0_, ...), custom_call_target="tpu_custom_call", output_to_operand_aliasing={{0}: (5, {}), {1}: (6, {}), {2}: (7, {})} | custom-call | flops 805306368 | bytes 7340032 | tf_op jit(solution)/shard_map/scores/pallas_call | solution.py:104
  56.8 13.3 %collective-permute-done.7.refs_1_ = bf16[512,768]{1,0:T(8,128)(2,1)S(1)} collective-permute-done((bf16[512,768]{1,0:T(8,128)(2,1)S(1)}, bf16[512,768]{1,0:T(8,128)(2,1)S(1)}, u32[]{:S(2)}, u32[]{:S(2)}) %collective-permute-start.7) | collective-permute-done | bytes 786464 | tf_op jit(solution)/shard_map/ppermute | solution.py:269
  70.2 1.9 %collective-permute-start.10 = (bf16[512,768]{1,0:T(8,128)(2,1)S(1)}, bf16[512,768]{1,0:T(8,128)(2,1)S(1)}, u32[]{:S(2)}, u32[]{:S(2)}) collective-permute-start(bf16[512,768]{1,0:T(8,128)(2,1)S(1)} %collective-permute-done.7.refs_1_), channel_id=1, source_target_pairs={{0,1},{1,0},{2,3},{3,2},{4,5},{5,4},{6,7},{7,6},{24,25},{25,24},{2... | collective-permute-start | bytes 2359304 | tf_op jit(solution)/shard_map/ppermute | solution.py:251
  72.1 3.2 %scores.14 = (f32[1024,4096]{1,0:T(8,128)}, bf16[4096,768]{1,0:T(8,128)(2,1)}, f32[8,1,512]{2,1,0:T(1,128)S(1)}) custom-call(s32[2]{0:T(128)S(1)} %pad_add_fusion.ids, bf16[512,768]{1,0:T(8,128)(2,1)S(1)} %collective-permute-done.4.refs_0_, ...), custom_call_target="tpu_custom_call", output_to_operand_aliasing={{0}: (5, {}), {1}: (6, {}), {2}: (7, {})} | custom-call | flops 805306368 | bytes 7340032 | tf_op jit(solution)/shard_map/scores/pallas_call | solution.py:104
  75.3 3.2 %scores.15 = (f32[1024,4096]{1,0:T(8,128)}, bf16[4096,768]{1,0:T(8,128)(2,1)}, f32[8,1,512]{2,1,0:T(1,128)S(1)}) custom-call(s32[2]{0:T(128)S(1)} %pad_add_fusion.ids, bf16[512,768]{1,0:T(8,128)(2,1)S(1)} %collective-permute-done.6.refs_0_, ...), custom_call_target="tpu_custom_call", output_to_operand_aliasing={{0}: (5, {}), {1}: (6, {}), {2}: (7, {})} | custom-call | flops 805306368 | bytes 7340032 | tf_op jit(solution)/shard_map/scores/pallas_call | solution.py:104
  80.0 3.2 %collective-permute-start.13 = (f32[8,1,512]{2,1,0:T(1,128)S(1)}, f32[8,1,512]{2,1,0:T(1,128)S(1)}, u32[]{:S(2)}, u32[]{:S(2)}) collective-permute-start(f32[8,1,512]{2,1,0:T(1,128)S(1)} %add.96.refs_0_), channel_id=1, source_target_pairs={{0,16},{8,24},{16,0},{24,8},{1,17},{9,25},{17,1},{25,9},{2,18},{10... | collective-permute-start | bytes 49160 | tf_op jit(solution)/shard_map/ppermute | solution.py:329
  83.8 1.8 %collective-permute-done.12.refs_1_ = f32[8,1,512]{2,1,0:T(1,128)S(1)} collective-permute-done((f32[8,1,512]{2,1,0:T(1,128)S(1)}, f32[8,1,512]{2,1,0:T(1,128)S(1)}, u32[]{:S(2)}, u32[]{:S(2)}) %collective-permute-start.12) | collective-permute-done | bytes 16416 | tf_op jit(solution)/shard_map/ppermute | solution.py:329
  85.6 1.3 collective-permute-done.14.refs_3_
  86.9 14.0 %sums.1 = (bf16[3,256,768]{2,1,0:T(8,128)(2,1)S(1)}, f32[256,768]{1,0:T(8,128)S(1)}, f32[1,1024]{1,0:T(1,128)S(1)}) custom-call(s32[2]{0:T(128)S(1)} %pad_add_fusion.ids, f32[8,1,512]{2,1,0:T(1,128)S(1)} %add.96.refs_0_, f32[8,1,512]{2,1,0:T(1,128)S(1)} %collective-permute-done.12.refs_1_, f32[8,1,512]{2,1,0:T(1,128)S(1)} %collective-permute-done.13.refs_2_, ...), custom_call_target="tpu_custom_call" | custom-call | flops 6442450944 | bytes 26214400 | tf_op jit(solution)/shard_map/sums/pallas_call | solution.py:195
  101.0 1.6 %collective-permute-start.15 = (bf16[256,768]{1,0:T(8,128)(2,1)S(1)}, bf16[256,768]{1,0:T(8,128)(2,1)S(1)}, u32[]{:S(2)}, u32[]{:S(2)}) collective-permute-start(bf16[256,768]{1,0:T(8,128)(2,1)S(1)} %get-tuple-element.86), channel_id=1, source_target_pairs={{0,2},{1,3},{2,0},{3,1},{4,6},{5,7},{6,4},{7,5},{8,10},{9,11},{10,... | collective-permute-start | bytes 1179656 | tf_op jit(solution)/shard_map/ppermute | solution.py:245
  102.6 1.5 %collective-permute-start.16 = (bf16[256,768]{1,0:T(8,128)(2,1)S(1)}, bf16[256,768]{1,0:T(8,128)(2,1)S(1)}, u32[]{:S(2)}, u32[]{:S(2)}) collective-permute-start(bf16[256,768]{1,0:T(8,128)(2,1)S(1)} %get-tuple-element.88), channel_id=1, source_target_pairs={{0,4},{1,5},{2,6},{3,7},{4,0},{5,1},{6,2},{7,3},{8,12},{9,13},{10,... | collective-permute-start | bytes 1179656 | tf_op jit(solution)/shard_map/ppermute | solution.py:245
  104.6 8.6 %collective-permute-done.15 = bf16[256,768]{1,0:T(8,128)(2,1)S(1)} collective-permute-done((bf16[256,768]{1,0:T(8,128)(2,1)S(1)}, bf16[256,768]{1,0:T(8,128)(2,1)S(1)}, u32[]{:S(2)}, u32[]{:S(2)}) %collective-permute-start.15) | collective-permute-done | bytes 393248 | tf_op jit(solution)/shard_map/ppermute | solution.py:245
  113.1 7.4 %collective-permute-done.16 = bf16[256,768]{1,0:T(8,128)(2,1)S(1)} collective-permute-done((bf16[256,768]{1,0:T(8,128)(2,1)S(1)}, bf16[256,768]{1,0:T(8,128)(2,1)S(1)}, u32[]{:S(2)}, u32[]{:S(2)}) %collective-permute-start.16) | collective-permute-done | bytes 393248 | tf_op jit(solution)/shard_map/ppermute | solution.py:245
  121.5 1.3 collective-permute-start.19
  123.6 1.4 collective-permute-start.23
  125.1 1.2 collective-permute-start.25
  126.3 12.5 %collective-permute-done.25 = f32[1,1024]{1,0:T(1,128)S(1)} collective-permute-done((f32[1,1024]{1,0:T(1,128)S(1)}, f32[1,1024]{1,0:T(1,128)S(1)}, u32[]{:S(2)}, u32[]{:S(2)}) %collective-permute-start.25) | collective-permute-done | bytes 4128 | tf_op jit(solution)/shard_map/ppermute | solution.py:245
  139.4 3.1 %collective-permute-done.26 = f32[1,1024]{1,0:T(1,128)S(1)} collective-permute-done((f32[1,1024]{1,0:T(1,128)S(1)}, f32[1,1024]{1,0:T(1,128)S(1)}, u32[]{:S(2)}, u32[]{:S(2)}) %collective-permute-start.26) | collective-permute-done | bytes 4128 | tf_op jit(solution)/shard_map/ppermute | solution.py:245
  (59 shorter events, 18.3 us)
Async XLA Ops:
  0.6 12.8 %collective-permute-start.2 = (bf16[512,768]{1,0:T(8,128)(2,1)}, bf16[512,768]{1,0:T(8,128)(2,1)S(1)}, u32[]{:S(2)}, u32[]{:S(2)}) collective-permute-start(bf16[512,768]{1,0:T(8,128)(2,1)} %refs_0_.1), channel_id=1, source_target_pairs={{0,1},{1,0},{2,3},{3,2},{4,5},{5,4},{6,7},{7,6},{8,9},{9,8},{10,11... | collective-permute-start | bytes 2359304 | tf_op jit(solution)/shard_map/ppermute | solution.py:251
  1.1 21.0 %collective-permute-start = (bf16[512,768]{1,0:T(8,128)(2,1)}, bf16[512,768]{1,0:T(8,128)(2,1)S(1)}, u32[]{:S(2)}, u32[]{:S(2)}) collective-permute-start(bf16[512,768]{1,0:T(8,128)(2,1)} %refs_0_.1), channel_id=1, source_target_pairs={{8,0},{0,8},{24,16},{16,24},{9,1},{1,9},{25,17},{17,25},{10,2},{2,... | collective-permute-start | bytes 2359304 | tf_op jit(solution)/shard_map/ppermute | solution.py:269
  3.8 18.3 %collective-permute-start.1 = (bf16[512,768]{1,0:T(8,128)(2,1)}, bf16[512,768]{1,0:T(8,128)(2,1)S(1)}, u32[]{:S(2)}, u32[]{:S(2)}) collective-permute-start(bf16[512,768]{1,0:T(8,128)(2,1)} %refs_0_.1), channel_id=1, source_target_pairs={{16,8},{8,16},{17,9},{9,17},{18,10},{10,18},{19,11},{11,19},{20,12... | collective-permute-start | bytes 2359304 | tf_op jit(solution)/shard_map/ppermute | solution.py:269
  9.0 1.1 copy-start
  22.1 5.9 %collective-permute-start.5 = (bf16[512,768]{1,0:T(8,128)(2,1)S(1)}, bf16[512,768]{1,0:T(8,128)(2,1)S(1)}, u32[]{:S(2)}, u32[]{:S(2)}) collective-permute-start(bf16[512,768]{1,0:T(8,128)(2,1)S(1)} %collective-permute-done.refs_0_), channel_id=1, source_target_pairs={{0,1},{1,0},{2,3},{3,2},{4,5},{5,4},{6,7},{7,6},{8,9},{9,8},{10,11... | collective-permute-start | bytes 2359304 | tf_op jit(solution)/shard_map/ppermute | solution.py:251
  22.1 24.3 %collective-permute-start.3 = (bf16[512,768]{1,0:T(8,128)(2,1)S(1)}, bf16[512,768]{1,0:T(8,128)(2,1)S(1)}, u32[]{:S(2)}, u32[]{:S(2)}) collective-permute-start(bf16[512,768]{1,0:T(8,128)(2,1)S(1)} %collective-permute-done.1.refs_0_), channel_id=1, source_target_pairs={{8,0},{16,24},{9,1},{17,25},{10,2},{18,26},{11,3},{19,27},{12,4},{... | collective-permute-start | bytes 2359304 | tf_op jit(solution)/shard_map/ppermute | solution.py:269
  23.4 23.0 %collective-permute-start.4 = (bf16[512,768]{1,0:T(8,128)(2,1)S(1)}, bf16[512,768]{1,0:T(8,128)(2,1)S(1)}, u32[]{:S(2)}, u32[]{:S(2)}) collective-permute-start(bf16[512,768]{1,0:T(8,128)(2,1)S(1)} %collective-permute-done.refs_0_), channel_id=1, source_target_pairs={{16,8},{8,16},{17,9},{9,17},{18,10},{10,18},{19,11},{11,19},{20,12... | collective-permute-start | bytes 2359304 | tf_op jit(solution)/shard_map/ppermute | solution.py:269
  24.2 29.4 %collective-permute-start.8 = (bf16[512,768]{1,0:T(8,128)(2,1)S(1)}, bf16[512,768]{1,0:T(8,128)(2,1)S(1)}, u32[]{:S(2)}, u32[]{:S(2)}) collective-permute-start(bf16[512,768]{1,0:T(8,128)(2,1)S(1)} %collective-permute-done.1.refs_0_), channel_id=1, source_target_pairs={{8,9},{9,8},{10,11},{11,10},{12,13},{13,12},{14,15},{15,14},{16,17... | collective-permute-start | bytes 2359304 | tf_op jit(solution)/shard_map/ppermute | solution.py:251
  46.4 7.2 %collective-permute-start.9 = (bf16[512,768]{1,0:T(8,128)(2,1)S(1)}, bf16[512,768]{1,0:T(8,128)(2,1)S(1)}, u32[]{:S(2)}, u32[]{:S(2)}) collective-permute-start(bf16[512,768]{1,0:T(8,128)(2,1)S(1)} %collective-permute-done.3.refs_1_), channel_id=1, source_target_pairs={{0,1},{1,0},{2,3},{3,2},{4,5},{5,4},{6,7},{7,6},{24,25},{25,24},{2... | collective-permute-start | bytes 2359304 | tf_op jit(solution)/shard_map/ppermute | solution.py:251
  48.3 21.8 %collective-permute-start.7 = (bf16[512,768]{1,0:T(8,128)(2,1)S(1)}, bf16[512,768]{1,0:T(8,128)(2,1)S(1)}, u32[]{:S(2)}, u32[]{:S(2)}) collective-permute-start(bf16[512,768]{1,0:T(8,128)(2,1)S(1)} %collective-permute-done.4.refs_0_), channel_id=1, source_target_pairs={{8,0},{16,24},{9,1},{17,25},{10,2},{18,26},{11,3},{19,27},{12,4},{... | collective-permute-start | bytes 2359304 | tf_op jit(solution)/shard_map/ppermute | solution.py:269
  49.6 25.7 %collective-permute-start.6 = (bf16[512,768]{1,0:T(8,128)(2,1)S(1)}, bf16[512,768]{1,0:T(8,128)(2,1)S(1)}, u32[]{:S(2)}, u32[]{:S(2)}) collective-permute-start(bf16[512,768]{1,0:T(8,128)(2,1)S(1)} %collective-permute-done.4.refs_0_), channel_id=1, source_target_pairs={{8,9},{9,8},{10,11},{11,10},{12,13},{13,12},{14,15},{15,14},{16,17... | collective-permute-start | bytes 2359304 | tf_op jit(solution)/shard_map/ppermute | solution.py:251
  70.2 5.1 %collective-permute-start.10 = (bf16[512,768]{1,0:T(8,128)(2,1)S(1)}, bf16[512,768]{1,0:T(8,128)(2,1)S(1)}, u32[]{:S(2)}, u32[]{:S(2)}) collective-permute-start(bf16[512,768]{1,0:T(8,128)(2,1)S(1)} %collective-permute-done.7.refs_1_), channel_id=1, source_target_pairs={{0,1},{1,0},{2,3},{3,2},{4,5},{5,4},{6,7},{7,6},{24,25},{25,24},{2... | collective-permute-start | bytes 2359304 | tf_op jit(solution)/shard_map/ppermute | solution.py:251
  78.5 1.4 collective-permute-start.11
  79.9 5.7 %collective-permute-start.12 = (f32[8,1,512]{2,1,0:T(1,128)S(1)}, f32[8,1,512]{2,1,0:T(1,128)S(1)}, u32[]{:S(2)}, u32[]{:S(2)}) collective-permute-start(f32[8,1,512]{2,1,0:T(1,128)S(1)} %add.96.refs_0_), channel_id=1, source_target_pairs={{0,8},{8,16},{16,24},{24,0},{1,9},{9,17},{17,25},{25,1},{2,10},{10... | collective-permute-start | bytes 49160 | tf_op jit(solution)/shard_map/ppermute | solution.py:329
  80.0 5.6 %collective-permute-start.13 = (f32[8,1,512]{2,1,0:T(1,128)S(1)}, f32[8,1,512]{2,1,0:T(1,128)S(1)}, u32[]{:S(2)}, u32[]{:S(2)}) collective-permute-start(f32[8,1,512]{2,1,0:T(1,128)S(1)} %add.96.refs_0_), channel_id=1, source_target_pairs={{0,16},{8,24},{16,0},{24,8},{1,17},{9,25},{17,1},{25,9},{2,18},{10... | collective-permute-start | bytes 49160 | tf_op jit(solution)/shard_map/ppermute | solution.py:329
  83.2 3.7 %collective-permute-start.14 = (f32[8,1,512]{2,1,0:T(1,128)S(1)}, f32[8,1,512]{2,1,0:T(1,128)S(1)}, u32[]{:S(2)}, u32[]{:S(2)}) collective-permute-start(f32[8,1,512]{2,1,0:T(1,128)S(1)} %add.96.refs_0_), channel_id=1, source_target_pairs={{0,24},{8,0},{16,8},{24,16},{1,25},{9,1},{17,9},{25,17},{2,26},{10... | collective-permute-start | bytes 49160 | tf_op jit(solution)/shard_map/ppermute | solution.py:329
  101.0 12.1 %collective-permute-start.15 = (bf16[256,768]{1,0:T(8,128)(2,1)S(1)}, bf16[256,768]{1,0:T(8,128)(2,1)S(1)}, u32[]{:S(2)}, u32[]{:S(2)}) collective-permute-start(bf16[256,768]{1,0:T(8,128)(2,1)S(1)} %get-tuple-element.86), channel_id=1, source_target_pairs={{0,2},{1,3},{2,0},{3,1},{4,6},{5,7},{6,4},{7,5},{8,10},{9,11},{10,... | collective-permute-start | bytes 1179656 | tf_op jit(solution)/shard_map/ppermute | solution.py:245
  102.6 18.0 %collective-permute-start.16 = (bf16[256,768]{1,0:T(8,128)(2,1)S(1)}, bf16[256,768]{1,0:T(8,128)(2,1)S(1)}, u32[]{:S(2)}, u32[]{:S(2)}) collective-permute-start(bf16[256,768]{1,0:T(8,128)(2,1)S(1)} %get-tuple-element.88), channel_id=1, source_target_pairs={{0,4},{1,5},{2,6},{3,7},{4,0},{5,1},{6,2},{7,3},{8,12},{9,13},{10,... | collective-permute-start | bytes 1179656 | tf_op jit(solution)/shard_map/ppermute | solution.py:245
  104.1 16.5 %collective-permute-start.17 = (bf16[256,768]{1,0:T(8,128)(2,1)S(1)}, bf16[256,768]{1,0:T(8,128)(2,1)S(1)}, u32[]{:S(2)}, u32[]{:S(2)}) collective-permute-start(bf16[256,768]{1,0:T(8,128)(2,1)S(1)} %get-tuple-element.87), channel_id=1, source_target_pairs={{0,6},{1,7},{2,4},{3,5},{4,2},{5,3},{6,0},{7,1},{8,14},{9,15},{10,... | collective-permute-start | bytes 1179656 | tf_op jit(solution)/shard_map/ppermute | solution.py:245
  121.5 17.3 %copy-start.1 = (f32[2048,768]{1,0:T(8,128)}, f32[2048,768]{1,0:T(8,128)S(1)}, u32[]{:S(2)}) copy-start(f32[2048,768]{1,0:T(8,128)S(1)} %get-tuple-element.84) | copy-start | bytes 18874372
  121.5 22.8 %collective-permute-start.19 = (f16[256,768]{1,0:T(8,128)(2,1)S(1)}, f16[256,768]{1,0:T(8,128)(2,1)S(1)}, u32[]{:S(2)}, u32[]{:S(2)}) collective-permute-start(f16[256,768]{1,0:T(8,128)(2,1)S(1)} %get-tuple-element.85), channel_id=1, source_target_pairs={{0,2},{1,3},{2,0},{3,1},{4,6},{5,7},{6,4},{7,5},{8,10},{9,11},{10,... | collective-permute-start | bytes 1179656 | tf_op jit(solution)/shard_map/ppermute | solution.py:245
  122.8 21.7 %collective-permute-start.21 = (f16[256,768]{1,0:T(8,128)(2,1)S(1)}, f16[256,768]{1,0:T(8,128)(2,1)S(1)}, u32[]{:S(2)}, u32[]{:S(2)}) collective-permute-start(f16[256,768]{1,0:T(8,128)(2,1)S(1)} %get-tuple-element.85), channel_id=1, source_target_pairs={{0,4},{1,5},{2,6},{3,7},{4,0},{5,1},{6,2},{7,3},{8,12},{9,13},{10,... | collective-permute-start | bytes 1179656 | tf_op jit(solution)/shard_map/ppermute | solution.py:245
  123.6 21.2 %collective-permute-start.23 = (f16[256,768]{1,0:T(8,128)(2,1)S(1)}, f16[256,768]{1,0:T(8,128)(2,1)S(1)}, u32[]{:S(2)}, u32[]{:S(2)}) collective-permute-start(f16[256,768]{1,0:T(8,128)(2,1)S(1)} %get-tuple-element.85), channel_id=1, source_target_pairs={{0,6},{1,7},{2,4},{3,5},{4,2},{5,3},{6,0},{7,1},{8,14},{9,15},{10,... | collective-permute-start | bytes 1179656 | tf_op jit(solution)/shard_map/ppermute | solution.py:245
  125.1 19.9 %collective-permute-start.18 = (f16[256,768]{1,0:T(8,128)(2,1)S(1)}, f16[256,768]{1,0:T(8,128)(2,1)S(1)}, u32[]{:S(2)}, u32[]{:S(2)}) collective-permute-start(f16[256,768]{1,0:T(8,128)(2,1)S(1)} %get-tuple-element.85), channel_id=1, source_target_pairs={{0,1},{1,0},{2,3},{3,2},{4,5},{5,4},{6,7},{7,6},{8,9},{9,8},{10,11... | collective-permute-start | bytes 1179656 | tf_op jit(solution)/shard_map/ppermute | solution.py:245
  125.1 13.8 %collective-permute-start.25 = (f32[1,1024]{1,0:T(1,128)S(1)}, f32[1,1024]{1,0:T(1,128)S(1)}, u32[]{:S(2)}, u32[]{:S(2)}) collective-permute-start(f32[1,1024]{1,0:T(1,128)S(1)} %get-tuple-element.83), channel_id=1, source_target_pairs={{0,2},{1,3},{2,0},{3,1},{4,6},{5,7},{6,4},{7,5},{8,10},{9,11},{10,... | collective-permute-start | bytes 12296 | tf_op jit(solution)/shard_map/ppermute | solution.py:245
  138.8 3.7 %collective-permute-start.26 = (f32[1,1024]{1,0:T(1,128)S(1)}, f32[1,1024]{1,0:T(1,128)S(1)}, u32[]{:S(2)}, u32[]{:S(2)}) collective-permute-start(f32[1,1024]{1,0:T(1,128)S(1)} %add.118), channel_id=1, source_target_pairs={{0,4},{1,5},{2,6},{3,7},{4,0},{5,1},{6,2},{7,3},{8,12},{9,13},{10,... | collective-permute-start | bytes 12296 | tf_op jit(solution)/shard_map/ppermute | solution.py:245
  142.5 1.2 collective-permute-start.27
  144.3 2.6 %collective-permute-start.20 = (f16[256,768]{1,0:T(8,128)(2,1)S(1)}, f16[256,768]{1,0:T(8,128)(2,1)S(1)}, u32[]{:S(2)}, u32[]{:S(2)}) collective-permute-start(f16[256,768]{1,0:T(8,128)(2,1)S(1)} %collective-permute-done.19), channel_id=1, source_target_pairs={{0,1},{1,0},{2,3},{3,2},{4,5},{5,4},{6,7},{7,6},{8,9},{9,8},{10,11... | collective-permute-start | bytes 1179656 | tf_op jit(solution)/shard_map/ppermute | solution.py:245
  144.5 4.3 %collective-permute-start.22 = (f16[256,768]{1,0:T(8,128)(2,1)S(1)}, f16[256,768]{1,0:T(8,128)(2,1)S(1)}, u32[]{:S(2)}, u32[]{:S(2)}) collective-permute-start(f16[256,768]{1,0:T(8,128)(2,1)S(1)} %collective-permute-done.21), channel_id=1, source_target_pairs={{0,1},{1,0},{2,3},{3,2},{4,5},{5,4},{6,7},{7,6},{8,9},{9,8},{10,11... | collective-permute-start | bytes 1179656 | tf_op jit(solution)/shard_map/ppermute | solution.py:245
  144.8 5.8 %collective-permute-start.24 = (f16[256,768]{1,0:T(8,128)(2,1)S(1)}, f16[256,768]{1,0:T(8,128)(2,1)S(1)}, u32[]{:S(2)}, u32[]{:S(2)}) collective-permute-start(f16[256,768]{1,0:T(8,128)(2,1)S(1)} %collective-permute-done.23), channel_id=1, source_target_pairs={{0,1},{1,0},{2,3},{3,2},{4,5},{5,4},{6,7},{7,6},{8,9},{9,8},{10,11... | collective-permute-start | bytes 1179656 | tf_op jit(solution)/shard_map/ppermute | solution.py:245

commit v3 on v2

--- a/solution.py
+++ b/solution.py
@@ -85,14 +85,18 @@
     totals[0] += jnp.sum(value, axis=0, keepdims=True)
 
 
-def score_block(ids, sources, choice, blocks, who, units, offsets, carried, column, n_columns):
+def score_block(
+    ids, sources, choice, blocks, who, units, offsets, carried, column, n_columns, number, n_parts
+):
     part, depth = sources[0].shape
     count = units.shape[0]
     tile = math.gcd(count, 512)
+    held = part * n_parts
+    column = column * n_parts + number
     shapes = (
-        jax.ShapeDtypeStruct((count, n_columns * part), jnp.float32),
-        jax.ShapeDtypeStruct((n_columns * part, depth), jnp.bfloat16),
-        jax.ShapeDtypeStruct((n_columns, 1, part), jnp.float32),
+        jax.ShapeDtypeStruct((count, n_columns * held), jnp.float32),
+        jax.ShapeDtypeStruct((n_columns * held, depth), jnp.bfloat16),
+        jax.ShapeDtypeStruct((n_columns, 1, held), jnp.float32),
     )
     n_sources = len(sources)
     aliases = {}
@@ -117,7 +121,7 @@
                 pl.BlockSpec((part, depth), lambda t, s: (column, 0)),
                 pl.BlockSpec(
                     (1, 1, part),
-                    lambda t, s: (pick(s[0], blocks) * CORES + ((s[1] % CORES) ^ who), 0, 0),
+                    lambda t, s: (pick(s[0], blocks) * CORES + ((s[1] % CORES) ^ who), 0, number),
                 ),
             ],
             scratch_shapes=[
@@ -250,25 +254,39 @@
         ]
         return lax.ppermute(array, ("blk", "rows"), pairs)
 
-    slots = [[(embeddings, list(range(n_places)))]] + [[] for _ in range(n_places - 1)]
+    last_parts = 2 if held % (2 * LANES) == 0 and n_places > 2 else 1
+
+    def parts_of(slot):
+        return last_parts if slot == n_places - 1 else 1
+
+    slots = [[[] for _ in range(parts_of(slot))] for slot in range(n_places)]
+    slots[0][0].append((embeddings, list(range(n_places))))
+    moves = [move + (part,) for part in range(last_parts) for move in moves if part < parts_of(move[3])]
 
     def start_ready(moves):
         groups = {}
         left = []
         for move in moves:
-            source, target, source_slot, slot = move
-            holds = [n for n, (_, places) in enumerate(slots[source_slot]) if source in places]
+            source, target, source_slot, slot, part = move
+            whole = parts_of(source_slot) < parts_of(slot)
+            holders = slots[source_slot][0 if whole else part]
+            holds = [n for n, (_, places) in enumerate(holders) if source in places]
             if not holds:
                 left.append(move)
                 continue
             turn = 0
-            while any(source == s for s, _ in groups.get((slot, source_slot, holds[0], turn), [])):
+            key = lambda turn: (part, slot, source_slot, holds[0], turn)
+            while any(source == s for s, _ in groups.get(key(turn), [])):
                 turn += 1
-            groups.setdefault((slot, source_slot, holds[0], turn), []).append((source, target))
-        moved = [
-            (slot, lax.ppermute(slots[source_slot][hold][0], "blk", pairs), [p[1] for p in pairs])
-            for (slot, source_slot, hold, _), pairs in sorted(groups.items())
-        ]
+            groups.setdefault(key(turn), []).append((source, target))
+        moved = []
+        for (part, slot, source_slot, hold, _), pairs in sorted(groups.items()):
+            whole = parts_of(source_slot) < parts_of(slot)
+            array = slots[source_slot][0 if whole else part][hold][0]
+            if whole:
+                size = held // parts_of(slot)
+                array = array[part * size : (part + 1) * size]
+            moved.append((slot, part, lax.ppermute(array, "blk", pairs), [p[1] for p in pairs]))
         return moved, left
 
     def merged(candidates):
@@ -289,10 +307,11 @@
     n_columns = n_places * CORES
     carried = None
 
-    def scores_of(slot, carried):
+    def scores_of(slot, part, carried):
         blocks = [order[slot] for order in orders]
-        swapped = [(swap_cores(array, places), places) for array, places in slots[slot]]
-        for who, candidates in enumerate((slots[slot], swapped)):
+        arrived = slots[slot][part]
+        swapped = [(swap_cores(array, places), places) for array, places in arrived]
+        for who, candidates in enumerate((arrived, swapped)):
             choice = [
                 next(n for n, (_, places) in enumerate(candidates) if spot in places)
                 for spot in range(n_places)
@@ -308,21 +327,28 @@
                 carried,
                 slot * CORES + who,
                 n_columns,
+                part,
+                parts_of(slot),
             )
         return carried
 
+    def arrive(moved):
+        for slot, part, array, places in moved:
+            slots[slot][part].append((array, places))
+
     for turn in range(n_places):
-        while sum(len(places) for _, places in slots[turn]) < n_places:
+        for part in range(parts_of(turn)):
+            while sum(len(places) for _, places in slots[turn][part]) < n_places:
+                moved, moves = start_ready(moves)
+                arrive(moved)
+            slots[turn][part] = merged(slots[turn][part])
             moved, moves = start_ready(moves)
-            for slot, array, places in moved:
-                slots[slot].append((array, places))
-        slots[turn] = merged(slots[turn])
-        moved, moves = start_ready(moves)
-        carried = scores_of(turn, carried)
-        if moved:
-            arrays, carried = lax.optimization_barrier(([array for _, array, _ in moved], carried))
-            for (slot, _, places), array in zip(moved, arrays):
-                slots[slot].append((array, places))
+            carried = scores_of(turn, part, carried)
+            arrive([m for m in moved if m[1] + 1 < parts_of(m[0])])
+            moved = [m for m in moved if m[1] + 1 == parts_of(m[0])]
+            if moved:
+                arrays, carried = lax.optimization_barrier(([m[2] for m in moved], carried))
+                arrive([(slot, p, array, places) for (slot, p, _, places), array in zip(moved, arrays)])
     scores, rows, totals = carried
     totals = totals + exchange(totals, 1)
     all_totals = [totals] + [
@@ -333,13 +359,16 @@
     sent, summed, masses = sum_rows(ids, orders, all_totals, scores, rows, n_owners)
     far = [CORES * away for away in range(1, n_owners)]
     arrived = [exchange(sent[number], distance) for number, distance in enumerate(far)]
+    arrived_masses = [exchange(masses, distance) for distance in far]
+    arrived, arrived_masses = lax.optimization_barrier((arrived, arrived_masses))
     for array in arrived:
         summed = summed + array.astype(jnp.float32)
 
-    distance = CORES
-    while distance < n_rows:
-        masses = masses + exchange(masses, distance)
-        distance *= 2
+    unit = summed * lax.rsqrt(jnp.sum(summed * summed, axis=1, keepdims=True) + 1e-06)
+    unit = unit.astype(jnp.float16)
+    size = unit.shape[0]
+    pieces = [exchange(unit, distance) for distance in far]
+    masses = functools.reduce(jnp.add, arrived_masses, masses)
     masses = masses.reshape(half)
     other_masses = exchange(masses, 1)
     both = jnp.where(
@@ -347,16 +376,18 @@
         jnp.concatenate([masses, other_masses]),
         jnp.concatenate([other_masses, masses]),
     )
-
-    unit = summed * lax.rsqrt(jnp.sum(summed * summed, axis=1, keepdims=True) + 1e-06)
-    unit = unit.astype(jnp.float16)
-    size = unit.shape[0]
+    def place_piece(result, distance, flip, array):
+        start = (core ^ flip) * half + lax.div(me ^ distance, CORES) * size
+        return lax.dynamic_update_slice(result, array.astype(jnp.float32), (start, 0))
+
     result = jnp.zeros((local_centroids, depth), jnp.float32)
-    pieces = [(0, unit)] + [(distance, exchange(unit, distance)) for distance in far]
-    for distance, piece in pieces:
-        for flip, array in ((0, piece), (1, exchange(piece, 1))):
-            start = (core ^ flip) * half + lax.div(me ^ distance, CORES) * size
-            result = lax.dynamic_update_slice(result, array.astype(jnp.float32), (start, 0))
+    result = place_piece(result, 0, 0, unit)
+    result = place_piece(result, 0, 1, exchange(unit, 1))
+    pieces, result = lax.optimization_barrier((pieces, result))
+    swapped = [exchange(piece, 1) for piece in pieces]
+    for flip, arrays in ((0, pieces), (1, swapped)):
+        for distance, array in zip(far, arrays):
+            result = place_piece(result, distance, flip, array)
     count = local_centroids * n_places
     factor = count / (held * n_rows * n_places)
     return (result, both * factor)

time: 152 us -> 157 us (1.033)
  starting transfers between devices: 26.4 us -> 34.5 us
  waiting for transfers between devices: 70.7 us -> 63.3 us
  Pallas kernels: 39.7 us -> 43.9 us
    ppermute x5 -> x7, waiting for transfers between devices: 34 us -> 29.4 us  [start_ready(): lax.ppermute(array, 'blk', pairs)]
    pallas_call x8 -> x10, Pallas kernels: 25.6 us -> 29.8 us  [score_block(): pl.pallas_call(functools.partial(score_kernel, n_sources, choice), grid_s...]
    ppermute x14 -> x15, starting transfers between devices: 10.2 us -> 13.7 us  [exchange(): lax.ppermute(array, 'rows', [(i, i ^ distance) for i in range(n_rows)])]
    ppermute x14 -> x15, waiting for transfers between devices: 33.6 us -> 30.8 us  [exchange(): lax.ppermute(array, 'rows', [(i, i ^ distance) for i in range(n_rows)])]
    ppermute x6 -> x8, starting transfers between devices: 5.76 us -> 8.33 us  [swap_cores(): return lax.ppermute(array, ('blk', 'rows'), pairs)]
    ppermute x5 -> x7, starting transfers between devices: 6.64 us -> 8.59 us  [start_ready(): lax.ppermute(array, 'blk', pairs)]
  transfers between devices with their start and end apart: 28 -> 33, of which waited for: 11 -> 12; matrix products, arithmetic and copies ran while one was open for 7% -> 7% of each run, Pallas kernels for 15% -> 17%
where the time goes in v3:
time: 157 us
  waiting for transfers between devices  63.3 us (40%)
  Pallas kernels  43.9 us (28%)
  starting transfers between devices  34.5 us (22%)
  other arithmetic  12 us (8%)
  local copies, waits for them, and re-layouts  1.87 us (1%)
    ppermute x15, waiting for transfers between devices, exchange(): lax.ppermute(array, 'rows', [(i, i ^ distance) for i in range(n_rows)])  30.8 us
    pallas_call x10, Pallas kernels, score_block(): pl.pallas_call(functools.partial(score_kernel, n_sources, choice), grid_s...  29.8 us
    ppermute x7, waiting for transfers between devices, start_ready(): lax.ppermute(array, 'blk', pairs)  29.4 us
    pallas_call x1, Pallas kernels, sum_rows(): pl.pallas_call(functools.partial(sum_kernel, orders, len(totals)), grid_s...  14 us
    ppermute x15, starting transfers between devices, exchange(): lax.ppermute(array, 'rows', [(i, i ^ distance) for i in range(n_rows)])  13.7 us
    ppermute x7, starting transfers between devices, start_ready(): lax.ppermute(array, 'blk', pairs)  8.59 us
    ppermute x8, starting transfers between devices, swap_cores(): return lax.ppermute(array, ('blk', 'rows'), pairs)  8.33 us
    dynamic_update_slice x8, other arithmetic, place_piece(): lax.dynamic_update_slice(result, array.astype(jnp.float32), (start, 0))  6.75 us
  transfers between devices with their start and end apart: 33, of which 12 were waited for; matrix products, arithmetic and copies ran while one was open for 7% of the time, Pallas kernels for 17%

profile of v3, /device:TPU:0, one launch (start us, length us, event | category | flops | bytes accessed | tf_op | source)
XLA Modules:
  0.0 156.6 jit_solution(18378155167907927928)
XLA Ops:
  1.1 2.7 %collective-permute-start = (bf16[512,768]{1,0:T(8,128)(2,1)}, bf16[512,768]{1,0:T(8,128)(2,1)S(1)}, u32[]{:S(2)}, u32[]{:S(2)}) collective-permute-start(bf16[512,768]{1,0:T(8,128)(2,1)} %refs_0_.1), channel_id=1, source_target_pairs={{8,0},{0,8},{24,16},{16,24},{9,1},{1,9},{25,17},{17,25},{10,2},{2,... | collective-permute-start | bytes 2359304 | tf_op jit(solution)/shard_map/ppermute | solution.py:289
  4.6 1.8 %fusion = f32[1024]{0:T(1024)S(1)} fusion(bf16[2048,768]{1,0:T(8,128)(2,1)} %param.4, s32[]{:T(128)S(6)} %select_n.36), kind=kLoop, calls=%fused_computation.2 | loop fusion | flops 2358272 | bytes 1576964 | tf_op jit(solution)/shard_map/reduce_sum | solution.py:20
  7.1 1.7 %fusion.1.refs_1_.refs_2_ = bf16[1024,768]{1,0:T(8,128)(2,1)S(1)} fusion(f32[1024]{0:T(1024)S(1)} %add_rsqrt_fusion, bf16[2048,768]{1,0:T(8,128)(2,1)} %param.4, s32[]{:T(128)S(6)} %select_n.36), kind=kLoop, calls=%fused_computation.3 | loop fusion | flops 2359296 | bytes 3149828 | tf_op jit(solution)/shard_map/convert_element_type | solution.py:20
  10.1 3.3 %scores.10 = (f32[1024,4096]{1,0:T(8,128)}, bf16[4096,768]{1,0:T(8,128)(2,1)}, f32[8,1,512]{2,1,0:T(1,128)S(1)}) custom-call(s32[2]{0:T(128)S(1)} %pad_add_fusion.ids, bf16[512,768]{1,0:T(8,128)(2,1)S(1)} %copy-done, bf16[1024,768]{1,0:T(8,128)(2,1)S(1)} %fusion.1.refs_1_.refs_2_, f32[1024,128]{1,0:T(8,128)S(1)} %broadcast_in_dim.4.refs_2_.refs_3_), custom_call_target="tpu_custom_call" | custom-call | flops 805306368 | bytes 7340032 | tf_op jit(solution)/shard_map/scores/pallas_call | solution.py:108
  13.5 3.2 %scores.11 = (f32[1024,4096]{1,0:T(8,128)}, bf16[4096,768]{1,0:T(8,128)(2,1)}, f32[8,1,512]{2,1,0:T(1,128)S(1)}) custom-call(s32[2]{0:T(128)S(1)} %pad_add_fusion.ids, bf16[512,768]{1,0:T(8,128)(2,1)S(1)} %collective-permute-done.2.refs_0_, bf16[1024,768]{1,0:T(8,128)(2,1)S(1)} %fusion.1.refs_1_.refs_2_, ...), custom_call_target="tpu_custom_call", output_to_operand_aliasing={{0}: (4, {}), {1}: (5, {}), {2}: (6, {})} | custom-call | flops 805306368 | bytes 7340032 | tf_op jit(solution)/shard_map/scores/pallas_call | solution.py:108
  16.6 5.5 %collective-permute-done.refs_0_ = bf16[512,768]{1,0:T(8,128)(2,1)S(1)} collective-permute-done((bf16[512,768]{1,0:T(8,128)(2,1)}, bf16[512,768]{1,0:T(8,128)(2,1)S(1)}, u32[]{:S(2)}, u32[]{:S(2)}) %collective-permute-start) | collective-permute-done | bytes 786464 | tf_op jit(solution)/shard_map/ppermute | solution.py:289
  25.6 3.2 %scores.12 = (f32[1024,4096]{1,0:T(8,128)}, bf16[4096,768]{1,0:T(8,128)(2,1)}, f32[8,1,512]{2,1,0:T(1,128)S(1)}) custom-call(s32[2]{0:T(128)S(1)} %pad_add_fusion.ids, bf16[512,768]{1,0:T(8,128)(2,1)S(1)} %collective-permute-done.refs_0_, bf16[1024,768]{1,0:T(8,128)(2,1)S(1)} %fusion.1.refs_1_.refs_2_, ...), custom_call_target="tpu_custom_call", output_to_operand_aliasing={{0}: (4, {}), {1}: (5, {}), {2}: (6, {})} | custom-call | flops 805306368 | bytes 7340032 | tf_op jit(solution)/shard_map/scores/pallas_call | solution.py:108
  28.8 3.2 %scores.13 = (f32[1024,4096]{1,0:T(8,128)}, bf16[4096,768]{1,0:T(8,128)(2,1)}, f32[8,1,512]{2,1,0:T(1,128)S(1)}) custom-call(s32[2]{0:T(128)S(1)} %pad_add_fusion.ids, bf16[512,768]{1,0:T(8,128)(2,1)S(1)} %collective-permute-done.5.refs_0_, bf16[1024,768]{1,0:T(8,128)(2,1)S(1)} %fusion.1.refs_1_.refs_2_, ...), custom_call_target="tpu_custom_call", output_to_operand_aliasing={{0}: (4, {}), {1}: (5, {}), {2}: (6, {})} | custom-call | flops 805306368 | bytes 7340032 | tf_op jit(solution)/shard_map/scores/pallas_call | solution.py:108
  32.0 14.4 %collective-permute-done.3.refs_1_ = bf16[512,768]{1,0:T(8,128)(2,1)S(1)} collective-permute-done((bf16[512,768]{1,0:T(8,128)(2,1)S(1)}, bf16[512,768]{1,0:T(8,128)(2,1)S(1)}, u32[]{:S(2)}, u32[]{:S(2)}) %collective-permute-start.3) | collective-permute-done | bytes 786464 | tf_op jit(solution)/shard_map/ppermute | solution.py:289
  46.4 1.9 %collective-permute-start.9 = (bf16[512,768]{1,0:T(8,128)(2,1)S(1)}, bf16[512,768]{1,0:T(8,128)(2,1)S(1)}, u32[]{:S(2)}, u32[]{:S(2)}) collective-permute-start(bf16[512,768]{1,0:T(8,128)(2,1)S(1)} %collective-permute-done.3.refs_1_), channel_id=1, source_target_pairs={{0,1},{1,0},{2,3},{3,2},{4,5},{5,4},{6,7},{7,6},{24,25},{25,24},{2... | collective-permute-start | bytes 2359304 | tf_op jit(solution)/shard_map/ppermute | solution.py:255
  51.6 3.2 %scores.14 = (f32[1024,4096]{1,0:T(8,128)}, bf16[4096,768]{1,0:T(8,128)(2,1)}, f32[8,1,512]{2,1,0:T(1,128)S(1)}) custom-call(s32[2]{0:T(128)S(1)} %pad_add_fusion.ids, bf16[512,768]{1,0:T(8,128)(2,1)S(1)} %collective-permute-done.1.refs_0_, ...), custom_call_target="tpu_custom_call", output_to_operand_aliasing={{0}: (5, {}), {1}: (6, {}), {2}: (7, {})} | custom-call | flops 805306368 | bytes 7340032 | tf_op jit(solution)/shard_map/scores/pallas_call | solution.py:108
  55.6 6.6 %collective-permute-done.13.refs_1_ = bf16[256,768]{1,0:T(8,128)(2,1)S(1)} collective-permute-done((bf16[256,768]{1,0:T(8,128)(2,1)S(1)}, bf16[256,768]{1,0:T(8,128)(2,1)S(1)}, u32[]{:S(2)}, u32[]{:S(2)}) %collective-permute-start.13) | collective-permute-done | bytes 393248 | tf_op jit(solution)/shard_map/ppermute | solution.py:289
  62.1 1.9 %collective-permute-start.14 = (bf16[256,768]{1,0:T(8,128)(2,1)S(1)}, bf16[256,768]{1,0:T(8,128)(2,1)S(1)}, u32[]{:S(2)}, u32[]{:S(2)}) collective-permute-start(bf16[256,768]{1,0:T(8,128)(2,1)S(1)} %collective-permute-done.13.refs_1_), channel_id=1, source_target_pairs={{0,1},{1,0},{2,3},{3,2},{4,5},{5,4},{6,7},{7,6},{24,25},{25,24},{2... | collective-permute-start | bytes 1179656 | tf_op jit(solution)/shard_map/ppermute | solution.py:255
  64.1 3.2 %scores.15 = (f32[1024,4096]{1,0:T(8,128)}, bf16[4096,768]{1,0:T(8,128)(2,1)}, f32[8,1,512]{2,1,0:T(1,128)S(1)}) custom-call(s32[2]{0:T(128)S(1)} %pad_add_fusion.ids, bf16[512,768]{1,0:T(8,128)(2,1)S(1)} %collective-permute-done.8.refs_0_, ...), custom_call_target="tpu_custom_call", output_to_operand_aliasing={{0}: (5, {}), {1}: (6, {}), {2}: (7, {})} | custom-call | flops 805306368 | bytes 7340032 | tf_op jit(solution)/shard_map/scores/pallas_call | solution.py:108
  67.3 2.9 %collective-permute-done.7.refs_1_ = bf16[256,768]{1,0:T(8,128)(2,1)S(1)} collective-permute-done((bf16[256,768]{1,0:T(8,128)(2,1)S(1)}, bf16[256,768]{1,0:T(8,128)(2,1)S(1)}, u32[]{:S(2)}, u32[]{:S(2)}) %collective-permute-start.7) | collective-permute-done | bytes 393248 | tf_op jit(solution)/shard_map/ppermute | solution.py:289
  70.2 1.9 %collective-permute-start.10 = (bf16[256,768]{1,0:T(8,128)(2,1)S(1)}, bf16[256,768]{1,0:T(8,128)(2,1)S(1)}, u32[]{:S(2)}, u32[]{:S(2)}) collective-permute-start(bf16[256,768]{1,0:T(8,128)(2,1)S(1)} %collective-permute-done.7.refs_1_), channel_id=1, source_target_pairs={{0,1},{1,0},{2,3},{3,2},{4,5},{5,4},{6,7},{7,6},{24,25},{25,24},{2... | collective-permute-start | bytes 1179656 | tf_op jit(solution)/shard_map/ppermute | solution.py:255
  72.1 2.6 %scores.16 = (f32[1024,4096]{1,0:T(8,128)}, bf16[4096,768]{1,0:T(8,128)(2,1)}, f32[8,1,512]{2,1,0:T(1,128)S(1)}) custom-call(s32[2]{0:T(128)S(1)} %pad_add_fusion.ids, bf16[256,768]{1,0:T(8,128)(2,1)S(1)} %collective-permute-done.11.refs_0_, ...), custom_call_target="tpu_custom_call", output_to_operand_aliasing={{0}: (5, {}), {1}: (6, {}), {2}: (7, {})} | custom-call | flops 402653184 | bytes 5242880 | tf_op jit(solution)/shard_map/scores/pallas_call | solution.py:108
  74.7 2.7 %scores.17 = (f32[1024,4096]{1,0:T(8,128)}, bf16[4096,768]{1,0:T(8,128)(2,1)}, f32[8,1,512]{2,1,0:T(1,128)S(1)}) custom-call(s32[2]{0:T(128)S(1)} %pad_add_fusion.ids, bf16[256,768]{1,0:T(8,128)(2,1)S(1)} %collective-permute-done.12.refs_0_, ...), custom_call_target="tpu_custom_call", output_to_operand_aliasing={{0}: (5, {}), {1}: (6, {}), {2}: (7, {})} | custom-call | flops 402653184 | bytes 5242880 | tf_op jit(solution)/shard_map/scores/pallas_call | solution.py:108
  77.4 2.6 %scores.18 = (f32[1024,4096]{1,0:T(8,128)}, bf16[4096,768]{1,0:T(8,128)(2,1)}, f32[8,1,512]{2,1,0:T(1,128)S(1)}) custom-call(s32[2]{0:T(128)S(1)} %pad_add_fusion.ids, bf16[256,768]{1,0:T(8,128)(2,1)S(1)} %collective-permute-done.4.refs_0_, ...), custom_call_target="tpu_custom_call", output_to_operand_aliasing={{0}: (5, {}), {1}: (6, {}), {2}: (7, {})} | custom-call | flops 402653184 | bytes 5242880 | tf_op jit(solution)/shard_map/scores/pallas_call | solution.py:108
  80.1 2.6 %scores.19 = (f32[1024,4096]{1,0:T(8,128)}, bf16[4096,768]{1,0:T(8,128)(2,1)}, f32[8,1,512]{2,1,0:T(1,128)S(1)}) custom-call(s32[2]{0:T(128)S(1)} %pad_add_fusion.ids, bf16[256,768]{1,0:T(8,128)(2,1)S(1)} %collective-permute-done.6.refs_0_, ...), custom_call_target="tpu_custom_call", output_to_operand_aliasing={{0}: (5, {}), {1}: (6, {}), {2}: (7, {})} | custom-call | flops 402653184 | bytes 5242880 | tf_op jit(solution)/shard_map/scores/pallas_call | solution.py:108
  84.2 3.2 %collective-permute-start.17 = (f32[8,1,512]{2,1,0:T(1,128)S(1)}, f32[8,1,512]{2,1,0:T(1,128)S(1)}, u32[]{:S(2)}, u32[]{:S(2)}) collective-permute-start(f32[8,1,512]{2,1,0:T(1,128)S(1)} %add.99.refs_0_), channel_id=1, source_target_pairs={{0,16},{8,24},{16,0},{24,8},{1,17},{9,25},{17,1},{25,9},{2,18},{10... | collective-permute-start | bytes 49160 | tf_op jit(solution)/shard_map/ppermute | solution.py:355
  88.0 1.9 %collective-permute-done.16.refs_1_ = f32[8,1,512]{2,1,0:T(1,128)S(1)} collective-permute-done((f32[8,1,512]{2,1,0:T(1,128)S(1)}, f32[8,1,512]{2,1,0:T(1,128)S(1)}, u32[]{:S(2)}, u32[]{:S(2)}) %collective-permute-start.16) | collective-permute-done | bytes 16416 | tf_op jit(solution)/shard_map/ppermute | solution.py:355
  91.1 14.0 %sums.1 = (bf16[3,256,768]{2,1,0:T(8,128)(2,1)S(1)}, f32[256,768]{1,0:T(8,128)S(1)}, f32[1,1024]{1,0:T(1,128)S(1)}) custom-call(s32[2]{0:T(128)S(1)} %pad_add_fusion.ids, f32[8,1,512]{2,1,0:T(1,128)S(1)} %add.99.refs_0_, f32[8,1,512]{2,1,0:T(1,128)S(1)} %collective-permute-done.16.refs_1_, f32[8,1,512]{2,1,0:T(1,128)S(1)} %collective-permute-done.17.refs_2_, ...), custom_call_target="tpu_custom_call" | custom-call | flops 6442450944 | bytes 26214400 | tf_op jit(solution)/shard_map/sums/pallas_call | solution.py:199
  105.3 1.6 collective-permute-start.19
  106.8 1.5 collective-permute-start.20
  110.3 1.5 collective-permute-start.23
  111.8 11.9 %collective-permute-done.22 = f32[1,1024]{1,0:T(1,128)S(1)} collective-permute-done((f32[1,1024]{1,0:T(1,128)S(1)}, f32[1,1024]{1,0:T(1,128)S(1)}, u32[]{:S(2)}, u32[]{:S(2)}) %collective-permute-start.22) | collective-permute-done | bytes 4128 | tf_op jit(solution)/shard_map/ppermute | solution.py:249
  123.7 2.4 %collective-permute-start.24 = (f32[1,1024]{1,0:T(1,128)S(1)}, f32[1,1024]{1,0:T(1,128)S(1)}, u32[]{:S(2)}, u32[]{:S(2)}) collective-permute-start(f32[1,1024]{1,0:T(1,128)S(1)} %get-tuple-element.105), channel_id=1, source_target_pairs={{0,6},{1,7},{2,4},{3,5},{4,2},{5,3},{6,0},{7,1},{8,14},{9,15},{10,... | collective-permute-start | bytes 12296 | tf_op jit(solution)/shard_map/ppermute | solution.py:249
  126.1 2.1 %collective-permute-done.24 = f32[1,1024]{1,0:T(1,128)S(1)} collective-permute-done((f32[1,1024]{1,0:T(1,128)S(1)}, f32[1,1024]{1,0:T(1,128)S(1)}, u32[]{:S(2)}, u32[]{:S(2)}) %collective-permute-start.24) | collective-permute-done | bytes 4128 | tf_op jit(solution)/shard_map/ppermute | solution.py:249
  129.3 1.6 collective-permute-start.25
  135.6 5.6 %collective-permute-done.25 = f16[256,768]{1,0:T(8,128)(2,1)S(1)} collective-permute-done((f16[256,768]{1,0:T(8,128)(2,1)S(1)}, f16[256,768]{1,0:T(8,128)(2,1)S(1)}, u32[]{:S(2)}, u32[]{:S(2)}) %collective-permute-start.25) | collective-permute-done | bytes 393248 | tf_op jit(solution)/shard_map/ppermute | solution.py:249
  141.3 9.2 %collective-permute-done.26 = f16[256,768]{1,0:T(8,128)(2,1)S(1)} collective-permute-done((f16[256,768]{1,0:T(8,128)(2,1)S(1)}, f16[256,768]{1,0:T(8,128)(2,1)S(1)}, u32[]{:S(2)}, u32[]{:S(2)}) %collective-permute-start.26) | collective-permute-done | bytes 393248 | tf_op jit(solution)/shard_map/ppermute | solution.py:249
  (71 shorter events, 27.9 us)
Async XLA Ops:
  0.6 12.8 %collective-permute-start.2 = (bf16[512,768]{1,0:T(8,128)(2,1)}, bf16[512,768]{1,0:T(8,128)(2,1)S(1)}, u32[]{:S(2)}, u32[]{:S(2)}) collective-permute-start(bf16[512,768]{1,0:T(8,128)(2,1)} %refs_0_.1), channel_id=1, source_target_pairs={{0,1},{1,0},{2,3},{3,2},{4,5},{5,4},{6,7},{7,6},{8,9},{9,8},{10,11... | collective-permute-start | bytes 2359304 | tf_op jit(solution)/shard_map/ppermute | solution.py:255
  1.1 21.0 %collective-permute-start = (bf16[512,768]{1,0:T(8,128)(2,1)}, bf16[512,768]{1,0:T(8,128)(2,1)S(1)}, u32[]{:S(2)}, u32[]{:S(2)}) collective-permute-start(bf16[512,768]{1,0:T(8,128)(2,1)} %refs_0_.1), channel_id=1, source_target_pairs={{8,0},{0,8},{24,16},{16,24},{9,1},{1,9},{25,17},{17,25},{10,2},{2,... | collective-permute-start | bytes 2359304 | tf_op jit(solution)/shard_map/ppermute | solution.py:289
  3.8 18.3 %collective-permute-start.1 = (bf16[512,768]{1,0:T(8,128)(2,1)}, bf16[512,768]{1,0:T(8,128)(2,1)S(1)}, u32[]{:S(2)}, u32[]{:S(2)}) collective-permute-start(bf16[512,768]{1,0:T(8,128)(2,1)} %refs_0_.1), channel_id=1, source_target_pairs={{16,8},{8,16},{17,9},{9,17},{18,10},{10,18},{19,11},{11,19},{20,12... | collective-permute-start | bytes 2359304 | tf_op jit(solution)/shard_map/ppermute | solution.py:289
  22.1 6.6 %collective-permute-start.5 = (bf16[512,768]{1,0:T(8,128)(2,1)S(1)}, bf16[512,768]{1,0:T(8,128)(2,1)S(1)}, u32[]{:S(2)}, u32[]{:S(2)}) collective-permute-start(bf16[512,768]{1,0:T(8,128)(2,1)S(1)} %collective-permute-done.refs_0_), channel_id=1, source_target_pairs={{0,1},{1,0},{2,3},{3,2},{4,5},{5,4},{6,7},{7,6},{8,9},{9,8},{10,11... | collective-permute-start | bytes 2359304 | tf_op jit(solution)/shard_map/ppermute | solution.py:255
  22.1 24.3 %collective-permute-start.3 = (bf16[512,768]{1,0:T(8,128)(2,1)S(1)}, bf16[512,768]{1,0:T(8,128)(2,1)S(1)}, u32[]{:S(2)}, u32[]{:S(2)}) collective-permute-start(bf16[512,768]{1,0:T(8,128)(2,1)S(1)} %collective-permute-done.1.refs_0_), channel_id=1, source_target_pairs={{8,0},{16,24},{9,1},{17,25},{10,2},{18,26},{11,3},{19,27},{12,4},{... | collective-permute-start | bytes 2359304 | tf_op jit(solution)/shard_map/ppermute | solution.py:289
  23.5 8.5 %collective-permute-start.4 = (bf16[256,768]{1,0:T(8,128)(2,1)S(1)}, bf16[256,768]{1,0:T(8,128)(2,1)S(1)}, u32[]{:S(2)}, u32[]{:S(2)}) collective-permute-start(bf16[256,768]{1,0:T(8,128)(2,1)S(1)} %get-tuple-element.122), channel_id=1, source_target_pairs={{16,8},{8,16},{17,9},{9,17},{18,10},{10,18},{19,11},{11,19},{20,12... | collective-permute-start | bytes 1179656 | tf_op jit(solution)/shard_map/ppermute | solution.py:289
  24.2 30.7 %collective-permute-start.8 = (bf16[512,768]{1,0:T(8,128)(2,1)S(1)}, bf16[512,768]{1,0:T(8,128)(2,1)S(1)}, u32[]{:S(2)}, u32[]{:S(2)}) collective-permute-start(bf16[512,768]{1,0:T(8,128)(2,1)S(1)} %collective-permute-done.1.refs_0_), channel_id=1, source_target_pairs={{8,9},{9,8},{10,11},{11,10},{12,13},{13,12},{14,15},{15,14},{16,17... | collective-permute-start | bytes 2359304 | tf_op jit(solution)/shard_map/ppermute | solution.py:255
  24.9 23.4 %collective-permute-start.11 = (bf16[256,768]{1,0:T(8,128)(2,1)S(1)}, bf16[256,768]{1,0:T(8,128)(2,1)S(1)}, u32[]{:S(2)}, u32[]{:S(2)}) collective-permute-start(bf16[256,768]{1,0:T(8,128)(2,1)S(1)} %get-tuple-element.121), channel_id=1, source_target_pairs={{16,8},{8,16},{17,9},{9,17},{18,10},{10,18},{19,11},{11,19},{20,12... | collective-permute-start | bytes 1179656 | tf_op jit(solution)/shard_map/ppermute | solution.py:289
  46.4 17.7 %collective-permute-start.9 = (bf16[512,768]{1,0:T(8,128)(2,1)S(1)}, bf16[512,768]{1,0:T(8,128)(2,1)S(1)}, u32[]{:S(2)}, u32[]{:S(2)}) collective-permute-start(bf16[512,768]{1,0:T(8,128)(2,1)S(1)} %collective-permute-done.3.refs_1_), channel_id=1, source_target_pairs={{0,1},{1,0},{2,3},{3,2},{4,5},{5,4},{6,7},{7,6},{24,25},{25,24},{2... | collective-permute-start | bytes 2359304 | tf_op jit(solution)/shard_map/ppermute | solution.py:255
  48.3 13.8 %collective-permute-start.13 = (bf16[256,768]{1,0:T(8,128)(2,1)S(1)}, bf16[256,768]{1,0:T(8,128)(2,1)S(1)}, u32[]{:S(2)}, u32[]{:S(2)}) collective-permute-start(bf16[256,768]{1,0:T(8,128)(2,1)S(1)} %collective-permute-done.11.refs_0_), channel_id=1, source_target_pairs={{8,0},{16,24},{9,1},{17,25},{10,2},{18,26},{11,3},{19,27},{12,4},{... | collective-permute-start | bytes 1179656 | tf_op jit(solution)/shard_map/ppermute | solution.py:289
  49.6 20.5 %collective-permute-start.7 = (bf16[256,768]{1,0:T(8,128)(2,1)S(1)}, bf16[256,768]{1,0:T(8,128)(2,1)S(1)}, u32[]{:S(2)}, u32[]{:S(2)}) collective-permute-start(bf16[256,768]{1,0:T(8,128)(2,1)S(1)} %collective-permute-done.4.refs_0_), channel_id=1, source_target_pairs={{8,0},{16,24},{9,1},{17,25},{10,2},{18,26},{11,3},{19,27},{12,4},{... | collective-permute-start | bytes 1179656 | tf_op jit(solution)/shard_map/ppermute | solution.py:289
  50.9 23.8 %collective-permute-start.12 = (bf16[256,768]{1,0:T(8,128)(2,1)S(1)}, bf16[256,768]{1,0:T(8,128)(2,1)S(1)}, u32[]{:S(2)}, u32[]{:S(2)}) collective-permute-start(bf16[256,768]{1,0:T(8,128)(2,1)S(1)} %collective-permute-done.11.refs_0_), channel_id=1, source_target_pairs={{8,9},{9,8},{10,11},{11,10},{12,13},{13,12},{14,15},{15,14},{16,17... | collective-permute-start | bytes 1179656 | tf_op jit(solution)/shard_map/ppermute | solution.py:255
  54.9 25.2 %collective-permute-start.6 = (bf16[256,768]{1,0:T(8,128)(2,1)S(1)}, bf16[256,768]{1,0:T(8,128)(2,1)S(1)}, u32[]{:S(2)}, u32[]{:S(2)}) collective-permute-start(bf16[256,768]{1,0:T(8,128)(2,1)S(1)} %collective-permute-done.4.refs_0_), channel_id=1, source_target_pairs={{8,9},{9,8},{10,11},{11,10},{12,13},{13,12},{14,15},{15,14},{16,17... | collective-permute-start | bytes 1179656 | tf_op jit(solution)/shard_map/ppermute | solution.py:255
  62.1 12.6 %collective-permute-start.14 = (bf16[256,768]{1,0:T(8,128)(2,1)S(1)}, bf16[256,768]{1,0:T(8,128)(2,1)S(1)}, u32[]{:S(2)}, u32[]{:S(2)}) collective-permute-start(bf16[256,768]{1,0:T(8,128)(2,1)S(1)} %collective-permute-done.13.refs_1_), channel_id=1, source_target_pairs={{0,1},{1,0},{2,3},{3,2},{4,5},{5,4},{6,7},{7,6},{24,25},{25,24},{2... | collective-permute-start | bytes 1179656 | tf_op jit(solution)/shard_map/ppermute | solution.py:255
  70.2 9.9 %collective-permute-start.10 = (bf16[256,768]{1,0:T(8,128)(2,1)S(1)}, bf16[256,768]{1,0:T(8,128)(2,1)S(1)}, u32[]{:S(2)}, u32[]{:S(2)}) collective-permute-start(bf16[256,768]{1,0:T(8,128)(2,1)S(1)} %collective-permute-done.7.refs_1_), channel_id=1, source_target_pairs={{0,1},{1,0},{2,3},{3,2},{4,5},{5,4},{6,7},{7,6},{24,25},{25,24},{2... | collective-permute-start | bytes 1179656 | tf_op jit(solution)/shard_map/ppermute | solution.py:255
  82.7 1.4 collective-permute-start.15
  84.1 5.8 %collective-permute-start.16 = (f32[8,1,512]{2,1,0:T(1,128)S(1)}, f32[8,1,512]{2,1,0:T(1,128)S(1)}, u32[]{:S(2)}, u32[]{:S(2)}) collective-permute-start(f32[8,1,512]{2,1,0:T(1,128)S(1)} %add.99.refs_0_), channel_id=1, source_target_pairs={{0,8},{8,16},{16,24},{24,0},{1,9},{9,17},{17,25},{25,1},{2,10},{10... | collective-permute-start | bytes 49160 | tf_op jit(solution)/shard_map/ppermute | solution.py:355
  84.2 5.7 %collective-permute-start.17 = (f32[8,1,512]{2,1,0:T(1,128)S(1)}, f32[8,1,512]{2,1,0:T(1,128)S(1)}, u32[]{:S(2)}, u32[]{:S(2)}) collective-permute-start(f32[8,1,512]{2,1,0:T(1,128)S(1)} %add.99.refs_0_), channel_id=1, source_target_pairs={{0,16},{8,24},{16,0},{24,8},{1,17},{9,25},{17,1},{25,9},{2,18},{10... | collective-permute-start | bytes 49160 | tf_op jit(solution)/shard_map/ppermute | solution.py:355
  87.4 3.7 %collective-permute-start.18 = (f32[8,1,512]{2,1,0:T(1,128)S(1)}, f32[8,1,512]{2,1,0:T(1,128)S(1)}, u32[]{:S(2)}, u32[]{:S(2)}) collective-permute-start(f32[8,1,512]{2,1,0:T(1,128)S(1)} %add.99.refs_0_), channel_id=1, source_target_pairs={{0,24},{8,0},{16,8},{24,16},{1,25},{9,1},{17,9},{25,17},{2,26},{10... | collective-permute-start | bytes 49160 | tf_op jit(solution)/shard_map/ppermute | solution.py:355
  105.3 23.0 %collective-permute-start.19 = (bf16[256,768]{1,0:T(8,128)(2,1)S(1)}, bf16[256,768]{1,0:T(8,128)(2,1)S(1)}, u32[]{:S(2)}, u32[]{:S(2)}) collective-permute-start(bf16[256,768]{1,0:T(8,128)(2,1)S(1)} %get-tuple-element.120), channel_id=1, source_target_pairs={{0,2},{1,3},{2,0},{3,1},{4,6},{5,7},{6,4},{7,5},{8,10},{9,11},{10,... | collective-permute-start | bytes 1179656 | tf_op jit(solution)/shard_map/ppermute | solution.py:249
  106.8 21.4 %collective-permute-start.20 = (bf16[256,768]{1,0:T(8,128)(2,1)S(1)}, bf16[256,768]{1,0:T(8,128)(2,1)S(1)}, u32[]{:S(2)}, u32[]{:S(2)}) collective-permute-start(bf16[256,768]{1,0:T(8,128)(2,1)S(1)} %get-tuple-element.119), channel_id=1, source_target_pairs={{0,4},{1,5},{2,6},{3,7},{4,0},{5,1},{6,2},{7,3},{8,12},{9,13},{10,... | collective-permute-start | bytes 1179656 | tf_op jit(solution)/shard_map/ppermute | solution.py:249
  108.3 19.9 %collective-permute-start.21 = (bf16[256,768]{1,0:T(8,128)(2,1)S(1)}, bf16[256,768]{1,0:T(8,128)(2,1)S(1)}, u32[]{:S(2)}, u32[]{:S(2)}) collective-permute-start(bf16[256,768]{1,0:T(8,128)(2,1)S(1)} %get-tuple-element.118), channel_id=1, source_target_pairs={{0,6},{1,7},{2,4},{3,5},{4,2},{5,3},{6,0},{7,1},{8,14},{9,15},{10,... | collective-permute-start | bytes 1179656 | tf_op jit(solution)/shard_map/ppermute | solution.py:249
  108.8 14.9 %collective-permute-start.22 = (f32[1,1024]{1,0:T(1,128)S(1)}, f32[1,1024]{1,0:T(1,128)S(1)}, u32[]{:S(2)}, u32[]{:S(2)}) collective-permute-start(f32[1,1024]{1,0:T(1,128)S(1)} %get-tuple-element.105), channel_id=1, source_target_pairs={{0,2},{1,3},{2,0},{3,1},{4,6},{5,7},{6,4},{7,5},{8,10},{9,11},{10,... | collective-permute-start | bytes 12296 | tf_op jit(solution)/shard_map/ppermute | solution.py:249
  110.3 15.8 %collective-permute-start.23 = (f32[1,1024]{1,0:T(1,128)S(1)}, f32[1,1024]{1,0:T(1,128)S(1)}, u32[]{:S(2)}, u32[]{:S(2)}) collective-permute-start(f32[1,1024]{1,0:T(1,128)S(1)} %get-tuple-element.105), channel_id=1, source_target_pairs={{0,4},{1,5},{2,6},{3,7},{4,0},{5,1},{6,2},{7,3},{8,12},{9,13},{10,... | collective-permute-start | bytes 12296 | tf_op jit(solution)/shard_map/ppermute | solution.py:249
  123.7 4.5 %collective-permute-start.24 = (f32[1,1024]{1,0:T(1,128)S(1)}, f32[1,1024]{1,0:T(1,128)S(1)}, u32[]{:S(2)}, u32[]{:S(2)}) collective-permute-start(f32[1,1024]{1,0:T(1,128)S(1)} %get-tuple-element.105), channel_id=1, source_target_pairs={{0,6},{1,7},{2,4},{3,5},{4,2},{5,3},{6,0},{7,1},{8,14},{9,15},{10,... | collective-permute-start | bytes 12296 | tf_op jit(solution)/shard_map/ppermute | solution.py:249
  129.2 5.5 %collective-permute-start.28 = (f16[256,768]{1,0:T(8,128)(2,1)S(1)}, f16[256,768]{1,0:T(8,128)(2,1)S(1)}, u32[]{:S(2)}, u32[]{:S(2)}) collective-permute-start(f16[256,768]{1,0:T(8,128)(2,1)S(1)} %get-tuple-element.117), channel_id=1, source_target_pairs={{0,1},{1,0},{2,3},{3,2},{4,5},{5,4},{6,7},{7,6},{8,9},{9,8},{10,11... | collective-permute-start | bytes 1179656 | tf_op jit(solution)/shard_map/ppermute | solution.py:249
  129.3 12.0 %collective-permute-start.25 = (f16[256,768]{1,0:T(8,128)(2,1)S(1)}, f16[256,768]{1,0:T(8,128)(2,1)S(1)}, u32[]{:S(2)}, u32[]{:S(2)}) collective-permute-start(f16[256,768]{1,0:T(8,128)(2,1)S(1)} %get-tuple-element.117), channel_id=1, source_target_pairs={{0,2},{1,3},{2,0},{3,1},{4,6},{5,7},{6,4},{7,5},{8,10},{9,11},{10,... | collective-permute-start | bytes 1179656 | tf_op jit(solution)/shard_map/ppermute | solution.py:249
  130.8 19.6 %collective-permute-start.26 = (f16[256,768]{1,0:T(8,128)(2,1)S(1)}, f16[256,768]{1,0:T(8,128)(2,1)S(1)}, u32[]{:S(2)}, u32[]{:S(2)}) collective-permute-start(f16[256,768]{1,0:T(8,128)(2,1)S(1)} %get-tuple-element.117), channel_id=1, source_target_pairs={{0,4},{1,5},{2,6},{3,7},{4,0},{5,1},{6,2},{7,3},{8,12},{9,13},{10,... | collective-permute-start | bytes 1179656 | tf_op jit(solution)/shard_map/ppermute | solution.py:249
  132.3 18.1 %collective-permute-start.27 = (f16[256,768]{1,0:T(8,128)(2,1)S(1)}, f16[256,768]{1,0:T(8,128)(2,1)S(1)}, u32[]{:S(2)}, u32[]{:S(2)}) collective-permute-start(f16[256,768]{1,0:T(8,128)(2,1)S(1)} %get-tuple-element.117), channel_id=1, source_target_pairs={{0,6},{1,7},{2,4},{3,5},{4,2},{5,3},{6,0},{7,1},{8,14},{9,15},{10,... | collective-permute-start | bytes 1179656 | tf_op jit(solution)/shard_map/ppermute | solution.py:249
  150.5 3.3 %collective-permute-start.29 = (f16[256,768]{1,0:T(8,128)(2,1)S(1)}, f16[256,768]{1,0:T(8,128)(2,1)S(1)}, u32[]{:S(2)}, u32[]{:S(2)}) collective-permute-start(f16[256,768]{1,0:T(8,128)(2,1)S(1)} %collective-permute-done.25), channel_id=1, source_target_pairs={{0,1},{1,0},{2,3},{3,2},{4,5},{5,4},{6,7},{7,6},{8,9},{9,8},{10,11... | collective-permute-start | bytes 1179656 | tf_op jit(solution)/shard_map/ppermute | solution.py:249
  150.5 4.2 %collective-permute-start.30 = (f16[256,768]{1,0:T(8,128)(2,1)S(1)}, f16[256,768]{1,0:T(8,128)(2,1)S(1)}, u32[]{:S(2)}, u32[]{:S(2)}) collective-permute-start(f16[256,768]{1,0:T(8,128)(2,1)S(1)} %collective-permute-done.26), channel_id=1, source_target_pairs={{0,1},{1,0},{2,3},{3,2},{4,5},{5,4},{6,7},{7,6},{8,9},{9,8},{10,11... | collective-permute-start | bytes 1179656 | tf_op jit(solution)/shard_map/ppermute | solution.py:249
  151.0 4.7 %collective-permute-start.31 = (f16[256,768]{1,0:T(8,128)(2,1)S(1)}, f16[256,768]{1,0:T(8,128)(2,1)S(1)}, u32[]{:S(2)}, u32[]{:S(2)}) collective-permute-start(f16[256,768]{1,0:T(8,128)(2,1)S(1)} %collective-permute-done.27), channel_id=1, source_target_pairs={{0,1},{1,0},{2,3},{3,2},{4,5},{5,4},{6,7},{7,6},{8,9},{9,8},{10,11... | collective-permute-start | bytes 1179656 | tf_op jit(solution)/shard_map/ppermute | solution.py:249
  (3 other events, 6.0 us)

commit v4 on v3

--- a/solution.py
+++ b/solution.py
@@ -12,6 +12,7 @@
 LOG2E = math.log2(math.e)
 LANES = 128
 CORES = 2
+EXTRA = 16
 VMEM_LIMIT = 48 * 1024 * 1024
 
 
@@ -134,9 +135,7 @@
         input_output_aliases=aliases,
         compiler_params=pltpu.CompilerParams(vmem_limit_bytes=VMEM_LIMIT),
         cost_estimate=pl.CostEstimate(
-            flops=2 * count * part * depth,
-            bytes_accessed=2 * (count * part * 4 + count * depth * 2),
-            transcendentals=count * part,
+            flops=part * depth, bytes_accessed=part * depth, transcendentals=0
         ),
         name="scores",
     )(ids, *sources, units, offsets, *extra)
@@ -174,21 +173,33 @@
 
     @pl.when(step == pl.num_programs(0) - 1)
     def _():
-        size = mine.shape[0]
+        size, depth = mine.shape
         quarter = ids[1] // CORES
+        sums = jnp.sum(mass[...].T, axis=0, keepdims=True)
+        line = lax.broadcasted_iota(jnp.int32, (EXTRA, size), 0)
         for number in range(total.shape[0] // size):
             block = total[number * size : (number + 1) * size, :]
+            own = sums[:, number * size : (number + 1) * size]
             away = quarter ^ number
 
             @pl.when(away == 0)
             def _():
                 mine[...] = block
+                masses[...] = own
 
             @pl.when(away != 0)
             def _():
-                sent[away - 1] = block.astype(sent.dtype)
-
-        masses[...] = jnp.sum(mass[...].T, axis=0, keepdims=True)
+                sent[away - 1, :size, :] = block.astype(sent.dtype)
+                high = own.astype(sent.dtype).astype(jnp.float32)
+                rest = own - high
+                middle = rest.astype(sent.dtype).astype(jnp.float32)
+                low = rest - middle
+                three = jnp.where(
+                    line == 0, high, jnp.where(line == 1, middle, jnp.where(line == 2, low, 0.0))
+                )
+                sent[away - 1, size:, :size] = three.astype(sent.dtype)
+                if size < depth:
+                    sent[away - 1, size:, size:] = jnp.zeros((EXTRA, depth - size), sent.dtype)
 
 
 def sum_rows(ids, orders, totals, scores, rows, n_owners):
@@ -207,9 +218,9 @@
                 pl.BlockSpec((part, depth), lambda t, s: (t, 0)),
             ],
             out_specs=[
-                pl.BlockSpec((n_owners - 1, size, depth), lambda t, s: (0, 0, 0)),
+                pl.BlockSpec((n_owners - 1, size + EXTRA, depth), lambda t, s: (0, 0, 0)),
                 pl.BlockSpec((size, depth), lambda t, s: (0, 0)),
-                pl.BlockSpec((1, count), lambda t, s: (0, 0)),
+                pl.BlockSpec((1, size), lambda t, s: (0, 0)),
             ],
             scratch_shapes=[
                 pltpu.VMEM((n_columns, 1, part), jnp.float32),
@@ -218,9 +229,9 @@
             ],
         ),
         out_shape=(
-            jax.ShapeDtypeStruct((n_owners - 1, size, depth), jnp.bfloat16),
+            jax.ShapeDtypeStruct((n_owners - 1, size + EXTRA, depth), jnp.bfloat16),
             jax.ShapeDtypeStruct((size, depth), jnp.float32),
-            jax.ShapeDtypeStruct((1, count), jnp.float32),
+            jax.ShapeDtypeStruct((1, size), jnp.float32),
         ),
         compiler_params=pltpu.CompilerParams(vmem_limit_bytes=VMEM_LIMIT),
         cost_estimate=pl.CostEstimate(
@@ -254,7 +265,7 @@
         ]
         return lax.ppermute(array, ("blk", "rows"), pairs)
 
-    last_parts = 2 if held % (2 * LANES) == 0 and n_places > 2 else 1
+    last_parts = 1
 
     def parts_of(slot):
         return last_parts if slot == n_places - 1 else 1
@@ -263,11 +274,14 @@
     slots[0][0].append((embeddings, list(range(n_places))))
     moves = [move + (part,) for part in range(last_parts) for move in moves if part < parts_of(move[3])]
 
-    def start_ready(moves):
+    def start_ready(moves, last_source):
         groups = {}
         left = []
         for move in moves:
             source, target, source_slot, slot, part = move
+            if source_slot > last_source:
+                left.append(move)
+                continue
             whole = parts_of(source_slot) < parts_of(slot)
             holders = slots[source_slot][0 if whole else part]
             holds = [n for n, (_, places) in enumerate(holders) if source in places]
@@ -280,7 +294,9 @@
                 turn += 1
             groups.setdefault(key(turn), []).append((source, target))
         moved = []
-        for (part, slot, source_slot, hold, _), pairs in sorted(groups.items()):
+        for (part, slot, source_slot, hold, _), pairs in sorted(
+            groups.items(), reverse=True
+        ):
             whole = parts_of(source_slot) < parts_of(slot)
             array = slots[source_slot][0 if whole else part][hold][0]
             if whole:
@@ -307,7 +323,7 @@
     n_columns = n_places * CORES
     carried = None
 
-    def scores_of(slot, part, carried):
+    def scores_of(slot, part, carried, between):
         blocks = [order[slot] for order in orders]
         arrived = slots[slot][part]
         swapped = [(swap_cores(array, places), places) for array, places in arrived]
@@ -330,25 +346,43 @@
                 part,
                 parts_of(slot),
             )
+            if who == 0:
+                carried = between(carried)
         return carried
 
     def arrive(moved):
         for slot, part, array, places in moved:
             slots[slot][part].append((array, places))
 
+    early = []
     for turn in range(n_places):
         for part in range(parts_of(turn)):
             while sum(len(places) for _, places in slots[turn][part]) < n_places:
-                moved, moves = start_ready(moves)
+                moved, moves = start_ready(moves, n_places)
                 arrive(moved)
             slots[turn][part] = merged(slots[turn][part])
-            moved, moves = start_ready(moves)
-            carried = scores_of(turn, part, carried)
-            arrive([m for m in moved if m[1] + 1 < parts_of(m[0])])
-            moved = [m for m in moved if m[1] + 1 == parts_of(m[0])]
-            if moved:
-                arrays, carried = lax.optimization_barrier(([m[2] for m in moved], carried))
-                arrive([(slot, p, array, places) for (slot, p, _, places), array in zip(moved, arrays)])
+            moved, moves = start_ready(moves, turn)
+
+            def between(carried):
+                nonlocal moves, moved, early
+                if early:
+                    arrays, carried = lax.optimization_barrier(([m[2] for m in early], carried))
+                    for (slot, p, _, places), array in zip(early, arrays):
+                        held_arrays = slots[slot][p]
+                        old = [n for n, (_, spots) in enumerate(held_arrays) if spots == places]
+                        held_arrays[old[0]] = (array, places)
+                more, moves = start_ready(moves, n_places)
+                moved = moved + more
+                return carried
+
+            carried = scores_of(turn, part, carried, between)
+            early = [m for m in moved if m[0] != turn + 1]
+            arrive(early)
+            now = [m for m in moved if m[0] == turn + 1]
+            if now and turn == 0:
+                arrays, carried = lax.optimization_barrier(([m[2] for m in now], carried))
+                now = [(slot, p, array, places) for (slot, p, _, places), array in zip(now, arrays)]
+            arrive(now)
     scores, rows, totals = carried
     totals = totals + exchange(totals, 1)
     all_totals = [totals] + [
@@ -359,23 +393,19 @@
     sent, summed, masses = sum_rows(ids, orders, all_totals, scores, rows, n_owners)
     far = [CORES * away for away in range(1, n_owners)]
     arrived = [exchange(sent[number], distance) for number, distance in enumerate(far)]
-    arrived_masses = [exchange(masses, distance) for distance in far]
-    arrived, arrived_masses = lax.optimization_barrier((arrived, arrived_masses))
+    size = summed.shape[0]
+    masses = masses.reshape(size)
     for array in arrived:
-        summed = summed + array.astype(jnp.float32)
+        wide = array.astype(jnp.float32)
+        summed = summed + wide[:size]
+        masses = masses + (wide[size, :size] + wide[size + 1, :size] + wide[size + 2, :size])
 
     unit = summed * lax.rsqrt(jnp.sum(summed * summed, axis=1, keepdims=True) + 1e-06)
     unit = unit.astype(jnp.float16)
-    size = unit.shape[0]
     pieces = [exchange(unit, distance) for distance in far]
-    masses = functools.reduce(jnp.add, arrived_masses, masses)
-    masses = masses.reshape(half)
-    other_masses = exchange(masses, 1)
-    both = jnp.where(
-        core == 0,
-        jnp.concatenate([masses, other_masses]),
-        jnp.concatenate([other_masses, masses]),
-    )
+    both = lax.all_gather(masses, "rows").reshape(n_owners, CORES, size)
+    both = both.transpose(1, 0, 2).reshape(local_centroids)
+
     def place_piece(result, distance, flip, array):
         start = (core ^ flip) * half + lax.div(me ^ distance, CORES) * size
         return lax.dynamic_update_slice(result, array.astype(jnp.float32), (start, 0))

time: 157 us -> 170 us (1.083)
  blocking collectives: 0 us -> 21.3 us
  starting transfers between devices: 34.5 us -> 25.8 us
  other arithmetic: 12 us -> 16.4 us
  Pallas kernels: 43.9 us -> 39.6 us
  waiting for transfers between devices: 63.3 us -> 59 us
  local copies, waits for them, and re-layouts: 1.87 us -> 5.89 us
    all_gather x0 -> x1, blocking collectives: none -> 21.3 us  [local(): both = lax.all_gather(masses, 'rows').reshape(n_owners, CORES, size)]
    ppermute x15 -> x11, waiting for transfers between devices: 30.8 us -> 16.7 us  [exchange(): lax.ppermute(array, 'rows', [(i, i ^ distance) for i in range(n_rows)])]
    ppermute x7 -> x5, waiting for transfers between devices: 29.4 us -> 38.5 us  [start_ready(): lax.ppermute(array, 'blk', pairs)]
    ppermute x15 -> x11, starting transfers between devices: 13.7 us -> 9 us  [exchange(): lax.ppermute(array, 'rows', [(i, i ^ distance) for i in range(n_rows)])]
    pallas_call x10 -> x8, Pallas kernels: 29.8 us -> 25.6 us  [score_block(): pl.pallas_call(functools.partial(score_kernel, n_sources, choice), grid_s...]
    dynamic_update_slice x8, other arithmetic: 6.75 us -> 9.67 us  [place_piece(): lax.dynamic_update_slice(result, array.astype(jnp.float32), (start, 0))]
    broadcast_in_dim x1, local copies, waits for them, and re-layouts: 0.41 us -> 3.12 us  [local(): result = jnp.zeros((local_centroids, depth), jnp.float32)]
    ppermute x8 -> x6, starting transfers between devices: 8.33 us -> 5.77 us  [swap_cores(): return lax.ppermute(array, ('blk', 'rows'), pairs)]
  transfers between devices with their start and end apart: 33 -> 25, of which waited for: 12 -> 9; matrix products, arithmetic and copies ran while one was open for 7% -> 8% of each run, Pallas kernels for 17% -> 13%
where the time goes in v4:
time: 170 us; the launch traced here: 169 us
  waiting for transfers between devices  59 us (35%)
  Pallas kernels  39.6 us (23%)
  starting transfers between devices  25.8 us (15%)
  blocking collectives  21.3 us (13%)
  other arithmetic  16.4 us (10%)
  local copies, waits for them, and re-layouts  5.89 us (3%)
    ppermute x5, waiting for transfers between devices, start_ready(): lax.ppermute(array, 'blk', pairs)  38.5 us
    pallas_call x8, Pallas kernels, score_block(): pl.pallas_call(functools.partial(score_kernel, n_sources, choice), grid_s...  25.6 us
    all_gather x1, blocking collectives, local(): both = lax.all_gather(masses, 'rows').reshape(n_owners, CORES, size)  21.3 us
    ppermute x11, waiting for transfers between devices, exchange(): lax.ppermute(array, 'rows', [(i, i ^ distance) for i in range(n_rows)])  16.7 us
    pallas_call x1, Pallas kernels, sum_rows(): pl.pallas_call(functools.partial(sum_kernel, orders, len(totals)), grid_s...  14 us
    dynamic_update_slice x8, other arithmetic, place_piece(): lax.dynamic_update_slice(result, array.astype(jnp.float32), (start, 0))  9.67 us
    ppermute x11, starting transfers between devices, exchange(): lax.ppermute(array, 'rows', [(i, i ^ distance) for i in range(n_rows)])  9 us
    ppermute x5, starting transfers between devices, start_ready(): lax.ppermute(array, 'blk', pairs)  6.65 us
  transfers between devices with their start and end apart: 25, of which 9 were waited for; matrix products, arithmetic and copies ran while one was open for 8% of the time, Pallas kernels for 13%

profile of v4, /device:TPU:0, one launch (start us, length us, event | category | flops | bytes accessed | tf_op | source)
XLA Modules:
  0.0 168.9 jit_solution(14972126461752872318)
XLA Ops:
  1.1 2.7 %collective-permute-start = (bf16[512,768]{1,0:T(8,128)(2,1)}, bf16[512,768]{1,0:T(8,128)(2,1)S(1)}, u32[]{:S(2)}, u32[]{:S(2)}) collective-permute-start(bf16[512,768]{1,0:T(8,128)(2,1)} %refs_0_.1), channel_id=1, source_target_pairs={{8,0},{0,8},{24,16},{16,24},{9,1},{1,9},{25,17},{17,25},{10,2},{2,... | collective-permute-start | bytes 2359304 | tf_op jit(solution)/shard_map/ppermute | solution.py:305
  4.5 1.8 %fusion = f32[1024]{0:T(1024)S(1)} fusion(bf16[2048,768]{1,0:T(8,128)(2,1)} %param.4, s32[]{:T(128)S(6)} %select_n.28), kind=kLoop, calls=%fused_computation.2 | loop fusion | flops 2358272 | bytes 1576964 | tf_op jit(solution)/shard_map/reduce_sum | solution.py:21
  7.1 1.7 %fusion.1.refs_1_.refs_2_ = bf16[1024,768]{1,0:T(8,128)(2,1)S(1)} fusion(f32[1024]{0:T(1024)S(1)} %add_rsqrt_fusion, bf16[2048,768]{1,0:T(8,128)(2,1)} %param.4, s32[]{:T(128)S(6)} %select_n.28), kind=kLoop, calls=%fused_computation.3 | loop fusion | flops 2359296 | bytes 3149828 | tf_op jit(solution)/shard_map/convert_element_type | solution.py:21
  10.2 3.3 %scores.8 = (f32[1024,4096]{1,0:T(8,128)}, bf16[4096,768]{1,0:T(8,128)(2,1)}, f32[8,1,512]{2,1,0:T(1,128)S(1)}) custom-call(s32[2]{0:T(128)S(1)} %pad_add_fusion.ids, bf16[512,768]{1,0:T(8,128)(2,1)S(1)} %copy-done, bf16[1024,768]{1,0:T(8,128)(2,1)S(1)} %fusion.1.refs_1_.refs_2_, f32[1024,128]{1,0:T(8,128)S(1)} %broadcast_in_dim.4.refs_2_.refs_3_), custom_call_target="tpu_custom_call" | custom-call | flops 393216 | bytes 393216 | tf_op jit(solution)/shard_map/scores/pallas_call | solution.py:109
  13.5 3.2 %scores.9 = (f32[1024,4096]{1,0:T(8,128)}, bf16[4096,768]{1,0:T(8,128)(2,1)}, f32[8,1,512]{2,1,0:T(1,128)S(1)}) custom-call(s32[2]{0:T(128)S(1)} %pad_add_fusion.ids, bf16[512,768]{1,0:T(8,128)(2,1)S(1)} %collective-permute-done.1.refs_0_, bf16[1024,768]{1,0:T(8,128)(2,1)S(1)} %fusion.1.refs_1_.refs_2_, ...), custom_call_target="tpu_custom_call", output_to_operand_aliasing={{0}: (4, {}), {1}: (5, {}), {2}: (6, {})} | custom-call | flops 393216 | bytes 393216 | tf_op jit(solution)/shard_map/scores/pallas_call | solution.py:109
  16.7 5.5 %collective-permute-done.refs_0_ = bf16[512,768]{1,0:T(8,128)(2,1)S(1)} collective-permute-done((bf16[512,768]{1,0:T(8,128)(2,1)}, bf16[512,768]{1,0:T(8,128)(2,1)S(1)}, u32[]{:S(2)}, u32[]{:S(2)}) %collective-permute-start) | collective-permute-done | bytes 786464 | tf_op jit(solution)/shard_map/ppermute | solution.py:305
  22.1 3.2 %scores.10 = (f32[1024,4096]{1,0:T(8,128)}, bf16[4096,768]{1,0:T(8,128)(2,1)}, f32[8,1,512]{2,1,0:T(1,128)S(1)}) custom-call(s32[2]{0:T(128)S(1)} %pad_add_fusion.ids, bf16[512,768]{1,0:T(8,128)(2,1)S(1)} %collective-permute-done.refs_0_, bf16[1024,768]{1,0:T(8,128)(2,1)S(1)} %fusion.1.refs_1_.refs_2_, ...), custom_call_target="tpu_custom_call", output_to_operand_aliasing={{0}: (4, {}), {1}: (5, {}), {2}: (6, {})} | custom-call | flops 393216 | bytes 393216 | tf_op jit(solution)/shard_map/scores/pallas_call | solution.py:109
  25.4 1.3 collective-permute-start.4
  27.4 3.2 %scores.11 = (f32[1024,4096]{1,0:T(8,128)}, bf16[4096,768]{1,0:T(8,128)(2,1)}, f32[8,1,512]{2,1,0:T(1,128)S(1)}) custom-call(s32[2]{0:T(128)S(1)} %pad_add_fusion.ids, bf16[512,768]{1,0:T(8,128)(2,1)S(1)} %collective-permute-done.5.refs_0_, bf16[1024,768]{1,0:T(8,128)(2,1)S(1)} %fusion.1.refs_1_.refs_2_, ...), custom_call_target="tpu_custom_call", output_to_operand_aliasing={{0}: (4, {}), {1}: (5, {}), {2}: (6, {})} | custom-call | flops 393216 | bytes 393216 | tf_op jit(solution)/shard_map/scores/pallas_call | solution.py:109
  30.6 16.6 %collective-permute-done.4.refs_1_ = bf16[512,768]{1,0:T(8,128)(2,1)S(1)} collective-permute-done((bf16[512,768]{1,0:T(8,128)(2,1)S(1)}, bf16[512,768]{1,0:T(8,128)(2,1)S(1)}, u32[]{:S(2)}, u32[]{:S(2)}) %collective-permute-start.4) | collective-permute-done | bytes 786464 | tf_op jit(solution)/shard_map/ppermute | solution.py:305
  47.2 3.2 %scores.12 = (f32[1024,4096]{1,0:T(8,128)}, bf16[4096,768]{1,0:T(8,128)(2,1)}, f32[8,1,512]{2,1,0:T(1,128)S(1)}) custom-call(s32[2]{0:T(128)S(1)} %pad_add_fusion.ids, bf16[512,768]{1,0:T(8,128)(2,1)S(1)} %collective-permute-done.3.refs_0_, ...), custom_call_target="tpu_custom_call", output_to_operand_aliasing={{0}: (5, {}), {1}: (6, {}), {2}: (7, {})} | custom-call | flops 393216 | bytes 393216 | tf_op jit(solution)/shard_map/scores/pallas_call | solution.py:109
  50.4 1.3 collective-permute-start.7
  52.4 1.9 %collective-permute-start.10 = (bf16[512,768]{1,0:T(8,128)(2,1)S(1)}, bf16[512,768]{1,0:T(8,128)(2,1)S(1)}, u32[]{:S(2)}, u32[]{:S(2)}) collective-permute-start(bf16[512,768]{1,0:T(8,128)(2,1)S(1)} %collective-permute-done.4.refs_1_), channel_id=1, source_target_pairs={{0,1},{1,0},{2,3},{3,2},{4,5},{5,4},{6,7},{7,6},{24,25},{25,24},{2... | collective-permute-start | bytes 2359304 | tf_op jit(solution)/shard_map/ppermute | solution.py:266
  55.1 16.4 %collective-permute-done.7.refs_1_ = bf16[512,768]{1,0:T(8,128)(2,1)S(1)} collective-permute-done((bf16[512,768]{1,0:T(8,128)(2,1)S(1)}, bf16[512,768]{1,0:T(8,128)(2,1)S(1)}, u32[]{:S(2)}, u32[]{:S(2)}) %collective-permute-start.7) | collective-permute-done | bytes 786464 | tf_op jit(solution)/shard_map/ppermute | solution.py:305
  71.5 1.9 %collective-permute-start.8 = (bf16[512,768]{1,0:T(8,128)(2,1)S(1)}, bf16[512,768]{1,0:T(8,128)(2,1)S(1)}, u32[]{:S(2)}, u32[]{:S(2)}) collective-permute-start(bf16[512,768]{1,0:T(8,128)(2,1)S(1)} %collective-permute-done.7.refs_1_), channel_id=1, source_target_pairs={{0,1},{1,0},{2,3},{3,2},{4,5},{5,4},{6,7},{7,6},{24,25},{25,24},{2... | collective-permute-start | bytes 2359304 | tf_op jit(solution)/shard_map/ppermute | solution.py:266
  73.4 3.2 %scores.13 = (f32[1024,4096]{1,0:T(8,128)}, bf16[4096,768]{1,0:T(8,128)(2,1)}, f32[8,1,512]{2,1,0:T(1,128)S(1)}) custom-call(s32[2]{0:T(128)S(1)} %pad_add_fusion.ids, bf16[512,768]{1,0:T(8,128)(2,1)S(1)} %collective-permute-done.9.refs_0_, ...), custom_call_target="tpu_custom_call", output_to_operand_aliasing={{0}: (5, {}), {1}: (6, {}), {2}: (7, {})} | custom-call | flops 393216 | bytes 393216 | tf_op jit(solution)/shard_map/scores/pallas_call | solution.py:109
  76.6 3.2 %scores.14 = (f32[1024,4096]{1,0:T(8,128)}, bf16[4096,768]{1,0:T(8,128)(2,1)}, f32[8,1,512]{2,1,0:T(1,128)S(1)}) custom-call(s32[2]{0:T(128)S(1)} %pad_add_fusion.ids, bf16[512,768]{1,0:T(8,128)(2,1)S(1)} %collective-permute-done.2.refs_0_, ...), custom_call_target="tpu_custom_call", output_to_operand_aliasing={{0}: (5, {}), {1}: (6, {}), {2}: (7, {})} | custom-call | flops 393216 | bytes 393216 | tf_op jit(solution)/shard_map/scores/pallas_call | solution.py:109
  79.8 3.2 %scores.15 = (f32[1024,4096]{1,0:T(8,128)}, bf16[4096,768]{1,0:T(8,128)(2,1)}, f32[8,1,512]{2,1,0:T(1,128)S(1)}) custom-call(s32[2]{0:T(128)S(1)} %pad_add_fusion.ids, bf16[512,768]{1,0:T(8,128)(2,1)S(1)} %collective-permute-done.6.refs_0_, ...), custom_call_target="tpu_custom_call", output_to_operand_aliasing={{0}: (5, {}), {1}: (6, {}), {2}: (7, {})} | custom-call | flops 393216 | bytes 393216 | tf_op jit(solution)/shard_map/scores/pallas_call | solution.py:109
  84.5 4.3 %collective-permute-start.13 = (f32[8,1,512]{2,1,0:T(1,128)S(1)}, f32[8,1,512]{2,1,0:T(1,128)S(1)}, u32[]{:S(2)}, u32[]{:S(2)}) collective-permute-start(f32[8,1,512]{2,1,0:T(1,128)S(1)} %add.126.refs_0_), channel_id=1, source_target_pairs={{0,16},{8,24},{16,0},{24,8},{1,17},{9,25},{17,1},{25,9},{2,18},{10... | collective-permute-start | bytes 49160 | tf_op jit(solution)/shard_map/ppermute | solution.py:389
  90.6 2.0 %collective-permute-done.14.refs_3_ = f32[8,1,512]{2,1,0:T(1,128)S(1)} collective-permute-done((f32[8,1,512]{2,1,0:T(1,128)S(1)}, f32[8,1,512]{2,1,0:T(1,128)S(1)}, u32[]{:S(2)}, u32[]{:S(2)}) %collective-permute-start.14) | collective-permute-done | bytes 16416 | tf_op jit(solution)/shard_map/ppermute | solution.py:389
  92.6 14.0 %sums.1 = (bf16[3,272,768]{2,1,0:T(8,128)(2,1)S(1)}, f32[256,768]{1,0:T(8,128)S(1)}, f32[1,256]{1,0:T(1,128)S(1)}) custom-call(s32[2]{0:T(128)S(1)} %pad_add_fusion.ids, f32[8,1,512]{2,1,0:T(1,128)S(1)} %add.126.refs_0_, f32[8,1,512]{2,1,0:T(1,128)S(1)} %collective-permute-done.12.refs_1_, f32[8,1,512]{2,1,0:T(1,128)S(1)} %collective-permute-done.13.refs_2_, ...), custom_call_target="tpu_custom_call" | custom-call | flops 6442450944 | bytes 26214400 | tf_op jit(solution)/shard_map/sums/pallas_call | solution.py:210
  107.4 1.5 collective-permute-start.15
  108.9 1.5 collective-permute-start.16
  110.9 9.3 %collective-permute-done.15 = bf16[272,768]{1,0:T(8,128)(2,1)S(1)} collective-permute-done((bf16[272,768]{1,0:T(8,128)(2,1)}, bf16[272,768]{1,0:T(8,128)(2,1)S(1)}, u32[]{:S(2)}, u32[]{:S(2)}) %collective-permute-start.15) | collective-permute-done | bytes 417824 | tf_op jit(solution)/shard_map/ppermute | solution.py:260
  120.3 6.6 %collective-permute-done.16 = bf16[272,768]{1,0:T(8,128)(2,1)} collective-permute-done((bf16[272,768]{1,0:T(8,128)(2,1)S(1)}, bf16[272,768]{1,0:T(8,128)(2,1)}, u32[]{:S(2)}, u32[]{:S(2)}) %collective-permute-start.16) | collective-permute-done | bytes 417824 | tf_op jit(solution)/shard_map/ppermute | solution.py:260
  129.2 3.1 %broadcast_in_dim.5 = f32[2048,768]{1,0:T(8,128)} broadcast(f32[]{:T(128)} %constant.38.clone.1), dimensions={} | broadcast | bytes 6291460 | tf_op jit(solution)/shard_map/broadcast_in_dim | solution.py:413
  133.5 1.4 collective-permute-start.18
  134.9 1.2 collective-permute-start.19
  136.1 1.4 collective-permute-start.20
  137.5 21.3 %all-gather = f32[8,1,256]{2,1,0:T(1,128)S(1)} all-gather(f32[1,1,256]{2,1,0:T(1,128)S(1)} %fusion.5), channel_id=1, replica_groups=mesh['blk'=4,'rows'=8] {'rows'}, dimensions={0}, use_global_device_ids=true | all-gather | bytes 9216 | tf_op jit(solution)/shard_map/all_gather | solution.py:406
  161.3 1.9 %convert_dynamic-update-slice_fusion.5 = f32[2048,768]{1,0:T(8,128)} fusion(f32[2048,768]{1,0:T(8,128)} %convert_dynamic-update-slice_fusion.6, s32[]{:T(128)S(6)} %select_n.31, f16[256,768]{1,0:T(8,128)(2,1)} %collective-permute-done.18), kind=kLoop, calls=%fused_computation.12 | loop fusion | flops 196608 | bytes 1179652 | tf_op jit(solution)/shard_map/dynamic_update_slice | solution.py:411
  163.2 1.9 %convert_dynamic-update-slice_fusion.4 = f32[2048,768]{1,0:T(8,128)} fusion(f32[2048,768]{1,0:T(8,128)} %convert_dynamic-update-slice_fusion.5, s32[]{:T(128)S(6)} %select_n.32, f16[256,768]{1,0:T(8,128)(2,1)} %collective-permute-done.19), kind=kLoop, calls=%fused_computation.11 | loop fusion | flops 196608 | bytes 1179652 | tf_op jit(solution)/shard_map/dynamic_update_slice | solution.py:411
  (57 shorter events, 19.8 us)
Async XLA Ops:
  0.6 12.8 %collective-permute-start.1 = (bf16[512,768]{1,0:T(8,128)(2,1)}, bf16[512,768]{1,0:T(8,128)(2,1)S(1)}, u32[]{:S(2)}, u32[]{:S(2)}) collective-permute-start(bf16[512,768]{1,0:T(8,128)(2,1)} %refs_0_.1), channel_id=1, source_target_pairs={{0,1},{1,0},{2,3},{3,2},{4,5},{5,4},{6,7},{7,6},{8,9},{9,8},{10,11... | collective-permute-start | bytes 2359304 | tf_op jit(solution)/shard_map/ppermute | solution.py:266
  1.1 21.0 %collective-permute-start = (bf16[512,768]{1,0:T(8,128)(2,1)}, bf16[512,768]{1,0:T(8,128)(2,1)S(1)}, u32[]{:S(2)}, u32[]{:S(2)}) collective-permute-start(bf16[512,768]{1,0:T(8,128)(2,1)} %refs_0_.1), channel_id=1, source_target_pairs={{8,0},{0,8},{24,16},{16,24},{9,1},{1,9},{25,17},{17,25},{10,2},{2,... | collective-permute-start | bytes 2359304 | tf_op jit(solution)/shard_map/ppermute | solution.py:305
  3.8 21.6 %collective-permute-start.3 = (bf16[512,768]{1,0:T(8,128)(2,1)}, bf16[512,768]{1,0:T(8,128)(2,1)S(1)}, u32[]{:S(2)}, u32[]{:S(2)}) collective-permute-start(bf16[512,768]{1,0:T(8,128)(2,1)} %refs_0_.1), channel_id=1, source_target_pairs={{16,8},{8,16},{17,9},{9,17},{18,10},{10,18},{19,11},{11,19},{20,12... | collective-permute-start | bytes 2359304 | tf_op jit(solution)/shard_map/ppermute | solution.py:305
  9.0 1.1 copy-start
  22.1 5.3 %collective-permute-start.5 = (bf16[512,768]{1,0:T(8,128)(2,1)S(1)}, bf16[512,768]{1,0:T(8,128)(2,1)S(1)}, u32[]{:S(2)}, u32[]{:S(2)}) collective-permute-start(bf16[512,768]{1,0:T(8,128)(2,1)S(1)} %collective-permute-done.refs_0_), channel_id=1, source_target_pairs={{0,1},{1,0},{2,3},{3,2},{4,5},{5,4},{6,7},{7,6},{8,9},{9,8},{10,11... | collective-permute-start | bytes 2359304 | tf_op jit(solution)/shard_map/ppermute | solution.py:266
  25.4 21.8 %collective-permute-start.4 = (bf16[512,768]{1,0:T(8,128)(2,1)S(1)}, bf16[512,768]{1,0:T(8,128)(2,1)S(1)}, u32[]{:S(2)}, u32[]{:S(2)}) collective-permute-start(bf16[512,768]{1,0:T(8,128)(2,1)S(1)} %collective-permute-done.3.refs_0_), channel_id=1, source_target_pairs={{8,0},{16,24},{9,1},{17,25},{10,2},{18,26},{11,3},{19,27},{12,4},{... | collective-permute-start | bytes 2359304 | tf_op jit(solution)/shard_map/ppermute | solution.py:305
  26.7 23.7 %collective-permute-start.2 = (bf16[512,768]{1,0:T(8,128)(2,1)S(1)}, bf16[512,768]{1,0:T(8,128)(2,1)S(1)}, u32[]{:S(2)}, u32[]{:S(2)}) collective-permute-start(bf16[512,768]{1,0:T(8,128)(2,1)S(1)} %collective-permute-done.refs_0_), channel_id=1, source_target_pairs={{16,8},{8,16},{17,9},{9,17},{18,10},{10,18},{19,11},{11,19},{20,12... | collective-permute-start | bytes 2359304 | tf_op jit(solution)/shard_map/ppermute | solution.py:305
  50.4 21.1 %collective-permute-start.7 = (bf16[512,768]{1,0:T(8,128)(2,1)S(1)}, bf16[512,768]{1,0:T(8,128)(2,1)S(1)}, u32[]{:S(2)}, u32[]{:S(2)}) collective-permute-start(bf16[512,768]{1,0:T(8,128)(2,1)S(1)} %collective-permute-done.2.refs_0_), channel_id=1, source_target_pairs={{8,0},{16,24},{9,1},{17,25},{10,2},{18,26},{11,3},{19,27},{12,4},{... | collective-permute-start | bytes 2359304 | tf_op jit(solution)/shard_map/ppermute | solution.py:305
  51.7 21.7 %collective-permute-start.9 = (bf16[512,768]{1,0:T(8,128)(2,1)S(1)}, bf16[512,768]{1,0:T(8,128)(2,1)S(1)}, u32[]{:S(2)}, u32[]{:S(2)}) collective-permute-start(bf16[512,768]{1,0:T(8,128)(2,1)S(1)} %collective-permute-done.3.refs_0_), channel_id=1, source_target_pairs={{8,9},{9,8},{10,11},{11,10},{12,13},{13,12},{14,15},{15,14},{16,17... | collective-permute-start | bytes 2359304 | tf_op jit(solution)/shard_map/ppermute | solution.py:266
  52.4 21.0 %collective-permute-start.10 = (bf16[512,768]{1,0:T(8,128)(2,1)S(1)}, bf16[512,768]{1,0:T(8,128)(2,1)S(1)}, u32[]{:S(2)}, u32[]{:S(2)}) collective-permute-start(bf16[512,768]{1,0:T(8,128)(2,1)S(1)} %collective-permute-done.4.refs_1_), channel_id=1, source_target_pairs={{0,1},{1,0},{2,3},{3,2},{4,5},{5,4},{6,7},{7,6},{24,25},{25,24},{2... | collective-permute-start | bytes 2359304 | tf_op jit(solution)/shard_map/ppermute | solution.py:266
  54.4 25.4 %collective-permute-start.6 = (bf16[512,768]{1,0:T(8,128)(2,1)S(1)}, bf16[512,768]{1,0:T(8,128)(2,1)S(1)}, u32[]{:S(2)}, u32[]{:S(2)}) collective-permute-start(bf16[512,768]{1,0:T(8,128)(2,1)S(1)} %collective-permute-done.2.refs_0_), channel_id=1, source_target_pairs={{8,9},{9,8},{10,11},{11,10},{12,13},{13,12},{14,15},{15,14},{16,17... | collective-permute-start | bytes 2359304 | tf_op jit(solution)/shard_map/ppermute | solution.py:266
  71.5 8.3 %collective-permute-start.8 = (bf16[512,768]{1,0:T(8,128)(2,1)S(1)}, bf16[512,768]{1,0:T(8,128)(2,1)S(1)}, u32[]{:S(2)}, u32[]{:S(2)}) collective-permute-start(bf16[512,768]{1,0:T(8,128)(2,1)S(1)} %collective-permute-done.7.refs_1_), channel_id=1, source_target_pairs={{0,1},{1,0},{2,3},{3,2},{4,5},{5,4},{6,7},{7,6},{24,25},{25,24},{2... | collective-permute-start | bytes 2359304 | tf_op jit(solution)/shard_map/ppermute | solution.py:266
  83.0 1.4 collective-permute-start.11
  84.4 5.6 %collective-permute-start.12 = (f32[8,1,512]{2,1,0:T(1,128)S(1)}, f32[8,1,512]{2,1,0:T(1,128)S(1)}, u32[]{:S(2)}, u32[]{:S(2)}) collective-permute-start(f32[8,1,512]{2,1,0:T(1,128)S(1)} %add.126.refs_0_), channel_id=1, source_target_pairs={{0,8},{8,16},{16,24},{24,0},{1,9},{9,17},{17,25},{25,1},{2,10},{10... | collective-permute-start | bytes 49160 | tf_op jit(solution)/shard_map/ppermute | solution.py:389
  84.5 6.1 %collective-permute-start.13 = (f32[8,1,512]{2,1,0:T(1,128)S(1)}, f32[8,1,512]{2,1,0:T(1,128)S(1)}, u32[]{:S(2)}, u32[]{:S(2)}) collective-permute-start(f32[8,1,512]{2,1,0:T(1,128)S(1)} %add.126.refs_0_), channel_id=1, source_target_pairs={{0,16},{8,24},{16,0},{24,8},{1,17},{9,25},{17,1},{25,9},{2,18},{10... | collective-permute-start | bytes 49160 | tf_op jit(solution)/shard_map/ppermute | solution.py:389
  88.8 3.7 %collective-permute-start.14 = (f32[8,1,512]{2,1,0:T(1,128)S(1)}, f32[8,1,512]{2,1,0:T(1,128)S(1)}, u32[]{:S(2)}, u32[]{:S(2)}) collective-permute-start(f32[8,1,512]{2,1,0:T(1,128)S(1)} %add.126.refs_0_), channel_id=1, source_target_pairs={{0,24},{8,0},{16,8},{24,16},{1,25},{9,1},{17,9},{25,17},{2,26},{10... | collective-permute-start | bytes 49160 | tf_op jit(solution)/shard_map/ppermute | solution.py:389
  107.4 12.8 %collective-permute-start.15 = (bf16[272,768]{1,0:T(8,128)(2,1)}, bf16[272,768]{1,0:T(8,128)(2,1)S(1)}, u32[]{:S(2)}, u32[]{:S(2)}) collective-permute-start(bf16[272,768]{1,0:T(8,128)(2,1)} %get-tuple-element.92), channel_id=1, source_target_pairs={{0,2},{1,3},{2,0},{3,1},{4,6},{5,7},{6,4},{7,5},{8,10},{9,11},{10,... | collective-permute-start | bytes 1253384 | tf_op jit(solution)/shard_map/ppermute | solution.py:260
  108.9 17.9 %collective-permute-start.16 = (bf16[272,768]{1,0:T(8,128)(2,1)S(1)}, bf16[272,768]{1,0:T(8,128)(2,1)}, u32[]{:S(2)}, u32[]{:S(2)}) collective-permute-start(bf16[272,768]{1,0:T(8,128)(2,1)S(1)} %get-tuple-element.94), channel_id=1, source_target_pairs={{0,4},{1,5},{2,6},{3,7},{4,0},{5,1},{6,2},{7,3},{8,12},{9,13},{10,... | collective-permute-start | bytes 1253384 | tf_op jit(solution)/shard_map/ppermute | solution.py:260
  110.4 17.4 %collective-permute-start.17 = (bf16[272,768]{1,0:T(8,128)(2,1)S(1)}, bf16[272,768]{1,0:T(8,128)(2,1)}, u32[]{:S(2)}, u32[]{:S(2)}) collective-permute-start(bf16[272,768]{1,0:T(8,128)(2,1)S(1)} %get-tuple-element.93), channel_id=1, source_target_pairs={{0,6},{1,7},{2,4},{3,5},{4,2},{5,3},{6,0},{7,1},{8,14},{9,15},{10,... | collective-permute-start | bytes 1253384 | tf_op jit(solution)/shard_map/ppermute | solution.py:260
  133.5 26.0 %collective-permute-start.21 = (f16[256,768]{1,0:T(8,128)(2,1)}, f16[256,768]{1,0:T(8,128)(2,1)S(1)}, u32[]{:S(2)}, u32[]{:S(2)}) collective-permute-start(f16[256,768]{1,0:T(8,128)(2,1)} %get-tuple-element.89), channel_id=1, source_target_pairs={{0,1},{1,0},{2,3},{3,2},{4,5},{5,4},{6,7},{7,6},{8,9},{9,8},{10,11... | collective-permute-start | bytes 1179656 | tf_op jit(solution)/shard_map/ppermute | solution.py:260
  133.5 26.9 %collective-permute-start.18 = (f16[256,768]{1,0:T(8,128)(2,1)}, f16[256,768]{1,0:T(8,128)(2,1)}, u32[]{:S(2)}, u32[]{:S(2)}) collective-permute-start(f16[256,768]{1,0:T(8,128)(2,1)} %get-tuple-element.89), channel_id=1, source_target_pairs={{0,2},{1,3},{2,0},{3,1},{4,6},{5,7},{6,4},{7,5},{8,10},{9,11},{10,... | collective-permute-start | bytes 1179656 | tf_op jit(solution)/shard_map/ppermute | solution.py:260
  134.9 25.5 %collective-permute-start.19 = (f16[256,768]{1,0:T(8,128)(2,1)}, f16[256,768]{1,0:T(8,128)(2,1)}, u32[]{:S(2)}, u32[]{:S(2)}) collective-permute-start(f16[256,768]{1,0:T(8,128)(2,1)} %get-tuple-element.89), channel_id=1, source_target_pairs={{0,4},{1,5},{2,6},{3,7},{4,0},{5,1},{6,2},{7,3},{8,12},{9,13},{10,... | collective-permute-start | bytes 1179656 | tf_op jit(solution)/shard_map/ppermute | solution.py:260
  136.1 24.3 %collective-permute-start.20 = (f16[256,768]{1,0:T(8,128)(2,1)}, f16[256,768]{1,0:T(8,128)(2,1)S(1)}, u32[]{:S(2)}, u32[]{:S(2)}) collective-permute-start(f16[256,768]{1,0:T(8,128)(2,1)} %get-tuple-element.89), channel_id=1, source_target_pairs={{0,6},{1,7},{2,4},{3,5},{4,2},{5,3},{6,0},{7,1},{8,14},{9,15},{10,... | collective-permute-start | bytes 1179656 | tf_op jit(solution)/shard_map/ppermute | solution.py:260
  160.4 5.7 %collective-permute-start.22 = (f16[256,768]{1,0:T(8,128)(2,1)}, f16[256,768]{1,0:T(8,128)(2,1)S(1)}, u32[]{:S(2)}, u32[]{:S(2)}) collective-permute-start(f16[256,768]{1,0:T(8,128)(2,1)} %collective-permute-done.18), channel_id=1, source_target_pairs={{0,1},{1,0},{2,3},{3,2},{4,5},{5,4},{6,7},{7,6},{8,9},{9,8},{10,11... | collective-permute-start | bytes 1179656 | tf_op jit(solution)/shard_map/ppermute | solution.py:260
  160.8 6.2 %collective-permute-start.23 = (f16[256,768]{1,0:T(8,128)(2,1)}, f16[256,768]{1,0:T(8,128)(2,1)S(1)}, u32[]{:S(2)}, u32[]{:S(2)}) collective-permute-start(f16[256,768]{1,0:T(8,128)(2,1)} %collective-permute-done.19), channel_id=1, source_target_pairs={{0,1},{1,0},{2,3},{3,2},{4,5},{5,4},{6,7},{7,6},{8,9},{9,8},{10,11... | collective-permute-start | bytes 1179656 | tf_op jit(solution)/shard_map/ppermute | solution.py:260
  161.0 7.0 %collective-permute-start.24 = (f16[256,768]{1,0:T(8,128)(2,1)S(1)}, f16[256,768]{1,0:T(8,128)(2,1)S(1)}, u32[]{:S(2)}, u32[]{:S(2)}) collective-permute-start(f16[256,768]{1,0:T(8,128)(2,1)S(1)} %collective-permute-done.20), channel_id=1, source_target_pairs={{0,1},{1,0},{2,3},{3,2},{4,5},{5,4},{6,7},{7,6},{8,9},{9,8},{10,11... | collective-permute-start | bytes 1179656 | tf_op jit(solution)/shard_map/ppermute | solution.py:260

commit v5 on v2

--- a/solution.py
+++ b/solution.py
@@ -12,6 +12,7 @@
 LOG2E = math.log2(math.e)
 LANES = 128
 CORES = 2
+EXTRA = 16
 VMEM_LIMIT = 48 * 1024 * 1024
 
 
@@ -138,25 +139,63 @@
     )(ids, *sources, units, offsets, *extra)
 
 
-def sum_kernel(orders, n_totals, ids, *refs):
+def sum_plan(orders):
+    n = len(orders)
+    last = {order[-1] for order in orders}
+    sorted_slots = []
+    for order in orders:
+        slots = list(range(n))
+        sorted_slots.append(sorted(slots, key=lambda slot: (order[slot] in last, slot)))
+    steps = []
+    for turn in range(n):
+        slots = [sorted_slots[place][turn] for place in range(n)]
+        blocks = [orders[place][slot] for place, slot in enumerate(slots)]
+        for who in range(CORES):
+            steps.append(([slot * CORES + who for slot in slots], blocks, who))
+    return steps
+
+
+def three_rows(values, dtype, depth):
+    size = values.shape[1]
+    line = lax.broadcasted_iota(jnp.int32, (EXTRA, size), 0)
+    high = values.astype(dtype).astype(jnp.float32)
+    rest = values - high
+    middle = rest.astype(dtype).astype(jnp.float32)
+    low = rest - middle
+    rows = jnp.where(
+        line == 0, high, jnp.where(line == 1, middle, jnp.where(line == 2, low, 0.0))
+    )
+    if size < depth:
+        rows = jnp.concatenate([rows, jnp.zeros((EXTRA, depth - size), jnp.float32)], axis=1)
+    return rows.astype(dtype)
+
+
+def one_row(rows, size):
+    return jnp.sum(rows[:, :size].astype(jnp.float32), axis=0, keepdims=True)
+
+
+def sum_kernel(plan, n_totals, n_owners, first, last, ids, *refs):
     totals = refs[:n_totals]
-    scores, rows, sent, mine, masses, inverse, total, mass = refs[n_totals:]
+    scores, rows = refs[n_totals], refs[n_totals + 1]
+    state = refs[n_totals + 2 : n_totals + 4]
+    total, mass, inverse = refs[-3:]
+    outs = refs[n_totals + (2 if first else 4) : -3]
     step = pl.program_id(0)
-    n_columns = inverse.shape[0]
 
     @pl.when(step == 0)
     def _():
-        for column in range(n_columns):
-            slot, who = divmod(column, CORES)
-            place = pick(ids[0], [order[slot] for order in orders]) * CORES + (
-                (ids[1] % CORES) ^ who
-            )
+        for number, (_, blocks, who) in enumerate(plan):
+            place = pick(ids[0], blocks) * CORES + ((ids[1] % CORES) ^ who)
             value = totals[0][place]
             for more in totals[1:]:
                 value = value + more[place]
-            inverse[column] = 1.0 / value
-        total[...] = jnp.zeros_like(total)
-        mass[...] = jnp.zeros_like(mass)
+            inverse[number] = 1.0 / value
+        if first:
+            total[...] = jnp.zeros_like(total)
+            mass[...] = jnp.zeros_like(mass)
+        else:
+            total[...] = state[0][...]
+            mass[...] = state[1][...]
 
     resp = (scores[...] * inverse[step]).astype(jnp.bfloat16)
     total[...] += lax.dot_general(
@@ -170,62 +209,148 @@
 
     @pl.when(step == pl.num_programs(0) - 1)
     def _():
-        size = mine.shape[0]
+        if not last:
+            outs[0][...] = total[...]
+            outs[1][...] = mass[...]
+            return
+        sent = outs[:-2]
+        mine, masses = outs[-2:]
+        size, depth = mine.shape
         quarter = ids[1] // CORES
-        for number in range(total.shape[0] // size):
+        sums = jnp.sum(mass[...].T, axis=0, keepdims=True)
+        for number in range(n_owners):
             block = total[number * size : (number + 1) * size, :]
-            away = quarter ^ number
-
-            @pl.when(away == 0)
+            own = sums[:, number * size : (number + 1) * size]
+
+            @pl.when(quarter == number)
             def _():
                 mine[...] = block
-
-            @pl.when(away != 0)
-            def _():
-                sent[away - 1] = block.astype(sent.dtype)
-
-        masses[...] = jnp.sum(mass[...].T, axis=0, keepdims=True)
-
-
-def sum_rows(ids, orders, totals, scores, rows, n_owners):
-    count, width = scores.shape
+                masses[...] = own
+
+            for away in range(1, n_owners):
+
+                @pl.when(quarter ^ number == away)
+                def _():
+                    target = sent[away - 1]
+                    target[:size, :] = block.astype(target.dtype)
+                    target[size:, :] = three_rows(own, target.dtype, depth)
+
+
+def sum_rows(ids, plan, totals, scores, rows, n_owners, carried, last):
+    count = scores.shape[0]
     depth = rows.shape[1]
     size = count // n_owners
-    n_columns, _, part = totals[0].shape
+    part = totals[0].shape[2]
+    first = carried is None
+    column = lambda t, s: sum(
+        jnp.where(t == n, pick(s[0], columns), 0) for n, (columns, _, _) in enumerate(plan)
+    )
+    fixed = lambda shape: pl.BlockSpec(shape, lambda t, s: (0,) * len(shape))
+    in_specs = [fixed(totals[0].shape) for _ in totals] + [
+        pl.BlockSpec((count, part), lambda t, s: (0, column(t, s))),
+        pl.BlockSpec((part, depth), lambda t, s: (column(t, s), 0)),
+    ]
+    state = [(count, depth), (count, LANES)]
+    if not first:
+        in_specs += [fixed(shape) for shape in state]
+    if last:
+        shapes = [((size + EXTRA, depth), jnp.bfloat16)] * (n_owners - 1) + [
+            ((size, depth), jnp.float32),
+            ((1, size), jnp.float32),
+        ]
+    else:
+        shapes = [(shape, jnp.float32) for shape in state]
     return pl.pallas_call(
-        functools.partial(sum_kernel, orders, len(totals)),
+        functools.partial(sum_kernel, plan, len(totals), n_owners, first, last),
         grid_spec=pltpu.PrefetchScalarGridSpec(
             num_scalar_prefetch=1,
-            grid=(n_columns,),
-            in_specs=[pl.BlockSpec(totals[0].shape, lambda t, s: (0, 0, 0)) for _ in totals]
-            + [
-                pl.BlockSpec((count, part), lambda t, s: (0, t)),
-                pl.BlockSpec((part, depth), lambda t, s: (t, 0)),
-            ],
-            out_specs=[
-                pl.BlockSpec((n_owners - 1, size, depth), lambda t, s: (0, 0, 0)),
-                pl.BlockSpec((size, depth), lambda t, s: (0, 0)),
-                pl.BlockSpec((1, count), lambda t, s: (0, 0)),
-            ],
+            grid=(len(plan),),
+            in_specs=in_specs,
+            out_specs=[fixed(shape) for shape, _ in shapes],
             scratch_shapes=[
-                pltpu.VMEM((n_columns, 1, part), jnp.float32),
                 pltpu.VMEM((count, depth), jnp.float32),
                 pltpu.VMEM((count, LANES), jnp.float32),
+                pltpu.VMEM((len(plan), 1, part), jnp.float32),
             ],
         ),
-        out_shape=(
-            jax.ShapeDtypeStruct((n_owners - 1, size, depth), jnp.bfloat16),
-            jax.ShapeDtypeStruct((size, depth), jnp.float32),
-            jax.ShapeDtypeStruct((1, count), jnp.float32),
-        ),
+        out_shape=[jax.ShapeDtypeStruct(shape, dtype) for shape, dtype in shapes],
         compiler_params=pltpu.CompilerParams(vmem_limit_bytes=VMEM_LIMIT),
         cost_estimate=pl.CostEstimate(
-            flops=2 * count * width * depth,
-            bytes_accessed=count * (width * 4 + depth * 4) + width * depth * 2,
+            flops=2 * count * len(plan) * part * depth,
+            bytes_accessed=len(plan) * part * (count * 4 + depth * 2) + count * depth * 4,
             transcendentals=0,
         ),
         name="sums",
-    )(ids, *totals, scores, rows)
+    )(ids, *totals, scores, rows, *(carried or ()))
+
+
+def combine_kernel(mine, masses, *refs):
+    arrived, out = refs[:-1], refs[-1]
+    size, depth = mine.shape
+    total = mine[...]
+    mass = masses[...]
+    for ref in arrived:
+        total = total + ref[:size, :].astype(jnp.float32)
+        mass = mass + one_row(ref[size:, :], size)
+    square = jnp.sum(total * total, axis=1, keepdims=True)
+    out[:size, :] = (total * lax.rsqrt(square + 1e-06)).astype(out.dtype)
+    out[size:, :] = three_rows(mass, out.dtype, depth)
+
+
+def combine(mine, masses, arrived):
+    size, depth = mine.shape
+    return pl.pallas_call(
+        combine_kernel,
+        out_shape=jax.ShapeDtypeStruct((size + EXTRA, depth), jnp.bfloat16),
+        compiler_params=pltpu.CompilerParams(vmem_limit_bytes=VMEM_LIMIT),
+        name="combine",
+    )(mine, masses, *arrived)
+
+
+def assemble_kernel(factor, n_pieces, ids, *refs):
+    pieces = refs[:n_pieces]
+    units, weights = refs[-2:]
+    size = units.shape[0]
+    for number, piece in enumerate(pieces):
+
+        @pl.when(pl.program_id(0) == number)
+        def _():
+            units[...] = piece[:size, :].astype(jnp.float32)
+            weights[0] = one_row(piece[size:, :], size) * factor
+
+
+def assemble(ids, pieces, carried, n_blocks, factor):
+    size, depth = pieces[0][2].shape
+    size -= EXTRA
+    half = n_blocks // CORES
+    flips = [flip for flip, _, _ in pieces]
+    aways = [away for _, away, _ in pieces]
+
+    def block(t, s):
+        return ((s[1] % CORES) ^ pick(t, flips)) * half + ((s[1] // CORES) ^ pick(t, aways))
+
+    extra = carried or ()
+    aliases = {1 + len(pieces) + n: n for n in range(len(extra))}
+    return pl.pallas_call(
+        functools.partial(assemble_kernel, factor, len(pieces)),
+        grid_spec=pltpu.PrefetchScalarGridSpec(
+            num_scalar_prefetch=1,
+            grid=(len(pieces),),
+            in_specs=[pl.BlockSpec((size + EXTRA, depth), lambda t, s: (0, 0)) for _ in pieces]
+            + [pl.BlockSpec(memory_space=pl.ANY) for _ in extra],
+            out_specs=[
+                pl.BlockSpec((size, depth), lambda t, s: (block(t, s), 0)),
+                pl.BlockSpec((1, 1, size), lambda t, s: (block(t, s), 0, 0)),
+            ],
+        ),
+        out_shape=[
+            jax.ShapeDtypeStruct((n_blocks * size, depth), jnp.float32),
+            jax.ShapeDtypeStruct((n_blocks, 1, size), jnp.float32),
+        ],
+        input_output_aliases=aliases,
+        compiler_params=pltpu.CompilerParams(vmem_limit_bytes=VMEM_LIMIT),
+        name="assemble",
+    )(ids, *[payload for _, _, payload in pieces], *extra)
 
 
 def local(embeddings, centroids, log_mix):
@@ -311,6 +436,17 @@
             )
         return carried
 
+    def totals_of(own):
+        both = own + exchange(own, 1)
+        return [both] + [
+            lax.ppermute(both, "blk", [(i, (i + turn) % n_places) for i in range(n_places)])
+            for turn in range(1, n_places)
+        ]
+
+    settled = {
+        block for block in range(n_places) if all(order[-1] != block for order in orders)
+    }
+    early_totals = None
     for turn in range(n_places):
         while sum(len(places) for _, places in slots[turn]) < n_places:
             moved, moves = start_ready(moves)
@@ -319,47 +455,39 @@
         slots[turn] = merged(slots[turn])
         moved, moves = start_ready(moves)
         carried = scores_of(turn, carried)
+        if turn == n_places - 2 and settled:
+            early_totals = totals_of(carried[2])
+            early_totals, carried = lax.optimization_barrier((early_totals, carried))
         if moved:
             arrays, carried = lax.optimization_barrier(([array for _, array, _ in moved], carried))
             for (slot, _, places), array in zip(moved, arrays):
                 slots[slot].append((array, places))
     scores, rows, totals = carried
-    totals = totals + exchange(totals, 1)
-    all_totals = [totals] + [
-        lax.ppermute(totals, "blk", [(i, (i + turn) % n_places) for i in range(n_places)])
-        for turn in range(1, n_places)
-    ]
-
-    sent, summed, masses = sum_rows(ids, orders, all_totals, scores, rows, n_owners)
+    steps = sum_plan(orders)
+    late = totals_of(totals)
+    if early_totals is not None:
+        ready = [step for step in steps if all(block in settled for block in step[1])]
+        rest = [step for step in steps if step not in ready]
+        state = sum_rows(ids, ready, early_totals, scores, rows, n_owners, None, False)
+        late, state = lax.optimization_barrier((late, state))
+    else:
+        rest, state = steps, None
+    *sent, mine, masses = sum_rows(ids, rest, late, scores, rows, n_owners, state, True)
     far = [CORES * away for away in range(1, n_owners)]
-    arrived = [exchange(sent[number], distance) for number, distance in enumerate(far)]
-    for array in arrived:
-        summed = summed + array.astype(jnp.float32)
-
-    distance = CORES
-    while distance < n_rows:
-        masses = masses + exchange(masses, distance)
-        distance *= 2
-    masses = masses.reshape(half)
-    other_masses = exchange(masses, 1)
-    both = jnp.where(
-        core == 0,
-        jnp.concatenate([masses, other_masses]),
-        jnp.concatenate([other_masses, masses]),
-    )
-
-    unit = summed * lax.rsqrt(jnp.sum(summed * summed, axis=1, keepdims=True) + 1e-06)
-    unit = unit.astype(jnp.float16)
-    size = unit.shape[0]
-    result = jnp.zeros((local_centroids, depth), jnp.float32)
-    pieces = [(0, unit)] + [(distance, exchange(unit, distance)) for distance in far]
-    for distance, piece in pieces:
-        for flip, array in ((0, piece), (1, exchange(piece, 1))):
-            start = (core ^ flip) * half + lax.div(me ^ distance, CORES) * size
-            result = lax.dynamic_update_slice(result, array.astype(jnp.float32), (start, 0))
+    arrived = [exchange(array, distance) for array, distance in zip(sent, far)]
+    payload = combine(mine, masses, arrived)
+
     count = local_centroids * n_places
     factor = count / (held * n_rows * n_places)
-    return (result, both * factor)
+    pieces = [exchange(payload, distance) for distance in far]
+    done = assemble(
+        ids, [(0, 0, payload), (1, 0, exchange(payload, 1))], None, n_rows, factor
+    )
+    pieces, done = lax.optimization_barrier((pieces, done))
+    placed = [(0, away + 1, piece) for away, piece in enumerate(pieces)]
+    placed += [(1, away + 1, exchange(piece, 1)) for away, piece in enumerate(pieces)]
+    result, weights = assemble(ids, placed, done, n_rows, factor)
+    return (result, weights.reshape(local_centroids))
 
 
 def solution(mesh):

time: 152 us -> 152 us (level)
  Pallas kernels: 39.7 us -> 47.6 us
  other arithmetic: 12 us -> 4.32 us
  starting transfers between devices: 26.4 us -> 31.8 us
  waiting for transfers between devices: 70.7 us -> 65.7 us
    ppermute x5, waiting for transfers between devices: 34 us -> 20.6 us  [start_ready(): lax.ppermute(slots[source_slot][hold][0], 'blk', pairs)]
    pallas_call x1 -> x5, Pallas kernels: 14 us -> 21.9 us  [the longest x2 16.1 us: sum_rows(): pl.pallas_call(functools.partial(sum_kernel, plan, len(totals), n_owners,...]
    dynamic_update_slice x8 -> x0, other arithmetic: 6.75 us -> none  [local(): lax.dynamic_update_slice(result, array.astype(jnp.float32), (start, 0))]
    ppermute x3 -> x6, starting transfers between devices: 3.87 us -> 10.5 us  [totals_of(): lax.ppermute(both, 'blk', [(i, (i + turn) % n_places) for i in range(n_pl...]
    ppermute x14 -> x12, waiting for transfers between devices: 33.6 us -> 38.7 us  [exchange(): lax.ppermute(array, 'rows', [(i, i ^ distance) for i in range(n_rows)])]
    ppermute x3 -> x6, waiting for transfers between devices: 3.11 us -> 6.36 us  [totals_of(): lax.ppermute(both, 'blk', [(i, (i + turn) % n_places) for i in range(n_pl...]
    ppermute x14 -> x12, starting transfers between devices: 10.2 us -> 8.82 us  [exchange(): lax.ppermute(array, 'rows', [(i, i ^ distance) for i in range(n_rows)])]
  transfers between devices with their start and end apart: 28 -> 29, of which waited for: 11 -> 13; matrix products, arithmetic and copies ran while one was open for 7% -> 3% of each run, Pallas kernels for 15% -> 21%
where the time goes in v5:
time: 152 us
  waiting for transfers between devices  65.7 us (43%)
  Pallas kernels  47.6 us (31%)
  starting transfers between devices  31.8 us (21%)
  other arithmetic  4.32 us (3%)
    ppermute x12, waiting for transfers between devices, exchange(): lax.ppermute(array, 'rows', [(i, i ^ distance) for i in range(n_rows)])  38.7 us
    pallas_call x8, Pallas kernels, score_block(): pl.pallas_call(functools.partial(score_kernel, n_sources, choice), grid_s...  25.6 us
    ppermute x5, waiting for transfers between devices, start_ready(): lax.ppermute(slots[source_slot][hold][0], 'blk', pairs)  20.6 us
    pallas_call x2, Pallas kernels, sum_rows(): pl.pallas_call(functools.partial(sum_kernel, plan, len(totals), n_owners,...  16.1 us
    ppermute x6, starting transfers between devices, totals_of(): lax.ppermute(both, 'blk', [(i, (i + turn) % n_places) for i in range(n_pl...  10.5 us
    ppermute x12, starting transfers between devices, exchange(): lax.ppermute(array, 'rows', [(i, i ^ distance) for i in range(n_rows)])  8.82 us
    ppermute x5, starting transfers between devices, start_ready(): lax.ppermute(slots[source_slot][hold][0], 'blk', pairs)  6.64 us
    ppermute x6, waiting for transfers between devices, totals_of(): lax.ppermute(both, 'blk', [(i, (i + turn) % n_places) for i in range(n_pl...  6.36 us
  transfers between devices with their start and end apart: 29, of which 13 were waited for; matrix products, arithmetic and copies ran while one was open for 3% of the time, Pallas kernels for 21%

profile of v5, /device:TPU:0, one launch (start us, length us, event | category | flops | bytes accessed | tf_op | source)
XLA Modules:
  0.0 151.6 jit_solution(17710324795107014536)
XLA Ops:
  1.1 2.7 %collective-permute-start = (bf16[512,768]{1,0:T(8,128)(2,1)}, bf16[512,768]{1,0:T(8,128)(2,1)S(1)}, u32[]{:S(2)}, u32[]{:S(2)}) collective-permute-start(bf16[512,768]{1,0:T(8,128)(2,1)} %refs_0_.1), channel_id=1, source_target_pairs={{8,0},{0,8},{24,16},{16,24},{9,1},{1,9},{25,17},{17,25},{10,2},{2,... | collective-permute-start | bytes 2359304 | tf_op jit(solution)/shard_map/ppermute | solution.py:394
  4.6 1.8 %fusion = f32[1024]{0:T(1024)S(1)} fusion(bf16[2048,768]{1,0:T(8,128)(2,1)} %param.4, s32[]{:T(128)S(6)} %select_n.4), kind=kLoop, calls=%fused_computation.2 | loop fusion | flops 2358272 | bytes 1576964 | tf_op jit(solution)/shard_map/reduce_sum | solution.py:21
  7.1 1.7 %fusion.1.refs_1_.refs_2_ = bf16[1024,768]{1,0:T(8,128)(2,1)S(1)} fusion(f32[1024]{0:T(1024)S(1)} %add_rsqrt_fusion, bf16[2048,768]{1,0:T(8,128)(2,1)} %param.4, s32[]{:T(128)S(6)} %select_n.4), kind=kLoop, calls=%fused_computation.3 | loop fusion | flops 2359296 | bytes 3149828 | tf_op jit(solution)/shard_map/convert_element_type | solution.py:21
  10.1 3.3 %scores.8 = (f32[1024,4096]{1,0:T(8,128)}, bf16[4096,768]{1,0:T(8,128)(2,1)}, f32[8,1,512]{2,1,0:T(1,128)S(1)}) custom-call(s32[2]{0:T(128)S(1)} %pad_add_fusion.ids, bf16[512,768]{1,0:T(8,128)(2,1)S(1)} %copy-done, bf16[1024,768]{1,0:T(8,128)(2,1)S(1)} %fusion.1.refs_1_.refs_2_, f32[1024,128]{1,0:T(8,128)S(1)} %broadcast_in_dim.2.refs_2_.refs_3_), custom_call_target="tpu_custom_call" | custom-call | flops 805306368 | bytes 7340032 | tf_op jit(solution)/shard_map/scores/pallas_call | solution.py:105
  13.5 3.2 %scores.9 = (f32[1024,4096]{1,0:T(8,128)}, bf16[4096,768]{1,0:T(8,128)(2,1)}, f32[8,1,512]{2,1,0:T(1,128)S(1)}) custom-call(s32[2]{0:T(128)S(1)} %pad_add_fusion.ids, bf16[512,768]{1,0:T(8,128)(2,1)S(1)} %collective-permute-done.2.refs_0_, bf16[1024,768]{1,0:T(8,128)(2,1)S(1)} %fusion.1.refs_1_.refs_2_, ...), custom_call_target="tpu_custom_call", output_to_operand_aliasing={{0}: (4, {}), {1}: (5, {}), {2}: (6, {})} | custom-call | flops 805306368 | bytes 7340032 | tf_op jit(solution)/shard_map/scores/pallas_call | solution.py:105
  16.7 5.4 %collective-permute-done.refs_0_ = bf16[512,768]{1,0:T(8,128)(2,1)S(1)} collective-permute-done((bf16[512,768]{1,0:T(8,128)(2,1)}, bf16[512,768]{1,0:T(8,128)(2,1)S(1)}, u32[]{:S(2)}, u32[]{:S(2)}) %collective-permute-start) | collective-permute-done | bytes 786464 | tf_op jit(solution)/shard_map/ppermute | solution.py:394
  24.9 3.2 %scores.10 = (f32[1024,4096]{1,0:T(8,128)}, bf16[4096,768]{1,0:T(8,128)(2,1)}, f32[8,1,512]{2,1,0:T(1,128)S(1)}) custom-call(s32[2]{0:T(128)S(1)} %pad_add_fusion.ids, bf16[512,768]{1,0:T(8,128)(2,1)S(1)} %collective-permute-done.refs_0_, bf16[1024,768]{1,0:T(8,128)(2,1)S(1)} %fusion.1.refs_1_.refs_2_, ...), custom_call_target="tpu_custom_call", output_to_operand_aliasing={{0}: (4, {}), {1}: (5, {}), {2}: (6, {})} | custom-call | flops 805306368 | bytes 7340032 | tf_op jit(solution)/shard_map/scores/pallas_call | solution.py:105
  28.1 3.2 %scores.11 = (f32[1024,4096]{1,0:T(8,128)}, bf16[4096,768]{1,0:T(8,128)(2,1)}, f32[8,1,512]{2,1,0:T(1,128)S(1)}) custom-call(s32[2]{0:T(128)S(1)} %pad_add_fusion.ids, bf16[512,768]{1,0:T(8,128)(2,1)S(1)} %collective-permute-done.5.refs_0_, bf16[1024,768]{1,0:T(8,128)(2,1)S(1)} %fusion.1.refs_1_.refs_2_, ...), custom_call_target="tpu_custom_call", output_to_operand_aliasing={{0}: (4, {}), {1}: (5, {}), {2}: (6, {})} | custom-call | flops 805306368 | bytes 7340032 | tf_op jit(solution)/shard_map/scores/pallas_call | solution.py:105
  31.2 15.2 %collective-permute-done.3.refs_1_ = bf16[512,768]{1,0:T(8,128)(2,1)S(1)} collective-permute-done((bf16[512,768]{1,0:T(8,128)(2,1)S(1)}, bf16[512,768]{1,0:T(8,128)(2,1)S(1)}, u32[]{:S(2)}, u32[]{:S(2)}) %collective-permute-start.3) | collective-permute-done | bytes 786464 | tf_op jit(solution)/shard_map/ppermute | solution.py:394
  46.4 1.9 %collective-permute-start.9 = (bf16[512,768]{1,0:T(8,128)(2,1)S(1)}, bf16[512,768]{1,0:T(8,128)(2,1)S(1)}, u32[]{:S(2)}, u32[]{:S(2)}) collective-permute-start(bf16[512,768]{1,0:T(8,128)(2,1)S(1)} %collective-permute-done.3.refs_1_), channel_id=1, source_target_pairs={{0,1},{1,0},{2,3},{3,2},{4,5},{5,4},{6,7},{7,6},{24,25},{25,24},{2... | collective-permute-start | bytes 2359304 | tf_op jit(solution)/shard_map/ppermute | solution.py:376
  49.6 3.2 %scores.12 = (f32[1024,4096]{1,0:T(8,128)}, bf16[4096,768]{1,0:T(8,128)(2,1)}, f32[8,1,512]{2,1,0:T(1,128)S(1)}) custom-call(s32[2]{0:T(128)S(1)} %pad_add_fusion.ids, bf16[512,768]{1,0:T(8,128)(2,1)S(1)} %collective-permute-done.1.refs_0_, ...), custom_call_target="tpu_custom_call", output_to_operand_aliasing={{0}: (5, {}), {1}: (6, {}), {2}: (7, {})} | custom-call | flops 805306368 | bytes 7340032 | tf_op jit(solution)/shard_map/scores/pallas_call | solution.py:105
  52.9 3.2 %scores.13 = (f32[1024,4096]{1,0:T(8,128)}, bf16[4096,768]{1,0:T(8,128)(2,1)}, f32[8,1,512]{2,1,0:T(1,128)S(1)}) custom-call(s32[2]{0:T(128)S(1)} %pad_add_fusion.ids, bf16[512,768]{1,0:T(8,128)(2,1)S(1)} %collective-permute-done.8.refs_0_, ...), custom_call_target="tpu_custom_call", output_to_operand_aliasing={{0}: (5, {}), {1}: (6, {}), {2}: (7, {})} | custom-call | flops 805306368 | bytes 7340032 | tf_op jit(solution)/shard_map/scores/pallas_call | solution.py:105
  57.5 2.6 %collective-permute-start.11 = (f32[8,1,512]{2,1,0:T(1,128)S(1)}, f32[8,1,512]{2,1,0:T(1,128)S(1)}, u32[]{:S(2)}, u32[]{:S(2)}) collective-permute-start(f32[8,1,512]{2,1,0:T(1,128)S(1)} %add.25.refs_0_), channel_id=1, source_target_pairs={{0,8},{8,16},{16,24},{24,0},{1,9},{9,17},{17,25},{25,1},{2,10},{10... | collective-permute-start | bytes 49160 | tf_op jit(solution)/shard_map/ppermute | solution.py:442
  61.3 2.8 %collective-permute-start.13 = (f32[8,1,512]{2,1,0:T(1,128)S(1)}, f32[8,1,512]{2,1,0:T(1,128)S(1)}, u32[]{:S(2)}, u32[]{:S(2)}) collective-permute-start(f32[8,1,512]{2,1,0:T(1,128)S(1)} %add.25.refs_0_), channel_id=1, source_target_pairs={{0,24},{8,0},{16,8},{24,16},{1,25},{9,1},{17,9},{25,17},{2,26},{10... | collective-permute-start | bytes 49160 | tf_op jit(solution)/shard_map/ppermute | solution.py:442
  64.9 6.3 %collective-permute-done.13.refs_3_ = f32[8,1,512]{2,1,0:T(1,128)S(1)} collective-permute-done((f32[8,1,512]{2,1,0:T(1,128)S(1)}, f32[8,1,512]{2,1,0:T(1,128)S(1)}, u32[]{:S(2)}, u32[]{:S(2)}) %collective-permute-start.13) | collective-permute-done | bytes 16416 | tf_op jit(solution)/shard_map/ppermute | solution.py:442
  71.2 1.9 %collective-permute-start.14 = (bf16[512,768]{1,0:T(8,128)(2,1)S(1)}, bf16[512,768]{1,0:T(8,128)(2,1)S(1)}, u32[]{:S(2)}, u32[]{:S(2)}) collective-permute-start(bf16[512,768]{1,0:T(8,128)(2,1)S(1)} %collective-permute-done.7.refs_1_), channel_id=1, source_target_pairs={{0,1},{1,0},{2,3},{3,2},{4,5},{5,4},{6,7},{7,6},{24,25},{25,24},{2... | collective-permute-start | bytes 2359304 | tf_op jit(solution)/shard_map/ppermute | solution.py:376
  73.1 3.2 %scores.14 = (f32[1024,4096]{1,0:T(8,128)}, bf16[4096,768]{1,0:T(8,128)(2,1)}, f32[8,1,512]{2,1,0:T(1,128)S(1)}) custom-call(s32[2]{0:T(128)S(1)} %pad_add_fusion.ids, bf16[512,768]{1,0:T(8,128)(2,1)S(1)} %collective-permute-done.4.refs_0_, ...), custom_call_target="tpu_custom_call", output_to_operand_aliasing={{0}: (5, {}), {1}: (6, {}), {2}: (7, {})} | custom-call | flops 805306368 | bytes 7340032 | tf_op jit(solution)/shard_map/scores/pallas_call | solution.py:105
  76.3 3.2 %scores.15 = (f32[1024,4096]{1,0:T(8,128)}, bf16[4096,768]{1,0:T(8,128)(2,1)}, f32[8,1,512]{2,1,0:T(1,128)S(1)}) custom-call(s32[2]{0:T(128)S(1)} %pad_add_fusion.ids, bf16[512,768]{1,0:T(8,128)(2,1)S(1)} %collective-permute-done.6.refs_0_, ...), custom_call_target="tpu_custom_call", output_to_operand_aliasing={{0}: (5, {}), {1}: (6, {}), {2}: (7, {})} | custom-call | flops 805306368 | bytes 7340032 | tf_op jit(solution)/shard_map/scores/pallas_call | solution.py:105
  81.0 3.2 %collective-permute-start.17 = (f32[8,1,512]{2,1,0:T(1,128)S(1)}, f32[8,1,512]{2,1,0:T(1,128)S(1)}, u32[]{:S(2)}, u32[]{:S(2)}) collective-permute-start(f32[8,1,512]{2,1,0:T(1,128)S(1)} %add.26.refs_0_), channel_id=1, source_target_pairs={{0,16},{8,24},{16,0},{24,8},{1,17},{9,25},{17,1},{25,9},{2,18},{10... | collective-permute-start | bytes 49160 | tf_op jit(solution)/shard_map/ppermute | solution.py:442
  84.9 7.9 %sums.2 = (f32[1024,768]{1,0:T(8,128)S(1)}, f32[1024,128]{1,0:T(8,128)S(1)}) custom-call(s32[2]{0:T(128)S(1)} %pad_add_fusion.ids, f32[8,1,512]{2,1,0:T(1,128)S(1)} %add.25.refs_0_, f32[8,1,512]{2,1,0:T(1,128)S(1)} %collective-permute-done.11.refs_1_, f32[8,1,512]{2,1,0:T(1,128)S(1)} %collective-permute-done.12.refs_2_, ...), custom_call_target="tpu_custom_call" | custom-call | flops 3221225472 | bytes 14680064 | tf_op jit(solution)/shard_map/sums/pallas_call | solution.py:263
  92.8 8.2 %sums.3 = (bf16[272,768]{1,0:T(8,128)(2,1)S(1)}, bf16[272,768]{1,0:T(8,128)(2,1)S(1)}, bf16[272,768]{1,0:T(8,128)(2,1)S(1)}, f32[256,768]{1,0:T(8,128)S(1)}, f32[1,256]{1,0:T(1,128)S(1)}) custom-call(s32[2]{0:T(128)S(1)} %pad_add_fusion.ids, f32[8,1,512]{2,1,0:T(1,128)S(1)} %add.26.refs_0_, f32[8,1,512]{2,1,0:T(1,128)S(1)} %collective-permute-done.16.refs_1_, ...), custom_call_target="tpu_custom_call" | custom-call | flops 3221225472 | bytes 14680064 | tf_op jit(solution)/shard_map/sums/pallas_call | solution.py:263
  101.0 1.6 %collective-permute-start.19 = (bf16[272,768]{1,0:T(8,128)(2,1)S(1)}, bf16[272,768]{1,0:T(8,128)(2,1)S(1)}, u32[]{:S(2)}, u32[]{:S(2)}) collective-permute-start(bf16[272,768]{1,0:T(8,128)(2,1)S(1)} %get-tuple-element.124), channel_id=1, source_target_pairs={{0,2},{1,3},{2,0},{3,1},{4,6},{5,7},{6,4},{7,5},{8,10},{9,11},{10,... | collective-permute-start | bytes 1253384 | tf_op jit(solution)/shard_map/ppermute | solution.py:370
  102.6 1.5 %collective-permute-start.20 = (bf16[272,768]{1,0:T(8,128)(2,1)S(1)}, bf16[272,768]{1,0:T(8,128)(2,1)S(1)}, u32[]{:S(2)}, u32[]{:S(2)}) collective-permute-start(bf16[272,768]{1,0:T(8,128)(2,1)S(1)} %get-tuple-element.125), channel_id=1, source_target_pairs={{0,4},{1,5},{2,6},{3,7},{4,0},{5,1},{6,2},{7,3},{8,12},{9,13},{10,... | collective-permute-start | bytes 1253384 | tf_op jit(solution)/shard_map/ppermute | solution.py:370
  104.5 9.0 %collective-permute-done.19.refs_0_ = bf16[272,768]{1,0:T(8,128)(2,1)S(1)} collective-permute-done((bf16[272,768]{1,0:T(8,128)(2,1)S(1)}, bf16[272,768]{1,0:T(8,128)(2,1)S(1)}, u32[]{:S(2)}, u32[]{:S(2)}) %collective-permute-start.19) | collective-permute-done | bytes 417824 | tf_op jit(solution)/shard_map/ppermute | solution.py:370
  113.6 9.0 %collective-permute-done.20.refs_1_ = bf16[272,768]{1,0:T(8,128)(2,1)S(1)} collective-permute-done((bf16[272,768]{1,0:T(8,128)(2,1)S(1)}, bf16[272,768]{1,0:T(8,128)(2,1)S(1)}, u32[]{:S(2)}, u32[]{:S(2)}) %collective-permute-start.20) | collective-permute-done | bytes 417824 | tf_op jit(solution)/shard_map/ppermute | solution.py:370
  123.0 1.3 collective-permute-start.22
  125.1 1.4 collective-permute-start.24
  126.5 1.8 %assemble.2 = (f32[2048,768]{1,0:T(8,128)}, f32[8,1,256]{2,1,0:T(1,128)}) custom-call(s32[2]{0:T(128)S(1)} %pad_add_fusion.ids, bf16[272,768]{1,0:T(8,128)(2,1)S(1)} %combine.1.refs_0_, bf16[272,768]{1,0:T(8,128)(2,1)S(1)} %collective-permute-done.25.refs_1_), custom_call_target="tpu_custom_call" | custom-call | tf_op jit(solution)/shard_map/assemble/pallas_call | solution.py:334
  128.3 7.1 %collective-permute-done.22.refs_0_ = bf16[272,768]{1,0:T(8,128)(2,1)S(1)} collective-permute-done((bf16[272,768]{1,0:T(8,128)(2,1)S(1)}, bf16[272,768]{1,0:T(8,128)(2,1)S(1)}, u32[]{:S(2)}, u32[]{:S(2)}) %collective-permute-start.22) | collective-permute-done | bytes 417824 | tf_op jit(solution)/shard_map/ppermute | solution.py:370
  135.5 7.8 %collective-permute-done.23.refs_1_ = bf16[272,768]{1,0:T(8,128)(2,1)S(1)} collective-permute-done((bf16[272,768]{1,0:T(8,128)(2,1)S(1)}, bf16[272,768]{1,0:T(8,128)(2,1)S(1)}, u32[]{:S(2)}, u32[]{:S(2)}) %collective-permute-start.23) | collective-permute-done | bytes 417824 | tf_op jit(solution)/shard_map/ppermute | solution.py:370
  143.3 1.6 %collective-permute-done.24.refs_2_ = bf16[272,768]{1,0:T(8,128)(2,1)S(1)} collective-permute-done((bf16[272,768]{1,0:T(8,128)(2,1)S(1)}, bf16[272,768]{1,0:T(8,128)(2,1)S(1)}, u32[]{:S(2)}, u32[]{:S(2)}) %collective-permute-start.24) | collective-permute-done | bytes 417824 | tf_op jit(solution)/shard_map/ppermute | solution.py:370
  147.9 3.8 %assemble.3 = (f32[2048,768]{1,0:T(8,128)}, f32[8,1,256]{2,1,0:T(1,128)}) custom-call(s32[2]{0:T(128)S(1)} %pad_add_fusion.ids, bf16[272,768]{1,0:T(8,128)(2,1)S(1)} %collective-permute-done.22.refs_0_, bf16[272,768]{1,0:T(8,128)(2,1)S(1)} %collective-permute-done.23.refs_1_, ...), custom_call_target="tpu_custom_call", output_to_operand_aliasing={{0}: (7, {}), {1}: (8, {})} | custom-call | tf_op jit(solution)/shard_map/assemble/pallas_call | solution.py:334
  (49 shorter events, 17.4 us)
Async XLA Ops:
  0.6 12.9 %collective-permute-start.2 = (bf16[512,768]{1,0:T(8,128)(2,1)}, bf16[512,768]{1,0:T(8,128)(2,1)S(1)}, u32[]{:S(2)}, u32[]{:S(2)}) collective-permute-start(bf16[512,768]{1,0:T(8,128)(2,1)} %refs_0_.1), channel_id=1, source_target_pairs={{0,1},{1,0},{2,3},{3,2},{4,5},{5,4},{6,7},{7,6},{8,9},{9,8},{10,11... | collective-permute-start | bytes 2359304 | tf_op jit(solution)/shard_map/ppermute | solution.py:376
  1.1 21.0 %collective-permute-start = (bf16[512,768]{1,0:T(8,128)(2,1)}, bf16[512,768]{1,0:T(8,128)(2,1)S(1)}, u32[]{:S(2)}, u32[]{:S(2)}) collective-permute-start(bf16[512,768]{1,0:T(8,128)(2,1)} %refs_0_.1), channel_id=1, source_target_pairs={{8,0},{0,8},{24,16},{16,24},{9,1},{1,9},{25,17},{17,25},{10,2},{2,... | collective-permute-start | bytes 2359304 | tf_op jit(solution)/shard_map/ppermute | solution.py:394
  3.8 18.3 %collective-permute-start.1 = (bf16[512,768]{1,0:T(8,128)(2,1)}, bf16[512,768]{1,0:T(8,128)(2,1)S(1)}, u32[]{:S(2)}, u32[]{:S(2)}) collective-permute-start(bf16[512,768]{1,0:T(8,128)(2,1)} %refs_0_.1), channel_id=1, source_target_pairs={{16,8},{8,16},{17,9},{9,17},{18,10},{10,18},{19,11},{11,19},{20,12... | collective-permute-start | bytes 2359304 | tf_op jit(solution)/shard_map/ppermute | solution.py:394
  9.0 1.1 copy-start
  22.1 5.9 %collective-permute-start.5 = (bf16[512,768]{1,0:T(8,128)(2,1)S(1)}, bf16[512,768]{1,0:T(8,128)(2,1)S(1)}, u32[]{:S(2)}, u32[]{:S(2)}) collective-permute-start(bf16[512,768]{1,0:T(8,128)(2,1)S(1)} %collective-permute-done.refs_0_), channel_id=1, source_target_pairs={{0,1},{1,0},{2,3},{3,2},{4,5},{5,4},{6,7},{7,6},{8,9},{9,8},{10,11... | collective-permute-start | bytes 2359304 | tf_op jit(solution)/shard_map/ppermute | solution.py:376
  22.1 24.3 %collective-permute-start.3 = (bf16[512,768]{1,0:T(8,128)(2,1)S(1)}, bf16[512,768]{1,0:T(8,128)(2,1)S(1)}, u32[]{:S(2)}, u32[]{:S(2)}) collective-permute-start(bf16[512,768]{1,0:T(8,128)(2,1)S(1)} %collective-permute-done.1.refs_0_), channel_id=1, source_target_pairs={{8,0},{16,24},{9,1},{17,25},{10,2},{18,26},{11,3},{19,27},{12,4},{... | collective-permute-start | bytes 2359304 | tf_op jit(solution)/shard_map/ppermute | solution.py:394
  23.4 23.0 %collective-permute-start.4 = (bf16[512,768]{1,0:T(8,128)(2,1)S(1)}, bf16[512,768]{1,0:T(8,128)(2,1)S(1)}, u32[]{:S(2)}, u32[]{:S(2)}) collective-permute-start(bf16[512,768]{1,0:T(8,128)(2,1)S(1)} %collective-permute-done.refs_0_), channel_id=1, source_target_pairs={{16,8},{8,16},{17,9},{9,17},{18,10},{10,18},{19,11},{11,19},{20,12... | collective-permute-start | bytes 2359304 | tf_op jit(solution)/shard_map/ppermute | solution.py:394
  24.2 28.7 %collective-permute-start.8 = (bf16[512,768]{1,0:T(8,128)(2,1)S(1)}, bf16[512,768]{1,0:T(8,128)(2,1)S(1)}, u32[]{:S(2)}, u32[]{:S(2)}) collective-permute-start(bf16[512,768]{1,0:T(8,128)(2,1)S(1)} %collective-permute-done.1.refs_0_), channel_id=1, source_target_pairs={{8,9},{9,8},{10,11},{11,10},{12,13},{13,12},{14,15},{15,14},{16,17... | collective-permute-start | bytes 2359304 | tf_op jit(solution)/shard_map/ppermute | solution.py:376
  46.4 6.4 %collective-permute-start.9 = (bf16[512,768]{1,0:T(8,128)(2,1)S(1)}, bf16[512,768]{1,0:T(8,128)(2,1)S(1)}, u32[]{:S(2)}, u32[]{:S(2)}) collective-permute-start(bf16[512,768]{1,0:T(8,128)(2,1)S(1)} %collective-permute-done.3.refs_1_), channel_id=1, source_target_pairs={{0,1},{1,0},{2,3},{3,2},{4,5},{5,4},{6,7},{7,6},{24,25},{25,24},{2... | collective-permute-start | bytes 2359304 | tf_op jit(solution)/shard_map/ppermute | solution.py:376
  48.3 22.9 %collective-permute-start.7 = (bf16[512,768]{1,0:T(8,128)(2,1)S(1)}, bf16[512,768]{1,0:T(8,128)(2,1)S(1)}, u32[]{:S(2)}, u32[]{:S(2)}) collective-permute-start(bf16[512,768]{1,0:T(8,128)(2,1)S(1)} %collective-permute-done.4.refs_0_), channel_id=1, source_target_pairs={{8,0},{16,24},{9,1},{17,25},{10,2},{18,26},{11,3},{19,27},{12,4},{... | collective-permute-start | bytes 2359304 | tf_op jit(solution)/shard_map/ppermute | solution.py:394
  56.0 1.4 collective-permute-start.10
  57.5 7.4 %collective-permute-start.11 = (f32[8,1,512]{2,1,0:T(1,128)S(1)}, f32[8,1,512]{2,1,0:T(1,128)S(1)}, u32[]{:S(2)}, u32[]{:S(2)}) collective-permute-start(f32[8,1,512]{2,1,0:T(1,128)S(1)} %add.25.refs_0_), channel_id=1, source_target_pairs={{0,8},{8,16},{16,24},{24,0},{1,9},{9,17},{17,25},{25,1},{2,10},{10... | collective-permute-start | bytes 49160 | tf_op jit(solution)/shard_map/ppermute | solution.py:442
  60.0 4.8 %collective-permute-start.12 = (f32[8,1,512]{2,1,0:T(1,128)S(1)}, f32[8,1,512]{2,1,0:T(1,128)S(1)}, u32[]{:S(2)}, u32[]{:S(2)}) collective-permute-start(f32[8,1,512]{2,1,0:T(1,128)S(1)} %add.25.refs_0_), channel_id=1, source_target_pairs={{0,16},{8,24},{16,0},{24,8},{1,17},{9,25},{17,1},{25,9},{2,18},{10... | collective-permute-start | bytes 49160 | tf_op jit(solution)/shard_map/ppermute | solution.py:442
  61.3 9.9 %collective-permute-start.13 = (f32[8,1,512]{2,1,0:T(1,128)S(1)}, f32[8,1,512]{2,1,0:T(1,128)S(1)}, u32[]{:S(2)}, u32[]{:S(2)}) collective-permute-start(f32[8,1,512]{2,1,0:T(1,128)S(1)} %add.25.refs_0_), channel_id=1, source_target_pairs={{0,24},{8,0},{16,8},{24,16},{1,25},{9,1},{17,9},{25,17},{2,26},{10... | collective-permute-start | bytes 49160 | tf_op jit(solution)/shard_map/ppermute | solution.py:442
  64.1 12.2 %collective-permute-start.6 = (bf16[512,768]{1,0:T(8,128)(2,1)S(1)}, bf16[512,768]{1,0:T(8,128)(2,1)S(1)}, u32[]{:S(2)}, u32[]{:S(2)}) collective-permute-start(bf16[512,768]{1,0:T(8,128)(2,1)S(1)} %collective-permute-done.4.refs_0_), channel_id=1, source_target_pairs={{8,9},{9,8},{10,11},{11,10},{12,13},{13,12},{14,15},{15,14},{16,17... | collective-permute-start | bytes 2359304 | tf_op jit(solution)/shard_map/ppermute | solution.py:376
  71.2 5.1 %collective-permute-start.14 = (bf16[512,768]{1,0:T(8,128)(2,1)S(1)}, bf16[512,768]{1,0:T(8,128)(2,1)S(1)}, u32[]{:S(2)}, u32[]{:S(2)}) collective-permute-start(bf16[512,768]{1,0:T(8,128)(2,1)S(1)} %collective-permute-done.7.refs_1_), channel_id=1, source_target_pairs={{0,1},{1,0},{2,3},{3,2},{4,5},{5,4},{6,7},{7,6},{24,25},{25,24},{2... | collective-permute-start | bytes 2359304 | tf_op jit(solution)/shard_map/ppermute | solution.py:376
  79.6 1.4 collective-permute-start.15
  81.0 11.8 %collective-permute-start.16 = (f32[8,1,512]{2,1,0:T(1,128)S(1)}, f32[8,1,512]{2,1,0:T(1,128)S(1)}, u32[]{:S(2)}, u32[]{:S(2)}) collective-permute-start(f32[8,1,512]{2,1,0:T(1,128)S(1)} %add.26.refs_0_), channel_id=1, source_target_pairs={{0,8},{8,16},{16,24},{24,0},{1,9},{9,17},{17,25},{25,1},{2,10},{10... | collective-permute-start | bytes 49160 | tf_op jit(solution)/shard_map/ppermute | solution.py:442
  81.0 11.7 %collective-permute-start.17 = (f32[8,1,512]{2,1,0:T(1,128)S(1)}, f32[8,1,512]{2,1,0:T(1,128)S(1)}, u32[]{:S(2)}, u32[]{:S(2)}) collective-permute-start(f32[8,1,512]{2,1,0:T(1,128)S(1)} %add.26.refs_0_), channel_id=1, source_target_pairs={{0,16},{8,24},{16,0},{24,8},{1,17},{9,25},{17,1},{25,9},{2,18},{10... | collective-permute-start | bytes 49160 | tf_op jit(solution)/shard_map/ppermute | solution.py:442
  84.2 8.5 %collective-permute-start.18 = (f32[8,1,512]{2,1,0:T(1,128)S(1)}, f32[8,1,512]{2,1,0:T(1,128)S(1)}, u32[]{:S(2)}, u32[]{:S(2)}) collective-permute-start(f32[8,1,512]{2,1,0:T(1,128)S(1)} %add.26.refs_0_), channel_id=1, source_target_pairs={{0,24},{8,0},{16,8},{24,16},{1,25},{9,1},{17,9},{25,17},{2,26},{10... | collective-permute-start | bytes 49160 | tf_op jit(solution)/shard_map/ppermute | solution.py:442
  101.0 12.6 %collective-permute-start.19 = (bf16[272,768]{1,0:T(8,128)(2,1)S(1)}, bf16[272,768]{1,0:T(8,128)(2,1)S(1)}, u32[]{:S(2)}, u32[]{:S(2)}) collective-permute-start(bf16[272,768]{1,0:T(8,128)(2,1)S(1)} %get-tuple-element.124), channel_id=1, source_target_pairs={{0,2},{1,3},{2,0},{3,1},{4,6},{5,7},{6,4},{7,5},{8,10},{9,11},{10,... | collective-permute-start | bytes 1253384 | tf_op jit(solution)/shard_map/ppermute | solution.py:370
  102.6 20.0 %collective-permute-start.20 = (bf16[272,768]{1,0:T(8,128)(2,1)S(1)}, bf16[272,768]{1,0:T(8,128)(2,1)S(1)}, u32[]{:S(2)}, u32[]{:S(2)}) collective-permute-start(bf16[272,768]{1,0:T(8,128)(2,1)S(1)} %get-tuple-element.125), channel_id=1, source_target_pairs={{0,4},{1,5},{2,6},{3,7},{4,0},{5,1},{6,2},{7,3},{8,12},{9,13},{10,... | collective-permute-start | bytes 1253384 | tf_op jit(solution)/shard_map/ppermute | solution.py:370
  104.1 18.5 %collective-permute-start.21 = (bf16[272,768]{1,0:T(8,128)(2,1)S(1)}, bf16[272,768]{1,0:T(8,128)(2,1)S(1)}, u32[]{:S(2)}, u32[]{:S(2)}) collective-permute-start(bf16[272,768]{1,0:T(8,128)(2,1)S(1)} %get-tuple-element.126), channel_id=1, source_target_pairs={{0,6},{1,7},{2,4},{3,5},{4,2},{5,3},{6,0},{7,1},{8,14},{9,15},{10,... | collective-permute-start | bytes 1253384 | tf_op jit(solution)/shard_map/ppermute | solution.py:370
  122.9 3.6 %collective-permute-start.25 = (bf16[272,768]{1,0:T(8,128)(2,1)S(1)}, bf16[272,768]{1,0:T(8,128)(2,1)S(1)}, u32[]{:S(2)}, u32[]{:S(2)}) collective-permute-start(bf16[272,768]{1,0:T(8,128)(2,1)S(1)} %combine.1.refs_0_), channel_id=1, source_target_pairs={{0,1},{1,0},{2,3},{3,2},{4,5},{5,4},{6,7},{7,6},{8,9},{9,8},{10,11... | collective-permute-start | bytes 1253384 | tf_op jit(solution)/shard_map/ppermute | solution.py:370
  123.0 12.5 %collective-permute-start.22 = (bf16[272,768]{1,0:T(8,128)(2,1)S(1)}, bf16[272,768]{1,0:T(8,128)(2,1)S(1)}, u32[]{:S(2)}, u32[]{:S(2)}) collective-permute-start(bf16[272,768]{1,0:T(8,128)(2,1)S(1)} %combine.1.refs_0_), channel_id=1, source_target_pairs={{0,2},{1,3},{2,0},{3,1},{4,6},{5,7},{6,4},{7,5},{8,10},{9,11},{10,... | collective-permute-start | bytes 1253384 | tf_op jit(solution)/shard_map/ppermute | solution.py:370
  124.3 19.0 %collective-permute-start.23 = (bf16[272,768]{1,0:T(8,128)(2,1)S(1)}, bf16[272,768]{1,0:T(8,128)(2,1)S(1)}, u32[]{:S(2)}, u32[]{:S(2)}) collective-permute-start(bf16[272,768]{1,0:T(8,128)(2,1)S(1)} %combine.1.refs_0_), channel_id=1, source_target_pairs={{0,4},{1,5},{2,6},{3,7},{4,0},{5,1},{6,2},{7,3},{8,12},{9,13},{10,... | collective-permute-start | bytes 1253384 | tf_op jit(solution)/shard_map/ppermute | solution.py:370
  125.1 19.8 %collective-permute-start.24 = (bf16[272,768]{1,0:T(8,128)(2,1)S(1)}, bf16[272,768]{1,0:T(8,128)(2,1)S(1)}, u32[]{:S(2)}, u32[]{:S(2)}) collective-permute-start(bf16[272,768]{1,0:T(8,128)(2,1)S(1)} %combine.1.refs_0_), channel_id=1, source_target_pairs={{0,6},{1,7},{2,4},{3,5},{4,2},{5,3},{6,0},{7,1},{8,14},{9,15},{10,... | collective-permute-start | bytes 1253384 | tf_op jit(solution)/shard_map/ppermute | solution.py:370
  144.9 1.8 %collective-permute-start.26 = (bf16[272,768]{1,0:T(8,128)(2,1)S(1)}, bf16[272,768]{1,0:T(8,128)(2,1)S(1)}, u32[]{:S(2)}, u32[]{:S(2)}) collective-permute-start(bf16[272,768]{1,0:T(8,128)(2,1)S(1)} %collective-permute-done.22.refs_0_), channel_id=1, source_target_pairs={{0,1},{1,0},{2,3},{3,2},{4,5},{5,4},{6,7},{7,6},{8,9},{9,8},{10,11... | collective-permute-start | bytes 1253384 | tf_op jit(solution)/shard_map/ppermute | solution.py:370
  144.9 2.4 %collective-permute-start.27 = (bf16[272,768]{1,0:T(8,128)(2,1)S(1)}, bf16[272,768]{1,0:T(8,128)(2,1)S(1)}, u32[]{:S(2)}, u32[]{:S(2)}) collective-permute-start(bf16[272,768]{1,0:T(8,128)(2,1)S(1)} %collective-permute-done.23.refs_1_), channel_id=1, source_target_pairs={{0,1},{1,0},{2,3},{3,2},{4,5},{5,4},{6,7},{7,6},{8,9},{9,8},{10,11... | collective-permute-start | bytes 1253384 | tf_op jit(solution)/shard_map/ppermute | solution.py:370
  145.4 2.4 %collective-permute-start.28 = (bf16[272,768]{1,0:T(8,128)(2,1)S(1)}, bf16[272,768]{1,0:T(8,128)(2,1)S(1)}, u32[]{:S(2)}, u32[]{:S(2)}) collective-permute-start(bf16[272,768]{1,0:T(8,128)(2,1)S(1)} %collective-permute-done.24.refs_2_), channel_id=1, source_target_pairs={{0,1},{1,0},{2,3},{3,2},{4,5},{5,4},{6,7},{7,6},{8,9},{9,8},{10,11... | collective-permute-start | bytes 1253384 | tf_op jit(solution)/shard_map/ppermute | solution.py:370

commit v6 on v5

--- a/solution.py
+++ b/solution.py
@@ -216,6 +216,7 @@
         sent = outs[:-2]
         mine, masses = outs[-2:]
         size, depth = mine.shape
+        upper = size // 2
         quarter = ids[1] // CORES
         sums = jnp.sum(mass[...].T, axis=0, keepdims=True)
         for number in range(n_owners):
@@ -231,9 +232,10 @@
 
                 @pl.when(quarter ^ number == away)
                 def _():
-                    target = sent[away - 1]
-                    target[:size, :] = block.astype(target.dtype)
-                    target[size:, :] = three_rows(own, target.dtype, depth)
+                    first_half, second_half = sent[2 * away - 2 : 2 * away]
+                    first_half[...] = block[:upper].astype(first_half.dtype)
+                    second_half[: size - upper, :] = block[upper:].astype(second_half.dtype)
+                    second_half[size - upper :, :] = three_rows(own, second_half.dtype, depth)
 
 
 def sum_rows(ids, plan, totals, scores, rows, n_owners, carried, last):
@@ -254,10 +256,12 @@
     if not first:
         in_specs += [fixed(shape) for shape in state]
     if last:
-        shapes = [((size + EXTRA, depth), jnp.bfloat16)] * (n_owners - 1) + [
-            ((size, depth), jnp.float32),
-            ((1, size), jnp.float32),
-        ]
+        shapes = []
+        for away in range(1, n_owners):
+            kept = [n_owners == 4 and keep == away for keep in (2, 1)]
+            for keep, height in zip(kept, (size // 2, size - size // 2 + EXTRA)):
+                shapes.append(((height, depth), jnp.float32 if keep else jnp.bfloat16))
+        shapes += [((size, depth), jnp.float32), ((1, size), jnp.float32)]
     else:
         shapes = [(shape, jnp.float32) for shape in state]
     return pl.pallas_call(
@@ -284,44 +288,76 @@
     )(ids, *totals, scores, rows, *(carried or ()))
 
 
+def pass_on_kernel(has_masses, size, mine, arrived, out):
+    depth = mine.shape[1]
+    height = mine.shape[0] - (EXTRA if has_masses else 0)
+    total = mine[:height, :] + arrived[:height, :].astype(jnp.float32)
+    out[:height, :] = total.astype(out.dtype)
+    if has_masses:
+        mass = one_row(mine[height:, :], size) + one_row(arrived[height:, :], size)
+        out[height:, :] = three_rows(mass, out.dtype, depth)
+
+
+def pass_on(mine, arrived, has_masses, size):
+    return pl.pallas_call(
+        functools.partial(pass_on_kernel, has_masses, size),
+        out_shape=jax.ShapeDtypeStruct(arrived.shape, arrived.dtype),
+        compiler_params=pltpu.CompilerParams(vmem_limit_bytes=VMEM_LIMIT),
+        name="pass_on",
+    )(mine, arrived)
+
+
 def combine_kernel(mine, masses, *refs):
-    arrived, out = refs[:-1], refs[-1]
+    first_out, second_out = refs[-2:]
     size, depth = mine.shape
-    total = mine[...]
+    upper = size // 2
+    first = mine[:upper, :]
+    second = mine[upper:, :]
     mass = masses[...]
-    for ref in arrived:
-        total = total + ref[:size, :].astype(jnp.float32)
-        mass = mass + one_row(ref[size:, :], size)
-    square = jnp.sum(total * total, axis=1, keepdims=True)
-    out[:size, :] = (total * lax.rsqrt(square + 1e-06)).astype(out.dtype)
-    out[size:, :] = three_rows(mass, out.dtype, depth)
+    for ref in refs[:-2]:
+        if ref.shape[0] == upper:
+            first = first + ref[...].astype(jnp.float32)
+        else:
+            second = second + ref[: size - upper, :].astype(jnp.float32)
+            mass = mass + one_row(ref[size - upper :, :], size)
+    for total, out in ((first, first_out), (second, second_out)):
+        square = jnp.sum(total * total, axis=1, keepdims=True)
+        out[: total.shape[0], :] = (total * lax.rsqrt(square + 1e-06)).astype(out.dtype)
+    second_out[size - upper :, :] = three_rows(mass, second_out.dtype, depth)
 
 
 def combine(mine, masses, arrived):
     size, depth = mine.shape
+    upper = size // 2
     return pl.pallas_call(
         combine_kernel,
-        out_shape=jax.ShapeDtypeStruct((size + EXTRA, depth), jnp.bfloat16),
+        out_shape=[
+            jax.ShapeDtypeStruct((upper, depth), jnp.bfloat16),
+            jax.ShapeDtypeStruct((size - upper + EXTRA, depth), jnp.bfloat16),
+        ],
         compiler_params=pltpu.CompilerParams(vmem_limit_bytes=VMEM_LIMIT),
         name="combine",
     )(mine, masses, *arrived)
 
 
 def assemble_kernel(factor, n_pieces, ids, *refs):
-    pieces = refs[:n_pieces]
     units, weights = refs[-2:]
     size = units.shape[0]
-    for number, piece in enumerate(pieces):
+    upper = size // 2
+    for number in range(n_pieces):
 
         @pl.when(pl.program_id(0) == number)
         def _():
-            units[...] = piece[:size, :].astype(jnp.float32)
-            weights[0] = one_row(piece[size:, :], size) * factor
+            first, second = refs[2 * number : 2 * number + 2]
+            units[:upper, :] = first[...].astype(jnp.float32)
+            units[upper:, :] = second[: size - upper, :].astype(jnp.float32)
+            weights[0] = one_row(second[size - upper :, :], size) * factor
 
 
 def assemble(ids, pieces, carried, n_blocks, factor):
-    size, depth = pieces[0][2].shape
-    size -= EXTRA
+    arrays = [array for _, _, halves in pieces for array in halves]
+    depth = arrays[0].shape[1]
+    size = arrays[0].shape[0] + arrays[1].shape[0] - EXTRA
     half = n_blocks // CORES
     flips = [flip for flip, _, _ in pieces]
     aways = [away for _, away, _ in pieces]
@@ -330,13 +366,13 @@
         return ((s[1] % CORES) ^ pick(t, flips)) * half + ((s[1] // CORES) ^ pick(t, aways))
 
     extra = carried or ()
-    aliases = {1 + len(pieces) + n: n for n in range(len(extra))}
+    aliases = {1 + len(arrays) + n: n for n in range(len(extra))}
     return pl.pallas_call(
         functools.partial(assemble_kernel, factor, len(pieces)),
         grid_spec=pltpu.PrefetchScalarGridSpec(
             num_scalar_prefetch=1,
             grid=(len(pieces),),
-            in_specs=[pl.BlockSpec((size + EXTRA, depth), lambda t, s: (0, 0)) for _ in pieces]
+            in_specs=[pl.BlockSpec(array.shape, lambda t, s: (0, 0)) for array in arrays]
             + [pl.BlockSpec(memory_space=pl.ANY) for _ in extra],
             out_specs=[
                 pl.BlockSpec((size, depth), lambda t, s: (block(t, s), 0)),
@@ -350,7 +386,7 @@
         input_output_aliases=aliases,
         compiler_params=pltpu.CompilerParams(vmem_limit_bytes=VMEM_LIMIT),
         name="assemble",
-    )(ids, *[payload for _, _, payload in pieces], *extra)
+    )(ids, *arrays, *extra)
 
 
 def local(embeddings, centroids, log_mix):
@@ -473,20 +509,46 @@
     else:
         rest, state = steps, None
     *sent, mine, masses = sum_rows(ids, rest, late, scores, rows, n_owners, state, True)
-    far = [CORES * away for away in range(1, n_owners)]
-    arrived = [exchange(array, distance) for array, distance in zip(sent, far)]
+    size = mine.shape[0]
+    one, two = CORES, 2 * CORES
+    if n_owners == 4:
+        across, along, corner = sent[0:2], sent[2:4], sent[4:6]
+        passing = exchange(corner[0], one), exchange(corner[1], two)
+        arrived = [exchange(across[0], one), exchange(along[1], two)]
+        arrived.append(exchange(pass_on(along[0], passing[0], False, size), two))
+        arrived.append(exchange(pass_on(across[1], passing[1], True, size), one))
+    else:
+        arrived = [
+            exchange(array, CORES * (1 + number // 2)) for number, array in enumerate(sent)
+        ]
     payload = combine(mine, masses, arrived)
 
     count = local_centroids * n_places
     factor = count / (held * n_rows * n_places)
-    pieces = [exchange(payload, distance) for distance in far]
-    done = assemble(
-        ids, [(0, 0, payload), (1, 0, exchange(payload, 1))], None, n_rows, factor
-    )
-    pieces, done = lax.optimization_barrier((pieces, done))
-    placed = [(0, away + 1, piece) for away, piece in enumerate(pieces)]
-    placed += [(1, away + 1, exchange(piece, 1)) for away, piece in enumerate(pieces)]
-    result, weights = assemble(ids, placed, done, n_rows, factor)
+    if n_owners == 4:
+        first = exchange(payload[0], one), exchange(payload[1], two)
+        second = exchange(payload[1], one), exchange(payload[0], two)
+        third = exchange(first[0], two), exchange(first[1], one)
+        far = [(1, (first[0], second[0])), (2, (second[1], first[1])), (3, third)]
+    else:
+        far = [
+            (away, tuple(exchange(array, CORES * away) for array in payload))
+            for away in range(1, n_owners)
+        ]
+    swap = lambda halves: tuple(exchange(array, 1) for array in halves)
+    done = assemble(ids, [(0, 0, payload), (1, 0, swap(payload))], None, n_rows, factor)
+    swapped = [swap(halves) for _, halves in far[:-1]]
+    arrays, swapped, done = lax.optimization_barrier(
+        ([halves for _, halves in far], swapped, done)
+    )
+    swapped.append(swap(arrays[-1]))
+    placed = [(0, away, halves) for (away, _), halves in zip(far, arrays)]
+    placed += [(1, away, halves) for (away, _), halves in zip(far, swapped)]
+    last = [piece for piece in placed if piece[1] == n_owners - 1]
+    early = [piece for piece in placed if piece[1] != n_owners - 1]
+    done = assemble(ids, early, done, n_rows, factor)
+    done = assemble(ids, last, done, n_rows, factor)
+    result, weights = done
     return (result, weights.reshape(local_centroids))
 
 

time: 152 us -> 144 us (0.947)
  waiting for transfers between devices: 65.7 us -> 49.4 us
  starting transfers between devices: 31.8 us -> 39.2 us
    ppermute x12 -> x22, waiting for transfers between devices: 38.7 us -> 22.4 us  [exchange(): lax.ppermute(array, 'rows', [(i, i ^ distance) for i in range(n_rows)])]
    ppermute x12 -> x22, starting transfers between devices: 8.82 us -> 16.3 us  [exchange(): lax.ppermute(array, 'rows', [(i, i ^ distance) for i in range(n_rows)])]
    pallas_call x2 -> x3, Pallas kernels: 5.56 us -> 6.41 us  [assemble(): pl.pallas_call(functools.partial(assemble_kernel, factor, len(pieces)), g...]
  transfers between devices with their start and end apart: 29 -> 39, of which waited for: 13 -> 12; matrix products, arithmetic and copies ran while one was open for 3% -> 3% of each run, Pallas kernels for 21% -> 24%
where the time goes in v6:
time: 144 us
  waiting for transfers between devices  49.4 us (34%)
  Pallas kernels  48.5 us (34%)
  starting transfers between devices  39.2 us (27%)
  other arithmetic  4.32 us (3%)
    pallas_call x8, Pallas kernels, score_block(): pl.pallas_call(functools.partial(score_kernel, n_sources, choice), grid_s...  25.6 us
    ppermute x22, waiting for transfers between devices, exchange(): lax.ppermute(array, 'rows', [(i, i ^ distance) for i in range(n_rows)])  22.4 us
    ppermute x5, waiting for transfers between devices, start_ready(): lax.ppermute(slots[source_slot][hold][0], 'blk', pairs)  20.7 us
    ppermute x22, starting transfers between devices, exchange(): lax.ppermute(array, 'rows', [(i, i ^ distance) for i in range(n_rows)])  16.3 us
    pallas_call x2, Pallas kernels, sum_rows(): pl.pallas_call(functools.partial(sum_kernel, plan, len(totals), n_owners,...  16.1 us
    ppermute x6, starting transfers between devices, totals_of(): lax.ppermute(both, 'blk', [(i, (i + turn) % n_places) for i in range(n_pl...  10.5 us
    ppermute x5, starting transfers between devices, start_ready(): lax.ppermute(slots[source_slot][hold][0], 'blk', pairs)  6.64 us
    pallas_call x3, Pallas kernels, assemble(): pl.pallas_call(functools.partial(assemble_kernel, factor, len(pieces)), g...  6.41 us
  transfers between devices with their start and end apart: 39, of which 12 were waited for; matrix products, arithmetic and copies ran while one was open for 3% of the time, Pallas kernels for 24%

profile of v6, /device:TPU:0, one launch (start us, length us, event | category | flops | bytes accessed | tf_op | source)
XLA Modules:
  0.0 143.7 jit_solution(5951385518493295309)
XLA Ops:
  1.1 2.7 %collective-permute-start = (bf16[512,768]{1,0:T(8,128)(2,1)}, bf16[512,768]{1,0:T(8,128)(2,1)S(1)}, u32[]{:S(2)}, u32[]{:S(2)}) collective-permute-start(bf16[512,768]{1,0:T(8,128)(2,1)} %refs_0_.1), channel_id=1, source_target_pairs={{8,0},{0,8},{24,16},{16,24},{9,1},{1,9},{25,17},{17,25},{10,2},{2,... | collective-permute-start | bytes 2359304 | tf_op jit(solution)/shard_map/ppermute | solution.py:430
  4.6 1.8 %fusion = f32[1024]{0:T(1024)S(1)} fusion(bf16[2048,768]{1,0:T(8,128)(2,1)} %param.4, s32[]{:T(128)S(6)} %select_n.4), kind=kLoop, calls=%fused_computation.2 | loop fusion | flops 2358272 | bytes 1576964 | tf_op jit(solution)/shard_map/reduce_sum | solution.py:21
  7.1 1.7 %fusion.1.refs_1_.refs_2_ = bf16[1024,768]{1,0:T(8,128)(2,1)S(1)} fusion(f32[1024]{0:T(1024)S(1)} %add_rsqrt_fusion, bf16[2048,768]{1,0:T(8,128)(2,1)} %param.4, s32[]{:T(128)S(6)} %select_n.4), kind=kLoop, calls=%fused_computation.3 | loop fusion | flops 2359296 | bytes 3149828 | tf_op jit(solution)/shard_map/convert_element_type | solution.py:21
  10.1 3.3 %scores.8 = (f32[1024,4096]{1,0:T(8,128)}, bf16[4096,768]{1,0:T(8,128)(2,1)}, f32[8,1,512]{2,1,0:T(1,128)S(1)}) custom-call(s32[2]{0:T(128)S(1)} %pad_add_fusion.ids, bf16[512,768]{1,0:T(8,128)(2,1)S(1)} %copy-done, bf16[1024,768]{1,0:T(8,128)(2,1)S(1)} %fusion.1.refs_1_.refs_2_, f32[1024,128]{1,0:T(8,128)S(1)} %broadcast_in_dim.2.refs_2_.refs_3_), custom_call_target="tpu_custom_call" | custom-call | flops 805306368 | bytes 7340032 | tf_op jit(solution)/shard_map/scores/pallas_call | solution.py:105
  13.5 3.2 %scores.9 = (f32[1024,4096]{1,0:T(8,128)}, bf16[4096,768]{1,0:T(8,128)(2,1)}, f32[8,1,512]{2,1,0:T(1,128)S(1)}) custom-call(s32[2]{0:T(128)S(1)} %pad_add_fusion.ids, bf16[512,768]{1,0:T(8,128)(2,1)S(1)} %collective-permute-done.2.refs_0_, bf16[1024,768]{1,0:T(8,128)(2,1)S(1)} %fusion.1.refs_1_.refs_2_, ...), custom_call_target="tpu_custom_call", output_to_operand_aliasing={{0}: (4, {}), {1}: (5, {}), {2}: (6, {})} | custom-call | flops 805306368 | bytes 7340032 | tf_op jit(solution)/shard_map/scores/pallas_call | solution.py:105
  16.6 5.5 %collective-permute-done.refs_0_ = bf16[512,768]{1,0:T(8,128)(2,1)S(1)} collective-permute-done((bf16[512,768]{1,0:T(8,128)(2,1)}, bf16[512,768]{1,0:T(8,128)(2,1)S(1)}, u32[]{:S(2)}, u32[]{:S(2)}) %collective-permute-start) | collective-permute-done | bytes 786464 | tf_op jit(solution)/shard_map/ppermute | solution.py:430
  24.9 3.2 %scores.10 = (f32[1024,4096]{1,0:T(8,128)}, bf16[4096,768]{1,0:T(8,128)(2,1)}, f32[8,1,512]{2,1,0:T(1,128)S(1)}) custom-call(s32[2]{0:T(128)S(1)} %pad_add_fusion.ids, bf16[512,768]{1,0:T(8,128)(2,1)S(1)} %collective-permute-done.refs_0_, bf16[1024,768]{1,0:T(8,128)(2,1)S(1)} %fusion.1.refs_1_.refs_2_, ...), custom_call_target="tpu_custom_call", output_to_operand_aliasing={{0}: (4, {}), {1}: (5, {}), {2}: (6, {})} | custom-call | flops 805306368 | bytes 7340032 | tf_op jit(solution)/shard_map/scores/pallas_call | solution.py:105
  28.1 3.2 %scores.11 = (f32[1024,4096]{1,0:T(8,128)}, bf16[4096,768]{1,0:T(8,128)(2,1)}, f32[8,1,512]{2,1,0:T(1,128)S(1)}) custom-call(s32[2]{0:T(128)S(1)} %pad_add_fusion.ids, bf16[512,768]{1,0:T(8,128)(2,1)S(1)} %collective-permute-done.5.refs_0_, bf16[1024,768]{1,0:T(8,128)(2,1)S(1)} %fusion.1.refs_1_.refs_2_, ...), custom_call_target="tpu_custom_call", output_to_operand_aliasing={{0}: (4, {}), {1}: (5, {}), {2}: (6, {})} | custom-call | flops 805306368 | bytes 7340032 | tf_op jit(solution)/shard_map/scores/pallas_call | solution.py:105
  31.3 15.1 %collective-permute-done.3.refs_1_ = bf16[512,768]{1,0:T(8,128)(2,1)S(1)} collective-permute-done((bf16[512,768]{1,0:T(8,128)(2,1)S(1)}, bf16[512,768]{1,0:T(8,128)(2,1)S(1)}, u32[]{:S(2)}, u32[]{:S(2)}) %collective-permute-start.3) | collective-permute-done | bytes 786464 | tf_op jit(solution)/shard_map/ppermute | solution.py:430
  46.4 1.9 %collective-permute-start.9 = (bf16[512,768]{1,0:T(8,128)(2,1)S(1)}, bf16[512,768]{1,0:T(8,128)(2,1)S(1)}, u32[]{:S(2)}, u32[]{:S(2)}) collective-permute-start(bf16[512,768]{1,0:T(8,128)(2,1)S(1)} %collective-permute-done.3.refs_1_), channel_id=1, source_target_pairs={{0,1},{1,0},{2,3},{3,2},{4,5},{5,4},{6,7},{7,6},{24,25},{25,24},{2... | collective-permute-start | bytes 2359304 | tf_op jit(solution)/shard_map/ppermute | solution.py:412
  49.6 3.2 %scores.12 = (f32[1024,4096]{1,0:T(8,128)}, bf16[4096,768]{1,0:T(8,128)(2,1)}, f32[8,1,512]{2,1,0:T(1,128)S(1)}) custom-call(s32[2]{0:T(128)S(1)} %pad_add_fusion.ids, bf16[512,768]{1,0:T(8,128)(2,1)S(1)} %collective-permute-done.1.refs_0_, ...), custom_call_target="tpu_custom_call", output_to_operand_aliasing={{0}: (5, {}), {1}: (6, {}), {2}: (7, {})} | custom-call | flops 805306368 | bytes 7340032 | tf_op jit(solution)/shard_map/scores/pallas_call | solution.py:105
  52.9 3.2 %scores.13 = (f32[1024,4096]{1,0:T(8,128)}, bf16[4096,768]{1,0:T(8,128)(2,1)}, f32[8,1,512]{2,1,0:T(1,128)S(1)}) custom-call(s32[2]{0:T(128)S(1)} %pad_add_fusion.ids, bf16[512,768]{1,0:T(8,128)(2,1)S(1)} %collective-permute-done.8.refs_0_, ...), custom_call_target="tpu_custom_call", output_to_operand_aliasing={{0}: (5, {}), {1}: (6, {}), {2}: (7, {})} | custom-call | flops 805306368 | bytes 7340032 | tf_op jit(solution)/shard_map/scores/pallas_call | solution.py:105
  57.5 2.6 %collective-permute-start.11 = (f32[8,1,512]{2,1,0:T(1,128)S(1)}, f32[8,1,512]{2,1,0:T(1,128)S(1)}, u32[]{:S(2)}, u32[]{:S(2)}) collective-permute-start(f32[8,1,512]{2,1,0:T(1,128)S(1)} %add.25.refs_0_), channel_id=1, source_target_pairs={{0,8},{8,16},{16,24},{24,0},{1,9},{9,17},{17,25},{25,1},{2,10},{10... | collective-permute-start | bytes 49160 | tf_op jit(solution)/shard_map/ppermute | solution.py:478
  61.3 2.8 %collective-permute-start.13 = (f32[8,1,512]{2,1,0:T(1,128)S(1)}, f32[8,1,512]{2,1,0:T(1,128)S(1)}, u32[]{:S(2)}, u32[]{:S(2)}) collective-permute-start(f32[8,1,512]{2,1,0:T(1,128)S(1)} %add.25.refs_0_), channel_id=1, source_target_pairs={{0,24},{8,0},{16,8},{24,16},{1,25},{9,1},{17,9},{25,17},{2,26},{10... | collective-permute-start | bytes 49160 | tf_op jit(solution)/shard_map/ppermute | solution.py:478
  64.9 6.3 %collective-permute-done.13.refs_3_ = f32[8,1,512]{2,1,0:T(1,128)S(1)} collective-permute-done((f32[8,1,512]{2,1,0:T(1,128)S(1)}, f32[8,1,512]{2,1,0:T(1,128)S(1)}, u32[]{:S(2)}, u32[]{:S(2)}) %collective-permute-start.13) | collective-permute-done | bytes 16416 | tf_op jit(solution)/shard_map/ppermute | solution.py:478
  71.2 1.9 %collective-permute-start.14 = (bf16[512,768]{1,0:T(8,128)(2,1)S(1)}, bf16[512,768]{1,0:T(8,128)(2,1)S(1)}, u32[]{:S(2)}, u32[]{:S(2)}) collective-permute-start(bf16[512,768]{1,0:T(8,128)(2,1)S(1)} %collective-permute-done.7.refs_1_), channel_id=1, source_target_pairs={{0,1},{1,0},{2,3},{3,2},{4,5},{5,4},{6,7},{7,6},{24,25},{25,24},{2... | collective-permute-start | bytes 2359304 | tf_op jit(solution)/shard_map/ppermute | solution.py:412
  73.1 3.2 %scores.14 = (f32[1024,4096]{1,0:T(8,128)}, bf16[4096,768]{1,0:T(8,128)(2,1)}, f32[8,1,512]{2,1,0:T(1,128)S(1)}) custom-call(s32[2]{0:T(128)S(1)} %pad_add_fusion.ids, bf16[512,768]{1,0:T(8,128)(2,1)S(1)} %collective-permute-done.4.refs_0_, ...), custom_call_target="tpu_custom_call", output_to_operand_aliasing={{0}: (5, {}), {1}: (6, {}), {2}: (7, {})} | custom-call | flops 805306368 | bytes 7340032 | tf_op jit(solution)/shard_map/scores/pallas_call | solution.py:105
  76.4 3.2 %scores.15 = (f32[1024,4096]{1,0:T(8,128)}, bf16[4096,768]{1,0:T(8,128)(2,1)}, f32[8,1,512]{2,1,0:T(1,128)S(1)}) custom-call(s32[2]{0:T(128)S(1)} %pad_add_fusion.ids, bf16[512,768]{1,0:T(8,128)(2,1)S(1)} %collective-permute-done.6.refs_0_, ...), custom_call_target="tpu_custom_call", output_to_operand_aliasing={{0}: (5, {}), {1}: (6, {}), {2}: (7, {})} | custom-call | flops 805306368 | bytes 7340032 | tf_op jit(solution)/shard_map/scores/pallas_call | solution.py:105
  81.0 3.2 %collective-permute-start.17 = (f32[8,1,512]{2,1,0:T(1,128)S(1)}, f32[8,1,512]{2,1,0:T(1,128)S(1)}, u32[]{:S(2)}, u32[]{:S(2)}) collective-permute-start(f32[8,1,512]{2,1,0:T(1,128)S(1)} %add.26.refs_0_), channel_id=1, source_target_pairs={{0,16},{8,24},{16,0},{24,8},{1,17},{9,25},{17,1},{25,9},{2,18},{10... | collective-permute-start | bytes 49160 | tf_op jit(solution)/shard_map/ppermute | solution.py:478
  84.8 7.9 %sums.2 = (f32[1024,768]{1,0:T(8,128)S(1)}, f32[1024,128]{1,0:T(8,128)S(1)}) custom-call(s32[2]{0:T(128)S(1)} %pad_add_fusion.ids, f32[8,1,512]{2,1,0:T(1,128)S(1)} %add.25.refs_0_, f32[8,1,512]{2,1,0:T(1,128)S(1)} %collective-permute-done.11.refs_1_, f32[8,1,512]{2,1,0:T(1,128)S(1)} %collective-permute-done.12.refs_2_, ...), custom_call_target="tpu_custom_call" | custom-call | flops 3221225472 | bytes 14680064 | tf_op jit(solution)/shard_map/sums/pallas_call | solution.py:267
  92.8 8.2 %sums.3 = (bf16[128,768]{1,0:T(8,128)(2,1)S(1)}, f32[144,768]{1,0:T(8,128)S(1)}, f32[128,768]{1,0:T(8,128)S(1)}, bf16[144,768]{1,0:T(8,128)(2,1)S(1)}, bf16[128,...) custom-call(s32[2]{0:T(128)S(1)} %pad_add_fusion.ids, ...), custom_call_target="tpu_custom_call" | custom-call | flops 3221225472 | bytes 14680064 | tf_op jit(solution)/shard_map/sums/pallas_call | solution.py:267
  101.0 1.6 %collective-permute-start.23 = (bf16[144,768]{1,0:T(8,128)(2,1)S(1)}, bf16[144,768]{1,0:T(8,128)(2,1)S(1)}, u32[]{:S(2)}, u32[]{:S(2)}) collective-permute-start(bf16[144,768]{1,0:T(8,128)(2,1)S(1)} %get-tuple-element.143), channel_id=1, source_target_pairs={{0,4},{1,5},{2,6},{3,7},{4,0},{5,1},{6,2},{7,3},{8,12},{9,13},{10,... | collective-permute-start | bytes 663560 | tf_op jit(solution)/shard_map/ppermute | solution.py:406
  104.6 4.8 %collective-permute-done.23.arrived = bf16[144,768]{1,0:T(8,128)(2,1)S(1)} collective-permute-done((bf16[144,768]{1,0:T(8,128)(2,1)S(1)}, bf16[144,768]{1,0:T(8,128)(2,1)S(1)}, u32[]{:S(2)}, u32[]{:S(2)}) %collective-permute-start.23) | collective-permute-done | bytes 221216 | tf_op jit(solution)/shard_map/ppermute | solution.py:406
  111.6 1.6 %collective-permute-start.22 = (bf16[128,768]{1,0:T(8,128)(2,1)S(1)}, bf16[128,768]{1,0:T(8,128)(2,1)S(1)}, u32[]{:S(2)}, u32[]{:S(2)}) collective-permute-start(bf16[128,768]{1,0:T(8,128)(2,1)S(1)} %pass_on.2), channel_id=1, source_target_pairs={{0,4},{1,5},{2,6},{3,7},{4,0},{5,1},{6,2},{7,3},{8,12},{9,13},{10,... | collective-permute-start | bytes 589832 | tf_op jit(solution)/shard_map/ppermute | solution.py:406
  113.2 5.6 %collective-permute-done.19.refs_0_ = bf16[128,768]{1,0:T(8,128)(2,1)S(1)} collective-permute-done((bf16[128,768]{1,0:T(8,128)(2,1)S(1)}, bf16[128,768]{1,0:T(8,128)(2,1)S(1)}, u32[]{:S(2)}, u32[]{:S(2)}) %collective-permute-start.19) | collective-permute-done | bytes 196640 | tf_op jit(solution)/shard_map/ppermute | solution.py:406
  119.1 1.6 %collective-permute-start.25 = (bf16[128,768]{1,0:T(8,128)(2,1)S(1)}, bf16[128,768]{1,0:T(8,128)(2,1)S(1)}, u32[]{:S(2)}, u32[]{:S(2)}) collective-permute-start(bf16[128,768]{1,0:T(8,128)(2,1)S(1)} %get-tuple-element.144.refs_0_), channel_id=1, source_target_pairs={{0,2},{1,3},{2,0},{3,1},{4,6},{5,7},{6,4},{7,5},{8,10},{9,11},{10,... | collective-permute-start | bytes 589832 | tf_op jit(solution)/shard_map/ppermute | solution.py:406
  123.2 3.6 %collective-permute-done.25.refs_0_ = bf16[128,768]{1,0:T(8,128)(2,1)S(1)} collective-permute-done((bf16[128,768]{1,0:T(8,128)(2,1)S(1)}, bf16[128,768]{1,0:T(8,128)(2,1)S(1)}, u32[]{:S(2)}, u32[]{:S(2)}) %collective-permute-start.25) | collective-permute-done | bytes 196640 | tf_op jit(solution)/shard_map/ppermute | solution.py:406
  129.9 1.7 %collective-permute-done.26.refs_1_ = bf16[144,768]{1,0:T(8,128)(2,1)S(1)} collective-permute-done((bf16[144,768]{1,0:T(8,128)(2,1)S(1)}, bf16[144,768]{1,0:T(8,128)(2,1)S(1)}, u32[]{:S(2)}, u32[]{:S(2)}) %collective-permute-start.26) | collective-permute-done | bytes 221216 | tf_op jit(solution)/shard_map/ppermute | solution.py:406
  133.7 2.9 %collective-permute-done.29.refs_0_ = bf16[128,768]{1,0:T(8,128)(2,1)S(1)} collective-permute-done((bf16[128,768]{1,0:T(8,128)(2,1)S(1)}, bf16[128,768]{1,0:T(8,128)(2,1)S(1)}, u32[]{:S(2)}, u32[]{:S(2)}) %collective-permute-start.29) | collective-permute-done | bytes 196640 | tf_op jit(solution)/shard_map/ppermute | solution.py:406
  136.6 1.8 %assemble.3 = (f32[2048,768]{1,0:T(8,128)}, f32[8,1,256]{2,1,0:T(1,128)}) custom-call(s32[2]{0:T(128)S(1)} %pad_add_fusion.ids, bf16[128,768]{1,0:T(8,128)(2,1)S(1)} %get-tuple-element.144.refs_0_, bf16[144,768]{1,0:T(8,128)(2,1)S(1)} %get-tuple-element.145.refs_1_, bf16[128,768]{1,0:T(8,128)(2,1)S(1)} %collective-permute-done.35.refs_2_, ...), custom_call_target="tpu_custom_call" | custom-call | tf_op jit(solution)/shard_map/assemble/pallas_call | solution.py:370
  139.1 2.8 %assemble.4 = (f32[2048,768]{1,0:T(8,128)}, f32[8,1,256]{2,1,0:T(1,128)}) custom-call(s32[2]{0:T(128)S(1)} %pad_add_fusion.ids, bf16[128,768]{1,0:T(8,128)(2,1)S(1)} %collective-permute-done.25.refs_0_, bf16[144,768]{1,0:T(8,128)(2,1)S(1)} %collective-permute-done.26.refs_1_, ...), custom_call_target="tpu_custom_call", output_to_operand_aliasing={{0}: (9, {}), {1}: (10, {})} | custom-call | tf_op jit(solution)/shard_map/assemble/pallas_call | solution.py:370
  141.9 1.8 %assemble.5 = (f32[2048,768]{1,0:T(8,128)}, f32[8,1,256]{2,1,0:T(1,128)}) custom-call(s32[2]{0:T(128)S(1)} %pad_add_fusion.ids, bf16[128,768]{1,0:T(8,128)(2,1)S(1)} %collective-permute-done.29.refs_0_, bf16[144,768]{1,0:T(8,128)(2,1)S(1)} %collective-permute-done.30.refs_1_, ...), custom_call_target="tpu_custom_call", output_to_operand_aliasing={{0}: (5, {}), {1}: (6, {})} | custom-call | tf_op jit(solution)/shard_map/assemble/pallas_call | solution.py:370
  (72 shorter events, 25.6 us)
Async XLA Ops:
  0.6 12.8 %collective-permute-start.2 = (bf16[512,768]{1,0:T(8,128)(2,1)}, bf16[512,768]{1,0:T(8,128)(2,1)S(1)}, u32[]{:S(2)}, u32[]{:S(2)}) collective-permute-start(bf16[512,768]{1,0:T(8,128)(2,1)} %refs_0_.1), channel_id=1, source_target_pairs={{0,1},{1,0},{2,3},{3,2},{4,5},{5,4},{6,7},{7,6},{8,9},{9,8},{10,11... | collective-permute-start | bytes 2359304 | tf_op jit(solution)/shard_map/ppermute | solution.py:412
  1.1 21.0 %collective-permute-start = (bf16[512,768]{1,0:T(8,128)(2,1)}, bf16[512,768]{1,0:T(8,128)(2,1)S(1)}, u32[]{:S(2)}, u32[]{:S(2)}) collective-permute-start(bf16[512,768]{1,0:T(8,128)(2,1)} %refs_0_.1), channel_id=1, source_target_pairs={{8,0},{0,8},{24,16},{16,24},{9,1},{1,9},{25,17},{17,25},{10,2},{2,... | collective-permute-start | bytes 2359304 | tf_op jit(solution)/shard_map/ppermute | solution.py:430
  3.8 18.3 %collective-permute-start.1 = (bf16[512,768]{1,0:T(8,128)(2,1)}, bf16[512,768]{1,0:T(8,128)(2,1)S(1)}, u32[]{:S(2)}, u32[]{:S(2)}) collective-permute-start(bf16[512,768]{1,0:T(8,128)(2,1)} %refs_0_.1), channel_id=1, source_target_pairs={{16,8},{8,16},{17,9},{9,17},{18,10},{10,18},{19,11},{11,19},{20,12... | collective-permute-start | bytes 2359304 | tf_op jit(solution)/shard_map/ppermute | solution.py:430
  22.1 5.9 %collective-permute-start.5 = (bf16[512,768]{1,0:T(8,128)(2,1)S(1)}, bf16[512,768]{1,0:T(8,128)(2,1)S(1)}, u32[]{:S(2)}, u32[]{:S(2)}) collective-permute-start(bf16[512,768]{1,0:T(8,128)(2,1)S(1)} %collective-permute-done.refs_0_), channel_id=1, source_target_pairs={{0,1},{1,0},{2,3},{3,2},{4,5},{5,4},{6,7},{7,6},{8,9},{9,8},{10,11... | collective-permute-start | bytes 2359304 | tf_op jit(solution)/shard_map/ppermute | solution.py:412
  22.1 24.3 %collective-permute-start.3 = (bf16[512,768]{1,0:T(8,128)(2,1)S(1)}, bf16[512,768]{1,0:T(8,128)(2,1)S(1)}, u32[]{:S(2)}, u32[]{:S(2)}) collective-permute-start(bf16[512,768]{1,0:T(8,128)(2,1)S(1)} %collective-permute-done.1.refs_0_), channel_id=1, source_target_pairs={{8,0},{16,24},{9,1},{17,25},{10,2},{18,26},{11,3},{19,27},{12,4},{... | collective-permute-start | bytes 2359304 | tf_op jit(solution)/shard_map/ppermute | solution.py:430
  23.4 23.0 %collective-permute-start.4 = (bf16[512,768]{1,0:T(8,128)(2,1)S(1)}, bf16[512,768]{1,0:T(8,128)(2,1)S(1)}, u32[]{:S(2)}, u32[]{:S(2)}) collective-permute-start(bf16[512,768]{1,0:T(8,128)(2,1)S(1)} %collective-permute-done.refs_0_), channel_id=1, source_target_pairs={{16,8},{8,16},{17,9},{9,17},{18,10},{10,18},{19,11},{11,19},{20,12... | collective-permute-start | bytes 2359304 | tf_op jit(solution)/shard_map/ppermute | solution.py:430
  24.2 28.7 %collective-permute-start.8 = (bf16[512,768]{1,0:T(8,128)(2,1)S(1)}, bf16[512,768]{1,0:T(8,128)(2,1)S(1)}, u32[]{:S(2)}, u32[]{:S(2)}) collective-permute-start(bf16[512,768]{1,0:T(8,128)(2,1)S(1)} %collective-permute-done.1.refs_0_), channel_id=1, source_target_pairs={{8,9},{9,8},{10,11},{11,10},{12,13},{13,12},{14,15},{15,14},{16,17... | collective-permute-start | bytes 2359304 | tf_op jit(solution)/shard_map/ppermute | solution.py:412
  46.4 6.5 %collective-permute-start.9 = (bf16[512,768]{1,0:T(8,128)(2,1)S(1)}, bf16[512,768]{1,0:T(8,128)(2,1)S(1)}, u32[]{:S(2)}, u32[]{:S(2)}) collective-permute-start(bf16[512,768]{1,0:T(8,128)(2,1)S(1)} %collective-permute-done.3.refs_1_), channel_id=1, source_target_pairs={{0,1},{1,0},{2,3},{3,2},{4,5},{5,4},{6,7},{7,6},{24,25},{25,24},{2... | collective-permute-start | bytes 2359304 | tf_op jit(solution)/shard_map/ppermute | solution.py:412
  48.3 22.9 %collective-permute-start.7 = (bf16[512,768]{1,0:T(8,128)(2,1)S(1)}, bf16[512,768]{1,0:T(8,128)(2,1)S(1)}, u32[]{:S(2)}, u32[]{:S(2)}) collective-permute-start(bf16[512,768]{1,0:T(8,128)(2,1)S(1)} %collective-permute-done.4.refs_0_), channel_id=1, source_target_pairs={{8,0},{16,24},{9,1},{17,25},{10,2},{18,26},{11,3},{19,27},{12,4},{... | collective-permute-start | bytes 2359304 | tf_op jit(solution)/shard_map/ppermute | solution.py:430
  57.5 7.4 %collective-permute-start.11 = (f32[8,1,512]{2,1,0:T(1,128)S(1)}, f32[8,1,512]{2,1,0:T(1,128)S(1)}, u32[]{:S(2)}, u32[]{:S(2)}) collective-permute-start(f32[8,1,512]{2,1,0:T(1,128)S(1)} %add.25.refs_0_), channel_id=1, source_target_pairs={{0,8},{8,16},{16,24},{24,0},{1,9},{9,17},{17,25},{25,1},{2,10},{10... | collective-permute-start | bytes 49160 | tf_op jit(solution)/shard_map/ppermute | solution.py:478
  61.3 9.9 %collective-permute-start.13 = (f32[8,1,512]{2,1,0:T(1,128)S(1)}, f32[8,1,512]{2,1,0:T(1,128)S(1)}, u32[]{:S(2)}, u32[]{:S(2)}) collective-permute-start(f32[8,1,512]{2,1,0:T(1,128)S(1)} %add.25.refs_0_), channel_id=1, source_target_pairs={{0,24},{8,0},{16,8},{24,16},{1,25},{9,1},{17,9},{25,17},{2,26},{10... | collective-permute-start | bytes 49160 | tf_op jit(solution)/shard_map/ppermute | solution.py:478
  64.2 12.2 %collective-permute-start.6 = (bf16[512,768]{1,0:T(8,128)(2,1)S(1)}, bf16[512,768]{1,0:T(8,128)(2,1)S(1)}, u32[]{:S(2)}, u32[]{:S(2)}) collective-permute-start(bf16[512,768]{1,0:T(8,128)(2,1)S(1)} %collective-permute-done.4.refs_0_), channel_id=1, source_target_pairs={{8,9},{9,8},{10,11},{11,10},{12,13},{13,12},{14,15},{15,14},{16,17... | collective-permute-start | bytes 2359304 | tf_op jit(solution)/shard_map/ppermute | solution.py:412
  71.2 5.1 %collective-permute-start.14 = (bf16[512,768]{1,0:T(8,128)(2,1)S(1)}, bf16[512,768]{1,0:T(8,128)(2,1)S(1)}, u32[]{:S(2)}, u32[]{:S(2)}) collective-permute-start(bf16[512,768]{1,0:T(8,128)(2,1)S(1)} %collective-permute-done.7.refs_1_), channel_id=1, source_target_pairs={{0,1},{1,0},{2,3},{3,2},{4,5},{5,4},{6,7},{7,6},{24,25},{25,24},{2... | collective-permute-start | bytes 2359304 | tf_op jit(solution)/shard_map/ppermute | solution.py:412
  81.0 11.8 %collective-permute-start.16 = (f32[8,1,512]{2,1,0:T(1,128)S(1)}, f32[8,1,512]{2,1,0:T(1,128)S(1)}, u32[]{:S(2)}, u32[]{:S(2)}) collective-permute-start(f32[8,1,512]{2,1,0:T(1,128)S(1)} %add.26.refs_0_), channel_id=1, source_target_pairs={{0,8},{8,16},{16,24},{24,0},{1,9},{9,17},{17,25},{25,1},{2,10},{10... | collective-permute-start | bytes 49160 | tf_op jit(solution)/shard_map/ppermute | solution.py:478
  81.0 11.7 %collective-permute-start.17 = (f32[8,1,512]{2,1,0:T(1,128)S(1)}, f32[8,1,512]{2,1,0:T(1,128)S(1)}, u32[]{:S(2)}, u32[]{:S(2)}) collective-permute-start(f32[8,1,512]{2,1,0:T(1,128)S(1)} %add.26.refs_0_), channel_id=1, source_target_pairs={{0,16},{8,24},{16,0},{24,8},{1,17},{9,25},{17,1},{25,9},{2,18},{10... | collective-permute-start | bytes 49160 | tf_op jit(solution)/shard_map/ppermute | solution.py:478
  84.2 8.5 %collective-permute-start.18 = (f32[8,1,512]{2,1,0:T(1,128)S(1)}, f32[8,1,512]{2,1,0:T(1,128)S(1)}, u32[]{:S(2)}, u32[]{:S(2)}) collective-permute-start(f32[8,1,512]{2,1,0:T(1,128)S(1)} %add.26.refs_0_), channel_id=1, source_target_pairs={{0,24},{8,0},{16,8},{24,16},{1,25},{9,1},{17,9},{25,17},{2,26},{10... | collective-permute-start | bytes 49160 | tf_op jit(solution)/shard_map/ppermute | solution.py:478
  101.0 8.4 %collective-permute-start.23 = (bf16[144,768]{1,0:T(8,128)(2,1)S(1)}, bf16[144,768]{1,0:T(8,128)(2,1)S(1)}, u32[]{:S(2)}, u32[]{:S(2)}) collective-permute-start(bf16[144,768]{1,0:T(8,128)(2,1)S(1)} %get-tuple-element.143), channel_id=1, source_target_pairs={{0,4},{1,5},{2,6},{3,7},{4,0},{5,1},{6,2},{7,3},{8,12},{9,13},{10,... | collective-permute-start | bytes 663560 | tf_op jit(solution)/shard_map/ppermute | solution.py:406
  102.6 8.9 %collective-permute-start.21 = (bf16[128,768]{1,0:T(8,128)(2,1)S(1)}, bf16[128,768]{1,0:T(8,128)(2,1)S(1)}, u32[]{:S(2)}, u32[]{:S(2)}) collective-permute-start(bf16[128,768]{1,0:T(8,128)(2,1)S(1)} %get-tuple-element.141), channel_id=1, source_target_pairs={{0,2},{1,3},{2,0},{3,1},{4,6},{5,7},{6,4},{7,5},{8,10},{9,11},{10,... | collective-permute-start | bytes 589832 | tf_op jit(solution)/shard_map/ppermute | solution.py:406
  104.1 14.7 %collective-permute-start.20 = (bf16[144,768]{1,0:T(8,128)(2,1)S(1)}, bf16[144,768]{1,0:T(8,128)(2,1)S(1)}, u32[]{:S(2)}, u32[]{:S(2)}) collective-permute-start(bf16[144,768]{1,0:T(8,128)(2,1)S(1)} %get-tuple-element.139), channel_id=1, source_target_pairs={{0,4},{1,5},{2,6},{3,7},{4,0},{5,1},{6,2},{7,3},{8,12},{9,13},{10,... | collective-permute-start | bytes 663560 | tf_op jit(solution)/shard_map/ppermute | solution.py:406
  109.4 9.3 %collective-permute-start.24 = (bf16[144,768]{1,0:T(8,128)(2,1)S(1)}, bf16[144,768]{1,0:T(8,128)(2,1)S(1)}, u32[]{:S(2)}, u32[]{:S(2)}) collective-permute-start(bf16[144,768]{1,0:T(8,128)(2,1)S(1)} %pass_on.3), channel_id=1, source_target_pairs={{0,2},{1,3},{2,0},{3,1},{4,6},{5,7},{6,4},{7,5},{8,10},{9,11},{10,... | collective-permute-start | bytes 663560 | tf_op jit(solution)/shard_map/ppermute | solution.py:406
  111.0 7.7 %collective-permute-start.19 = (bf16[128,768]{1,0:T(8,128)(2,1)S(1)}, bf16[128,768]{1,0:T(8,128)(2,1)S(1)}, u32[]{:S(2)}, u32[]{:S(2)}) collective-permute-start(bf16[128,768]{1,0:T(8,128)(2,1)S(1)} %get-tuple-element.138), channel_id=1, source_target_pairs={{0,2},{1,3},{2,0},{3,1},{4,6},{5,7},{6,4},{7,5},{8,10},{9,11},{10,... | collective-permute-start | bytes 589832 | tf_op jit(solution)/shard_map/ppermute | solution.py:406
  111.6 7.2 %collective-permute-start.22 = (bf16[128,768]{1,0:T(8,128)(2,1)S(1)}, bf16[128,768]{1,0:T(8,128)(2,1)S(1)}, u32[]{:S(2)}, u32[]{:S(2)}) collective-permute-start(bf16[128,768]{1,0:T(8,128)(2,1)S(1)} %pass_on.2), channel_id=1, source_target_pairs={{0,4},{1,5},{2,6},{3,7},{4,0},{5,1},{6,2},{7,3},{8,12},{9,13},{10,... | collective-permute-start | bytes 589832 | tf_op jit(solution)/shard_map/ppermute | solution.py:406
  119.1 7.8 %collective-permute-start.25 = (bf16[128,768]{1,0:T(8,128)(2,1)S(1)}, bf16[128,768]{1,0:T(8,128)(2,1)S(1)}, u32[]{:S(2)}, u32[]{:S(2)}) collective-permute-start(bf16[128,768]{1,0:T(8,128)(2,1)S(1)} %get-tuple-element.144.refs_0_), channel_id=1, source_target_pairs={{0,2},{1,3},{2,0},{3,1},{4,6},{5,7},{6,4},{7,5},{8,10},{9,11},{10,... | collective-permute-start | bytes 589832 | tf_op jit(solution)/shard_map/ppermute | solution.py:406
  120.7 8.3 %collective-permute-start.28 = (bf16[144,768]{1,0:T(8,128)(2,1)S(1)}, bf16[144,768]{1,0:T(8,128)(2,1)S(1)}, u32[]{:S(2)}, u32[]{:S(2)}) collective-permute-start(bf16[144,768]{1,0:T(8,128)(2,1)S(1)} %get-tuple-element.145.refs_1_), channel_id=1, source_target_pairs={{0,4},{1,5},{2,6},{3,7},{4,0},{5,1},{6,2},{7,3},{8,12},{9,13},{10,... | collective-permute-start | bytes 663560 | tf_op jit(solution)/shard_map/ppermute | solution.py:406
  122.2 9.4 %collective-permute-start.26 = (bf16[144,768]{1,0:T(8,128)(2,1)S(1)}, bf16[144,768]{1,0:T(8,128)(2,1)S(1)}, u32[]{:S(2)}, u32[]{:S(2)}) collective-permute-start(bf16[144,768]{1,0:T(8,128)(2,1)S(1)} %get-tuple-element.145.refs_1_), channel_id=1, source_target_pairs={{0,2},{1,3},{2,0},{3,1},{4,6},{5,7},{6,4},{7,5},{8,10},{9,11},{10,... | collective-permute-start | bytes 663560 | tf_op jit(solution)/shard_map/ppermute | solution.py:406
  122.7 10.4 %collective-permute-start.36 = (bf16[144,768]{1,0:T(8,128)(2,1)S(1)}, bf16[144,768]{1,0:T(8,128)(2,1)S(1)}, u32[]{:S(2)}, u32[]{:S(2)}) collective-permute-start(bf16[144,768]{1,0:T(8,128)(2,1)S(1)} %get-tuple-element.145.refs_1_), channel_id=1, source_target_pairs={{0,1},{1,0},{2,3},{3,2},{4,5},{5,4},{6,7},{7,6},{8,9},{9,8},{10,11... | collective-permute-start | bytes 663560 | tf_op jit(solution)/shard_map/ppermute | solution.py:406
  122.7 10.4 %collective-permute-start.27 = (bf16[128,768]{1,0:T(8,128)(2,1)S(1)}, bf16[128,768]{1,0:T(8,128)(2,1)S(1)}, u32[]{:S(2)}, u32[]{:S(2)}) collective-permute-start(bf16[128,768]{1,0:T(8,128)(2,1)S(1)} %get-tuple-element.144.refs_0_), channel_id=1, source_target_pairs={{0,4},{1,5},{2,6},{3,7},{4,0},{5,1},{6,2},{7,3},{8,12},{9,13},{10,... | collective-permute-start | bytes 589832 | tf_op jit(solution)/shard_map/ppermute | solution.py:406
  126.9 9.7 %collective-permute-start.29 = (bf16[128,768]{1,0:T(8,128)(2,1)S(1)}, bf16[128,768]{1,0:T(8,128)(2,1)S(1)}, u32[]{:S(2)}, u32[]{:S(2)}) collective-permute-start(bf16[128,768]{1,0:T(8,128)(2,1)S(1)} %collective-permute-done.25.refs_0_), channel_id=1, source_target_pairs={{0,4},{1,5},{2,6},{3,7},{4,0},{5,1},{6,2},{7,3},{8,12},{9,13},{10,... | collective-permute-start | bytes 589832 | tf_op jit(solution)/shard_map/ppermute | solution.py:406
  129.0 9.5 %collective-permute-start.30 = (bf16[144,768]{1,0:T(8,128)(2,1)S(1)}, bf16[144,768]{1,0:T(8,128)(2,1)S(1)}, u32[]{:S(2)}, u32[]{:S(2)}) collective-permute-start(bf16[144,768]{1,0:T(8,128)(2,1)S(1)} %collective-permute-done.28.refs_3_), channel_id=1, source_target_pairs={{0,2},{1,3},{2,0},{3,1},{4,6},{5,7},{6,4},{7,5},{8,10},{9,11},{10,... | collective-permute-start | bytes 663560 | tf_op jit(solution)/shard_map/ppermute | solution.py:406
  131.6 6.8 %collective-permute-start.32 = (bf16[144,768]{1,0:T(8,128)(2,1)S(1)}, bf16[144,768]{1,0:T(8,128)(2,1)S(1)}, u32[]{:S(2)}, u32[]{:S(2)}) collective-permute-start(bf16[144,768]{1,0:T(8,128)(2,1)S(1)} %collective-permute-done.26.refs_1_), channel_id=1, source_target_pairs={{0,1},{1,0},{2,3},{3,2},{4,5},{5,4},{6,7},{7,6},{8,9},{9,8},{10,11... | collective-permute-start | bytes 663560 | tf_op jit(solution)/shard_map/ppermute | solution.py:406
  133.2 5.3 %collective-permute-start.34 = (bf16[144,768]{1,0:T(8,128)(2,1)S(1)}, bf16[144,768]{1,0:T(8,128)(2,1)S(1)}, u32[]{:S(2)}, u32[]{:S(2)}) collective-permute-start(bf16[144,768]{1,0:T(8,128)(2,1)S(1)} %collective-permute-done.28.refs_3_), channel_id=1, source_target_pairs={{0,1},{1,0},{2,3},{3,2},{4,5},{5,4},{6,7},{7,6},{8,9},{9,8},{10,11... | collective-permute-start | bytes 663560 | tf_op jit(solution)/shard_map/ppermute | solution.py:406
  133.2 5.3 %collective-permute-start.31 = (bf16[128,768]{1,0:T(8,128)(2,1)S(1)}, bf16[128,768]{1,0:T(8,128)(2,1)S(1)}, u32[]{:S(2)}, u32[]{:S(2)}) collective-permute-start(bf16[128,768]{1,0:T(8,128)(2,1)S(1)} %collective-permute-done.25.refs_0_), channel_id=1, source_target_pairs={{0,1},{1,0},{2,3},{3,2},{4,5},{5,4},{6,7},{7,6},{8,9},{9,8},{10,11... | collective-permute-start | bytes 589832 | tf_op jit(solution)/shard_map/ppermute | solution.py:406
  (8 other events, 20.6 us)

commit v7 on v6

--- a/solution.py
+++ b/solution.py
@@ -483,21 +483,31 @@
         block for block in range(n_places) if all(order[-1] != block for order in orders)
     }
     early_totals = None
+    def arrive(moved):
+        for slot, array, places in moved:
+            slots[slot].append((array, places))
+
+    def arrive_behind(moved, carried):
+        if moved:
+            arrays, carried = lax.optimization_barrier(([array for _, array, _ in moved], carried))
+            arrive([(slot, array, places) for (slot, _, places), array in zip(moved, arrays)])
+        return carried
+
     for turn in range(n_places):
         while sum(len(places) for _, places in slots[turn]) < n_places:
             moved, moves = start_ready(moves)
-            for slot, array, places in moved:
-                slots[slot].append((array, places))
+            arrive(moved)
         slots[turn] = merged(slots[turn])
         moved, moves = start_ready(moves)
+
         carried = scores_of(turn, carried)
         if turn == n_places - 2 and settled:
             early_totals = totals_of(carried[2])
             early_totals, carried = lax.optimization_barrier((early_totals, carried))
-        if moved:
-            arrays, carried = lax.optimization_barrier(([array for _, array, _ in moved], carried))
-            for (slot, _, places), array in zip(moved, arrays):
-                slots[slot].append((array, places))
+        if turn == 0:
+            arrive([m for m in moved if m[0] > turn + 1])
+            moved = [m for m in moved if m[0] <= turn + 1]
+        carried = arrive_behind(moved, carried)
     scores, rows, totals = carried
     steps = sum_plan(orders)
     late = totals_of(totals)

time: 144 us -> 144 us (level)
  transfers between devices with their start and end apart: 39 -> 39, of which waited for: 12 -> 13; matrix products, arithmetic and copies ran while one was open for 3% -> 3% of each run, Pallas kernels for 24% -> 24%
where the time goes in v7:
time: 144 us
  waiting for transfers between devices  50.3 us (35%)
  Pallas kernels  48.5 us (34%)
  starting transfers between devices  38.5 us (27%)
  other arithmetic  4.33 us (3%)
    pallas_call x8, Pallas kernels, score_block(): pl.pallas_call(functools.partial(score_kernel, n_sources, choice), grid_s...  25.6 us
    ppermute x22, waiting for transfers between devices, exchange(): lax.ppermute(array, 'rows', [(i, i ^ distance) for i in range(n_rows)])  22.4 us
    ppermute x5, waiting for transfers between devices, start_ready(): lax.ppermute(slots[source_slot][hold][0], 'blk', pairs)  20.8 us
    ppermute x22, starting transfers between devices, exchange(): lax.ppermute(array, 'rows', [(i, i ^ distance) for i in range(n_rows)])  16.3 us
    pallas_call x2, Pallas kernels, sum_rows(): pl.pallas_call(functools.partial(sum_kernel, plan, len(totals), n_owners,...  16.1 us
    ppermute x6, starting transfers between devices, totals_of(): lax.ppermute(both, 'blk', [(i, (i + turn) % n_places) for i in range(n_pl...  9.81 us
    ppermute x6, waiting for transfers between devices, totals_of(): lax.ppermute(both, 'blk', [(i, (i + turn) % n_places) for i in range(n_pl...  7.05 us
    ppermute x5, starting transfers between devices, start_ready(): lax.ppermute(slots[source_slot][hold][0], 'blk', pairs)  6.63 us
  transfers between devices with their start and end apart: 39, of which 13 were waited for; matrix products, arithmetic and copies ran while one was open for 3% of the time, Pallas kernels for 24%

profile of v7, /device:TPU:0, one launch (start us, length us, event | category | flops | bytes accessed | tf_op | source)
XLA Modules:
  0.0 143.9 jit_solution(7319031956758299781)
XLA Ops:
  1.1 2.7 %collective-permute-start.2 = (bf16[512,768]{1,0:T(8,128)(2,1)}, bf16[512,768]{1,0:T(8,128)(2,1)S(1)}, u32[]{:S(2)}, u32[]{:S(2)}) collective-permute-start(bf16[512,768]{1,0:T(8,128)(2,1)} %refs_0_.1), channel_id=1, source_target_pairs={{8,0},{0,8},{24,16},{16,24},{9,1},{1,9},{25,17},{17,25},{10,2},{2,... | collective-permute-start | bytes 2359304 | tf_op jit(solution)/shard_map/ppermute | solution.py:430
  5.3 1.8 %fusion = f32[1024]{0:T(1024)S(1)} fusion(bf16[2048,768]{1,0:T(8,128)(2,1)} %param.4, s32[]{:T(128)S(6)} %select_n.4), kind=kLoop, calls=%fused_computation.2 | loop fusion | flops 2358272 | bytes 1576964 | tf_op jit(solution)/shard_map/reduce_sum | solution.py:21
  7.1 1.7 %fusion.1.refs_1_.refs_2_ = bf16[1024,768]{1,0:T(8,128)(2,1)S(1)} fusion(f32[1024]{0:T(1024)S(1)} %add_rsqrt_fusion, bf16[2048,768]{1,0:T(8,128)(2,1)} %param.4, s32[]{:T(128)S(6)} %select_n.4), kind=kLoop, calls=%fused_computation.3 | loop fusion | flops 2359296 | bytes 3149828 | tf_op jit(solution)/shard_map/convert_element_type | solution.py:21
  10.2 3.3 %scores.8 = (f32[1024,4096]{1,0:T(8,128)}, bf16[4096,768]{1,0:T(8,128)(2,1)}, f32[8,1,512]{2,1,0:T(1,128)S(1)}) custom-call(s32[2]{0:T(128)S(1)} %pad_add_fusion.ids, bf16[512,768]{1,0:T(8,128)(2,1)S(1)} %copy-done, bf16[1024,768]{1,0:T(8,128)(2,1)S(1)} %fusion.1.refs_1_.refs_2_, f32[1024,128]{1,0:T(8,128)S(1)} %broadcast_in_dim.2.refs_2_.refs_3_), custom_call_target="tpu_custom_call" | custom-call | flops 805306368 | bytes 7340032 | tf_op jit(solution)/shard_map/scores/pallas_call | solution.py:105
  13.5 3.2 %scores.9 = (f32[1024,4096]{1,0:T(8,128)}, bf16[4096,768]{1,0:T(8,128)(2,1)}, f32[8,1,512]{2,1,0:T(1,128)S(1)}) custom-call(s32[2]{0:T(128)S(1)} %pad_add_fusion.ids, bf16[512,768]{1,0:T(8,128)(2,1)S(1)} %collective-permute-done.3.refs_0_, bf16[1024,768]{1,0:T(8,128)(2,1)S(1)} %fusion.1.refs_1_.refs_2_, ...), custom_call_target="tpu_custom_call", output_to_operand_aliasing={{0}: (4, {}), {1}: (5, {}), {2}: (6, {})} | custom-call | flops 805306368 | bytes 7340032 | tf_op jit(solution)/shard_map/scores/pallas_call | solution.py:105
  16.6 5.5 %collective-permute-done.2.refs_0_ = bf16[512,768]{1,0:T(8,128)(2,1)S(1)} collective-permute-done((bf16[512,768]{1,0:T(8,128)(2,1)}, bf16[512,768]{1,0:T(8,128)(2,1)S(1)}, u32[]{:S(2)}, u32[]{:S(2)}) %collective-permute-start.2) | collective-permute-done | bytes 786464 | tf_op jit(solution)/shard_map/ppermute | solution.py:430
  24.9 3.2 %scores.10 = (f32[1024,4096]{1,0:T(8,128)}, bf16[4096,768]{1,0:T(8,128)(2,1)}, f32[8,1,512]{2,1,0:T(1,128)S(1)}) custom-call(s32[2]{0:T(128)S(1)} %pad_add_fusion.ids, bf16[512,768]{1,0:T(8,128)(2,1)S(1)} %collective-permute-done.2.refs_0_, bf16[1024,768]{1,0:T(8,128)(2,1)S(1)} %fusion.1.refs_1_.refs_2_, ...), custom_call_target="tpu_custom_call", output_to_operand_aliasing={{0}: (4, {}), {1}: (5, {}), {2}: (6, {})} | custom-call | flops 805306368 | bytes 7340032 | tf_op jit(solution)/shard_map/scores/pallas_call | solution.py:105
  28.1 3.2 %scores.11 = (f32[1024,4096]{1,0:T(8,128)}, bf16[4096,768]{1,0:T(8,128)(2,1)}, f32[8,1,512]{2,1,0:T(1,128)S(1)}) custom-call(s32[2]{0:T(128)S(1)} %pad_add_fusion.ids, bf16[512,768]{1,0:T(8,128)(2,1)S(1)} %collective-permute-done.5.refs_0_, bf16[1024,768]{1,0:T(8,128)(2,1)S(1)} %fusion.1.refs_1_.refs_2_, ...), custom_call_target="tpu_custom_call", output_to_operand_aliasing={{0}: (4, {}), {1}: (5, {}), {2}: (6, {})} | custom-call | flops 805306368 | bytes 7340032 | tf_op jit(solution)/shard_map/scores/pallas_call | solution.py:105
  31.3 15.3 %collective-permute-done.1.refs_1_ = bf16[512,768]{1,0:T(8,128)(2,1)S(1)} collective-permute-done((bf16[512,768]{1,0:T(8,128)(2,1)S(1)}, bf16[512,768]{1,0:T(8,128)(2,1)S(1)}, u32[]{:S(2)}, u32[]{:S(2)}) %collective-permute-start.1) | collective-permute-done | bytes 786464 | tf_op jit(solution)/shard_map/ppermute | solution.py:430
  46.6 1.9 %collective-permute-start.9 = (bf16[512,768]{1,0:T(8,128)(2,1)S(1)}, bf16[512,768]{1,0:T(8,128)(2,1)S(1)}, u32[]{:S(2)}, u32[]{:S(2)}) collective-permute-start(bf16[512,768]{1,0:T(8,128)(2,1)S(1)} %collective-permute-done.1.refs_1_), channel_id=1, source_target_pairs={{0,1},{1,0},{2,3},{3,2},{4,5},{5,4},{6,7},{7,6},{24,25},{25,24},{2... | collective-permute-start | bytes 2359304 | tf_op jit(solution)/shard_map/ppermute | solution.py:412
  49.8 3.2 %scores.12 = (f32[1024,4096]{1,0:T(8,128)}, bf16[4096,768]{1,0:T(8,128)(2,1)}, f32[8,1,512]{2,1,0:T(1,128)S(1)}) custom-call(s32[2]{0:T(128)S(1)} %pad_add_fusion.ids, bf16[512,768]{1,0:T(8,128)(2,1)S(1)} %collective-permute-done.refs_0_, ...), custom_call_target="tpu_custom_call", output_to_operand_aliasing={{0}: (5, {}), {1}: (6, {}), {2}: (7, {})} | custom-call | flops 805306368 | bytes 7340032 | tf_op jit(solution)/shard_map/scores/pallas_call | solution.py:105
  53.1 3.2 %scores.13 = (f32[1024,4096]{1,0:T(8,128)}, bf16[4096,768]{1,0:T(8,128)(2,1)}, f32[8,1,512]{2,1,0:T(1,128)S(1)}) custom-call(s32[2]{0:T(128)S(1)} %pad_add_fusion.ids, bf16[512,768]{1,0:T(8,128)(2,1)S(1)} %collective-permute-done.8.refs_0_, ...), custom_call_target="tpu_custom_call", output_to_operand_aliasing={{0}: (5, {}), {1}: (6, {}), {2}: (7, {})} | custom-call | flops 805306368 | bytes 7340032 | tf_op jit(solution)/shard_map/scores/pallas_call | solution.py:105
  57.7 2.6 %collective-permute-start.11 = (f32[8,1,512]{2,1,0:T(1,128)S(1)}, f32[8,1,512]{2,1,0:T(1,128)S(1)}, u32[]{:S(2)}, u32[]{:S(2)}) collective-permute-start(f32[8,1,512]{2,1,0:T(1,128)S(1)} %add.25.refs_0_), channel_id=1, source_target_pairs={{0,8},{8,16},{16,24},{24,0},{1,9},{9,17},{17,25},{25,1},{2,10},{10... | collective-permute-start | bytes 49160 | tf_op jit(solution)/shard_map/ppermute | solution.py:478
  60.8 2.8 %collective-permute-start.13 = (f32[8,1,512]{2,1,0:T(1,128)S(1)}, f32[8,1,512]{2,1,0:T(1,128)S(1)}, u32[]{:S(2)}, u32[]{:S(2)}) collective-permute-start(f32[8,1,512]{2,1,0:T(1,128)S(1)} %add.25.refs_0_), channel_id=1, source_target_pairs={{0,24},{8,0},{16,8},{24,16},{1,25},{9,1},{17,9},{25,17},{2,26},{10... | collective-permute-start | bytes 49160 | tf_op jit(solution)/shard_map/ppermute | solution.py:478
  65.0 6.4 %collective-permute-done.13.refs_3_ = f32[8,1,512]{2,1,0:T(1,128)S(1)} collective-permute-done((f32[8,1,512]{2,1,0:T(1,128)S(1)}, f32[8,1,512]{2,1,0:T(1,128)S(1)}, u32[]{:S(2)}, u32[]{:S(2)}) %collective-permute-start.13) | collective-permute-done | bytes 16416 | tf_op jit(solution)/shard_map/ppermute | solution.py:478
  71.4 1.9 %collective-permute-start.14 = (bf16[512,768]{1,0:T(8,128)(2,1)S(1)}, bf16[512,768]{1,0:T(8,128)(2,1)S(1)}, u32[]{:S(2)}, u32[]{:S(2)}) collective-permute-start(bf16[512,768]{1,0:T(8,128)(2,1)S(1)} %collective-permute-done.7.refs_1_), channel_id=1, source_target_pairs={{0,1},{1,0},{2,3},{3,2},{4,5},{5,4},{6,7},{7,6},{24,25},{25,24},{2... | collective-permute-start | bytes 2359304 | tf_op jit(solution)/shard_map/ppermute | solution.py:412
  73.3 3.2 %scores.14 = (f32[1024,4096]{1,0:T(8,128)}, bf16[4096,768]{1,0:T(8,128)(2,1)}, f32[8,1,512]{2,1,0:T(1,128)S(1)}) custom-call(s32[2]{0:T(128)S(1)} %pad_add_fusion.ids, bf16[512,768]{1,0:T(8,128)(2,1)S(1)} %collective-permute-done.4.refs_0_, ...), custom_call_target="tpu_custom_call", output_to_operand_aliasing={{0}: (5, {}), {1}: (6, {}), {2}: (7, {})} | custom-call | flops 805306368 | bytes 7340032 | tf_op jit(solution)/shard_map/scores/pallas_call | solution.py:105
  76.6 3.2 %scores.15 = (f32[1024,4096]{1,0:T(8,128)}, bf16[4096,768]{1,0:T(8,128)(2,1)}, f32[8,1,512]{2,1,0:T(1,128)S(1)}) custom-call(s32[2]{0:T(128)S(1)} %pad_add_fusion.ids, bf16[512,768]{1,0:T(8,128)(2,1)S(1)} %collective-permute-done.6.refs_0_, ...), custom_call_target="tpu_custom_call", output_to_operand_aliasing={{0}: (5, {}), {1}: (6, {}), {2}: (7, {})} | custom-call | flops 805306368 | bytes 7340032 | tf_op jit(solution)/shard_map/scores/pallas_call | solution.py:105
  81.2 2.5 %collective-permute-start.17 = (f32[8,1,512]{2,1,0:T(1,128)S(1)}, f32[8,1,512]{2,1,0:T(1,128)S(1)}, u32[]{:S(2)}, u32[]{:S(2)}) collective-permute-start(f32[8,1,512]{2,1,0:T(1,128)S(1)} %add.26.refs_0_), channel_id=1, source_target_pairs={{0,16},{8,24},{16,0},{24,8},{1,17},{9,25},{17,1},{25,9},{2,18},{10... | collective-permute-start | bytes 49160 | tf_op jit(solution)/shard_map/ppermute | solution.py:478
  85.0 7.9 %sums.2 = (f32[1024,768]{1,0:T(8,128)S(1)}, f32[1024,128]{1,0:T(8,128)S(1)}) custom-call(s32[2]{0:T(128)S(1)} %pad_add_fusion.ids, f32[8,1,512]{2,1,0:T(1,128)S(1)} %add.25.refs_0_, f32[8,1,512]{2,1,0:T(1,128)S(1)} %collective-permute-done.11.refs_1_, f32[8,1,512]{2,1,0:T(1,128)S(1)} %collective-permute-done.12.refs_2_, ...), custom_call_target="tpu_custom_call" | custom-call | flops 3221225472 | bytes 14680064 | tf_op jit(solution)/shard_map/sums/pallas_call | solution.py:267
  92.9 8.2 %sums.3 = (bf16[128,768]{1,0:T(8,128)(2,1)S(1)}, f32[144,768]{1,0:T(8,128)S(1)}, f32[128,768]{1,0:T(8,128)S(1)}, bf16[144,768]{1,0:T(8,128)(2,1)S(1)}, bf16[128,...) custom-call(s32[2]{0:T(128)S(1)} %pad_add_fusion.ids, ...), custom_call_target="tpu_custom_call" | custom-call | flops 3221225472 | bytes 14680064 | tf_op jit(solution)/shard_map/sums/pallas_call | solution.py:267
  101.2 1.6 %collective-permute-start.23 = (bf16[144,768]{1,0:T(8,128)(2,1)S(1)}, bf16[144,768]{1,0:T(8,128)(2,1)S(1)}, u32[]{:S(2)}, u32[]{:S(2)}) collective-permute-start(bf16[144,768]{1,0:T(8,128)(2,1)S(1)} %get-tuple-element.141), channel_id=1, source_target_pairs={{0,4},{1,5},{2,6},{3,7},{4,0},{5,1},{6,2},{7,3},{8,12},{9,13},{10,... | collective-permute-start | bytes 663560 | tf_op jit(solution)/shard_map/ppermute | solution.py:406
  104.8 4.8 %collective-permute-done.23.arrived = bf16[144,768]{1,0:T(8,128)(2,1)S(1)} collective-permute-done((bf16[144,768]{1,0:T(8,128)(2,1)S(1)}, bf16[144,768]{1,0:T(8,128)(2,1)S(1)}, u32[]{:S(2)}, u32[]{:S(2)}) %collective-permute-start.23) | collective-permute-done | bytes 221216 | tf_op jit(solution)/shard_map/ppermute | solution.py:406
  111.8 1.6 %collective-permute-start.22 = (bf16[128,768]{1,0:T(8,128)(2,1)S(1)}, bf16[128,768]{1,0:T(8,128)(2,1)S(1)}, u32[]{:S(2)}, u32[]{:S(2)}) collective-permute-start(bf16[128,768]{1,0:T(8,128)(2,1)S(1)} %pass_on.2), channel_id=1, source_target_pairs={{0,4},{1,5},{2,6},{3,7},{4,0},{5,1},{6,2},{7,3},{8,12},{9,13},{10,... | collective-permute-start | bytes 589832 | tf_op jit(solution)/shard_map/ppermute | solution.py:406
  113.4 5.6 %collective-permute-done.19.refs_0_ = bf16[128,768]{1,0:T(8,128)(2,1)S(1)} collective-permute-done((bf16[128,768]{1,0:T(8,128)(2,1)S(1)}, bf16[128,768]{1,0:T(8,128)(2,1)S(1)}, u32[]{:S(2)}, u32[]{:S(2)}) %collective-permute-start.19) | collective-permute-done | bytes 196640 | tf_op jit(solution)/shard_map/ppermute | solution.py:406
  119.3 1.6 %collective-permute-start.25 = (bf16[128,768]{1,0:T(8,128)(2,1)S(1)}, bf16[128,768]{1,0:T(8,128)(2,1)S(1)}, u32[]{:S(2)}, u32[]{:S(2)}) collective-permute-start(bf16[128,768]{1,0:T(8,128)(2,1)S(1)} %get-tuple-element.142.refs_0_), channel_id=1, source_target_pairs={{0,2},{1,3},{2,0},{3,1},{4,6},{5,7},{6,4},{7,5},{8,10},{9,11},{10,... | collective-permute-start | bytes 589832 | tf_op jit(solution)/shard_map/ppermute | solution.py:406
  123.4 3.6 %collective-permute-done.25.refs_0_ = bf16[128,768]{1,0:T(8,128)(2,1)S(1)} collective-permute-done((bf16[128,768]{1,0:T(8,128)(2,1)S(1)}, bf16[128,768]{1,0:T(8,128)(2,1)S(1)}, u32[]{:S(2)}, u32[]{:S(2)}) %collective-permute-start.25) | collective-permute-done | bytes 196640 | tf_op jit(solution)/shard_map/ppermute | solution.py:406
  130.1 1.7 %collective-permute-done.26.refs_1_ = bf16[144,768]{1,0:T(8,128)(2,1)S(1)} collective-permute-done((bf16[144,768]{1,0:T(8,128)(2,1)S(1)}, bf16[144,768]{1,0:T(8,128)(2,1)S(1)}, u32[]{:S(2)}, u32[]{:S(2)}) %collective-permute-start.26) | collective-permute-done | bytes 221216 | tf_op jit(solution)/shard_map/ppermute | solution.py:406
  133.9 2.9 %collective-permute-done.29.refs_0_ = bf16[128,768]{1,0:T(8,128)(2,1)S(1)} collective-permute-done((bf16[128,768]{1,0:T(8,128)(2,1)S(1)}, bf16[128,768]{1,0:T(8,128)(2,1)S(1)}, u32[]{:S(2)}, u32[]{:S(2)}) %collective-permute-start.29) | collective-permute-done | bytes 196640 | tf_op jit(solution)/shard_map/ppermute | solution.py:406
  136.8 1.8 %assemble.3 = (f32[2048,768]{1,0:T(8,128)}, f32[8,1,256]{2,1,0:T(1,128)}) custom-call(s32[2]{0:T(128)S(1)} %pad_add_fusion.ids, bf16[128,768]{1,0:T(8,128)(2,1)S(1)} %get-tuple-element.142.refs_0_, bf16[144,768]{1,0:T(8,128)(2,1)S(1)} %get-tuple-element.143.refs_1_, bf16[128,768]{1,0:T(8,128)(2,1)S(1)} %collective-permute-done.35.refs_2_, ...), custom_call_target="tpu_custom_call" | custom-call | tf_op jit(solution)/shard_map/assemble/pallas_call | solution.py:370
  139.3 2.8 %assemble.4 = (f32[2048,768]{1,0:T(8,128)}, f32[8,1,256]{2,1,0:T(1,128)}) custom-call(s32[2]{0:T(128)S(1)} %pad_add_fusion.ids, bf16[128,768]{1,0:T(8,128)(2,1)S(1)} %collective-permute-done.25.refs_0_, bf16[144,768]{1,0:T(8,128)(2,1)S(1)} %collective-permute-done.26.refs_1_, ...), custom_call_target="tpu_custom_call", output_to_operand_aliasing={{0}: (9, {}), {1}: (10, {})} | custom-call | tf_op jit(solution)/shard_map/assemble/pallas_call | solution.py:370
  142.1 1.8 %assemble.5 = (f32[2048,768]{1,0:T(8,128)}, f32[8,1,256]{2,1,0:T(1,128)}) custom-call(s32[2]{0:T(128)S(1)} %pad_add_fusion.ids, bf16[128,768]{1,0:T(8,128)(2,1)S(1)} %collective-permute-done.29.refs_0_, bf16[144,768]{1,0:T(8,128)(2,1)S(1)} %collective-permute-done.30.refs_1_, ...), custom_call_target="tpu_custom_call", output_to_operand_aliasing={{0}: (5, {}), {1}: (6, {})} | custom-call | tf_op jit(solution)/shard_map/assemble/pallas_call | solution.py:370
  (72 shorter events, 26.3 us)
Async XLA Ops:
  0.6 12.8 %collective-permute-start.3 = (bf16[512,768]{1,0:T(8,128)(2,1)}, bf16[512,768]{1,0:T(8,128)(2,1)S(1)}, u32[]{:S(2)}, u32[]{:S(2)}) collective-permute-start(bf16[512,768]{1,0:T(8,128)(2,1)} %refs_0_.1), channel_id=1, source_target_pairs={{0,1},{1,0},{2,3},{3,2},{4,5},{5,4},{6,7},{7,6},{8,9},{9,8},{10,11... | collective-permute-start | bytes 2359304 | tf_op jit(solution)/shard_map/ppermute | solution.py:412
  1.1 21.0 %collective-permute-start.2 = (bf16[512,768]{1,0:T(8,128)(2,1)}, bf16[512,768]{1,0:T(8,128)(2,1)S(1)}, u32[]{:S(2)}, u32[]{:S(2)}) collective-permute-start(bf16[512,768]{1,0:T(8,128)(2,1)} %refs_0_.1), channel_id=1, source_target_pairs={{8,0},{0,8},{24,16},{16,24},{9,1},{1,9},{25,17},{17,25},{10,2},{2,... | collective-permute-start | bytes 2359304 | tf_op jit(solution)/shard_map/ppermute | solution.py:430
  3.8 19.1 %collective-permute-start = (bf16[512,768]{1,0:T(8,128)(2,1)}, bf16[512,768]{1,0:T(8,128)(2,1)S(1)}, u32[]{:S(2)}, u32[]{:S(2)}) collective-permute-start(bf16[512,768]{1,0:T(8,128)(2,1)} %refs_0_.1), channel_id=1, source_target_pairs={{16,8},{8,16},{17,9},{9,17},{18,10},{10,18},{19,11},{11,19},{20,12... | collective-permute-start | bytes 2359304 | tf_op jit(solution)/shard_map/ppermute | solution.py:430
  22.1 5.9 %collective-permute-start.5 = (bf16[512,768]{1,0:T(8,128)(2,1)S(1)}, bf16[512,768]{1,0:T(8,128)(2,1)S(1)}, u32[]{:S(2)}, u32[]{:S(2)}) collective-permute-start(bf16[512,768]{1,0:T(8,128)(2,1)S(1)} %collective-permute-done.2.refs_0_), channel_id=1, source_target_pairs={{0,1},{1,0},{2,3},{3,2},{4,5},{5,4},{6,7},{7,6},{8,9},{9,8},{10,11... | collective-permute-start | bytes 2359304 | tf_op jit(solution)/shard_map/ppermute | solution.py:412
  22.1 9.1 %collective-permute-start.4 = (bf16[512,768]{1,0:T(8,128)(2,1)S(1)}, bf16[512,768]{1,0:T(8,128)(2,1)S(1)}, u32[]{:S(2)}, u32[]{:S(2)}) collective-permute-start(bf16[512,768]{1,0:T(8,128)(2,1)S(1)} %collective-permute-done.2.refs_0_), channel_id=1, source_target_pairs={{16,8},{8,16},{17,9},{9,17},{18,10},{10,18},{19,11},{11,19},{20,12... | collective-permute-start | bytes 2359304 | tf_op jit(solution)/shard_map/ppermute | solution.py:430
  22.9 23.7 %collective-permute-start.1 = (bf16[512,768]{1,0:T(8,128)(2,1)S(1)}, bf16[512,768]{1,0:T(8,128)(2,1)S(1)}, u32[]{:S(2)}, u32[]{:S(2)}) collective-permute-start(bf16[512,768]{1,0:T(8,128)(2,1)S(1)} %collective-permute-done.refs_0_), channel_id=1, source_target_pairs={{8,0},{16,24},{9,1},{17,25},{10,2},{18,26},{11,3},{19,27},{12,4},{... | collective-permute-start | bytes 2359304 | tf_op jit(solution)/shard_map/ppermute | solution.py:430
  24.2 28.9 %collective-permute-start.8 = (bf16[512,768]{1,0:T(8,128)(2,1)S(1)}, bf16[512,768]{1,0:T(8,128)(2,1)S(1)}, u32[]{:S(2)}, u32[]{:S(2)}) collective-permute-start(bf16[512,768]{1,0:T(8,128)(2,1)S(1)} %collective-permute-done.refs_0_), channel_id=1, source_target_pairs={{8,9},{9,8},{10,11},{11,10},{12,13},{13,12},{14,15},{15,14},{16,17... | collective-permute-start | bytes 2359304 | tf_op jit(solution)/shard_map/ppermute | solution.py:412
  46.6 6.5 %collective-permute-start.9 = (bf16[512,768]{1,0:T(8,128)(2,1)S(1)}, bf16[512,768]{1,0:T(8,128)(2,1)S(1)}, u32[]{:S(2)}, u32[]{:S(2)}) collective-permute-start(bf16[512,768]{1,0:T(8,128)(2,1)S(1)} %collective-permute-done.1.refs_1_), channel_id=1, source_target_pairs={{0,1},{1,0},{2,3},{3,2},{4,5},{5,4},{6,7},{7,6},{24,25},{25,24},{2... | collective-permute-start | bytes 2359304 | tf_op jit(solution)/shard_map/ppermute | solution.py:412
  48.5 22.9 %collective-permute-start.7 = (bf16[512,768]{1,0:T(8,128)(2,1)S(1)}, bf16[512,768]{1,0:T(8,128)(2,1)S(1)}, u32[]{:S(2)}, u32[]{:S(2)}) collective-permute-start(bf16[512,768]{1,0:T(8,128)(2,1)S(1)} %collective-permute-done.4.refs_0_), channel_id=1, source_target_pairs={{8,0},{16,24},{9,1},{17,25},{10,2},{18,26},{11,3},{19,27},{12,4},{... | collective-permute-start | bytes 2359304 | tf_op jit(solution)/shard_map/ppermute | solution.py:430
  57.7 6.7 %collective-permute-start.11 = (f32[8,1,512]{2,1,0:T(1,128)S(1)}, f32[8,1,512]{2,1,0:T(1,128)S(1)}, u32[]{:S(2)}, u32[]{:S(2)}) collective-permute-start(f32[8,1,512]{2,1,0:T(1,128)S(1)} %add.25.refs_0_), channel_id=1, source_target_pairs={{0,8},{8,16},{16,24},{24,0},{1,9},{9,17},{17,25},{25,1},{2,10},{10... | collective-permute-start | bytes 49160 | tf_op jit(solution)/shard_map/ppermute | solution.py:478
  60.8 10.6 %collective-permute-start.13 = (f32[8,1,512]{2,1,0:T(1,128)S(1)}, f32[8,1,512]{2,1,0:T(1,128)S(1)}, u32[]{:S(2)}, u32[]{:S(2)}) collective-permute-start(f32[8,1,512]{2,1,0:T(1,128)S(1)} %add.25.refs_0_), channel_id=1, source_target_pairs={{0,24},{8,0},{16,8},{24,16},{1,25},{9,1},{17,9},{25,17},{2,26},{10... | collective-permute-start | bytes 49160 | tf_op jit(solution)/shard_map/ppermute | solution.py:478
  63.6 12.9 %collective-permute-start.6 = (bf16[512,768]{1,0:T(8,128)(2,1)S(1)}, bf16[512,768]{1,0:T(8,128)(2,1)S(1)}, u32[]{:S(2)}, u32[]{:S(2)}) collective-permute-start(bf16[512,768]{1,0:T(8,128)(2,1)S(1)} %collective-permute-done.4.refs_0_), channel_id=1, source_target_pairs={{8,9},{9,8},{10,11},{11,10},{12,13},{13,12},{14,15},{15,14},{16,17... | collective-permute-start | bytes 2359304 | tf_op jit(solution)/shard_map/ppermute | solution.py:412
  71.4 5.1 %collective-permute-start.14 = (bf16[512,768]{1,0:T(8,128)(2,1)S(1)}, bf16[512,768]{1,0:T(8,128)(2,1)S(1)}, u32[]{:S(2)}, u32[]{:S(2)}) collective-permute-start(bf16[512,768]{1,0:T(8,128)(2,1)S(1)} %collective-permute-done.7.refs_1_), channel_id=1, source_target_pairs={{0,1},{1,0},{2,3},{3,2},{4,5},{5,4},{6,7},{7,6},{24,25},{25,24},{2... | collective-permute-start | bytes 2359304 | tf_op jit(solution)/shard_map/ppermute | solution.py:412
  81.2 11.8 %collective-permute-start.16 = (f32[8,1,512]{2,1,0:T(1,128)S(1)}, f32[8,1,512]{2,1,0:T(1,128)S(1)}, u32[]{:S(2)}, u32[]{:S(2)}) collective-permute-start(f32[8,1,512]{2,1,0:T(1,128)S(1)} %add.26.refs_0_), channel_id=1, source_target_pairs={{0,8},{8,16},{16,24},{24,0},{1,9},{9,17},{17,25},{25,1},{2,10},{10... | collective-permute-start | bytes 49160 | tf_op jit(solution)/shard_map/ppermute | solution.py:478
  81.2 11.7 %collective-permute-start.17 = (f32[8,1,512]{2,1,0:T(1,128)S(1)}, f32[8,1,512]{2,1,0:T(1,128)S(1)}, u32[]{:S(2)}, u32[]{:S(2)}) collective-permute-start(f32[8,1,512]{2,1,0:T(1,128)S(1)} %add.26.refs_0_), channel_id=1, source_target_pairs={{0,16},{8,24},{16,0},{24,8},{1,17},{9,25},{17,1},{25,9},{2,18},{10... | collective-permute-start | bytes 49160 | tf_op jit(solution)/shard_map/ppermute | solution.py:478
  83.7 9.3 %collective-permute-start.18 = (f32[8,1,512]{2,1,0:T(1,128)S(1)}, f32[8,1,512]{2,1,0:T(1,128)S(1)}, u32[]{:S(2)}, u32[]{:S(2)}) collective-permute-start(f32[8,1,512]{2,1,0:T(1,128)S(1)} %add.26.refs_0_), channel_id=1, source_target_pairs={{0,24},{8,0},{16,8},{24,16},{1,25},{9,1},{17,9},{25,17},{2,26},{10... | collective-permute-start | bytes 49160 | tf_op jit(solution)/shard_map/ppermute | solution.py:478
  101.2 8.4 %collective-permute-start.23 = (bf16[144,768]{1,0:T(8,128)(2,1)S(1)}, bf16[144,768]{1,0:T(8,128)(2,1)S(1)}, u32[]{:S(2)}, u32[]{:S(2)}) collective-permute-start(bf16[144,768]{1,0:T(8,128)(2,1)S(1)} %get-tuple-element.141), channel_id=1, source_target_pairs={{0,4},{1,5},{2,6},{3,7},{4,0},{5,1},{6,2},{7,3},{8,12},{9,13},{10,... | collective-permute-start | bytes 663560 | tf_op jit(solution)/shard_map/ppermute | solution.py:406
  102.8 8.9 %collective-permute-start.21 = (bf16[128,768]{1,0:T(8,128)(2,1)S(1)}, bf16[128,768]{1,0:T(8,128)(2,1)S(1)}, u32[]{:S(2)}, u32[]{:S(2)}) collective-permute-start(bf16[128,768]{1,0:T(8,128)(2,1)S(1)} %get-tuple-element.139), channel_id=1, source_target_pairs={{0,2},{1,3},{2,0},{3,1},{4,6},{5,7},{6,4},{7,5},{8,10},{9,11},{10,... | collective-permute-start | bytes 589832 | tf_op jit(solution)/shard_map/ppermute | solution.py:406
  104.3 14.7 %collective-permute-start.20 = (bf16[144,768]{1,0:T(8,128)(2,1)S(1)}, bf16[144,768]{1,0:T(8,128)(2,1)S(1)}, u32[]{:S(2)}, u32[]{:S(2)}) collective-permute-start(bf16[144,768]{1,0:T(8,128)(2,1)S(1)} %get-tuple-element.137), channel_id=1, source_target_pairs={{0,4},{1,5},{2,6},{3,7},{4,0},{5,1},{6,2},{7,3},{8,12},{9,13},{10,... | collective-permute-start | bytes 663560 | tf_op jit(solution)/shard_map/ppermute | solution.py:406
  109.6 9.3 %collective-permute-start.24 = (bf16[144,768]{1,0:T(8,128)(2,1)S(1)}, bf16[144,768]{1,0:T(8,128)(2,1)S(1)}, u32[]{:S(2)}, u32[]{:S(2)}) collective-permute-start(bf16[144,768]{1,0:T(8,128)(2,1)S(1)} %pass_on.3), channel_id=1, source_target_pairs={{0,2},{1,3},{2,0},{3,1},{4,6},{5,7},{6,4},{7,5},{8,10},{9,11},{10,... | collective-permute-start | bytes 663560 | tf_op jit(solution)/shard_map/ppermute | solution.py:406
  111.2 7.7 %collective-permute-start.19 = (bf16[128,768]{1,0:T(8,128)(2,1)S(1)}, bf16[128,768]{1,0:T(8,128)(2,1)S(1)}, u32[]{:S(2)}, u32[]{:S(2)}) collective-permute-start(bf16[128,768]{1,0:T(8,128)(2,1)S(1)} %get-tuple-element.136), channel_id=1, source_target_pairs={{0,2},{1,3},{2,0},{3,1},{4,6},{5,7},{6,4},{7,5},{8,10},{9,11},{10,... | collective-permute-start | bytes 589832 | tf_op jit(solution)/shard_map/ppermute | solution.py:406
  111.8 7.2 %collective-permute-start.22 = (bf16[128,768]{1,0:T(8,128)(2,1)S(1)}, bf16[128,768]{1,0:T(8,128)(2,1)S(1)}, u32[]{:S(2)}, u32[]{:S(2)}) collective-permute-start(bf16[128,768]{1,0:T(8,128)(2,1)S(1)} %pass_on.2), channel_id=1, source_target_pairs={{0,4},{1,5},{2,6},{3,7},{4,0},{5,1},{6,2},{7,3},{8,12},{9,13},{10,... | collective-permute-start | bytes 589832 | tf_op jit(solution)/shard_map/ppermute | solution.py:406
  119.3 7.8 %collective-permute-start.25 = (bf16[128,768]{1,0:T(8,128)(2,1)S(1)}, bf16[128,768]{1,0:T(8,128)(2,1)S(1)}, u32[]{:S(2)}, u32[]{:S(2)}) collective-permute-start(bf16[128,768]{1,0:T(8,128)(2,1)S(1)} %get-tuple-element.142.refs_0_), channel_id=1, source_target_pairs={{0,2},{1,3},{2,0},{3,1},{4,6},{5,7},{6,4},{7,5},{8,10},{9,11},{10,... | collective-permute-start | bytes 589832 | tf_op jit(solution)/shard_map/ppermute | solution.py:406
  120.9 8.3 %collective-permute-start.28 = (bf16[144,768]{1,0:T(8,128)(2,1)S(1)}, bf16[144,768]{1,0:T(8,128)(2,1)S(1)}, u32[]{:S(2)}, u32[]{:S(2)}) collective-permute-start(bf16[144,768]{1,0:T(8,128)(2,1)S(1)} %get-tuple-element.143.refs_1_), channel_id=1, source_target_pairs={{0,4},{1,5},{2,6},{3,7},{4,0},{5,1},{6,2},{7,3},{8,12},{9,13},{10,... | collective-permute-start | bytes 663560 | tf_op jit(solution)/shard_map/ppermute | solution.py:406
  122.4 9.4 %collective-permute-start.26 = (bf16[144,768]{1,0:T(8,128)(2,1)S(1)}, bf16[144,768]{1,0:T(8,128)(2,1)S(1)}, u32[]{:S(2)}, u32[]{:S(2)}) collective-permute-start(bf16[144,768]{1,0:T(8,128)(2,1)S(1)} %get-tuple-element.143.refs_1_), channel_id=1, source_target_pairs={{0,2},{1,3},{2,0},{3,1},{4,6},{5,7},{6,4},{7,5},{8,10},{9,11},{10,... | collective-permute-start | bytes 663560 | tf_op jit(solution)/shard_map/ppermute | solution.py:406
  122.9 10.4 %collective-permute-start.36 = (bf16[144,768]{1,0:T(8,128)(2,1)S(1)}, bf16[144,768]{1,0:T(8,128)(2,1)S(1)}, u32[]{:S(2)}, u32[]{:S(2)}) collective-permute-start(bf16[144,768]{1,0:T(8,128)(2,1)S(1)} %get-tuple-element.143.refs_1_), channel_id=1, source_target_pairs={{0,1},{1,0},{2,3},{3,2},{4,5},{5,4},{6,7},{7,6},{8,9},{9,8},{10,11... | collective-permute-start | bytes 663560 | tf_op jit(solution)/shard_map/ppermute | solution.py:406
  122.9 10.4 %collective-permute-start.27 = (bf16[128,768]{1,0:T(8,128)(2,1)S(1)}, bf16[128,768]{1,0:T(8,128)(2,1)S(1)}, u32[]{:S(2)}, u32[]{:S(2)}) collective-permute-start(bf16[128,768]{1,0:T(8,128)(2,1)S(1)} %get-tuple-element.142.refs_0_), channel_id=1, source_target_pairs={{0,4},{1,5},{2,6},{3,7},{4,0},{5,1},{6,2},{7,3},{8,12},{9,13},{10,... | collective-permute-start | bytes 589832 | tf_op jit(solution)/shard_map/ppermute | solution.py:406
  127.1 9.7 %collective-permute-start.29 = (bf16[128,768]{1,0:T(8,128)(2,1)S(1)}, bf16[128,768]{1,0:T(8,128)(2,1)S(1)}, u32[]{:S(2)}, u32[]{:S(2)}) collective-permute-start(bf16[128,768]{1,0:T(8,128)(2,1)S(1)} %collective-permute-done.25.refs_0_), channel_id=1, source_target_pairs={{0,4},{1,5},{2,6},{3,7},{4,0},{5,1},{6,2},{7,3},{8,12},{9,13},{10,... | collective-permute-start | bytes 589832 | tf_op jit(solution)/shard_map/ppermute | solution.py:406
  129.1 9.5 %collective-permute-start.30 = (bf16[144,768]{1,0:T(8,128)(2,1)S(1)}, bf16[144,768]{1,0:T(8,128)(2,1)S(1)}, u32[]{:S(2)}, u32[]{:S(2)}) collective-permute-start(bf16[144,768]{1,0:T(8,128)(2,1)S(1)} %collective-permute-done.28.refs_3_), channel_id=1, source_target_pairs={{0,2},{1,3},{2,0},{3,1},{4,6},{5,7},{6,4},{7,5},{8,10},{9,11},{10,... | collective-permute-start | bytes 663560 | tf_op jit(solution)/shard_map/ppermute | solution.py:406
  131.8 6.8 %collective-permute-start.32 = (bf16[144,768]{1,0:T(8,128)(2,1)S(1)}, bf16[144,768]{1,0:T(8,128)(2,1)S(1)}, u32[]{:S(2)}, u32[]{:S(2)}) collective-permute-start(bf16[144,768]{1,0:T(8,128)(2,1)S(1)} %collective-permute-done.26.refs_1_), channel_id=1, source_target_pairs={{0,1},{1,0},{2,3},{3,2},{4,5},{5,4},{6,7},{7,6},{8,9},{9,8},{10,11... | collective-permute-start | bytes 663560 | tf_op jit(solution)/shard_map/ppermute | solution.py:406
  133.4 5.3 %collective-permute-start.34 = (bf16[144,768]{1,0:T(8,128)(2,1)S(1)}, bf16[144,768]{1,0:T(8,128)(2,1)S(1)}, u32[]{:S(2)}, u32[]{:S(2)}) collective-permute-start(bf16[144,768]{1,0:T(8,128)(2,1)S(1)} %collective-permute-done.28.refs_3_), channel_id=1, source_target_pairs={{0,1},{1,0},{2,3},{3,2},{4,5},{5,4},{6,7},{7,6},{8,9},{9,8},{10,11... | collective-permute-start | bytes 663560 | tf_op jit(solution)/shard_map/ppermute | solution.py:406
  133.4 5.3 %collective-permute-start.31 = (bf16[128,768]{1,0:T(8,128)(2,1)S(1)}, bf16[128,768]{1,0:T(8,128)(2,1)S(1)}, u32[]{:S(2)}, u32[]{:S(2)}) collective-permute-start(bf16[128,768]{1,0:T(8,128)(2,1)S(1)} %collective-permute-done.25.refs_0_), channel_id=1, source_target_pairs={{0,1},{1,0},{2,3},{3,2},{4,5},{5,4},{6,7},{7,6},{8,9},{9,8},{10,11... | collective-permute-start | bytes 589832 | tf_op jit(solution)/shard_map/ppermute | solution.py:406
  (8 other events, 20.5 us)

commit v8 on v7

--- a/solution.py
+++ b/solution.py
@@ -13,7 +13,7 @@
 LANES = 128
 CORES = 2
 EXTRA = 16
-VMEM_LIMIT = 48 * 1024 * 1024
+VMEM_LIMIT = 20 * 1024 * 1024
 
 
 def to_unit(values):
@@ -82,7 +82,7 @@
     if repeats > 1:
         offset = jnp.concatenate([offset] * repeats, axis=1)
     value = jnp.exp2(cosines * (concentration * LOG2E) + offset)
-    scores[...] = value
+    scores[0] = value
     totals[0] += jnp.sum(value, axis=0, keepdims=True)
 
 
@@ -91,7 +91,7 @@
     count = units.shape[0]
     tile = math.gcd(count, 512)
     shapes = (
-        jax.ShapeDtypeStruct((count, n_columns * part), jnp.float32),
+        jax.ShapeDtypeStruct((n_columns, count, part), jnp.float32),
         jax.ShapeDtypeStruct((n_columns * part, depth), jnp.bfloat16),
         jax.ShapeDtypeStruct((n_columns, 1, part), jnp.float32),
     )
@@ -114,7 +114,7 @@
             ]
             + [anywhere] * len(extra),
             out_specs=[
-                pl.BlockSpec((tile, part), lambda t, s: (t, column)),
+                pl.BlockSpec((1, tile, part), lambda t, s: (column, t, 0)),
                 pl.BlockSpec((part, depth), lambda t, s: (column, 0)),
                 pl.BlockSpec(
                     (1, 1, part),
@@ -197,7 +197,7 @@
             total[...] = state[0][...]
             mass[...] = state[1][...]
 
-    resp = (scores[...] * inverse[step]).astype(jnp.bfloat16)
+    resp = (scores[0] * inverse[step]).astype(jnp.bfloat16)
     total[...] += lax.dot_general(
         resp, rows[...], (((1,), (0,)), ((), ())), preferred_element_type=jnp.float32
     )
@@ -239,7 +239,7 @@
 
 
 def sum_rows(ids, plan, totals, scores, rows, n_owners, carried, last):
-    count = scores.shape[0]
+    count = scores.shape[1]
     depth = rows.shape[1]
     size = count // n_owners
     part = totals[0].shape[2]
@@ -249,7 +249,7 @@
     )
     fixed = lambda shape: pl.BlockSpec(shape, lambda t, s: (0,) * len(shape))
     in_specs = [fixed(totals[0].shape) for _ in totals] + [
-        pl.BlockSpec((count, part), lambda t, s: (0, column(t, s))),
+        pl.BlockSpec((1, count, part), lambda t, s: (column(t, s), 0, 0)),
         pl.BlockSpec((part, depth), lambda t, s: (column(t, s), 0)),
     ]
     state = [(count, depth), (count, LANES)]

time: 144 us -> 137 us (0.951)
  Pallas kernels: 48.5 us -> 37.1 us
  waiting for transfers between devices: 50.3 us -> 52.9 us
  starting transfers between devices: 38.5 us -> 40.4 us
    pallas_call x8, Pallas kernels: 25.6 us -> 19.5 us  [score_block(): pl.pallas_call(functools.partial(score_kernel, n_sources, choice), grid_s...]
    pallas_call x2, Pallas kernels: 16.1 us -> 10.8 us  [sum_rows(): pl.pallas_call(functools.partial(sum_kernel, plan, len(totals), n_owners,...]
    ppermute x5, waiting for transfers between devices: 20.8 us -> 22.3 us  [start_ready(): lax.ppermute(slots[source_slot][hold][0], 'blk', pairs)]
  transfers between devices with their start and end apart: 39 -> 39, of which waited for: 13 -> 14; matrix products, arithmetic and copies ran while one was open for 3% -> 3% of each run, Pallas kernels for 24% -> 20%
where the time goes in v8:
time: 137 us
  waiting for transfers between devices  52.9 us (39%)
  starting transfers between devices  40.4 us (29%)
  Pallas kernels  37.1 us (27%)
  other arithmetic  4.32 us (3%)
    ppermute x22, waiting for transfers between devices, exchange(): lax.ppermute(array, 'rows', [(i, i ^ distance) for i in range(n_rows)])  22.4 us
    ppermute x5, waiting for transfers between devices, start_ready(): lax.ppermute(slots[source_slot][hold][0], 'blk', pairs)  22.3 us
    pallas_call x8, Pallas kernels, score_block(): pl.pallas_call(functools.partial(score_kernel, n_sources, choice), grid_s...  19.5 us
    ppermute x22, starting transfers between devices, exchange(): lax.ppermute(array, 'rows', [(i, i ^ distance) for i in range(n_rows)])  16.2 us
    ppermute x6, starting transfers between devices, totals_of(): lax.ppermute(both, 'blk', [(i, (i + turn) % n_places) for i in range(n_pl...  10.9 us
    pallas_call x2, Pallas kernels, sum_rows(): pl.pallas_call(functools.partial(sum_kernel, plan, len(totals), n_owners,...  10.8 us
    ppermute x6, waiting for transfers between devices, totals_of(): lax.ppermute(both, 'blk', [(i, (i + turn) % n_places) for i in range(n_pl...  8.05 us
    ppermute x5, starting transfers between devices, start_ready(): lax.ppermute(slots[source_slot][hold][0], 'blk', pairs)  7.5 us
  transfers between devices with their start and end apart: 39, of which 14 were waited for; matrix products, arithmetic and copies ran while one was open for 3% of the time, Pallas kernels for 20%

profile of v8, /device:TPU:0, one launch (start us, length us, event | category | flops | bytes accessed | tf_op | source)
XLA Modules:
  0.0 137.0 jit_solution(12474030197397250104)
XLA Ops:
  1.1 2.7 %collective-permute-start.2 = (bf16[512,768]{1,0:T(8,128)(2,1)}, bf16[512,768]{1,0:T(8,128)(2,1)}, u32[]{:S(2)}, u32[]{:S(2)}) collective-permute-start(bf16[512,768]{1,0:T(8,128)(2,1)} %refs_0_.1), channel_id=1, source_target_pairs={{8,0},{0,8},{24,16},{16,24},{9,1},{1,9},{25,17},{17,25},{10,2},{2,... | collective-permute-start | bytes 2359304 | tf_op jit(solution)/shard_map/ppermute | solution.py:430
  6.1 1.8 %fusion = f32[1024]{0:T(1024)S(1)} fusion(bf16[2048,768]{1,0:T(8,128)(2,1)} %param.4, s32[]{:T(128)S(6)} %select_n.4), kind=kLoop, calls=%fused_computation.2 | loop fusion | flops 2358272 | bytes 1576964 | tf_op jit(solution)/shard_map/reduce_sum | solution.py:21
  7.9 1.7 %fusion.1.refs_1_.refs_2_ = bf16[1024,768]{1,0:T(8,128)(2,1)S(1)} fusion(f32[1024]{0:T(1024)S(1)} %add_rsqrt_fusion, bf16[2048,768]{1,0:T(8,128)(2,1)} %param.4, s32[]{:T(128)S(6)} %select_n.4), kind=kLoop, calls=%fused_computation.3 | loop fusion | flops 2359296 | bytes 3149828 | tf_op jit(solution)/shard_map/convert_element_type | solution.py:21
  11.0 2.2 %scores.8 = (f32[8,1024,512]{2,1,0:T(8,128)S(1)}, bf16[4096,768]{1,0:T(8,128)(2,1)S(1)}, f32[8,1,512]{2,1,0:T(1,128)S(1)}) custom-call(s32[2]{0:T(128)S(1)} %pad_add_fusion.ids, bf16[512,768]{1,0:T(8,128)(2,1)S(1)} %copy-done, bf16[1024,768]{1,0:T(8,128)(2,1)S(1)} %fusion.1.refs_1_.refs_2_, f32[1024,128]{1,0:T(8,128)S(1)} %broadcast_in_dim.2.refs_2_.refs_3_), custom_call_target="tpu_custom_call" | custom-call | flops 805306368 | bytes 7340032 | tf_op jit(solution)/shard_map/scores/pallas_call | solution.py:105
  13.2 3.2 %scores.9 = (f32[8,1024,512]{2,1,0:T(8,128)S(1)}, bf16[4096,768]{1,0:T(8,128)(2,1)S(1)}, f32[8,1,512]{2,1,0:T(1,128)S(1)}) custom-call(s32[2]{0:T(128)S(1)} %pad_add_fusion.ids, bf16[512,768]{1,0:T(8,128)(2,1)} %collective-permute-done.3.refs_0_, ...), custom_call_target="tpu_custom_call", output_to_operand_aliasing={{0}: (4, {}), {1}: (5, {}), {2}: (6, {})} | custom-call | flops 805306368 | bytes 7340032 | tf_op jit(solution)/shard_map/scores/pallas_call | solution.py:105
  16.4 5.8 %collective-permute-done.2.refs_0_ = bf16[512,768]{1,0:T(8,128)(2,1)} collective-permute-done((bf16[512,768]{1,0:T(8,128)(2,1)}, bf16[512,768]{1,0:T(8,128)(2,1)}, u32[]{:S(2)}, u32[]{:S(2)}) %collective-permute-start.2) | collective-permute-done | bytes 786464 | tf_op jit(solution)/shard_map/ppermute | solution.py:430
  25.0 3.2 %scores.10 = (f32[8,1024,512]{2,1,0:T(8,128)S(1)}, bf16[4096,768]{1,0:T(8,128)(2,1)S(1)}, f32[8,1,512]{2,1,0:T(1,128)S(1)}) custom-call(s32[2]{0:T(128)S(1)} %pad_add_fusion.ids, bf16[512,768]{1,0:T(8,128)(2,1)} %collective-permute-done.2.refs_0_, ...), custom_call_target="tpu_custom_call", output_to_operand_aliasing={{0}: (4, {}), {1}: (5, {}), {2}: (6, {})} | custom-call | flops 805306368 | bytes 7340032 | tf_op jit(solution)/shard_map/scores/pallas_call | solution.py:105
  28.2 2.2 %scores.11 = (f32[8,1024,512]{2,1,0:T(8,128)S(1)}, bf16[4096,768]{1,0:T(8,128)(2,1)S(1)}, f32[8,1,512]{2,1,0:T(1,128)S(1)}) custom-call(s32[2]{0:T(128)S(1)} %pad_add_fusion.ids, bf16[512,768]{1,0:T(8,128)(2,1)S(1)} %collective-permute-done.5.refs_0_, ...), custom_call_target="tpu_custom_call", output_to_operand_aliasing={{0}: (4, {}), {1}: (5, {}), {2}: (6, {})} | custom-call | flops 805306368 | bytes 7340032 | tf_op jit(solution)/shard_map/scores/pallas_call | solution.py:105
  30.4 16.5 %collective-permute-done.1.refs_1_ = bf16[512,768]{1,0:T(8,128)(2,1)S(1)} collective-permute-done((bf16[512,768]{1,0:T(8,128)(2,1)}, bf16[512,768]{1,0:T(8,128)(2,1)S(1)}, u32[]{:S(2)}, u32[]{:S(2)}) %collective-permute-start.1) | collective-permute-done | bytes 786464 | tf_op jit(solution)/shard_map/ppermute | solution.py:430
  46.9 1.9 %collective-permute-start.9 = (bf16[512,768]{1,0:T(8,128)(2,1)S(1)}, bf16[512,768]{1,0:T(8,128)(2,1)S(1)}, u32[]{:S(2)}, u32[]{:S(2)}) collective-permute-start(bf16[512,768]{1,0:T(8,128)(2,1)S(1)} %collective-permute-done.1.refs_1_), channel_id=1, source_target_pairs={{0,1},{1,0},{2,3},{3,2},{4,5},{5,4},{6,7},{7,6},{24,25},{25,24},{2... | collective-permute-start | bytes 2359304 | tf_op jit(solution)/shard_map/ppermute | solution.py:412
  50.1 2.2 %scores.12 = (f32[8,1024,512]{2,1,0:T(8,128)S(1)}, bf16[4096,768]{1,0:T(8,128)(2,1)S(1)}, f32[8,1,512]{2,1,0:T(1,128)S(1)}) custom-call(s32[2]{0:T(128)S(1)} %pad_add_fusion.ids, bf16[512,768]{1,0:T(8,128)(2,1)} %collective-permute-done.refs_0_, ...), custom_call_target="tpu_custom_call", output_to_operand_aliasing={{0}: (5, {}), {1}: (6, {}), {2}: (7, {})} | custom-call | flops 805306368 | bytes 7340032 | tf_op jit(solution)/shard_map/scores/pallas_call | solution.py:105
  52.3 2.2 %scores.13 = (f32[8,1024,512]{2,1,0:T(8,128)S(1)}, bf16[4096,768]{1,0:T(8,128)(2,1)S(1)}, f32[8,1,512]{2,1,0:T(1,128)S(1)}) custom-call(s32[2]{0:T(128)S(1)} %pad_add_fusion.ids, bf16[512,768]{1,0:T(8,128)(2,1)S(1)} %collective-permute-done.8.refs_0_, ...), custom_call_target="tpu_custom_call", output_to_operand_aliasing={{0}: (5, {}), {1}: (6, {}), {2}: (7, {})} | custom-call | flops 805306368 | bytes 7340032 | tf_op jit(solution)/shard_map/scores/pallas_call | solution.py:105
  55.9 3.7 %collective-permute-start.11 = (f32[8,1,512]{2,1,0:T(1,128)S(1)}, f32[8,1,512]{2,1,0:T(1,128)S(1)}, u32[]{:S(2)}, u32[]{:S(2)}) collective-permute-start(f32[8,1,512]{2,1,0:T(1,128)S(1)} %add.25.refs_0_), channel_id=1, source_target_pairs={{0,8},{8,16},{16,24},{24,0},{1,9},{9,17},{17,25},{25,1},{2,10},{10... | collective-permute-start | bytes 49160 | tf_op jit(solution)/shard_map/ppermute | solution.py:478
  60.1 2.8 %collective-permute-start.13 = (f32[8,1,512]{2,1,0:T(1,128)S(1)}, f32[8,1,512]{2,1,0:T(1,128)S(1)}, u32[]{:S(2)}, u32[]{:S(2)}) collective-permute-start(f32[8,1,512]{2,1,0:T(1,128)S(1)} %add.25.refs_0_), channel_id=1, source_target_pairs={{0,24},{8,0},{16,8},{24,16},{1,25},{9,1},{17,9},{25,17},{2,26},{10... | collective-permute-start | bytes 49160 | tf_op jit(solution)/shard_map/ppermute | solution.py:478
  64.4 7.4 %collective-permute-done.13.refs_3_ = f32[8,1,512]{2,1,0:T(1,128)S(1)} collective-permute-done((f32[8,1,512]{2,1,0:T(1,128)S(1)}, f32[8,1,512]{2,1,0:T(1,128)S(1)}, u32[]{:S(2)}, u32[]{:S(2)}) %collective-permute-start.13) | collective-permute-done | bytes 16416 | tf_op jit(solution)/shard_map/ppermute | solution.py:478
  71.7 1.9 %collective-permute-start.14 = (bf16[512,768]{1,0:T(8,128)(2,1)S(1)}, bf16[512,768]{1,0:T(8,128)(2,1)S(1)}, u32[]{:S(2)}, u32[]{:S(2)}) collective-permute-start(bf16[512,768]{1,0:T(8,128)(2,1)S(1)} %collective-permute-done.7.refs_1_), channel_id=1, source_target_pairs={{0,1},{1,0},{2,3},{3,2},{4,5},{5,4},{6,7},{7,6},{24,25},{25,24},{2... | collective-permute-start | bytes 2359304 | tf_op jit(solution)/shard_map/ppermute | solution.py:412
  73.6 2.2 %scores.14 = (f32[8,1024,512]{2,1,0:T(8,128)S(1)}, bf16[4096,768]{1,0:T(8,128)(2,1)S(1)}, f32[8,1,512]{2,1,0:T(1,128)S(1)}) custom-call(s32[2]{0:T(128)S(1)} %pad_add_fusion.ids, bf16[512,768]{1,0:T(8,128)(2,1)S(1)} %collective-permute-done.4.refs_0_, ...), custom_call_target="tpu_custom_call", output_to_operand_aliasing={{0}: (5, {}), {1}: (6, {}), {2}: (7, {})} | custom-call | flops 805306368 | bytes 7340032 | tf_op jit(solution)/shard_map/scores/pallas_call | solution.py:105
  75.9 2.2 %scores.15 = (f32[8,1024,512]{2,1,0:T(8,128)S(1)}, bf16[4096,768]{1,0:T(8,128)(2,1)S(1)}, f32[8,1,512]{2,1,0:T(1,128)S(1)}) custom-call(s32[2]{0:T(128)S(1)} %pad_add_fusion.ids, bf16[512,768]{1,0:T(8,128)(2,1)S(1)} %collective-permute-done.6.refs_0_, ...), custom_call_target="tpu_custom_call", output_to_operand_aliasing={{0}: (5, {}), {1}: (6, {}), {2}: (7, {})} | custom-call | flops 805306368 | bytes 7340032 | tf_op jit(solution)/shard_map/scores/pallas_call | solution.py:105
  79.5 2.5 %collective-permute-start.17 = (f32[8,1,512]{2,1,0:T(1,128)S(1)}, f32[8,1,512]{2,1,0:T(1,128)S(1)}, u32[]{:S(2)}, u32[]{:S(2)}) collective-permute-start(f32[8,1,512]{2,1,0:T(1,128)S(1)} %add.26.refs_0_), channel_id=1, source_target_pairs={{0,16},{8,24},{16,0},{24,8},{1,17},{9,25},{17,1},{25,9},{2,18},{10... | collective-permute-start | bytes 49160 | tf_op jit(solution)/shard_map/ppermute | solution.py:478
  83.3 5.2 %sums.2 = (f32[1024,768]{1,0:T(8,128)S(1)}, f32[1024,128]{1,0:T(8,128)S(1)}) custom-call(s32[2]{0:T(128)S(1)} %pad_add_fusion.ids, f32[8,1,512]{2,1,0:T(1,128)S(1)} %add.25.refs_0_, f32[8,1,512]{2,1,0:T(1,128)S(1)} %collective-permute-done.11.refs_1_, f32[8,1,512]{2,1,0:T(1,128)S(1)} %collective-permute-done.12.refs_2_, ...), custom_call_target="tpu_custom_call" | custom-call | flops 3221225472 | bytes 14680064 | tf_op jit(solution)/shard_map/sums/pallas_call | solution.py:267
  88.6 5.6 %sums.3 = (bf16[128,768]{1,0:T(8,128)(2,1)S(1)}, f32[144,768]{1,0:T(8,128)S(1)}, f32[128,768]{1,0:T(8,128)S(1)}, bf16[144,768]{1,0:T(8,128)(2,1)S(1)}, bf16[128,...) custom-call(s32[2]{0:T(128)S(1)} %pad_add_fusion.ids, ...), custom_call_target="tpu_custom_call" | custom-call | flops 3221225472 | bytes 14680064 | tf_op jit(solution)/shard_map/sums/pallas_call | solution.py:267
  94.2 1.6 %collective-permute-start.23 = (bf16[144,768]{1,0:T(8,128)(2,1)S(1)}, bf16[144,768]{1,0:T(8,128)(2,1)S(1)}, u32[]{:S(2)}, u32[]{:S(2)}) collective-permute-start(bf16[144,768]{1,0:T(8,128)(2,1)S(1)} %get-tuple-element.141), channel_id=1, source_target_pairs={{0,4},{1,5},{2,6},{3,7},{4,0},{5,1},{6,2},{7,3},{8,12},{9,13},{10,... | collective-permute-start | bytes 663560 | tf_op jit(solution)/shard_map/ppermute | solution.py:406
  97.8 4.8 %collective-permute-done.23.arrived = bf16[144,768]{1,0:T(8,128)(2,1)S(1)} collective-permute-done((bf16[144,768]{1,0:T(8,128)(2,1)S(1)}, bf16[144,768]{1,0:T(8,128)(2,1)S(1)}, u32[]{:S(2)}, u32[]{:S(2)}) %collective-permute-start.23) | collective-permute-done | bytes 221216 | tf_op jit(solution)/shard_map/ppermute | solution.py:406
  102.7 1.6 %collective-permute-start.24 = (bf16[144,768]{1,0:T(8,128)(2,1)S(1)}, bf16[144,768]{1,0:T(8,128)(2,1)S(1)}, u32[]{:S(2)}, u32[]{:S(2)}) collective-permute-start(bf16[144,768]{1,0:T(8,128)(2,1)S(1)} %pass_on.3), channel_id=1, source_target_pairs={{0,2},{1,3},{2,0},{3,1},{4,6},{5,7},{6,4},{7,5},{8,10},{9,11},{10,... | collective-permute-start | bytes 663560 | tf_op jit(solution)/shard_map/ppermute | solution.py:406
  104.8 1.6 %collective-permute-start.22 = (bf16[128,768]{1,0:T(8,128)(2,1)S(1)}, bf16[128,768]{1,0:T(8,128)(2,1)S(1)}, u32[]{:S(2)}, u32[]{:S(2)}) collective-permute-start(bf16[128,768]{1,0:T(8,128)(2,1)S(1)} %pass_on.2), channel_id=1, source_target_pairs={{0,4},{1,5},{2,6},{3,7},{4,0},{5,1},{6,2},{7,3},{8,12},{9,13},{10,... | collective-permute-start | bytes 589832 | tf_op jit(solution)/shard_map/ppermute | solution.py:406
  106.4 5.6 %collective-permute-done.19.refs_0_ = bf16[128,768]{1,0:T(8,128)(2,1)S(1)} collective-permute-done((bf16[128,768]{1,0:T(8,128)(2,1)S(1)}, bf16[128,768]{1,0:T(8,128)(2,1)S(1)}, u32[]{:S(2)}, u32[]{:S(2)}) %collective-permute-start.19) | collective-permute-done | bytes 196640 | tf_op jit(solution)/shard_map/ppermute | solution.py:406
  116.5 3.6 %collective-permute-done.25.refs_0_ = bf16[128,768]{1,0:T(8,128)(2,1)S(1)} collective-permute-done((bf16[128,768]{1,0:T(8,128)(2,1)S(1)}, bf16[128,768]{1,0:T(8,128)(2,1)S(1)}, u32[]{:S(2)}, u32[]{:S(2)}) %collective-permute-start.25) | collective-permute-done | bytes 196640 | tf_op jit(solution)/shard_map/ppermute | solution.py:406
  123.1 1.7 %collective-permute-done.26.refs_1_ = bf16[144,768]{1,0:T(8,128)(2,1)S(1)} collective-permute-done((bf16[144,768]{1,0:T(8,128)(2,1)S(1)}, bf16[144,768]{1,0:T(8,128)(2,1)S(1)}, u32[]{:S(2)}, u32[]{:S(2)}) %collective-permute-start.26) | collective-permute-done | bytes 221216 | tf_op jit(solution)/shard_map/ppermute | solution.py:406
  126.9 2.9 %collective-permute-done.29.refs_0_ = bf16[128,768]{1,0:T(8,128)(2,1)S(1)} collective-permute-done((bf16[128,768]{1,0:T(8,128)(2,1)S(1)}, bf16[128,768]{1,0:T(8,128)(2,1)S(1)}, u32[]{:S(2)}, u32[]{:S(2)}) %collective-permute-start.29) | collective-permute-done | bytes 196640 | tf_op jit(solution)/shard_map/ppermute | solution.py:406
  129.8 1.8 %assemble.3 = (f32[2048,768]{1,0:T(8,128)}, f32[8,1,256]{2,1,0:T(1,128)}) custom-call(s32[2]{0:T(128)S(1)} %pad_add_fusion.ids, bf16[128,768]{1,0:T(8,128)(2,1)S(1)} %get-tuple-element.142.refs_0_, bf16[144,768]{1,0:T(8,128)(2,1)S(1)} %get-tuple-element.143.refs_1_, bf16[128,768]{1,0:T(8,128)(2,1)S(1)} %collective-permute-done.35.refs_2_, ...), custom_call_target="tpu_custom_call" | custom-call | tf_op jit(solution)/shard_map/assemble/pallas_call | solution.py:370
  132.4 2.8 %assemble.4 = (f32[2048,768]{1,0:T(8,128)}, f32[8,1,256]{2,1,0:T(1,128)}) custom-call(s32[2]{0:T(128)S(1)} %pad_add_fusion.ids, bf16[128,768]{1,0:T(8,128)(2,1)S(1)} %collective-permute-done.25.refs_0_, bf16[144,768]{1,0:T(8,128)(2,1)S(1)} %collective-permute-done.26.refs_1_, ...), custom_call_target="tpu_custom_call", output_to_operand_aliasing={{0}: (9, {}), {1}: (10, {})} | custom-call | tf_op jit(solution)/shard_map/assemble/pallas_call | solution.py:370
  135.1 1.8 %assemble.5 = (f32[2048,768]{1,0:T(8,128)}, f32[8,1,256]{2,1,0:T(1,128)}) custom-call(s32[2]{0:T(128)S(1)} %pad_add_fusion.ids, bf16[128,768]{1,0:T(8,128)(2,1)S(1)} %collective-permute-done.29.refs_0_, bf16[144,768]{1,0:T(8,128)(2,1)S(1)} %collective-permute-done.30.refs_1_, ...), custom_call_target="tpu_custom_call", output_to_operand_aliasing={{0}: (5, {}), {1}: (6, {})} | custom-call | tf_op jit(solution)/shard_map/assemble/pallas_call | solution.py:370
  (72 shorter events, 27.2 us)
Async XLA Ops:
  0.6 12.5 %collective-permute-start.3 = (bf16[512,768]{1,0:T(8,128)(2,1)}, bf16[512,768]{1,0:T(8,128)(2,1)}, u32[]{:S(2)}, u32[]{:S(2)}) collective-permute-start(bf16[512,768]{1,0:T(8,128)(2,1)} %refs_0_.1), channel_id=1, source_target_pairs={{0,1},{1,0},{2,3},{3,2},{4,5},{5,4},{6,7},{7,6},{8,9},{9,8},{10,11... | collective-permute-start | bytes 2359304 | tf_op jit(solution)/shard_map/ppermute | solution.py:412
  1.1 21.1 %collective-permute-start.2 = (bf16[512,768]{1,0:T(8,128)(2,1)}, bf16[512,768]{1,0:T(8,128)(2,1)}, u32[]{:S(2)}, u32[]{:S(2)}) collective-permute-start(bf16[512,768]{1,0:T(8,128)(2,1)} %refs_0_.1), channel_id=1, source_target_pairs={{8,0},{0,8},{24,16},{16,24},{9,1},{1,9},{25,17},{17,25},{10,2},{2,... | collective-permute-start | bytes 2359304 | tf_op jit(solution)/shard_map/ppermute | solution.py:430
  3.8 19.2 %collective-permute-start = (bf16[512,768]{1,0:T(8,128)(2,1)}, bf16[512,768]{1,0:T(8,128)(2,1)}, u32[]{:S(2)}, u32[]{:S(2)}) collective-permute-start(bf16[512,768]{1,0:T(8,128)(2,1)} %refs_0_.1), channel_id=1, source_target_pairs={{16,8},{8,16},{17,9},{9,17},{18,10},{10,18},{19,11},{11,19},{20,12... | collective-permute-start | bytes 2359304 | tf_op jit(solution)/shard_map/ppermute | solution.py:430
  22.2 6.0 %collective-permute-start.5 = (bf16[512,768]{1,0:T(8,128)(2,1)}, bf16[512,768]{1,0:T(8,128)(2,1)S(1)}, u32[]{:S(2)}, u32[]{:S(2)}) collective-permute-start(bf16[512,768]{1,0:T(8,128)(2,1)} %collective-permute-done.2.refs_0_), channel_id=1, source_target_pairs={{0,1},{1,0},{2,3},{3,2},{4,5},{5,4},{6,7},{7,6},{8,9},{9,8},{10,11... | collective-permute-start | bytes 2359304 | tf_op jit(solution)/shard_map/ppermute | solution.py:412
  22.3 8.2 %collective-permute-start.4 = (bf16[512,768]{1,0:T(8,128)(2,1)}, bf16[512,768]{1,0:T(8,128)(2,1)S(1)}, u32[]{:S(2)}, u32[]{:S(2)}) collective-permute-start(bf16[512,768]{1,0:T(8,128)(2,1)} %collective-permute-done.2.refs_0_), channel_id=1, source_target_pairs={{16,8},{8,16},{17,9},{9,17},{18,10},{10,18},{19,11},{11,19},{20,12... | collective-permute-start | bytes 2359304 | tf_op jit(solution)/shard_map/ppermute | solution.py:430
  23.0 23.9 %collective-permute-start.1 = (bf16[512,768]{1,0:T(8,128)(2,1)}, bf16[512,768]{1,0:T(8,128)(2,1)S(1)}, u32[]{:S(2)}, u32[]{:S(2)}) collective-permute-start(bf16[512,768]{1,0:T(8,128)(2,1)} %collective-permute-done.refs_0_), channel_id=1, source_target_pairs={{8,0},{16,24},{9,1},{17,25},{10,2},{18,26},{11,3},{19,27},{12,4},{... | collective-permute-start | bytes 2359304 | tf_op jit(solution)/shard_map/ppermute | solution.py:430
  24.3 28.0 %collective-permute-start.8 = (bf16[512,768]{1,0:T(8,128)(2,1)}, bf16[512,768]{1,0:T(8,128)(2,1)S(1)}, u32[]{:S(2)}, u32[]{:S(2)}) collective-permute-start(bf16[512,768]{1,0:T(8,128)(2,1)} %collective-permute-done.refs_0_), channel_id=1, source_target_pairs={{8,9},{9,8},{10,11},{11,10},{12,13},{13,12},{14,15},{15,14},{16,17... | collective-permute-start | bytes 2359304 | tf_op jit(solution)/shard_map/ppermute | solution.py:412
  46.9 5.4 %collective-permute-start.9 = (bf16[512,768]{1,0:T(8,128)(2,1)S(1)}, bf16[512,768]{1,0:T(8,128)(2,1)S(1)}, u32[]{:S(2)}, u32[]{:S(2)}) collective-permute-start(bf16[512,768]{1,0:T(8,128)(2,1)S(1)} %collective-permute-done.1.refs_1_), channel_id=1, source_target_pairs={{0,1},{1,0},{2,3},{3,2},{4,5},{5,4},{6,7},{7,6},{24,25},{25,24},{2... | collective-permute-start | bytes 2359304 | tf_op jit(solution)/shard_map/ppermute | solution.py:412
  48.8 22.9 %collective-permute-start.7 = (bf16[512,768]{1,0:T(8,128)(2,1)S(1)}, bf16[512,768]{1,0:T(8,128)(2,1)S(1)}, u32[]{:S(2)}, u32[]{:S(2)}) collective-permute-start(bf16[512,768]{1,0:T(8,128)(2,1)S(1)} %collective-permute-done.4.refs_0_), channel_id=1, source_target_pairs={{8,0},{16,24},{9,1},{17,25},{10,2},{18,26},{11,3},{19,27},{12,4},{... | collective-permute-start | bytes 2359304 | tf_op jit(solution)/shard_map/ppermute | solution.py:430
  55.9 7.7 %collective-permute-start.11 = (f32[8,1,512]{2,1,0:T(1,128)S(1)}, f32[8,1,512]{2,1,0:T(1,128)S(1)}, u32[]{:S(2)}, u32[]{:S(2)}) collective-permute-start(f32[8,1,512]{2,1,0:T(1,128)S(1)} %add.25.refs_0_), channel_id=1, source_target_pairs={{0,8},{8,16},{16,24},{24,0},{1,9},{9,17},{17,25},{25,1},{2,10},{10... | collective-permute-start | bytes 49160 | tf_op jit(solution)/shard_map/ppermute | solution.py:478
  59.6 4.7 %collective-permute-start.12 = (f32[8,1,512]{2,1,0:T(1,128)S(1)}, f32[8,1,512]{2,1,0:T(1,128)S(1)}, u32[]{:S(2)}, u32[]{:S(2)}) collective-permute-start(f32[8,1,512]{2,1,0:T(1,128)S(1)} %add.25.refs_0_), channel_id=1, source_target_pairs={{0,16},{8,24},{16,0},{24,8},{1,17},{9,25},{17,1},{25,9},{2,18},{10... | collective-permute-start | bytes 49160 | tf_op jit(solution)/shard_map/ppermute | solution.py:478
  60.1 11.6 %collective-permute-start.13 = (f32[8,1,512]{2,1,0:T(1,128)S(1)}, f32[8,1,512]{2,1,0:T(1,128)S(1)}, u32[]{:S(2)}, u32[]{:S(2)}) collective-permute-start(f32[8,1,512]{2,1,0:T(1,128)S(1)} %add.25.refs_0_), channel_id=1, source_target_pairs={{0,24},{8,0},{16,8},{24,16},{1,25},{9,1},{17,9},{25,17},{2,26},{10... | collective-permute-start | bytes 49160 | tf_op jit(solution)/shard_map/ppermute | solution.py:478
  63.0 12.9 %collective-permute-start.6 = (bf16[512,768]{1,0:T(8,128)(2,1)S(1)}, bf16[512,768]{1,0:T(8,128)(2,1)S(1)}, u32[]{:S(2)}, u32[]{:S(2)}) collective-permute-start(bf16[512,768]{1,0:T(8,128)(2,1)S(1)} %collective-permute-done.4.refs_0_), channel_id=1, source_target_pairs={{8,9},{9,8},{10,11},{11,10},{12,13},{13,12},{14,15},{15,14},{16,17... | collective-permute-start | bytes 2359304 | tf_op jit(solution)/shard_map/ppermute | solution.py:412
  79.5 9.1 %collective-permute-start.16 = (f32[8,1,512]{2,1,0:T(1,128)S(1)}, f32[8,1,512]{2,1,0:T(1,128)S(1)}, u32[]{:S(2)}, u32[]{:S(2)}) collective-permute-start(f32[8,1,512]{2,1,0:T(1,128)S(1)} %add.26.refs_0_), channel_id=1, source_target_pairs={{0,8},{8,16},{16,24},{24,0},{1,9},{9,17},{17,25},{25,1},{2,10},{10... | collective-permute-start | bytes 49160 | tf_op jit(solution)/shard_map/ppermute | solution.py:478
  79.5 9.1 %collective-permute-start.17 = (f32[8,1,512]{2,1,0:T(1,128)S(1)}, f32[8,1,512]{2,1,0:T(1,128)S(1)}, u32[]{:S(2)}, u32[]{:S(2)}) collective-permute-start(f32[8,1,512]{2,1,0:T(1,128)S(1)} %add.26.refs_0_), channel_id=1, source_target_pairs={{0,16},{8,24},{16,0},{24,8},{1,17},{9,25},{17,1},{25,9},{2,18},{10... | collective-permute-start | bytes 49160 | tf_op jit(solution)/shard_map/ppermute | solution.py:478
  82.0 6.6 %collective-permute-start.18 = (f32[8,1,512]{2,1,0:T(1,128)S(1)}, f32[8,1,512]{2,1,0:T(1,128)S(1)}, u32[]{:S(2)}, u32[]{:S(2)}) collective-permute-start(f32[8,1,512]{2,1,0:T(1,128)S(1)} %add.26.refs_0_), channel_id=1, source_target_pairs={{0,24},{8,0},{16,8},{24,16},{1,25},{9,1},{17,9},{25,17},{2,26},{10... | collective-permute-start | bytes 49160 | tf_op jit(solution)/shard_map/ppermute | solution.py:478
  94.2 8.4 %collective-permute-start.23 = (bf16[144,768]{1,0:T(8,128)(2,1)S(1)}, bf16[144,768]{1,0:T(8,128)(2,1)S(1)}, u32[]{:S(2)}, u32[]{:S(2)}) collective-permute-start(bf16[144,768]{1,0:T(8,128)(2,1)S(1)} %get-tuple-element.141), channel_id=1, source_target_pairs={{0,4},{1,5},{2,6},{3,7},{4,0},{5,1},{6,2},{7,3},{8,12},{9,13},{10,... | collective-permute-start | bytes 663560 | tf_op jit(solution)/shard_map/ppermute | solution.py:406
  95.8 8.9 %collective-permute-start.21 = (bf16[128,768]{1,0:T(8,128)(2,1)S(1)}, bf16[128,768]{1,0:T(8,128)(2,1)S(1)}, u32[]{:S(2)}, u32[]{:S(2)}) collective-permute-start(bf16[128,768]{1,0:T(8,128)(2,1)S(1)} %get-tuple-element.139), channel_id=1, source_target_pairs={{0,2},{1,3},{2,0},{3,1},{4,6},{5,7},{6,4},{7,5},{8,10},{9,11},{10,... | collective-permute-start | bytes 589832 | tf_op jit(solution)/shard_map/ppermute | solution.py:406
  97.3 14.7 %collective-permute-start.20 = (bf16[144,768]{1,0:T(8,128)(2,1)S(1)}, bf16[144,768]{1,0:T(8,128)(2,1)S(1)}, u32[]{:S(2)}, u32[]{:S(2)}) collective-permute-start(bf16[144,768]{1,0:T(8,128)(2,1)S(1)} %get-tuple-element.137), channel_id=1, source_target_pairs={{0,4},{1,5},{2,6},{3,7},{4,0},{5,1},{6,2},{7,3},{8,12},{9,13},{10,... | collective-permute-start | bytes 663560 | tf_op jit(solution)/shard_map/ppermute | solution.py:406
  102.7 9.3 %collective-permute-start.24 = (bf16[144,768]{1,0:T(8,128)(2,1)S(1)}, bf16[144,768]{1,0:T(8,128)(2,1)S(1)}, u32[]{:S(2)}, u32[]{:S(2)}) collective-permute-start(bf16[144,768]{1,0:T(8,128)(2,1)S(1)} %pass_on.3), channel_id=1, source_target_pairs={{0,2},{1,3},{2,0},{3,1},{4,6},{5,7},{6,4},{7,5},{8,10},{9,11},{10,... | collective-permute-start | bytes 663560 | tf_op jit(solution)/shard_map/ppermute | solution.py:406
  104.3 7.7 %collective-permute-start.19 = (bf16[128,768]{1,0:T(8,128)(2,1)S(1)}, bf16[128,768]{1,0:T(8,128)(2,1)S(1)}, u32[]{:S(2)}, u32[]{:S(2)}) collective-permute-start(bf16[128,768]{1,0:T(8,128)(2,1)S(1)} %get-tuple-element.136), channel_id=1, source_target_pairs={{0,2},{1,3},{2,0},{3,1},{4,6},{5,7},{6,4},{7,5},{8,10},{9,11},{10,... | collective-permute-start | bytes 589832 | tf_op jit(solution)/shard_map/ppermute | solution.py:406
  104.8 7.2 %collective-permute-start.22 = (bf16[128,768]{1,0:T(8,128)(2,1)S(1)}, bf16[128,768]{1,0:T(8,128)(2,1)S(1)}, u32[]{:S(2)}, u32[]{:S(2)}) collective-permute-start(bf16[128,768]{1,0:T(8,128)(2,1)S(1)} %pass_on.2), channel_id=1, source_target_pairs={{0,4},{1,5},{2,6},{3,7},{4,0},{5,1},{6,2},{7,3},{8,12},{9,13},{10,... | collective-permute-start | bytes 589832 | tf_op jit(solution)/shard_map/ppermute | solution.py:406
  112.3 7.8 %collective-permute-start.25 = (bf16[128,768]{1,0:T(8,128)(2,1)S(1)}, bf16[128,768]{1,0:T(8,128)(2,1)S(1)}, u32[]{:S(2)}, u32[]{:S(2)}) collective-permute-start(bf16[128,768]{1,0:T(8,128)(2,1)S(1)} %get-tuple-element.142.refs_0_), channel_id=1, source_target_pairs={{0,2},{1,3},{2,0},{3,1},{4,6},{5,7},{6,4},{7,5},{8,10},{9,11},{10,... | collective-permute-start | bytes 589832 | tf_op jit(solution)/shard_map/ppermute | solution.py:406
  113.9 8.3 %collective-permute-start.28 = (bf16[144,768]{1,0:T(8,128)(2,1)S(1)}, bf16[144,768]{1,0:T(8,128)(2,1)S(1)}, u32[]{:S(2)}, u32[]{:S(2)}) collective-permute-start(bf16[144,768]{1,0:T(8,128)(2,1)S(1)} %get-tuple-element.143.refs_1_), channel_id=1, source_target_pairs={{0,4},{1,5},{2,6},{3,7},{4,0},{5,1},{6,2},{7,3},{8,12},{9,13},{10,... | collective-permute-start | bytes 663560 | tf_op jit(solution)/shard_map/ppermute | solution.py:406
  115.4 9.4 %collective-permute-start.26 = (bf16[144,768]{1,0:T(8,128)(2,1)S(1)}, bf16[144,768]{1,0:T(8,128)(2,1)S(1)}, u32[]{:S(2)}, u32[]{:S(2)}) collective-permute-start(bf16[144,768]{1,0:T(8,128)(2,1)S(1)} %get-tuple-element.143.refs_1_), channel_id=1, source_target_pairs={{0,2},{1,3},{2,0},{3,1},{4,6},{5,7},{6,4},{7,5},{8,10},{9,11},{10,... | collective-permute-start | bytes 663560 | tf_op jit(solution)/shard_map/ppermute | solution.py:406
  116.0 10.4 %collective-permute-start.36 = (bf16[144,768]{1,0:T(8,128)(2,1)S(1)}, bf16[144,768]{1,0:T(8,128)(2,1)S(1)}, u32[]{:S(2)}, u32[]{:S(2)}) collective-permute-start(bf16[144,768]{1,0:T(8,128)(2,1)S(1)} %get-tuple-element.143.refs_1_), channel_id=1, source_target_pairs={{0,1},{1,0},{2,3},{3,2},{4,5},{5,4},{6,7},{7,6},{8,9},{9,8},{10,11... | collective-permute-start | bytes 663560 | tf_op jit(solution)/shard_map/ppermute | solution.py:406
  116.0 10.4 %collective-permute-start.27 = (bf16[128,768]{1,0:T(8,128)(2,1)S(1)}, bf16[128,768]{1,0:T(8,128)(2,1)S(1)}, u32[]{:S(2)}, u32[]{:S(2)}) collective-permute-start(bf16[128,768]{1,0:T(8,128)(2,1)S(1)} %get-tuple-element.142.refs_0_), channel_id=1, source_target_pairs={{0,4},{1,5},{2,6},{3,7},{4,0},{5,1},{6,2},{7,3},{8,12},{9,13},{10,... | collective-permute-start | bytes 589832 | tf_op jit(solution)/shard_map/ppermute | solution.py:406
  120.1 9.7 %collective-permute-start.29 = (bf16[128,768]{1,0:T(8,128)(2,1)S(1)}, bf16[128,768]{1,0:T(8,128)(2,1)S(1)}, u32[]{:S(2)}, u32[]{:S(2)}) collective-permute-start(bf16[128,768]{1,0:T(8,128)(2,1)S(1)} %collective-permute-done.25.refs_0_), channel_id=1, source_target_pairs={{0,4},{1,5},{2,6},{3,7},{4,0},{5,1},{6,2},{7,3},{8,12},{9,13},{10,... | collective-permute-start | bytes 589832 | tf_op jit(solution)/shard_map/ppermute | solution.py:406
  122.2 9.5 %collective-permute-start.30 = (bf16[144,768]{1,0:T(8,128)(2,1)S(1)}, bf16[144,768]{1,0:T(8,128)(2,1)S(1)}, u32[]{:S(2)}, u32[]{:S(2)}) collective-permute-start(bf16[144,768]{1,0:T(8,128)(2,1)S(1)} %collective-permute-done.28.refs_3_), channel_id=1, source_target_pairs={{0,2},{1,3},{2,0},{3,1},{4,6},{5,7},{6,4},{7,5},{8,10},{9,11},{10,... | collective-permute-start | bytes 663560 | tf_op jit(solution)/shard_map/ppermute | solution.py:406
  124.8 6.8 %collective-permute-start.32 = (bf16[144,768]{1,0:T(8,128)(2,1)S(1)}, bf16[144,768]{1,0:T(8,128)(2,1)S(1)}, u32[]{:S(2)}, u32[]{:S(2)}) collective-permute-start(bf16[144,768]{1,0:T(8,128)(2,1)S(1)} %collective-permute-done.26.refs_1_), channel_id=1, source_target_pairs={{0,1},{1,0},{2,3},{3,2},{4,5},{5,4},{6,7},{7,6},{8,9},{9,8},{10,11... | collective-permute-start | bytes 663560 | tf_op jit(solution)/shard_map/ppermute | solution.py:406
  126.4 5.3 %collective-permute-start.34 = (bf16[144,768]{1,0:T(8,128)(2,1)S(1)}, bf16[144,768]{1,0:T(8,128)(2,1)S(1)}, u32[]{:S(2)}, u32[]{:S(2)}) collective-permute-start(bf16[144,768]{1,0:T(8,128)(2,1)S(1)} %collective-permute-done.28.refs_3_), channel_id=1, source_target_pairs={{0,1},{1,0},{2,3},{3,2},{4,5},{5,4},{6,7},{7,6},{8,9},{9,8},{10,11... | collective-permute-start | bytes 663560 | tf_op jit(solution)/shard_map/ppermute | solution.py:406
  126.4 5.3 %collective-permute-start.31 = (bf16[128,768]{1,0:T(8,128)(2,1)S(1)}, bf16[128,768]{1,0:T(8,128)(2,1)S(1)}, u32[]{:S(2)}, u32[]{:S(2)}) collective-permute-start(bf16[128,768]{1,0:T(8,128)(2,1)S(1)} %collective-permute-done.25.refs_0_), channel_id=1, source_target_pairs={{0,1},{1,0},{2,3},{3,2},{4,5},{5,4},{6,7},{7,6},{8,9},{9,8},{10,11... | collective-permute-start | bytes 589832 | tf_op jit(solution)/shard_map/ppermute | solution.py:406
  (8 other events, 19.9 us)

commit v9 on v8

--- a/solution.py
+++ b/solution.py
@@ -340,50 +340,53 @@
     )(mine, masses, *arrived)
 
 
-def assemble_kernel(factor, n_pieces, ids, *refs):
-    units, weights = refs[-2:]
-    size = units.shape[0]
+def assemble_kernel(factor, spots, half, ids, *refs):
+    units, weights, wide, light, sems = refs[-5:]
+    size = wide.shape[1]
     upper = size // 2
-    for number in range(n_pieces):
-
-        @pl.when(pl.program_id(0) == number)
-        def _():
-            first, second = refs[2 * number : 2 * number + 2]
-            units[:upper, :] = first[...].astype(jnp.float32)
-            units[upper:, :] = second[: size - upper, :].astype(jnp.float32)
-            weights[0] = one_row(second[size - upper :, :], size) * factor
+    copies = []
+    for number, (flip, away) in enumerate(spots):
+        first, second = refs[2 * number : 2 * number + 2]
+        wide[number, :upper, :] = first[...].astype(jnp.float32)
+        wide[number, upper:, :] = second[: size - upper, :].astype(jnp.float32)
+        light[number] = one_row(second[size - upper :, :], size) * factor
+        block = ((ids[1] % CORES) ^ flip) * half + ((ids[1] // CORES) ^ away)
+        place = pl.ds(pl.multiple_of(block * size, size), size)
+        copies.append(
+            pltpu.make_async_copy(wide.at[number], units.at[place], sems.at[2 * number])
+        )
+        copies.append(
+            pltpu.make_async_copy(light.at[number], weights.at[block], sems.at[2 * number + 1])
+        )
+        copies[-2].start()
+        copies[-1].start()
+    for copy in copies:
+        copy.wait()
 
 
 def assemble(ids, pieces, carried, n_blocks, factor):
     arrays = [array for _, _, halves in pieces for array in halves]
     depth = arrays[0].shape[1]
     size = arrays[0].shape[0] + arrays[1].shape[0] - EXTRA
-    half = n_blocks // CORES
-    flips = [flip for flip, _, _ in pieces]
-    aways = [away for _, away, _ in pieces]
-
-    def block(t, s):
-        return ((s[1] % CORES) ^ pick(t, flips)) * half + ((s[1] // CORES) ^ pick(t, aways))
-
+    spots = [(flip, away) for flip, away, _ in pieces]
     extra = carried or ()
-    aliases = {1 + len(arrays) + n: n for n in range(len(extra))}
+    anywhere = pl.BlockSpec(memory_space=pl.ANY)
     return pl.pallas_call(
-        functools.partial(assemble_kernel, factor, len(pieces)),
-        grid_spec=pltpu.PrefetchScalarGridSpec(
-            num_scalar_prefetch=1,
-            grid=(len(pieces),),
-            in_specs=[pl.BlockSpec(array.shape, lambda t, s: (0, 0)) for array in arrays]
-            + [pl.BlockSpec(memory_space=pl.ANY) for _ in extra],
-            out_specs=[
-                pl.BlockSpec((size, depth), lambda t, s: (block(t, s), 0)),
-                pl.BlockSpec((1, 1, size), lambda t, s: (block(t, s), 0, 0)),
-            ],
-        ),
+        functools.partial(assemble_kernel, factor, spots, n_blocks // CORES),
+        in_specs=[pl.BlockSpec(memory_space=pltpu.SMEM)]
+        + [pl.BlockSpec(memory_space=pltpu.VMEM)] * len(arrays)
+        + [anywhere] * len(extra),
+        out_specs=[anywhere, anywhere],
         out_shape=[
             jax.ShapeDtypeStruct((n_blocks * size, depth), jnp.float32),
             jax.ShapeDtypeStruct((n_blocks, 1, size), jnp.float32),
         ],
-        input_output_aliases=aliases,
+        scratch_shapes=[
+            pltpu.VMEM((len(pieces), size, depth), jnp.float32),
+            pltpu.VMEM((len(pieces), 1, size), jnp.float32),
+            pltpu.SemaphoreType.DMA((2 * len(pieces),)),
+        ],
+        input_output_aliases={1 + len(arrays) + n: n for n in range(len(extra))},
         compiler_params=pltpu.CompilerParams(vmem_limit_bytes=VMEM_LIMIT),
         name="assemble",
     )(ids, *arrays, *extra)

time: 137 us -> 137 us (level)
  no operation moved by 1% of the time
where the time goes in v9:
time: 137 us
  waiting for transfers between devices  52.9 us (39%)
  starting transfers between devices  40.4 us (29%)
  Pallas kernels  36.6 us (27%)
  other arithmetic  4.32 us (3%)
    ppermute x22, waiting for transfers between devices, exchange(): lax.ppermute(array, 'rows', [(i, i ^ distance) for i in range(n_rows)])  22.4 us
    ppermute x5, waiting for transfers between devices, start_ready(): lax.ppermute(slots[source_slot][hold][0], 'blk', pairs)  22.3 us
    pallas_call x8, Pallas kernels, score_block(): pl.pallas_call(functools.partial(score_kernel, n_sources, choice), grid_s...  19.5 us
    ppermute x22, starting transfers between devices, exchange(): lax.ppermute(array, 'rows', [(i, i ^ distance) for i in range(n_rows)])  16.2 us
    ppermute x6, starting transfers between devices, totals_of(): lax.ppermute(both, 'blk', [(i, (i + turn) % n_places) for i in range(n_pl...  10.9 us
    pallas_call x2, Pallas kernels, sum_rows(): pl.pallas_call(functools.partial(sum_kernel, plan, len(totals), n_owners,...  10.8 us
    ppermute x6, waiting for transfers between devices, totals_of(): lax.ppermute(both, 'blk', [(i, (i + turn) % n_places) for i in range(n_pl...  8.05 us
    ppermute x5, starting transfers between devices, start_ready(): lax.ppermute(slots[source_slot][hold][0], 'blk', pairs)  7.5 us
  transfers between devices with their start and end apart: 39, of which 14 were waited for; matrix products, arithmetic and copies ran while one was open for 3% of the time, Pallas kernels for 20%

profile of v9, /device:TPU:0, one launch (start us, length us, event | category | flops | bytes accessed | tf_op | source)
XLA Modules:
  0.0 136.6 jit_solution(12828442621701693578)
XLA Ops:
  1.1 2.7 %collective-permute-start.2 = (bf16[512,768]{1,0:T(8,128)(2,1)}, bf16[512,768]{1,0:T(8,128)(2,1)}, u32[]{:S(2)}, u32[]{:S(2)}) collective-permute-start(bf16[512,768]{1,0:T(8,128)(2,1)} %refs_0_.1), channel_id=1, source_target_pairs={{8,0},{0,8},{24,16},{16,24},{9,1},{1,9},{25,17},{17,25},{10,2},{2,... | collective-permute-start | bytes 2359304 | tf_op jit(solution)/shard_map/ppermute | solution.py:433
  6.1 1.8 %fusion = f32[1024]{0:T(1024)S(1)} fusion(bf16[2048,768]{1,0:T(8,128)(2,1)} %param.4, s32[]{:T(128)S(6)} %select_n.4), kind=kLoop, calls=%fused_computation.2 | loop fusion | flops 2358272 | bytes 1576964 | tf_op jit(solution)/shard_map/reduce_sum | solution.py:21
  7.9 1.7 %fusion.1.refs_1_.refs_2_ = bf16[1024,768]{1,0:T(8,128)(2,1)S(1)} fusion(f32[1024]{0:T(1024)S(1)} %add_rsqrt_fusion, bf16[2048,768]{1,0:T(8,128)(2,1)} %param.4, s32[]{:T(128)S(6)} %select_n.4), kind=kLoop, calls=%fused_computation.3 | loop fusion | flops 2359296 | bytes 3149828 | tf_op jit(solution)/shard_map/convert_element_type | solution.py:21
  11.0 2.2 %scores.8 = (f32[8,1024,512]{2,1,0:T(8,128)S(1)}, bf16[4096,768]{1,0:T(8,128)(2,1)S(1)}, f32[8,1,512]{2,1,0:T(1,128)S(1)}) custom-call(s32[2]{0:T(128)S(1)} %pad_add_fusion.ids, bf16[512,768]{1,0:T(8,128)(2,1)S(1)} %copy-done, bf16[1024,768]{1,0:T(8,128)(2,1)S(1)} %fusion.1.refs_1_.refs_2_, f32[1024,128]{1,0:T(8,128)S(1)} %broadcast_in_dim.2.refs_2_.refs_3_), custom_call_target="tpu_custom_call" | custom-call | flops 805306368 | bytes 7340032 | tf_op jit(solution)/shard_map/scores/pallas_call | solution.py:105
  13.2 3.2 %scores.9 = (f32[8,1024,512]{2,1,0:T(8,128)S(1)}, bf16[4096,768]{1,0:T(8,128)(2,1)S(1)}, f32[8,1,512]{2,1,0:T(1,128)S(1)}) custom-call(s32[2]{0:T(128)S(1)} %pad_add_fusion.ids, bf16[512,768]{1,0:T(8,128)(2,1)} %collective-permute-done.3.refs_0_, ...), custom_call_target="tpu_custom_call", output_to_operand_aliasing={{0}: (4, {}), {1}: (5, {}), {2}: (6, {})} | custom-call | flops 805306368 | bytes 7340032 | tf_op jit(solution)/shard_map/scores/pallas_call | solution.py:105
  16.4 5.8 %collective-permute-done.2.refs_0_ = bf16[512,768]{1,0:T(8,128)(2,1)} collective-permute-done((bf16[512,768]{1,0:T(8,128)(2,1)}, bf16[512,768]{1,0:T(8,128)(2,1)}, u32[]{:S(2)}, u32[]{:S(2)}) %collective-permute-start.2) | collective-permute-done | bytes 786464 | tf_op jit(solution)/shard_map/ppermute | solution.py:433
  25.0 3.2 %scores.10 = (f32[8,1024,512]{2,1,0:T(8,128)S(1)}, bf16[4096,768]{1,0:T(8,128)(2,1)S(1)}, f32[8,1,512]{2,1,0:T(1,128)S(1)}) custom-call(s32[2]{0:T(128)S(1)} %pad_add_fusion.ids, bf16[512,768]{1,0:T(8,128)(2,1)} %collective-permute-done.2.refs_0_, ...), custom_call_target="tpu_custom_call", output_to_operand_aliasing={{0}: (4, {}), {1}: (5, {}), {2}: (6, {})} | custom-call | flops 805306368 | bytes 7340032 | tf_op jit(solution)/shard_map/scores/pallas_call | solution.py:105
  28.2 2.2 %scores.11 = (f32[8,1024,512]{2,1,0:T(8,128)S(1)}, bf16[4096,768]{1,0:T(8,128)(2,1)S(1)}, f32[8,1,512]{2,1,0:T(1,128)S(1)}) custom-call(s32[2]{0:T(128)S(1)} %pad_add_fusion.ids, bf16[512,768]{1,0:T(8,128)(2,1)S(1)} %collective-permute-done.5.refs_0_, ...), custom_call_target="tpu_custom_call", output_to_operand_aliasing={{0}: (4, {}), {1}: (5, {}), {2}: (6, {})} | custom-call | flops 805306368 | bytes 7340032 | tf_op jit(solution)/shard_map/scores/pallas_call | solution.py:105
  30.4 16.5 %collective-permute-done.1.refs_1_ = bf16[512,768]{1,0:T(8,128)(2,1)S(1)} collective-permute-done((bf16[512,768]{1,0:T(8,128)(2,1)}, bf16[512,768]{1,0:T(8,128)(2,1)S(1)}, u32[]{:S(2)}, u32[]{:S(2)}) %collective-permute-start.1) | collective-permute-done | bytes 786464 | tf_op jit(solution)/shard_map/ppermute | solution.py:433
  46.9 1.9 %collective-permute-start.9 = (bf16[512,768]{1,0:T(8,128)(2,1)S(1)}, bf16[512,768]{1,0:T(8,128)(2,1)S(1)}, u32[]{:S(2)}, u32[]{:S(2)}) collective-permute-start(bf16[512,768]{1,0:T(8,128)(2,1)S(1)} %collective-permute-done.1.refs_1_), channel_id=1, source_target_pairs={{0,1},{1,0},{2,3},{3,2},{4,5},{5,4},{6,7},{7,6},{24,25},{25,24},{2... | collective-permute-start | bytes 2359304 | tf_op jit(solution)/shard_map/ppermute | solution.py:415
  50.1 2.2 %scores.12 = (f32[8,1024,512]{2,1,0:T(8,128)S(1)}, bf16[4096,768]{1,0:T(8,128)(2,1)S(1)}, f32[8,1,512]{2,1,0:T(1,128)S(1)}) custom-call(s32[2]{0:T(128)S(1)} %pad_add_fusion.ids, bf16[512,768]{1,0:T(8,128)(2,1)} %collective-permute-done.refs_0_, ...), custom_call_target="tpu_custom_call", output_to_operand_aliasing={{0}: (5, {}), {1}: (6, {}), {2}: (7, {})} | custom-call | flops 805306368 | bytes 7340032 | tf_op jit(solution)/shard_map/scores/pallas_call | solution.py:105
  52.3 2.2 %scores.13 = (f32[8,1024,512]{2,1,0:T(8,128)S(1)}, bf16[4096,768]{1,0:T(8,128)(2,1)S(1)}, f32[8,1,512]{2,1,0:T(1,128)S(1)}) custom-call(s32[2]{0:T(128)S(1)} %pad_add_fusion.ids, bf16[512,768]{1,0:T(8,128)(2,1)S(1)} %collective-permute-done.8.refs_0_, ...), custom_call_target="tpu_custom_call", output_to_operand_aliasing={{0}: (5, {}), {1}: (6, {}), {2}: (7, {})} | custom-call | flops 805306368 | bytes 7340032 | tf_op jit(solution)/shard_map/scores/pallas_call | solution.py:105
  55.9 3.7 %collective-permute-start.11 = (f32[8,1,512]{2,1,0:T(1,128)S(1)}, f32[8,1,512]{2,1,0:T(1,128)S(1)}, u32[]{:S(2)}, u32[]{:S(2)}) collective-permute-start(f32[8,1,512]{2,1,0:T(1,128)S(1)} %add.25.refs_0_), channel_id=1, source_target_pairs={{0,8},{8,16},{16,24},{24,0},{1,9},{9,17},{17,25},{25,1},{2,10},{10... | collective-permute-start | bytes 49160 | tf_op jit(solution)/shard_map/ppermute | solution.py:481
  60.1 2.8 %collective-permute-start.13 = (f32[8,1,512]{2,1,0:T(1,128)S(1)}, f32[8,1,512]{2,1,0:T(1,128)S(1)}, u32[]{:S(2)}, u32[]{:S(2)}) collective-permute-start(f32[8,1,512]{2,1,0:T(1,128)S(1)} %add.25.refs_0_), channel_id=1, source_target_pairs={{0,24},{8,0},{16,8},{24,16},{1,25},{9,1},{17,9},{25,17},{2,26},{10... | collective-permute-start | bytes 49160 | tf_op jit(solution)/shard_map/ppermute | solution.py:481
  64.4 7.4 %collective-permute-done.13.refs_3_ = f32[8,1,512]{2,1,0:T(1,128)S(1)} collective-permute-done((f32[8,1,512]{2,1,0:T(1,128)S(1)}, f32[8,1,512]{2,1,0:T(1,128)S(1)}, u32[]{:S(2)}, u32[]{:S(2)}) %collective-permute-start.13) | collective-permute-done | bytes 16416 | tf_op jit(solution)/shard_map/ppermute | solution.py:481
  71.7 1.9 %collective-permute-start.14 = (bf16[512,768]{1,0:T(8,128)(2,1)S(1)}, bf16[512,768]{1,0:T(8,128)(2,1)S(1)}, u32[]{:S(2)}, u32[]{:S(2)}) collective-permute-start(bf16[512,768]{1,0:T(8,128)(2,1)S(1)} %collective-permute-done.7.refs_1_), channel_id=1, source_target_pairs={{0,1},{1,0},{2,3},{3,2},{4,5},{5,4},{6,7},{7,6},{24,25},{25,24},{2... | collective-permute-start | bytes 2359304 | tf_op jit(solution)/shard_map/ppermute | solution.py:415
  73.6 2.2 %scores.14 = (f32[8,1024,512]{2,1,0:T(8,128)S(1)}, bf16[4096,768]{1,0:T(8,128)(2,1)S(1)}, f32[8,1,512]{2,1,0:T(1,128)S(1)}) custom-call(s32[2]{0:T(128)S(1)} %pad_add_fusion.ids, bf16[512,768]{1,0:T(8,128)(2,1)S(1)} %collective-permute-done.4.refs_0_, ...), custom_call_target="tpu_custom_call", output_to_operand_aliasing={{0}: (5, {}), {1}: (6, {}), {2}: (7, {})} | custom-call | flops 805306368 | bytes 7340032 | tf_op jit(solution)/shard_map/scores/pallas_call | solution.py:105
  75.9 2.2 %scores.15 = (f32[8,1024,512]{2,1,0:T(8,128)S(1)}, bf16[4096,768]{1,0:T(8,128)(2,1)S(1)}, f32[8,1,512]{2,1,0:T(1,128)S(1)}) custom-call(s32[2]{0:T(128)S(1)} %pad_add_fusion.ids, bf16[512,768]{1,0:T(8,128)(2,1)S(1)} %collective-permute-done.6.refs_0_, ...), custom_call_target="tpu_custom_call", output_to_operand_aliasing={{0}: (5, {}), {1}: (6, {}), {2}: (7, {})} | custom-call | flops 805306368 | bytes 7340032 | tf_op jit(solution)/shard_map/scores/pallas_call | solution.py:105
  79.5 2.5 %collective-permute-start.17 = (f32[8,1,512]{2,1,0:T(1,128)S(1)}, f32[8,1,512]{2,1,0:T(1,128)S(1)}, u32[]{:S(2)}, u32[]{:S(2)}) collective-permute-start(f32[8,1,512]{2,1,0:T(1,128)S(1)} %add.26.refs_0_), channel_id=1, source_target_pairs={{0,16},{8,24},{16,0},{24,8},{1,17},{9,25},{17,1},{25,9},{2,18},{10... | collective-permute-start | bytes 49160 | tf_op jit(solution)/shard_map/ppermute | solution.py:481
  83.3 5.2 %sums.2 = (f32[1024,768]{1,0:T(8,128)S(1)}, f32[1024,128]{1,0:T(8,128)S(1)}) custom-call(s32[2]{0:T(128)S(1)} %pad_add_fusion.ids, f32[8,1,512]{2,1,0:T(1,128)S(1)} %add.25.refs_0_, f32[8,1,512]{2,1,0:T(1,128)S(1)} %collective-permute-done.11.refs_1_, f32[8,1,512]{2,1,0:T(1,128)S(1)} %collective-permute-done.12.refs_2_, ...), custom_call_target="tpu_custom_call" | custom-call | flops 3221225472 | bytes 14680064 | tf_op jit(solution)/shard_map/sums/pallas_call | solution.py:267
  88.6 5.6 %sums.3 = (bf16[128,768]{1,0:T(8,128)(2,1)S(1)}, f32[144,768]{1,0:T(8,128)S(1)}, f32[128,768]{1,0:T(8,128)S(1)}, bf16[144,768]{1,0:T(8,128)(2,1)S(1)}, bf16[128,...) custom-call(s32[2]{0:T(128)S(1)} %pad_add_fusion.ids, ...), custom_call_target="tpu_custom_call" | custom-call | flops 3221225472 | bytes 14680064 | tf_op jit(solution)/shard_map/sums/pallas_call | solution.py:267
  94.2 1.6 %collective-permute-start.23 = (bf16[144,768]{1,0:T(8,128)(2,1)S(1)}, bf16[144,768]{1,0:T(8,128)(2,1)S(1)}, u32[]{:S(2)}, u32[]{:S(2)}) collective-permute-start(bf16[144,768]{1,0:T(8,128)(2,1)S(1)} %get-tuple-element.141), channel_id=1, source_target_pairs={{0,4},{1,5},{2,6},{3,7},{4,0},{5,1},{6,2},{7,3},{8,12},{9,13},{10,... | collective-permute-start | bytes 663560 | tf_op jit(solution)/shard_map/ppermute | solution.py:409
  97.8 4.8 %collective-permute-done.23.arrived = bf16[144,768]{1,0:T(8,128)(2,1)S(1)} collective-permute-done((bf16[144,768]{1,0:T(8,128)(2,1)S(1)}, bf16[144,768]{1,0:T(8,128)(2,1)S(1)}, u32[]{:S(2)}, u32[]{:S(2)}) %collective-permute-start.23) | collective-permute-done | bytes 221216 | tf_op jit(solution)/shard_map/ppermute | solution.py:409
  102.7 1.6 %collective-permute-start.24 = (bf16[144,768]{1,0:T(8,128)(2,1)S(1)}, bf16[144,768]{1,0:T(8,128)(2,1)S(1)}, u32[]{:S(2)}, u32[]{:S(2)}) collective-permute-start(bf16[144,768]{1,0:T(8,128)(2,1)S(1)} %pass_on.3), channel_id=1, source_target_pairs={{0,2},{1,3},{2,0},{3,1},{4,6},{5,7},{6,4},{7,5},{8,10},{9,11},{10,... | collective-permute-start | bytes 663560 | tf_op jit(solution)/shard_map/ppermute | solution.py:409
  104.8 1.6 %collective-permute-start.22 = (bf16[128,768]{1,0:T(8,128)(2,1)S(1)}, bf16[128,768]{1,0:T(8,128)(2,1)S(1)}, u32[]{:S(2)}, u32[]{:S(2)}) collective-permute-start(bf16[128,768]{1,0:T(8,128)(2,1)S(1)} %pass_on.2), channel_id=1, source_target_pairs={{0,4},{1,5},{2,6},{3,7},{4,0},{5,1},{6,2},{7,3},{8,12},{9,13},{10,... | collective-permute-start | bytes 589832 | tf_op jit(solution)/shard_map/ppermute | solution.py:409
  106.4 5.6 %collective-permute-done.19.refs_0_ = bf16[128,768]{1,0:T(8,128)(2,1)S(1)} collective-permute-done((bf16[128,768]{1,0:T(8,128)(2,1)S(1)}, bf16[128,768]{1,0:T(8,128)(2,1)S(1)}, u32[]{:S(2)}, u32[]{:S(2)}) %collective-permute-start.19) | collective-permute-done | bytes 196640 | tf_op jit(solution)/shard_map/ppermute | solution.py:409
  116.5 3.6 %collective-permute-done.25.refs_0_ = bf16[128,768]{1,0:T(8,128)(2,1)S(1)} collective-permute-done((bf16[128,768]{1,0:T(8,128)(2,1)S(1)}, bf16[128,768]{1,0:T(8,128)(2,1)S(1)}, u32[]{:S(2)}, u32[]{:S(2)}) %collective-permute-start.25) | collective-permute-done | bytes 196640 | tf_op jit(solution)/shard_map/ppermute | solution.py:409
  123.1 1.7 %collective-permute-done.26.refs_1_ = bf16[144,768]{1,0:T(8,128)(2,1)S(1)} collective-permute-done((bf16[144,768]{1,0:T(8,128)(2,1)S(1)}, bf16[144,768]{1,0:T(8,128)(2,1)S(1)}, u32[]{:S(2)}, u32[]{:S(2)}) %collective-permute-start.26) | collective-permute-done | bytes 221216 | tf_op jit(solution)/shard_map/ppermute | solution.py:409
  126.9 2.9 %collective-permute-done.29.refs_0_ = bf16[128,768]{1,0:T(8,128)(2,1)S(1)} collective-permute-done((bf16[128,768]{1,0:T(8,128)(2,1)S(1)}, bf16[128,768]{1,0:T(8,128)(2,1)S(1)}, u32[]{:S(2)}, u32[]{:S(2)}) %collective-permute-start.29) | collective-permute-done | bytes 196640 | tf_op jit(solution)/shard_map/ppermute | solution.py:409
  129.8 1.8 %assemble.3 = (f32[2048,768]{1,0:T(8,128)}, f32[8,1,256]{2,1,0:T(1,128)}) custom-call(s32[2]{0:T(128)S(1)} %pad_add_fusion.ids, bf16[128,768]{1,0:T(8,128)(2,1)S(1)} %get-tuple-element.142.refs_0_, bf16[144,768]{1,0:T(8,128)(2,1)S(1)} %get-tuple-element.143.refs_1_, bf16[128,768]{1,0:T(8,128)(2,1)S(1)} %collective-permute-done.35.refs_2_, ...), custom_call_target="tpu_custom_call" | custom-call | tf_op jit(solution)/shard_map/assemble/pallas_call | solution.py:374
  132.3 2.3 %assemble.4 = (f32[2048,768]{1,0:T(8,128)}, f32[8,1,256]{2,1,0:T(1,128)}) custom-call(s32[2]{0:T(128)S(1)} %pad_add_fusion.ids, bf16[128,768]{1,0:T(8,128)(2,1)S(1)} %collective-permute-done.25.refs_0_, bf16[144,768]{1,0:T(8,128)(2,1)S(1)} %collective-permute-done.26.refs_1_, ...), custom_call_target="tpu_custom_call", output_to_operand_aliasing={{0}: (9, {}), {1}: (10, {})} | custom-call | tf_op jit(solution)/shard_map/assemble/pallas_call | solution.py:374
  134.7 1.8 %assemble.5 = (f32[2048,768]{1,0:T(8,128)}, f32[8,1,256]{2,1,0:T(1,128)}) custom-call(s32[2]{0:T(128)S(1)} %pad_add_fusion.ids, bf16[128,768]{1,0:T(8,128)(2,1)S(1)} %collective-permute-done.29.refs_0_, bf16[144,768]{1,0:T(8,128)(2,1)S(1)} %collective-permute-done.30.refs_1_, ...), custom_call_target="tpu_custom_call", output_to_operand_aliasing={{0}: (5, {}), {1}: (6, {})} | custom-call | tf_op jit(solution)/shard_map/assemble/pallas_call | solution.py:374
  (72 shorter events, 27.2 us)
Async XLA Ops:
  0.6 12.5 %collective-permute-start.3 = (bf16[512,768]{1,0:T(8,128)(2,1)}, bf16[512,768]{1,0:T(8,128)(2,1)}, u32[]{:S(2)}, u32[]{:S(2)}) collective-permute-start(bf16[512,768]{1,0:T(8,128)(2,1)} %refs_0_.1), channel_id=1, source_target_pairs={{0,1},{1,0},{2,3},{3,2},{4,5},{5,4},{6,7},{7,6},{8,9},{9,8},{10,11... | collective-permute-start | bytes 2359304 | tf_op jit(solution)/shard_map/ppermute | solution.py:415
  1.1 21.1 %collective-permute-start.2 = (bf16[512,768]{1,0:T(8,128)(2,1)}, bf16[512,768]{1,0:T(8,128)(2,1)}, u32[]{:S(2)}, u32[]{:S(2)}) collective-permute-start(bf16[512,768]{1,0:T(8,128)(2,1)} %refs_0_.1), channel_id=1, source_target_pairs={{8,0},{0,8},{24,16},{16,24},{9,1},{1,9},{25,17},{17,25},{10,2},{2,... | collective-permute-start | bytes 2359304 | tf_op jit(solution)/shard_map/ppermute | solution.py:433
  3.8 19.2 %collective-permute-start = (bf16[512,768]{1,0:T(8,128)(2,1)}, bf16[512,768]{1,0:T(8,128)(2,1)}, u32[]{:S(2)}, u32[]{:S(2)}) collective-permute-start(bf16[512,768]{1,0:T(8,128)(2,1)} %refs_0_.1), channel_id=1, source_target_pairs={{16,8},{8,16},{17,9},{9,17},{18,10},{10,18},{19,11},{11,19},{20,12... | collective-permute-start | bytes 2359304 | tf_op jit(solution)/shard_map/ppermute | solution.py:433
  22.2 6.0 %collective-permute-start.5 = (bf16[512,768]{1,0:T(8,128)(2,1)}, bf16[512,768]{1,0:T(8,128)(2,1)S(1)}, u32[]{:S(2)}, u32[]{:S(2)}) collective-permute-start(bf16[512,768]{1,0:T(8,128)(2,1)} %collective-permute-done.2.refs_0_), channel_id=1, source_target_pairs={{0,1},{1,0},{2,3},{3,2},{4,5},{5,4},{6,7},{7,6},{8,9},{9,8},{10,11... | collective-permute-start | bytes 2359304 | tf_op jit(solution)/shard_map/ppermute | solution.py:415
  22.3 8.2 %collective-permute-start.4 = (bf16[512,768]{1,0:T(8,128)(2,1)}, bf16[512,768]{1,0:T(8,128)(2,1)S(1)}, u32[]{:S(2)}, u32[]{:S(2)}) collective-permute-start(bf16[512,768]{1,0:T(8,128)(2,1)} %collective-permute-done.2.refs_0_), channel_id=1, source_target_pairs={{16,8},{8,16},{17,9},{9,17},{18,10},{10,18},{19,11},{11,19},{20,12... | collective-permute-start | bytes 2359304 | tf_op jit(solution)/shard_map/ppermute | solution.py:433
  23.0 23.9 %collective-permute-start.1 = (bf16[512,768]{1,0:T(8,128)(2,1)}, bf16[512,768]{1,0:T(8,128)(2,1)S(1)}, u32[]{:S(2)}, u32[]{:S(2)}) collective-permute-start(bf16[512,768]{1,0:T(8,128)(2,1)} %collective-permute-done.refs_0_), channel_id=1, source_target_pairs={{8,0},{16,24},{9,1},{17,25},{10,2},{18,26},{11,3},{19,27},{12,4},{... | collective-permute-start | bytes 2359304 | tf_op jit(solution)/shard_map/ppermute | solution.py:433
  24.3 28.0 %collective-permute-start.8 = (bf16[512,768]{1,0:T(8,128)(2,1)}, bf16[512,768]{1,0:T(8,128)(2,1)S(1)}, u32[]{:S(2)}, u32[]{:S(2)}) collective-permute-start(bf16[512,768]{1,0:T(8,128)(2,1)} %collective-permute-done.refs_0_), channel_id=1, source_target_pairs={{8,9},{9,8},{10,11},{11,10},{12,13},{13,12},{14,15},{15,14},{16,17... | collective-permute-start | bytes 2359304 | tf_op jit(solution)/shard_map/ppermute | solution.py:415
  46.9 5.4 %collective-permute-start.9 = (bf16[512,768]{1,0:T(8,128)(2,1)S(1)}, bf16[512,768]{1,0:T(8,128)(2,1)S(1)}, u32[]{:S(2)}, u32[]{:S(2)}) collective-permute-start(bf16[512,768]{1,0:T(8,128)(2,1)S(1)} %collective-permute-done.1.refs_1_), channel_id=1, source_target_pairs={{0,1},{1,0},{2,3},{3,2},{4,5},{5,4},{6,7},{7,6},{24,25},{25,24},{2... | collective-permute-start | bytes 2359304 | tf_op jit(solution)/shard_map/ppermute | solution.py:415
  48.8 22.9 %collective-permute-start.7 = (bf16[512,768]{1,0:T(8,128)(2,1)S(1)}, bf16[512,768]{1,0:T(8,128)(2,1)S(1)}, u32[]{:S(2)}, u32[]{:S(2)}) collective-permute-start(bf16[512,768]{1,0:T(8,128)(2,1)S(1)} %collective-permute-done.4.refs_0_), channel_id=1, source_target_pairs={{8,0},{16,24},{9,1},{17,25},{10,2},{18,26},{11,3},{19,27},{12,4},{... | collective-permute-start | bytes 2359304 | tf_op jit(solution)/shard_map/ppermute | solution.py:433
  55.9 7.7 %collective-permute-start.11 = (f32[8,1,512]{2,1,0:T(1,128)S(1)}, f32[8,1,512]{2,1,0:T(1,128)S(1)}, u32[]{:S(2)}, u32[]{:S(2)}) collective-permute-start(f32[8,1,512]{2,1,0:T(1,128)S(1)} %add.25.refs_0_), channel_id=1, source_target_pairs={{0,8},{8,16},{16,24},{24,0},{1,9},{9,17},{17,25},{25,1},{2,10},{10... | collective-permute-start | bytes 49160 | tf_op jit(solution)/shard_map/ppermute | solution.py:481
  59.6 4.7 %collective-permute-start.12 = (f32[8,1,512]{2,1,0:T(1,128)S(1)}, f32[8,1,512]{2,1,0:T(1,128)S(1)}, u32[]{:S(2)}, u32[]{:S(2)}) collective-permute-start(f32[8,1,512]{2,1,0:T(1,128)S(1)} %add.25.refs_0_), channel_id=1, source_target_pairs={{0,16},{8,24},{16,0},{24,8},{1,17},{9,25},{17,1},{25,9},{2,18},{10... | collective-permute-start | bytes 49160 | tf_op jit(solution)/shard_map/ppermute | solution.py:481
  60.1 11.6 %collective-permute-start.13 = (f32[8,1,512]{2,1,0:T(1,128)S(1)}, f32[8,1,512]{2,1,0:T(1,128)S(1)}, u32[]{:S(2)}, u32[]{:S(2)}) collective-permute-start(f32[8,1,512]{2,1,0:T(1,128)S(1)} %add.25.refs_0_), channel_id=1, source_target_pairs={{0,24},{8,0},{16,8},{24,16},{1,25},{9,1},{17,9},{25,17},{2,26},{10... | collective-permute-start | bytes 49160 | tf_op jit(solution)/shard_map/ppermute | solution.py:481
  63.0 12.9 %collective-permute-start.6 = (bf16[512,768]{1,0:T(8,128)(2,1)S(1)}, bf16[512,768]{1,0:T(8,128)(2,1)S(1)}, u32[]{:S(2)}, u32[]{:S(2)}) collective-permute-start(bf16[512,768]{1,0:T(8,128)(2,1)S(1)} %collective-permute-done.4.refs_0_), channel_id=1, source_target_pairs={{8,9},{9,8},{10,11},{11,10},{12,13},{13,12},{14,15},{15,14},{16,17... | collective-permute-start | bytes 2359304 | tf_op jit(solution)/shard_map/ppermute | solution.py:415
  79.5 9.1 %collective-permute-start.16 = (f32[8,1,512]{2,1,0:T(1,128)S(1)}, f32[8,1,512]{2,1,0:T(1,128)S(1)}, u32[]{:S(2)}, u32[]{:S(2)}) collective-permute-start(f32[8,1,512]{2,1,0:T(1,128)S(1)} %add.26.refs_0_), channel_id=1, source_target_pairs={{0,8},{8,16},{16,24},{24,0},{1,9},{9,17},{17,25},{25,1},{2,10},{10... | collective-permute-start | bytes 49160 | tf_op jit(solution)/shard_map/ppermute | solution.py:481
  79.5 9.1 %collective-permute-start.17 = (f32[8,1,512]{2,1,0:T(1,128)S(1)}, f32[8,1,512]{2,1,0:T(1,128)S(1)}, u32[]{:S(2)}, u32[]{:S(2)}) collective-permute-start(f32[8,1,512]{2,1,0:T(1,128)S(1)} %add.26.refs_0_), channel_id=1, source_target_pairs={{0,16},{8,24},{16,0},{24,8},{1,17},{9,25},{17,1},{25,9},{2,18},{10... | collective-permute-start | bytes 49160 | tf_op jit(solution)/shard_map/ppermute | solution.py:481
  82.0 6.6 %collective-permute-start.18 = (f32[8,1,512]{2,1,0:T(1,128)S(1)}, f32[8,1,512]{2,1,0:T(1,128)S(1)}, u32[]{:S(2)}, u32[]{:S(2)}) collective-permute-start(f32[8,1,512]{2,1,0:T(1,128)S(1)} %add.26.refs_0_), channel_id=1, source_target_pairs={{0,24},{8,0},{16,8},{24,16},{1,25},{9,1},{17,9},{25,17},{2,26},{10... | collective-permute-start | bytes 49160 | tf_op jit(solution)/shard_map/ppermute | solution.py:481
  94.2 8.4 %collective-permute-start.23 = (bf16[144,768]{1,0:T(8,128)(2,1)S(1)}, bf16[144,768]{1,0:T(8,128)(2,1)S(1)}, u32[]{:S(2)}, u32[]{:S(2)}) collective-permute-start(bf16[144,768]{1,0:T(8,128)(2,1)S(1)} %get-tuple-element.141), channel_id=1, source_target_pairs={{0,4},{1,5},{2,6},{3,7},{4,0},{5,1},{6,2},{7,3},{8,12},{9,13},{10,... | collective-permute-start | bytes 663560 | tf_op jit(solution)/shard_map/ppermute | solution.py:409
  95.8 8.9 %collective-permute-start.21 = (bf16[128,768]{1,0:T(8,128)(2,1)S(1)}, bf16[128,768]{1,0:T(8,128)(2,1)S(1)}, u32[]{:S(2)}, u32[]{:S(2)}) collective-permute-start(bf16[128,768]{1,0:T(8,128)(2,1)S(1)} %get-tuple-element.139), channel_id=1, source_target_pairs={{0,2},{1,3},{2,0},{3,1},{4,6},{5,7},{6,4},{7,5},{8,10},{9,11},{10,... | collective-permute-start | bytes 589832 | tf_op jit(solution)/shard_map/ppermute | solution.py:409
  97.3 14.7 %collective-permute-start.20 = (bf16[144,768]{1,0:T(8,128)(2,1)S(1)}, bf16[144,768]{1,0:T(8,128)(2,1)S(1)}, u32[]{:S(2)}, u32[]{:S(2)}) collective-permute-start(bf16[144,768]{1,0:T(8,128)(2,1)S(1)} %get-tuple-element.137), channel_id=1, source_target_pairs={{0,4},{1,5},{2,6},{3,7},{4,0},{5,1},{6,2},{7,3},{8,12},{9,13},{10,... | collective-permute-start | bytes 663560 | tf_op jit(solution)/shard_map/ppermute | solution.py:409
  102.7 9.3 %collective-permute-start.24 = (bf16[144,768]{1,0:T(8,128)(2,1)S(1)}, bf16[144,768]{1,0:T(8,128)(2,1)S(1)}, u32[]{:S(2)}, u32[]{:S(2)}) collective-permute-start(bf16[144,768]{1,0:T(8,128)(2,1)S(1)} %pass_on.3), channel_id=1, source_target_pairs={{0,2},{1,3},{2,0},{3,1},{4,6},{5,7},{6,4},{7,5},{8,10},{9,11},{10,... | collective-permute-start | bytes 663560 | tf_op jit(solution)/shard_map/ppermute | solution.py:409
  104.3 7.7 %collective-permute-start.19 = (bf16[128,768]{1,0:T(8,128)(2,1)S(1)}, bf16[128,768]{1,0:T(8,128)(2,1)S(1)}, u32[]{:S(2)}, u32[]{:S(2)}) collective-permute-start(bf16[128,768]{1,0:T(8,128)(2,1)S(1)} %get-tuple-element.136), channel_id=1, source_target_pairs={{0,2},{1,3},{2,0},{3,1},{4,6},{5,7},{6,4},{7,5},{8,10},{9,11},{10,... | collective-permute-start | bytes 589832 | tf_op jit(solution)/shard_map/ppermute | solution.py:409
  104.8 7.2 %collective-permute-start.22 = (bf16[128,768]{1,0:T(8,128)(2,1)S(1)}, bf16[128,768]{1,0:T(8,128)(2,1)S(1)}, u32[]{:S(2)}, u32[]{:S(2)}) collective-permute-start(bf16[128,768]{1,0:T(8,128)(2,1)S(1)} %pass_on.2), channel_id=1, source_target_pairs={{0,4},{1,5},{2,6},{3,7},{4,0},{5,1},{6,2},{7,3},{8,12},{9,13},{10,... | collective-permute-start | bytes 589832 | tf_op jit(solution)/shard_map/ppermute | solution.py:409
  112.3 7.8 %collective-permute-start.25 = (bf16[128,768]{1,0:T(8,128)(2,1)S(1)}, bf16[128,768]{1,0:T(8,128)(2,1)S(1)}, u32[]{:S(2)}, u32[]{:S(2)}) collective-permute-start(bf16[128,768]{1,0:T(8,128)(2,1)S(1)} %get-tuple-element.142.refs_0_), channel_id=1, source_target_pairs={{0,2},{1,3},{2,0},{3,1},{4,6},{5,7},{6,4},{7,5},{8,10},{9,11},{10,... | collective-permute-start | bytes 589832 | tf_op jit(solution)/shard_map/ppermute | solution.py:409
  113.9 8.3 %collective-permute-start.28 = (bf16[144,768]{1,0:T(8,128)(2,1)S(1)}, bf16[144,768]{1,0:T(8,128)(2,1)S(1)}, u32[]{:S(2)}, u32[]{:S(2)}) collective-permute-start(bf16[144,768]{1,0:T(8,128)(2,1)S(1)} %get-tuple-element.143.refs_1_), channel_id=1, source_target_pairs={{0,4},{1,5},{2,6},{3,7},{4,0},{5,1},{6,2},{7,3},{8,12},{9,13},{10,... | collective-permute-start | bytes 663560 | tf_op jit(solution)/shard_map/ppermute | solution.py:409
  115.4 9.4 %collective-permute-start.26 = (bf16[144,768]{1,0:T(8,128)(2,1)S(1)}, bf16[144,768]{1,0:T(8,128)(2,1)S(1)}, u32[]{:S(2)}, u32[]{:S(2)}) collective-permute-start(bf16[144,768]{1,0:T(8,128)(2,1)S(1)} %get-tuple-element.143.refs_1_), channel_id=1, source_target_pairs={{0,2},{1,3},{2,0},{3,1},{4,6},{5,7},{6,4},{7,5},{8,10},{9,11},{10,... | collective-permute-start | bytes 663560 | tf_op jit(solution)/shard_map/ppermute | solution.py:409
  116.0 10.4 %collective-permute-start.36 = (bf16[144,768]{1,0:T(8,128)(2,1)S(1)}, bf16[144,768]{1,0:T(8,128)(2,1)S(1)}, u32[]{:S(2)}, u32[]{:S(2)}) collective-permute-start(bf16[144,768]{1,0:T(8,128)(2,1)S(1)} %get-tuple-element.143.refs_1_), channel_id=1, source_target_pairs={{0,1},{1,0},{2,3},{3,2},{4,5},{5,4},{6,7},{7,6},{8,9},{9,8},{10,11... | collective-permute-start | bytes 663560 | tf_op jit(solution)/shard_map/ppermute | solution.py:409
  116.0 10.4 %collective-permute-start.27 = (bf16[128,768]{1,0:T(8,128)(2,1)S(1)}, bf16[128,768]{1,0:T(8,128)(2,1)S(1)}, u32[]{:S(2)}, u32[]{:S(2)}) collective-permute-start(bf16[128,768]{1,0:T(8,128)(2,1)S(1)} %get-tuple-element.142.refs_0_), channel_id=1, source_target_pairs={{0,4},{1,5},{2,6},{3,7},{4,0},{5,1},{6,2},{7,3},{8,12},{9,13},{10,... | collective-permute-start | bytes 589832 | tf_op jit(solution)/shard_map/ppermute | solution.py:409
  120.1 9.7 %collective-permute-start.29 = (bf16[128,768]{1,0:T(8,128)(2,1)S(1)}, bf16[128,768]{1,0:T(8,128)(2,1)S(1)}, u32[]{:S(2)}, u32[]{:S(2)}) collective-permute-start(bf16[128,768]{1,0:T(8,128)(2,1)S(1)} %collective-permute-done.25.refs_0_), channel_id=1, source_target_pairs={{0,4},{1,5},{2,6},{3,7},{4,0},{5,1},{6,2},{7,3},{8,12},{9,13},{10,... | collective-permute-start | bytes 589832 | tf_op jit(solution)/shard_map/ppermute | solution.py:409
  122.2 9.5 %collective-permute-start.30 = (bf16[144,768]{1,0:T(8,128)(2,1)S(1)}, bf16[144,768]{1,0:T(8,128)(2,1)S(1)}, u32[]{:S(2)}, u32[]{:S(2)}) collective-permute-start(bf16[144,768]{1,0:T(8,128)(2,1)S(1)} %collective-permute-done.28.refs_3_), channel_id=1, source_target_pairs={{0,2},{1,3},{2,0},{3,1},{4,6},{5,7},{6,4},{7,5},{8,10},{9,11},{10,... | collective-permute-start | bytes 663560 | tf_op jit(solution)/shard_map/ppermute | solution.py:409
  124.8 6.8 %collective-permute-start.32 = (bf16[144,768]{1,0:T(8,128)(2,1)S(1)}, bf16[144,768]{1,0:T(8,128)(2,1)S(1)}, u32[]{:S(2)}, u32[]{:S(2)}) collective-permute-start(bf16[144,768]{1,0:T(8,128)(2,1)S(1)} %collective-permute-done.26.refs_1_), channel_id=1, source_target_pairs={{0,1},{1,0},{2,3},{3,2},{4,5},{5,4},{6,7},{7,6},{8,9},{9,8},{10,11... | collective-permute-start | bytes 663560 | tf_op jit(solution)/shard_map/ppermute | solution.py:409
  126.4 5.3 %collective-permute-start.34 = (bf16[144,768]{1,0:T(8,128)(2,1)S(1)}, bf16[144,768]{1,0:T(8,128)(2,1)S(1)}, u32[]{:S(2)}, u32[]{:S(2)}) collective-permute-start(bf16[144,768]{1,0:T(8,128)(2,1)S(1)} %collective-permute-done.28.refs_3_), channel_id=1, source_target_pairs={{0,1},{1,0},{2,3},{3,2},{4,5},{5,4},{6,7},{7,6},{8,9},{9,8},{10,11... | collective-permute-start | bytes 663560 | tf_op jit(solution)/shard_map/ppermute | solution.py:409
  126.4 5.2 %collective-permute-start.31 = (bf16[128,768]{1,0:T(8,128)(2,1)S(1)}, bf16[128,768]{1,0:T(8,128)(2,1)S(1)}, u32[]{:S(2)}, u32[]{:S(2)}) collective-permute-start(bf16[128,768]{1,0:T(8,128)(2,1)S(1)} %collective-permute-done.25.refs_0_), channel_id=1, source_target_pairs={{0,1},{1,0},{2,3},{3,2},{4,5},{5,4},{6,7},{7,6},{8,9},{9,8},{10,11... | collective-permute-start | bytes 589832 | tf_op jit(solution)/shard_map/ppermute | solution.py:409
  (8 other events, 19.0 us)

commit v10 on v9

--- a/solution.py
+++ b/solution.py
@@ -13,7 +13,7 @@
 LANES = 128
 CORES = 2
 EXTRA = 16
-VMEM_LIMIT = 20 * 1024 * 1024
+VMEM_LIMIT = 16 * 1024 * 1024
 
 
 def to_unit(values):
@@ -89,7 +89,7 @@
 def score_block(ids, sources, choice, blocks, who, units, offsets, carried, column, n_columns):
     part, depth = sources[0].shape
     count = units.shape[0]
-    tile = math.gcd(count, 512)
+    tile = math.gcd(count, 1024)
     shapes = (
         jax.ShapeDtypeStruct((n_columns, count, part), jnp.float32),
         jax.ShapeDtypeStruct((n_columns * part, depth), jnp.bfloat16),
@@ -550,6 +550,9 @@
         ]
     swap = lambda halves: tuple(exchange(array, 1) for array in halves)
     done = assemble(ids, [(0, 0, payload), (1, 0, swap(payload))], None, n_rows, factor)
+    if n_owners == 4:
+        last_half, done = lax.optimization_barrier((second[1], done))
+        far[1] = (2, (last_half, first[1]))
     swapped = [swap(halves) for _, halves in far[:-1]]
     arrays, swapped, done = lax.optimization_barrier(
         ([halves for _, halves in far], swapped, done)

time: 137 us -> 135 us (0.985)
  waiting for transfers between devices: 52.9 us -> 58.2 us
  Pallas kernels: 36.6 us -> 31.7 us
  starting transfers between devices: 40.4 us -> 38.1 us
    pallas_call x8, Pallas kernels: 19.5 us -> 14.7 us  [score_block(): pl.pallas_call(functools.partial(score_kernel, n_sources, choice), grid_s...]
    ppermute x5, waiting for transfers between devices: 22.3 us -> 26.3 us  [start_ready(): lax.ppermute(slots[source_slot][hold][0], 'blk', pairs)]
    ppermute x6, waiting for transfers between devices: 8.05 us -> 9.78 us  [totals_of(): lax.ppermute(both, 'blk', [(i, (i + turn) % n_places) for i in range(n_pl...]
  transfers between devices with their start and end apart: 39 -> 39, of which waited for: 14 -> 14; matrix products, arithmetic and copies ran while one was open for 3% -> 3% of each run, Pallas kernels for 20% -> 17%
where the time goes in v10:
time: 135 us
  waiting for transfers between devices  58.2 us (43%)
  starting transfers between devices  38.1 us (28%)
  Pallas kernels  31.7 us (23%)
  other arithmetic  4.33 us (3%)
    ppermute x5, waiting for transfers between devices, start_ready(): lax.ppermute(slots[source_slot][hold][0], 'blk', pairs)  26.3 us
    ppermute x22, waiting for transfers between devices, exchange(): lax.ppermute(array, 'rows', [(i, i ^ distance) for i in range(n_rows)])  21.8 us
    ppermute x22, starting transfers between devices, exchange(): lax.ppermute(array, 'rows', [(i, i ^ distance) for i in range(n_rows)])  15.9 us
    pallas_call x8, Pallas kernels, score_block(): pl.pallas_call(functools.partial(score_kernel, n_sources, choice), grid_s...  14.7 us
    pallas_call x2, Pallas kernels, sum_rows(): pl.pallas_call(functools.partial(sum_kernel, plan, len(totals), n_owners,...  10.8 us
    ppermute x6, starting transfers between devices, totals_of(): lax.ppermute(both, 'blk', [(i, (i + turn) % n_places) for i in range(n_pl...  9.82 us
    ppermute x6, waiting for transfers between devices, totals_of(): lax.ppermute(both, 'blk', [(i, (i + turn) % n_places) for i in range(n_pl...  9.78 us
    ppermute x5, starting transfers between devices, start_ready(): lax.ppermute(slots[source_slot][hold][0], 'blk', pairs)  6.63 us
  transfers between devices with their start and end apart: 39, of which 14 were waited for; matrix products, arithmetic and copies ran while one was open for 3% of the time, Pallas kernels for 17%

profile of v10, /device:TPU:0, one launch (start us, length us, event | category | flops | bytes accessed | tf_op | source)
XLA Modules:
  0.0 135.0 jit_solution(10776820389996617134)
XLA Ops:
  1.1 2.7 %collective-permute-start.2 = (bf16[512,768]{1,0:T(8,128)(2,1)}, bf16[512,768]{1,0:T(8,128)(2,1)S(1)}, u32[]{:S(2)}, u32[]{:S(2)}) collective-permute-start(bf16[512,768]{1,0:T(8,128)(2,1)} %refs_0_.1), channel_id=1, source_target_pairs={{8,0},{0,8},{24,16},{16,24},{9,1},{1,9},{25,17},{17,25},{10,2},{2,... | collective-permute-start | bytes 2359304 | tf_op jit(solution)/shard_map/ppermute | solution.py:433
  5.3 1.8 %fusion = f32[1024]{0:T(1024)S(1)} fusion(bf16[2048,768]{1,0:T(8,128)(2,1)} %param.4, s32[]{:T(128)S(6)} %select_n.4), kind=kLoop, calls=%fused_computation.2 | loop fusion | flops 2358272 | bytes 1576964 | tf_op jit(solution)/shard_map/reduce_sum | solution.py:21
  7.1 1.7 %fusion.1.refs_1_.refs_2_ = bf16[1024,768]{1,0:T(8,128)(2,1)S(1)} fusion(f32[1024]{0:T(1024)S(1)} %add_rsqrt_fusion, bf16[2048,768]{1,0:T(8,128)(2,1)} %param.4, s32[]{:T(128)S(6)} %select_n.4), kind=kLoop, calls=%fused_computation.3 | loop fusion | flops 2359296 | bytes 3149828 | tf_op jit(solution)/shard_map/convert_element_type | solution.py:21
  10.2 1.8 %scores.8 = (f32[8,1024,512]{2,1,0:T(8,128)S(1)}, bf16[4096,768]{1,0:T(8,128)(2,1)S(1)}, f32[8,1,512]{2,1,0:T(1,128)S(1)}) custom-call(s32[2]{0:T(128)S(1)} %pad_add_fusion.ids, bf16[512,768]{1,0:T(8,128)(2,1)S(1)} %copy-done, bf16[1024,768]{1,0:T(8,128)(2,1)S(1)} %fusion.1.refs_1_.refs_2_, f32[1024,128]{1,0:T(8,128)S(1)} %broadcast_in_dim.2.refs_2_.refs_3_), custom_call_target="tpu_custom_call" | custom-call | flops 805306368 | bytes 7340032 | tf_op jit(solution)/shard_map/scores/pallas_call | solution.py:105
  12.0 1.8 %scores.9 = (f32[8,1024,512]{2,1,0:T(8,128)S(1)}, bf16[4096,768]{1,0:T(8,128)(2,1)S(1)}, f32[8,1,512]{2,1,0:T(1,128)S(1)}) custom-call(s32[2]{0:T(128)S(1)} %pad_add_fusion.ids, bf16[512,768]{1,0:T(8,128)(2,1)S(1)} %collective-permute-done.3.refs_0_, ...), custom_call_target="tpu_custom_call", output_to_operand_aliasing={{0}: (4, {}), {1}: (5, {}), {2}: (6, {})} | custom-call | flops 805306368 | bytes 7340032 | tf_op jit(solution)/shard_map/scores/pallas_call | solution.py:105
  13.9 8.3 %collective-permute-done.2.refs_0_ = bf16[512,768]{1,0:T(8,128)(2,1)S(1)} collective-permute-done((bf16[512,768]{1,0:T(8,128)(2,1)}, bf16[512,768]{1,0:T(8,128)(2,1)S(1)}, u32[]{:S(2)}, u32[]{:S(2)}) %collective-permute-start.2) | collective-permute-done | bytes 786464 | tf_op jit(solution)/shard_map/ppermute | solution.py:433
  24.9 1.8 %scores.10 = (f32[8,1024,512]{2,1,0:T(8,128)S(1)}, bf16[4096,768]{1,0:T(8,128)(2,1)S(1)}, f32[8,1,512]{2,1,0:T(1,128)S(1)}) custom-call(s32[2]{0:T(128)S(1)} %pad_add_fusion.ids, bf16[512,768]{1,0:T(8,128)(2,1)S(1)} %collective-permute-done.2.refs_0_, ...), custom_call_target="tpu_custom_call", output_to_operand_aliasing={{0}: (4, {}), {1}: (5, {}), {2}: (6, {})} | custom-call | flops 805306368 | bytes 7340032 | tf_op jit(solution)/shard_map/scores/pallas_call | solution.py:105
  26.7 1.8 %scores.11 = (f32[8,1024,512]{2,1,0:T(8,128)S(1)}, bf16[4096,768]{1,0:T(8,128)(2,1)S(1)}, f32[8,1,512]{2,1,0:T(1,128)S(1)}) custom-call(s32[2]{0:T(128)S(1)} %pad_add_fusion.ids, bf16[512,768]{1,0:T(8,128)(2,1)S(1)} %collective-permute-done.5.refs_0_, ...), custom_call_target="tpu_custom_call", output_to_operand_aliasing={{0}: (4, {}), {1}: (5, {}), {2}: (6, {})} | custom-call | flops 805306368 | bytes 7340032 | tf_op jit(solution)/shard_map/scores/pallas_call | solution.py:105
  28.6 18.0 %collective-permute-done.1.refs_1_ = bf16[512,768]{1,0:T(8,128)(2,1)S(1)} collective-permute-done((bf16[512,768]{1,0:T(8,128)(2,1)S(1)}, bf16[512,768]{1,0:T(8,128)(2,1)S(1)}, u32[]{:S(2)}, u32[]{:S(2)}) %collective-permute-start.1) | collective-permute-done | bytes 786464 | tf_op jit(solution)/shard_map/ppermute | solution.py:433
  46.6 1.9 %collective-permute-start.9 = (bf16[512,768]{1,0:T(8,128)(2,1)S(1)}, bf16[512,768]{1,0:T(8,128)(2,1)S(1)}, u32[]{:S(2)}, u32[]{:S(2)}) collective-permute-start(bf16[512,768]{1,0:T(8,128)(2,1)S(1)} %collective-permute-done.1.refs_1_), channel_id=1, source_target_pairs={{0,1},{1,0},{2,3},{3,2},{4,5},{5,4},{6,7},{7,6},{24,25},{25,24},{2... | collective-permute-start | bytes 2359304 | tf_op jit(solution)/shard_map/ppermute | solution.py:415
  49.8 1.8 %scores.12 = (f32[8,1024,512]{2,1,0:T(8,128)S(1)}, bf16[4096,768]{1,0:T(8,128)(2,1)S(1)}, f32[8,1,512]{2,1,0:T(1,128)S(1)}) custom-call(s32[2]{0:T(128)S(1)} %pad_add_fusion.ids, bf16[512,768]{1,0:T(8,128)(2,1)S(1)} %collective-permute-done.refs_0_, ...), custom_call_target="tpu_custom_call", output_to_operand_aliasing={{0}: (5, {}), {1}: (6, {}), {2}: (7, {})} | custom-call | flops 805306368 | bytes 7340032 | tf_op jit(solution)/shard_map/scores/pallas_call | solution.py:105
  51.7 1.8 %scores.13 = (f32[8,1024,512]{2,1,0:T(8,128)S(1)}, bf16[4096,768]{1,0:T(8,128)(2,1)S(1)}, f32[8,1,512]{2,1,0:T(1,128)S(1)}) custom-call(s32[2]{0:T(128)S(1)} %pad_add_fusion.ids, bf16[512,768]{1,0:T(8,128)(2,1)S(1)} %collective-permute-done.8.refs_0_, ...), custom_call_target="tpu_custom_call", output_to_operand_aliasing={{0}: (5, {}), {1}: (6, {}), {2}: (7, {})} | custom-call | flops 805306368 | bytes 7340032 | tf_op jit(solution)/shard_map/scores/pallas_call | solution.py:105
  55.0 2.6 %collective-permute-start.11 = (f32[8,1,512]{2,1,0:T(1,128)S(1)}, f32[8,1,512]{2,1,0:T(1,128)S(1)}, u32[]{:S(2)}, u32[]{:S(2)}) collective-permute-start(f32[8,1,512]{2,1,0:T(1,128)S(1)} %add.25.refs_0_), channel_id=1, source_target_pairs={{0,8},{8,16},{16,24},{24,0},{1,9},{9,17},{17,25},{25,1},{2,10},{10... | collective-permute-start | bytes 49160 | tf_op jit(solution)/shard_map/ppermute | solution.py:481
  58.1 2.8 %collective-permute-start.13 = (f32[8,1,512]{2,1,0:T(1,128)S(1)}, f32[8,1,512]{2,1,0:T(1,128)S(1)}, u32[]{:S(2)}, u32[]{:S(2)}) collective-permute-start(f32[8,1,512]{2,1,0:T(1,128)S(1)} %add.25.refs_0_), channel_id=1, source_target_pairs={{0,24},{8,0},{16,8},{24,16},{1,25},{9,1},{17,9},{25,17},{2,26},{10... | collective-permute-start | bytes 49160 | tf_op jit(solution)/shard_map/ppermute | solution.py:481
  62.3 9.1 %collective-permute-done.13.refs_3_ = f32[8,1,512]{2,1,0:T(1,128)S(1)} collective-permute-done((f32[8,1,512]{2,1,0:T(1,128)S(1)}, f32[8,1,512]{2,1,0:T(1,128)S(1)}, u32[]{:S(2)}, u32[]{:S(2)}) %collective-permute-start.13) | collective-permute-done | bytes 16416 | tf_op jit(solution)/shard_map/ppermute | solution.py:481
  71.4 1.9 %collective-permute-start.14 = (bf16[512,768]{1,0:T(8,128)(2,1)S(1)}, bf16[512,768]{1,0:T(8,128)(2,1)S(1)}, u32[]{:S(2)}, u32[]{:S(2)}) collective-permute-start(bf16[512,768]{1,0:T(8,128)(2,1)S(1)} %collective-permute-done.7.refs_1_), channel_id=1, source_target_pairs={{0,1},{1,0},{2,3},{3,2},{4,5},{5,4},{6,7},{7,6},{24,25},{25,24},{2... | collective-permute-start | bytes 2359304 | tf_op jit(solution)/shard_map/ppermute | solution.py:415
  73.3 1.8 %scores.14 = (f32[8,1024,512]{2,1,0:T(8,128)S(1)}, bf16[4096,768]{1,0:T(8,128)(2,1)S(1)}, f32[8,1,512]{2,1,0:T(1,128)S(1)}) custom-call(s32[2]{0:T(128)S(1)} %pad_add_fusion.ids, bf16[512,768]{1,0:T(8,128)(2,1)S(1)} %collective-permute-done.4.refs_0_, ...), custom_call_target="tpu_custom_call", output_to_operand_aliasing={{0}: (5, {}), {1}: (6, {}), {2}: (7, {})} | custom-call | flops 805306368 | bytes 7340032 | tf_op jit(solution)/shard_map/scores/pallas_call | solution.py:105
  75.6 1.8 %scores.15 = (f32[8,1024,512]{2,1,0:T(8,128)S(1)}, bf16[4096,768]{1,0:T(8,128)(2,1)S(1)}, f32[8,1,512]{2,1,0:T(1,128)S(1)}) custom-call(s32[2]{0:T(128)S(1)} %pad_add_fusion.ids, bf16[512,768]{1,0:T(8,128)(2,1)S(1)} %collective-permute-done.6.refs_0_, ...), custom_call_target="tpu_custom_call", output_to_operand_aliasing={{0}: (5, {}), {1}: (6, {}), {2}: (7, {})} | custom-call | flops 805306368 | bytes 7340032 | tf_op jit(solution)/shard_map/scores/pallas_call | solution.py:105
  78.8 2.5 %collective-permute-start.17 = (f32[8,1,512]{2,1,0:T(1,128)S(1)}, f32[8,1,512]{2,1,0:T(1,128)S(1)}, u32[]{:S(2)}, u32[]{:S(2)}) collective-permute-start(f32[8,1,512]{2,1,0:T(1,128)S(1)} %add.26.refs_0_), channel_id=1, source_target_pairs={{0,16},{8,24},{16,0},{24,8},{1,17},{9,25},{17,1},{25,9},{2,18},{10... | collective-permute-start | bytes 49160 | tf_op jit(solution)/shard_map/ppermute | solution.py:481
  82.6 5.2 %sums.2 = (f32[1024,768]{1,0:T(8,128)S(1)}, f32[1024,128]{1,0:T(8,128)S(1)}) custom-call(s32[2]{0:T(128)S(1)} %pad_add_fusion.ids, f32[8,1,512]{2,1,0:T(1,128)S(1)} %add.25.refs_0_, f32[8,1,512]{2,1,0:T(1,128)S(1)} %collective-permute-done.11.refs_1_, f32[8,1,512]{2,1,0:T(1,128)S(1)} %collective-permute-done.12.refs_2_, ...), custom_call_target="tpu_custom_call" | custom-call | flops 3221225472 | bytes 14680064 | tf_op jit(solution)/shard_map/sums/pallas_call | solution.py:267
  87.8 5.6 %sums.3 = (bf16[128,768]{1,0:T(8,128)(2,1)S(1)}, f32[144,768]{1,0:T(8,128)S(1)}, f32[128,768]{1,0:T(8,128)S(1)}, bf16[144,768]{1,0:T(8,128)(2,1)S(1)}, bf16[128,...) custom-call(s32[2]{0:T(128)S(1)} %pad_add_fusion.ids, ...), custom_call_target="tpu_custom_call" | custom-call | flops 3221225472 | bytes 14680064 | tf_op jit(solution)/shard_map/sums/pallas_call | solution.py:267
  93.4 1.6 %collective-permute-start.23 = (bf16[144,768]{1,0:T(8,128)(2,1)S(1)}, bf16[144,768]{1,0:T(8,128)(2,1)S(1)}, u32[]{:S(2)}, u32[]{:S(2)}) collective-permute-start(bf16[144,768]{1,0:T(8,128)(2,1)S(1)} %get-tuple-element.144), channel_id=1, source_target_pairs={{0,4},{1,5},{2,6},{3,7},{4,0},{5,1},{6,2},{7,3},{8,12},{9,13},{10,... | collective-permute-start | bytes 663560 | tf_op jit(solution)/shard_map/ppermute | solution.py:409
  97.0 4.8 %collective-permute-done.23.arrived = bf16[144,768]{1,0:T(8,128)(2,1)S(1)} collective-permute-done((bf16[144,768]{1,0:T(8,128)(2,1)S(1)}, bf16[144,768]{1,0:T(8,128)(2,1)S(1)}, u32[]{:S(2)}, u32[]{:S(2)}) %collective-permute-start.23) | collective-permute-done | bytes 221216 | tf_op jit(solution)/shard_map/ppermute | solution.py:409
  104.0 1.6 %collective-permute-start.22 = (bf16[128,768]{1,0:T(8,128)(2,1)S(1)}, bf16[128,768]{1,0:T(8,128)(2,1)S(1)}, u32[]{:S(2)}, u32[]{:S(2)}) collective-permute-start(bf16[128,768]{1,0:T(8,128)(2,1)S(1)} %pass_on.2), channel_id=1, source_target_pairs={{0,4},{1,5},{2,6},{3,7},{4,0},{5,1},{6,2},{7,3},{8,12},{9,13},{10,... | collective-permute-start | bytes 589832 | tf_op jit(solution)/shard_map/ppermute | solution.py:409
  105.6 5.1 %collective-permute-done.19.refs_0_ = bf16[128,768]{1,0:T(8,128)(2,1)S(1)} collective-permute-done((bf16[128,768]{1,0:T(8,128)(2,1)S(1)}, bf16[128,768]{1,0:T(8,128)(2,1)S(1)}, u32[]{:S(2)}, u32[]{:S(2)}) %collective-permute-start.19) | collective-permute-done | bytes 196640 | tf_op jit(solution)/shard_map/ppermute | solution.py:409
  111.1 1.6 %collective-permute-start.25 = (bf16[128,768]{1,0:T(8,128)(2,1)S(1)}, bf16[128,768]{1,0:T(8,128)(2,1)S(1)}, u32[]{:S(2)}, u32[]{:S(2)}) collective-permute-start(bf16[128,768]{1,0:T(8,128)(2,1)S(1)} %get-tuple-element.145.refs_0_), channel_id=1, source_target_pairs={{0,2},{1,3},{2,0},{3,1},{4,6},{5,7},{6,4},{7,5},{8,10},{9,11},{10,... | collective-permute-start | bytes 589832 | tf_op jit(solution)/shard_map/ppermute | solution.py:409
  115.2 3.6 %collective-permute-done.25.refs_0_ = bf16[128,768]{1,0:T(8,128)(2,1)S(1)} collective-permute-done((bf16[128,768]{1,0:T(8,128)(2,1)S(1)}, bf16[128,768]{1,0:T(8,128)(2,1)S(1)}, u32[]{:S(2)}, u32[]{:S(2)}) %collective-permute-start.25) | collective-permute-done | bytes 196640 | tf_op jit(solution)/shard_map/ppermute | solution.py:409
  121.9 1.7 %collective-permute-done.26.refs_1_ = bf16[144,768]{1,0:T(8,128)(2,1)S(1)} collective-permute-done((bf16[144,768]{1,0:T(8,128)(2,1)S(1)}, bf16[144,768]{1,0:T(8,128)(2,1)S(1)}, u32[]{:S(2)}, u32[]{:S(2)}) %collective-permute-start.26) | collective-permute-done | bytes 221216 | tf_op jit(solution)/shard_map/ppermute | solution.py:409
  124.1 1.8 %assemble.3 = (f32[2048,768]{1,0:T(8,128)}, f32[8,1,256]{2,1,0:T(1,128)}) custom-call(s32[2]{0:T(128)S(1)} %pad_add_fusion.ids, bf16[128,768]{1,0:T(8,128)(2,1)S(1)} %get-tuple-element.145.refs_0_, bf16[144,768]{1,0:T(8,128)(2,1)S(1)} %get-tuple-element.146.refs_1_, bf16[128,768]{1,0:T(8,128)(2,1)S(1)} %collective-permute-done.28.refs_2_, ...), custom_call_target="tpu_custom_call" | custom-call | tf_op jit(solution)/shard_map/assemble/pallas_call | solution.py:374
  126.0 2.6 %collective-permute-done.31.refs_0_ = bf16[128,768]{1,0:T(8,128)(2,1)S(1)} collective-permute-done((bf16[128,768]{1,0:T(8,128)(2,1)S(1)}, bf16[128,768]{1,0:T(8,128)(2,1)S(1)}, u32[]{:S(2)}, u32[]{:S(2)}) %collective-permute-start.31) | collective-permute-done | bytes 196640 | tf_op jit(solution)/shard_map/ppermute | solution.py:409
  130.7 2.3 %assemble.4 = (f32[2048,768]{1,0:T(8,128)}, f32[8,1,256]{2,1,0:T(1,128)}) custom-call(s32[2]{0:T(128)S(1)} %pad_add_fusion.ids, bf16[128,768]{1,0:T(8,128)(2,1)S(1)} %collective-permute-done.25.refs_0_, bf16[144,768]{1,0:T(8,128)(2,1)S(1)} %collective-permute-done.26.refs_1_, ...), custom_call_target="tpu_custom_call", output_to_operand_aliasing={{0}: (9, {}), {1}: (10, {})} | custom-call | tf_op jit(solution)/shard_map/assemble/pallas_call | solution.py:374
  133.0 1.8 %assemble.5 = (f32[2048,768]{1,0:T(8,128)}, f32[8,1,256]{2,1,0:T(1,128)}) custom-call(s32[2]{0:T(128)S(1)} %pad_add_fusion.ids, bf16[128,768]{1,0:T(8,128)(2,1)S(1)} %collective-permute-done.31.refs_0_, bf16[144,768]{1,0:T(8,128)(2,1)S(1)} %collective-permute-done.32.refs_1_, ...), custom_call_target="tpu_custom_call", output_to_operand_aliasing={{0}: (5, {}), {1}: (6, {})} | custom-call | tf_op jit(solution)/shard_map/assemble/pallas_call | solution.py:374
  (72 shorter events, 26.5 us)
Async XLA Ops:
  0.6 11.4 %collective-permute-start.3 = (bf16[512,768]{1,0:T(8,128)(2,1)}, bf16[512,768]{1,0:T(8,128)(2,1)S(1)}, u32[]{:S(2)}, u32[]{:S(2)}) collective-permute-start(bf16[512,768]{1,0:T(8,128)(2,1)} %refs_0_.1), channel_id=1, source_target_pairs={{0,1},{1,0},{2,3},{3,2},{4,5},{5,4},{6,7},{7,6},{8,9},{9,8},{10,11... | collective-permute-start | bytes 2359304 | tf_op jit(solution)/shard_map/ppermute | solution.py:415
  1.1 21.0 %collective-permute-start.2 = (bf16[512,768]{1,0:T(8,128)(2,1)}, bf16[512,768]{1,0:T(8,128)(2,1)S(1)}, u32[]{:S(2)}, u32[]{:S(2)}) collective-permute-start(bf16[512,768]{1,0:T(8,128)(2,1)} %refs_0_.1), channel_id=1, source_target_pairs={{8,0},{0,8},{24,16},{16,24},{9,1},{1,9},{25,17},{17,25},{10,2},{2,... | collective-permute-start | bytes 2359304 | tf_op jit(solution)/shard_map/ppermute | solution.py:433
  3.8 19.1 %collective-permute-start = (bf16[512,768]{1,0:T(8,128)(2,1)}, bf16[512,768]{1,0:T(8,128)(2,1)S(1)}, u32[]{:S(2)}, u32[]{:S(2)}) collective-permute-start(bf16[512,768]{1,0:T(8,128)(2,1)} %refs_0_.1), channel_id=1, source_target_pairs={{16,8},{8,16},{17,9},{9,17},{18,10},{10,18},{19,11},{11,19},{20,12... | collective-permute-start | bytes 2359304 | tf_op jit(solution)/shard_map/ppermute | solution.py:433
  22.1 4.6 %collective-permute-start.5 = (bf16[512,768]{1,0:T(8,128)(2,1)S(1)}, bf16[512,768]{1,0:T(8,128)(2,1)S(1)}, u32[]{:S(2)}, u32[]{:S(2)}) collective-permute-start(bf16[512,768]{1,0:T(8,128)(2,1)S(1)} %collective-permute-done.2.refs_0_), channel_id=1, source_target_pairs={{0,1},{1,0},{2,3},{3,2},{4,5},{5,4},{6,7},{7,6},{8,9},{9,8},{10,11... | collective-permute-start | bytes 2359304 | tf_op jit(solution)/shard_map/ppermute | solution.py:415
  22.1 6.4 %collective-permute-start.4 = (bf16[512,768]{1,0:T(8,128)(2,1)S(1)}, bf16[512,768]{1,0:T(8,128)(2,1)S(1)}, u32[]{:S(2)}, u32[]{:S(2)}) collective-permute-start(bf16[512,768]{1,0:T(8,128)(2,1)S(1)} %collective-permute-done.2.refs_0_), channel_id=1, source_target_pairs={{16,8},{8,16},{17,9},{9,17},{18,10},{10,18},{19,11},{11,19},{20,12... | collective-permute-start | bytes 2359304 | tf_op jit(solution)/shard_map/ppermute | solution.py:433
  22.9 23.7 %collective-permute-start.1 = (bf16[512,768]{1,0:T(8,128)(2,1)S(1)}, bf16[512,768]{1,0:T(8,128)(2,1)S(1)}, u32[]{:S(2)}, u32[]{:S(2)}) collective-permute-start(bf16[512,768]{1,0:T(8,128)(2,1)S(1)} %collective-permute-done.refs_0_), channel_id=1, source_target_pairs={{8,0},{16,24},{9,1},{17,25},{10,2},{18,26},{11,3},{19,27},{12,4},{... | collective-permute-start | bytes 2359304 | tf_op jit(solution)/shard_map/ppermute | solution.py:433
  24.2 27.5 %collective-permute-start.8 = (bf16[512,768]{1,0:T(8,128)(2,1)S(1)}, bf16[512,768]{1,0:T(8,128)(2,1)S(1)}, u32[]{:S(2)}, u32[]{:S(2)}) collective-permute-start(bf16[512,768]{1,0:T(8,128)(2,1)S(1)} %collective-permute-done.refs_0_), channel_id=1, source_target_pairs={{8,9},{9,8},{10,11},{11,10},{12,13},{13,12},{14,15},{15,14},{16,17... | collective-permute-start | bytes 2359304 | tf_op jit(solution)/shard_map/ppermute | solution.py:415
  46.6 5.1 %collective-permute-start.9 = (bf16[512,768]{1,0:T(8,128)(2,1)S(1)}, bf16[512,768]{1,0:T(8,128)(2,1)S(1)}, u32[]{:S(2)}, u32[]{:S(2)}) collective-permute-start(bf16[512,768]{1,0:T(8,128)(2,1)S(1)} %collective-permute-done.1.refs_1_), channel_id=1, source_target_pairs={{0,1},{1,0},{2,3},{3,2},{4,5},{5,4},{6,7},{7,6},{24,25},{25,24},{2... | collective-permute-start | bytes 2359304 | tf_op jit(solution)/shard_map/ppermute | solution.py:415
  48.5 22.9 %collective-permute-start.7 = (bf16[512,768]{1,0:T(8,128)(2,1)S(1)}, bf16[512,768]{1,0:T(8,128)(2,1)S(1)}, u32[]{:S(2)}, u32[]{:S(2)}) collective-permute-start(bf16[512,768]{1,0:T(8,128)(2,1)S(1)} %collective-permute-done.4.refs_0_), channel_id=1, source_target_pairs={{8,0},{16,24},{9,1},{17,25},{10,2},{18,26},{11,3},{19,27},{12,4},{... | collective-permute-start | bytes 2359304 | tf_op jit(solution)/shard_map/ppermute | solution.py:433
  55.0 6.7 %collective-permute-start.11 = (f32[8,1,512]{2,1,0:T(1,128)S(1)}, f32[8,1,512]{2,1,0:T(1,128)S(1)}, u32[]{:S(2)}, u32[]{:S(2)}) collective-permute-start(f32[8,1,512]{2,1,0:T(1,128)S(1)} %add.25.refs_0_), channel_id=1, source_target_pairs={{0,8},{8,16},{16,24},{24,0},{1,9},{9,17},{17,25},{25,1},{2,10},{10... | collective-permute-start | bytes 49160 | tf_op jit(solution)/shard_map/ppermute | solution.py:481
  57.6 4.7 %collective-permute-start.12 = (f32[8,1,512]{2,1,0:T(1,128)S(1)}, f32[8,1,512]{2,1,0:T(1,128)S(1)}, u32[]{:S(2)}, u32[]{:S(2)}) collective-permute-start(f32[8,1,512]{2,1,0:T(1,128)S(1)} %add.25.refs_0_), channel_id=1, source_target_pairs={{0,16},{8,24},{16,0},{24,8},{1,17},{9,25},{17,1},{25,9},{2,18},{10... | collective-permute-start | bytes 49160 | tf_op jit(solution)/shard_map/ppermute | solution.py:481
  58.1 13.3 %collective-permute-start.13 = (f32[8,1,512]{2,1,0:T(1,128)S(1)}, f32[8,1,512]{2,1,0:T(1,128)S(1)}, u32[]{:S(2)}, u32[]{:S(2)}) collective-permute-start(f32[8,1,512]{2,1,0:T(1,128)S(1)} %add.25.refs_0_), channel_id=1, source_target_pairs={{0,24},{8,0},{16,8},{24,16},{1,25},{9,1},{17,9},{25,17},{2,26},{10... | collective-permute-start | bytes 49160 | tf_op jit(solution)/shard_map/ppermute | solution.py:481
  60.9 14.3 %collective-permute-start.6 = (bf16[512,768]{1,0:T(8,128)(2,1)S(1)}, bf16[512,768]{1,0:T(8,128)(2,1)S(1)}, u32[]{:S(2)}, u32[]{:S(2)}) collective-permute-start(bf16[512,768]{1,0:T(8,128)(2,1)S(1)} %collective-permute-done.4.refs_0_), channel_id=1, source_target_pairs={{8,9},{9,8},{10,11},{11,10},{12,13},{13,12},{14,15},{15,14},{16,17... | collective-permute-start | bytes 2359304 | tf_op jit(solution)/shard_map/ppermute | solution.py:415
  71.4 4.2 %collective-permute-start.14 = (bf16[512,768]{1,0:T(8,128)(2,1)S(1)}, bf16[512,768]{1,0:T(8,128)(2,1)S(1)}, u32[]{:S(2)}, u32[]{:S(2)}) collective-permute-start(bf16[512,768]{1,0:T(8,128)(2,1)S(1)} %collective-permute-done.7.refs_1_), channel_id=1, source_target_pairs={{0,1},{1,0},{2,3},{3,2},{4,5},{5,4},{6,7},{7,6},{24,25},{25,24},{2... | collective-permute-start | bytes 2359304 | tf_op jit(solution)/shard_map/ppermute | solution.py:415
  78.7 9.1 %collective-permute-start.16 = (f32[8,1,512]{2,1,0:T(1,128)S(1)}, f32[8,1,512]{2,1,0:T(1,128)S(1)}, u32[]{:S(2)}, u32[]{:S(2)}) collective-permute-start(f32[8,1,512]{2,1,0:T(1,128)S(1)} %add.26.refs_0_), channel_id=1, source_target_pairs={{0,8},{8,16},{16,24},{24,0},{1,9},{9,17},{17,25},{25,1},{2,10},{10... | collective-permute-start | bytes 49160 | tf_op jit(solution)/shard_map/ppermute | solution.py:481
  78.8 9.0 %collective-permute-start.17 = (f32[8,1,512]{2,1,0:T(1,128)S(1)}, f32[8,1,512]{2,1,0:T(1,128)S(1)}, u32[]{:S(2)}, u32[]{:S(2)}) collective-permute-start(f32[8,1,512]{2,1,0:T(1,128)S(1)} %add.26.refs_0_), channel_id=1, source_target_pairs={{0,16},{8,24},{16,0},{24,8},{1,17},{9,25},{17,1},{25,9},{2,18},{10... | collective-permute-start | bytes 49160 | tf_op jit(solution)/shard_map/ppermute | solution.py:481
  81.2 6.6 %collective-permute-start.18 = (f32[8,1,512]{2,1,0:T(1,128)S(1)}, f32[8,1,512]{2,1,0:T(1,128)S(1)}, u32[]{:S(2)}, u32[]{:S(2)}) collective-permute-start(f32[8,1,512]{2,1,0:T(1,128)S(1)} %add.26.refs_0_), channel_id=1, source_target_pairs={{0,24},{8,0},{16,8},{24,16},{1,25},{9,1},{17,9},{25,17},{2,26},{10... | collective-permute-start | bytes 49160 | tf_op jit(solution)/shard_map/ppermute | solution.py:481
  93.4 8.4 %collective-permute-start.23 = (bf16[144,768]{1,0:T(8,128)(2,1)S(1)}, bf16[144,768]{1,0:T(8,128)(2,1)S(1)}, u32[]{:S(2)}, u32[]{:S(2)}) collective-permute-start(bf16[144,768]{1,0:T(8,128)(2,1)S(1)} %get-tuple-element.144), channel_id=1, source_target_pairs={{0,4},{1,5},{2,6},{3,7},{4,0},{5,1},{6,2},{7,3},{8,12},{9,13},{10,... | collective-permute-start | bytes 663560 | tf_op jit(solution)/shard_map/ppermute | solution.py:409
  95.0 9.0 %collective-permute-start.21 = (bf16[128,768]{1,0:T(8,128)(2,1)S(1)}, bf16[128,768]{1,0:T(8,128)(2,1)S(1)}, u32[]{:S(2)}, u32[]{:S(2)}) collective-permute-start(bf16[128,768]{1,0:T(8,128)(2,1)S(1)} %get-tuple-element.142), channel_id=1, source_target_pairs={{0,2},{1,3},{2,0},{3,1},{4,6},{5,7},{6,4},{7,5},{8,10},{9,11},{10,... | collective-permute-start | bytes 589832 | tf_op jit(solution)/shard_map/ppermute | solution.py:409
  96.5 14.3 %collective-permute-start.20 = (bf16[144,768]{1,0:T(8,128)(2,1)S(1)}, bf16[144,768]{1,0:T(8,128)(2,1)S(1)}, u32[]{:S(2)}, u32[]{:S(2)}) collective-permute-start(bf16[144,768]{1,0:T(8,128)(2,1)S(1)} %get-tuple-element.140), channel_id=1, source_target_pairs={{0,4},{1,5},{2,6},{3,7},{4,0},{5,1},{6,2},{7,3},{8,12},{9,13},{10,... | collective-permute-start | bytes 663560 | tf_op jit(solution)/shard_map/ppermute | solution.py:409
  101.9 8.9 %collective-permute-start.24 = (bf16[144,768]{1,0:T(8,128)(2,1)S(1)}, bf16[144,768]{1,0:T(8,128)(2,1)S(1)}, u32[]{:S(2)}, u32[]{:S(2)}) collective-permute-start(bf16[144,768]{1,0:T(8,128)(2,1)S(1)} %pass_on.3), channel_id=1, source_target_pairs={{0,2},{1,3},{2,0},{3,1},{4,6},{5,7},{6,4},{7,5},{8,10},{9,11},{10,... | collective-permute-start | bytes 663560 | tf_op jit(solution)/shard_map/ppermute | solution.py:409
  103.5 7.3 %collective-permute-start.19 = (bf16[128,768]{1,0:T(8,128)(2,1)S(1)}, bf16[128,768]{1,0:T(8,128)(2,1)S(1)}, u32[]{:S(2)}, u32[]{:S(2)}) collective-permute-start(bf16[128,768]{1,0:T(8,128)(2,1)S(1)} %get-tuple-element.139), channel_id=1, source_target_pairs={{0,2},{1,3},{2,0},{3,1},{4,6},{5,7},{6,4},{7,5},{8,10},{9,11},{10,... | collective-permute-start | bytes 589832 | tf_op jit(solution)/shard_map/ppermute | solution.py:409
  104.0 6.7 %collective-permute-start.22 = (bf16[128,768]{1,0:T(8,128)(2,1)S(1)}, bf16[128,768]{1,0:T(8,128)(2,1)S(1)}, u32[]{:S(2)}, u32[]{:S(2)}) collective-permute-start(bf16[128,768]{1,0:T(8,128)(2,1)S(1)} %pass_on.2), channel_id=1, source_target_pairs={{0,4},{1,5},{2,6},{3,7},{4,0},{5,1},{6,2},{7,3},{8,12},{9,13},{10,... | collective-permute-start | bytes 589832 | tf_op jit(solution)/shard_map/ppermute | solution.py:409
  111.1 7.8 %collective-permute-start.25 = (bf16[128,768]{1,0:T(8,128)(2,1)S(1)}, bf16[128,768]{1,0:T(8,128)(2,1)S(1)}, u32[]{:S(2)}, u32[]{:S(2)}) collective-permute-start(bf16[128,768]{1,0:T(8,128)(2,1)S(1)} %get-tuple-element.145.refs_0_), channel_id=1, source_target_pairs={{0,2},{1,3},{2,0},{3,1},{4,6},{5,7},{6,4},{7,5},{8,10},{9,11},{10,... | collective-permute-start | bytes 589832 | tf_op jit(solution)/shard_map/ppermute | solution.py:409
  112.7 8.3 %collective-permute-start.30 = (bf16[144,768]{1,0:T(8,128)(2,1)S(1)}, bf16[144,768]{1,0:T(8,128)(2,1)S(1)}, u32[]{:S(2)}, u32[]{:S(2)}) collective-permute-start(bf16[144,768]{1,0:T(8,128)(2,1)S(1)} %get-tuple-element.146.refs_1_), channel_id=1, source_target_pairs={{0,4},{1,5},{2,6},{3,7},{4,0},{5,1},{6,2},{7,3},{8,12},{9,13},{10,... | collective-permute-start | bytes 663560 | tf_op jit(solution)/shard_map/ppermute | solution.py:409
  114.2 9.4 %collective-permute-start.26 = (bf16[144,768]{1,0:T(8,128)(2,1)S(1)}, bf16[144,768]{1,0:T(8,128)(2,1)S(1)}, u32[]{:S(2)}, u32[]{:S(2)}) collective-permute-start(bf16[144,768]{1,0:T(8,128)(2,1)S(1)} %get-tuple-element.146.refs_1_), channel_id=1, source_target_pairs={{0,2},{1,3},{2,0},{3,1},{4,6},{5,7},{6,4},{7,5},{8,10},{9,11},{10,... | collective-permute-start | bytes 663560 | tf_op jit(solution)/shard_map/ppermute | solution.py:409
  114.8 8.9 %collective-permute-start.29 = (bf16[144,768]{1,0:T(8,128)(2,1)S(1)}, bf16[144,768]{1,0:T(8,128)(2,1)S(1)}, u32[]{:S(2)}, u32[]{:S(2)}) collective-permute-start(bf16[144,768]{1,0:T(8,128)(2,1)S(1)} %get-tuple-element.146.refs_1_), channel_id=1, source_target_pairs={{0,1},{1,0},{2,3},{3,2},{4,5},{5,4},{6,7},{7,6},{8,9},{9,8},{10,11... | collective-permute-start | bytes 663560 | tf_op jit(solution)/shard_map/ppermute | solution.py:409
  114.8 11.1 %collective-permute-start.27 = (bf16[128,768]{1,0:T(8,128)(2,1)S(1)}, bf16[128,768]{1,0:T(8,128)(2,1)S(1)}, u32[]{:S(2)}, u32[]{:S(2)}) collective-permute-start(bf16[128,768]{1,0:T(8,128)(2,1)S(1)} %get-tuple-element.145.refs_0_), channel_id=1, source_target_pairs={{0,4},{1,5},{2,6},{3,7},{4,0},{5,1},{6,2},{7,3},{8,12},{9,13},{10,... | collective-permute-start | bytes 589832 | tf_op jit(solution)/shard_map/ppermute | solution.py:409
  118.9 9.8 %collective-permute-start.31 = (bf16[128,768]{1,0:T(8,128)(2,1)S(1)}, bf16[128,768]{1,0:T(8,128)(2,1)S(1)}, u32[]{:S(2)}, u32[]{:S(2)}) collective-permute-start(bf16[128,768]{1,0:T(8,128)(2,1)S(1)} %collective-permute-done.25.refs_0_), channel_id=1, source_target_pairs={{0,4},{1,5},{2,6},{3,7},{4,0},{5,1},{6,2},{7,3},{8,12},{9,13},{10,... | collective-permute-start | bytes 589832 | tf_op jit(solution)/shard_map/ppermute | solution.py:409
  121.0 9.1 %collective-permute-start.32 = (bf16[144,768]{1,0:T(8,128)(2,1)S(1)}, bf16[144,768]{1,0:T(8,128)(2,1)S(1)}, u32[]{:S(2)}, u32[]{:S(2)}) collective-permute-start(bf16[144,768]{1,0:T(8,128)(2,1)S(1)} %collective-permute-done.30.refs_3_), channel_id=1, source_target_pairs={{0,2},{1,3},{2,0},{3,1},{4,6},{5,7},{6,4},{7,5},{8,10},{9,11},{10,... | collective-permute-start | bytes 663560 | tf_op jit(solution)/shard_map/ppermute | solution.py:409
  123.6 6.5 %collective-permute-start.34 = (bf16[144,768]{1,0:T(8,128)(2,1)S(1)}, bf16[144,768]{1,0:T(8,128)(2,1)S(1)}, u32[]{:S(2)}, u32[]{:S(2)}) collective-permute-start(bf16[144,768]{1,0:T(8,128)(2,1)S(1)} %collective-permute-done.26.refs_1_), channel_id=1, source_target_pairs={{0,1},{1,0},{2,3},{3,2},{4,5},{5,4},{6,7},{7,6},{8,9},{9,8},{10,11... | collective-permute-start | bytes 663560 | tf_op jit(solution)/shard_map/ppermute | solution.py:409
  123.6 6.5 %collective-permute-start.36 = (bf16[144,768]{1,0:T(8,128)(2,1)S(1)}, bf16[144,768]{1,0:T(8,128)(2,1)S(1)}, u32[]{:S(2)}, u32[]{:S(2)}) collective-permute-start(bf16[144,768]{1,0:T(8,128)(2,1)S(1)} %collective-permute-done.30.refs_3_), channel_id=1, source_target_pairs={{0,1},{1,0},{2,3},{3,2},{4,5},{5,4},{6,7},{7,6},{8,9},{9,8},{10,11... | collective-permute-start | bytes 663560 | tf_op jit(solution)/shard_map/ppermute | solution.py:409
  (8 other events, 17.3 us)

commit v11 on v10

--- a/solution.py
+++ b/solution.py
@@ -482,10 +482,6 @@
             for turn in range(1, n_places)
         ]
 
-    settled = {
-        block for block in range(n_places) if all(order[-1] != block for order in orders)
-    }
-    early_totals = None
     def arrive(moved):
         for slot, array, places in moved:
             slots[slot].append((array, places))
@@ -504,24 +500,15 @@
         moved, moves = start_ready(moves)
 
         carried = scores_of(turn, carried)
-        if turn == n_places - 2 and settled:
-            early_totals = totals_of(carried[2])
-            early_totals, carried = lax.optimization_barrier((early_totals, carried))
         if turn == 0:
             arrive([m for m in moved if m[0] > turn + 1])
             moved = [m for m in moved if m[0] <= turn + 1]
         carried = arrive_behind(moved, carried)
     scores, rows, totals = carried
     steps = sum_plan(orders)
-    late = totals_of(totals)
-    if early_totals is not None:
-        ready = [step for step in steps if all(block in settled for block in step[1])]
-        rest = [step for step in steps if step not in ready]
-        state = sum_rows(ids, ready, early_totals, scores, rows, n_owners, None, False)
-        late, state = lax.optimization_barrier((late, state))
-    else:
-        rest, state = steps, None
-    *sent, mine, masses = sum_rows(ids, rest, late, scores, rows, n_owners, state, True)
+    *sent, mine, masses = sum_rows(
+        ids, steps, totals_of(totals), scores, rows, n_owners, None, True
+    )
     size = mine.shape[0]
     one, two = CORES, 2 * CORES
     if n_owners == 4:

time: 135 us -> 135 us (level)
  waiting for transfers between devices: 58.2 us -> 65.3 us
  starting transfers between devices: 38.1 us -> 31.7 us
    ppermute x5, waiting for transfers between devices: 26.3 us -> 42.4 us  [start_ready(): lax.ppermute(slots[source_slot][hold][0], 'blk', pairs)]
    ppermute x6 -> x3, waiting for transfers between devices: 9.78 us -> 2.37 us  [totals_of(): lax.ppermute(both, 'blk', [(i, (i + turn) % n_places) for i in range(n_pl...]
    ppermute x6 -> x3, starting transfers between devices: 9.82 us -> 3.87 us  [totals_of(): lax.ppermute(both, 'blk', [(i, (i + turn) % n_places) for i in range(n_pl...]
    ppermute x22 -> x21, waiting for transfers between devices: 21.8 us -> 20.1 us  [exchange(): lax.ppermute(array, 'rows', [(i, i ^ distance) for i in range(n_rows)])]
    pallas_call x2 -> x1, Pallas kernels: 10.8 us -> 9.8 us  [sum_rows(): pl.pallas_call(functools.partial(sum_kernel, plan, len(totals), n_owners,...]
    ppermute x22 -> x21, starting transfers between devices: 15.9 us -> 15.4 us  [exchange(): lax.ppermute(array, 'rows', [(i, i ^ distance) for i in range(n_rows)])]
  transfers between devices with their start and end apart: 39 -> 35, of which waited for: 14 -> 14; matrix products, arithmetic and copies ran while one was open for 3% -> 3% of each run, Pallas kernels for 17% -> 13%
where the time goes in v11:
time: 135 us; the launch traced here: 134 us
  waiting for transfers between devices  65.3 us (48%)
  starting transfers between devices  31.7 us (23%)
  Pallas kernels  30.8 us (23%)
  other arithmetic  4.31 us (3%)
    ppermute x5, waiting for transfers between devices, start_ready(): lax.ppermute(slots[source_slot][hold][0], 'blk', pairs)  42.4 us
    ppermute x21, waiting for transfers between devices, exchange(): lax.ppermute(array, 'rows', [(i, i ^ distance) for i in range(n_rows)])  20.1 us
    ppermute x21, starting transfers between devices, exchange(): lax.ppermute(array, 'rows', [(i, i ^ distance) for i in range(n_rows)])  15.4 us
    pallas_call x8, Pallas kernels, score_block(): pl.pallas_call(functools.partial(score_kernel, n_sources, choice), grid_s...  14.8 us
    pallas_call x1, Pallas kernels, sum_rows(): pl.pallas_call(functools.partial(sum_kernel, plan, len(totals), n_owners,...  9.8 us
    ppermute x5, starting transfers between devices, start_ready(): lax.ppermute(slots[source_slot][hold][0], 'blk', pairs)  6.63 us
    pallas_call x3, Pallas kernels, assemble(): pl.pallas_call(functools.partial(assemble_kernel, factor, spots, n_blocks...  5.87 us
    ppermute x6, starting transfers between devices, swap_cores(): return lax.ppermute(array, ('blk', 'rows'), pairs)  5.76 us
  transfers between devices with their start and end apart: 35, of which 14 were waited for; matrix products, arithmetic and copies ran while one was open for 3% of the time, Pallas kernels for 13%

profile of v11, /device:TPU:0, one launch (start us, length us, event | category | flops | bytes accessed | tf_op | source)
XLA Modules:
  0.0 134.5 jit_solution(15442752018121165491)
XLA Ops:
  1.1 2.7 %collective-permute-start.2 = (bf16[512,768]{1,0:T(8,128)(2,1)}, bf16[512,768]{1,0:T(8,128)(2,1)S(1)}, u32[]{:S(2)}, u32[]{:S(2)}) collective-permute-start(bf16[512,768]{1,0:T(8,128)(2,1)} %refs_0_.1), channel_id=1, source_target_pairs={{8,0},{0,8},{24,16},{16,24},{9,1},{1,9},{25,17},{17,25},{10,2},{2,... | collective-permute-start | bytes 2359304 | tf_op jit(solution)/shard_map/ppermute | solution.py:433
  5.3 1.8 %fusion = f32[1024]{0:T(1024)S(1)} fusion(bf16[2048,768]{1,0:T(8,128)(2,1)} %param.4, s32[]{:T(128)S(6)} %select_n.4), kind=kLoop, calls=%fused_computation.2 | loop fusion | flops 2358272 | bytes 1576964 | tf_op jit(solution)/shard_map/reduce_sum | solution.py:21
  7.1 1.7 %fusion.1.refs_1_.refs_2_ = bf16[1024,768]{1,0:T(8,128)(2,1)S(1)} fusion(f32[1024]{0:T(1024)S(1)} %add_rsqrt_fusion, bf16[2048,768]{1,0:T(8,128)(2,1)} %param.4, s32[]{:T(128)S(6)} %select_n.4), kind=kLoop, calls=%fused_computation.3 | loop fusion | flops 2359296 | bytes 3149828 | tf_op jit(solution)/shard_map/convert_element_type | solution.py:21
  10.2 1.8 %scores.8 = (f32[8,1024,512]{2,1,0:T(8,128)S(1)}, bf16[4096,768]{1,0:T(8,128)(2,1)S(1)}, f32[8,1,512]{2,1,0:T(1,128)S(1)}) custom-call(s32[2]{0:T(128)S(1)} %pad_add_fusion.ids, bf16[512,768]{1,0:T(8,128)(2,1)S(1)} %copy-done, bf16[1024,768]{1,0:T(8,128)(2,1)S(1)} %fusion.1.refs_1_.refs_2_, f32[1024,128]{1,0:T(8,128)S(1)} %broadcast_in_dim.2.refs_2_.refs_3_), custom_call_target="tpu_custom_call" | custom-call | flops 805306368 | bytes 7340032 | tf_op jit(solution)/shard_map/scores/pallas_call | solution.py:105
  12.0 1.8 %scores.9 = (f32[8,1024,512]{2,1,0:T(8,128)S(1)}, bf16[4096,768]{1,0:T(8,128)(2,1)S(1)}, f32[8,1,512]{2,1,0:T(1,128)S(1)}) custom-call(s32[2]{0:T(128)S(1)} %pad_add_fusion.ids, bf16[512,768]{1,0:T(8,128)(2,1)S(1)} %collective-permute-done.3.refs_0_, ...), custom_call_target="tpu_custom_call", output_to_operand_aliasing={{0}: (4, {}), {1}: (5, {}), {2}: (6, {})} | custom-call | flops 805306368 | bytes 7340032 | tf_op jit(solution)/shard_map/scores/pallas_call | solution.py:105
  13.9 8.3 %collective-permute-done.2.refs_0_ = bf16[512,768]{1,0:T(8,128)(2,1)S(1)} collective-permute-done((bf16[512,768]{1,0:T(8,128)(2,1)}, bf16[512,768]{1,0:T(8,128)(2,1)S(1)}, u32[]{:S(2)}, u32[]{:S(2)}) %collective-permute-start.2) | collective-permute-done | bytes 786464 | tf_op jit(solution)/shard_map/ppermute | solution.py:433
  24.9 1.8 %scores.10 = (f32[8,1024,512]{2,1,0:T(8,128)S(1)}, bf16[4096,768]{1,0:T(8,128)(2,1)S(1)}, f32[8,1,512]{2,1,0:T(1,128)S(1)}) custom-call(s32[2]{0:T(128)S(1)} %pad_add_fusion.ids, bf16[512,768]{1,0:T(8,128)(2,1)S(1)} %collective-permute-done.2.refs_0_, ...), custom_call_target="tpu_custom_call", output_to_operand_aliasing={{0}: (4, {}), {1}: (5, {}), {2}: (6, {})} | custom-call | flops 805306368 | bytes 7340032 | tf_op jit(solution)/shard_map/scores/pallas_call | solution.py:105
  26.7 1.8 %scores.11 = (f32[8,1024,512]{2,1,0:T(8,128)S(1)}, bf16[4096,768]{1,0:T(8,128)(2,1)S(1)}, f32[8,1,512]{2,1,0:T(1,128)S(1)}) custom-call(s32[2]{0:T(128)S(1)} %pad_add_fusion.ids, bf16[512,768]{1,0:T(8,128)(2,1)S(1)} %collective-permute-done.5.refs_0_, ...), custom_call_target="tpu_custom_call", output_to_operand_aliasing={{0}: (4, {}), {1}: (5, {}), {2}: (6, {})} | custom-call | flops 805306368 | bytes 7340032 | tf_op jit(solution)/shard_map/scores/pallas_call | solution.py:105
  28.6 18.0 %collective-permute-done.1.refs_1_ = bf16[512,768]{1,0:T(8,128)(2,1)S(1)} collective-permute-done((bf16[512,768]{1,0:T(8,128)(2,1)S(1)}, bf16[512,768]{1,0:T(8,128)(2,1)S(1)}, u32[]{:S(2)}, u32[]{:S(2)}) %collective-permute-start.1) | collective-permute-done | bytes 786464 | tf_op jit(solution)/shard_map/ppermute | solution.py:433
  46.6 1.9 %collective-permute-start.9 = (bf16[512,768]{1,0:T(8,128)(2,1)S(1)}, bf16[512,768]{1,0:T(8,128)(2,1)S(1)}, u32[]{:S(2)}, u32[]{:S(2)}) collective-permute-start(bf16[512,768]{1,0:T(8,128)(2,1)S(1)} %collective-permute-done.1.refs_1_), channel_id=1, source_target_pairs={{0,1},{1,0},{2,3},{3,2},{4,5},{5,4},{6,7},{7,6},{24,25},{25,24},{2... | collective-permute-start | bytes 2359304 | tf_op jit(solution)/shard_map/ppermute | solution.py:415
  50.5 1.8 %scores.12 = (f32[8,1024,512]{2,1,0:T(8,128)S(1)}, bf16[4096,768]{1,0:T(8,128)(2,1)S(1)}, f32[8,1,512]{2,1,0:T(1,128)S(1)}) custom-call(s32[2]{0:T(128)S(1)} %pad_add_fusion.ids, bf16[512,768]{1,0:T(8,128)(2,1)S(1)} %collective-permute-done.refs_0_, ...), custom_call_target="tpu_custom_call", output_to_operand_aliasing={{0}: (5, {}), {1}: (6, {}), {2}: (7, {})} | custom-call | flops 805306368 | bytes 7340032 | tf_op jit(solution)/shard_map/scores/pallas_call | solution.py:105
  52.4 1.8 %scores.13 = (f32[8,1024,512]{2,1,0:T(8,128)S(1)}, bf16[4096,768]{1,0:T(8,128)(2,1)S(1)}, f32[8,1,512]{2,1,0:T(1,128)S(1)}) custom-call(s32[2]{0:T(128)S(1)} %pad_add_fusion.ids, bf16[512,768]{1,0:T(8,128)(2,1)S(1)} %collective-permute-done.8.refs_0_, ...), custom_call_target="tpu_custom_call", output_to_operand_aliasing={{0}: (5, {}), {1}: (6, {}), {2}: (7, {})} | custom-call | flops 805306368 | bytes 7340032 | tf_op jit(solution)/shard_map/scores/pallas_call | solution.py:105
  54.3 16.1 %collective-permute-done.7.refs_1_ = bf16[512,768]{1,0:T(8,128)(2,1)S(1)} collective-permute-done((bf16[512,768]{1,0:T(8,128)(2,1)S(1)}, bf16[512,768]{1,0:T(8,128)(2,1)S(1)}, u32[]{:S(2)}, u32[]{:S(2)}) %collective-permute-start.7) | collective-permute-done | bytes 786464 | tf_op jit(solution)/shard_map/ppermute | solution.py:433
  70.4 1.9 %collective-permute-start.10 = (bf16[512,768]{1,0:T(8,128)(2,1)S(1)}, bf16[512,768]{1,0:T(8,128)(2,1)S(1)}, u32[]{:S(2)}, u32[]{:S(2)}) collective-permute-start(bf16[512,768]{1,0:T(8,128)(2,1)S(1)} %collective-permute-done.7.refs_1_), channel_id=1, source_target_pairs={{0,1},{1,0},{2,3},{3,2},{4,5},{5,4},{6,7},{7,6},{24,25},{25,24},{2... | collective-permute-start | bytes 2359304 | tf_op jit(solution)/shard_map/ppermute | solution.py:415
  72.3 1.8 %scores.14 = (f32[8,1024,512]{2,1,0:T(8,128)S(1)}, bf16[4096,768]{1,0:T(8,128)(2,1)S(1)}, f32[8,1,512]{2,1,0:T(1,128)S(1)}) custom-call(s32[2]{0:T(128)S(1)} %pad_add_fusion.ids, bf16[512,768]{1,0:T(8,128)(2,1)S(1)} %collective-permute-done.4.refs_0_, ...), custom_call_target="tpu_custom_call", output_to_operand_aliasing={{0}: (5, {}), {1}: (6, {}), {2}: (7, {})} | custom-call | flops 805306368 | bytes 7340032 | tf_op jit(solution)/shard_map/scores/pallas_call | solution.py:105
  74.5 1.8 %scores.15 = (f32[8,1024,512]{2,1,0:T(8,128)S(1)}, bf16[4096,768]{1,0:T(8,128)(2,1)S(1)}, f32[8,1,512]{2,1,0:T(1,128)S(1)}) custom-call(s32[2]{0:T(128)S(1)} %pad_add_fusion.ids, bf16[512,768]{1,0:T(8,128)(2,1)S(1)} %collective-permute-done.6.refs_0_, ...), custom_call_target="tpu_custom_call", output_to_operand_aliasing={{0}: (5, {}), {1}: (6, {}), {2}: (7, {})} | custom-call | flops 805306368 | bytes 7340032 | tf_op jit(solution)/shard_map/scores/pallas_call | solution.py:105
  77.7 2.4 %collective-permute-start.13 = (f32[8,1,512]{2,1,0:T(1,128)S(1)}, f32[8,1,512]{2,1,0:T(1,128)S(1)}, u32[]{:S(2)}, u32[]{:S(2)}) collective-permute-start(f32[8,1,512]{2,1,0:T(1,128)S(1)} %add.22.refs_0_), channel_id=1, source_target_pairs={{0,16},{8,24},{16,0},{24,8},{1,17},{9,25},{17,1},{25,9},{2,18},{10... | collective-permute-start | bytes 49160 | tf_op jit(solution)/shard_map/ppermute | solution.py:481
  81.5 1.7 %collective-permute-done.12.refs_1_ = f32[8,1,512]{2,1,0:T(1,128)S(1)} collective-permute-done((f32[8,1,512]{2,1,0:T(1,128)S(1)}, f32[8,1,512]{2,1,0:T(1,128)S(1)}, u32[]{:S(2)}, u32[]{:S(2)}) %collective-permute-start.12) | collective-permute-done | bytes 16416 | tf_op jit(solution)/shard_map/ppermute | solution.py:481
  83.9 9.8 %sums.1 = (bf16[128,768]{1,0:T(8,128)(2,1)S(1)}, f32[144,768]{1,0:T(8,128)S(1)}, f32[128,768]{1,0:T(8,128)S(1)}, bf16[144,768]{1,0:T(8,128)(2,1)S(1)}, bf16[128,...) custom-call(s32[2]{0:T(128)S(1)} %pad_add_fusion.ids, ...), custom_call_target="tpu_custom_call" | custom-call | flops 6442450944 | bytes 26214400 | tf_op jit(solution)/shard_map/sums/pallas_call | solution.py:267
  93.7 1.6 %collective-permute-start.19 = (bf16[144,768]{1,0:T(8,128)(2,1)S(1)}, bf16[144,768]{1,0:T(8,128)(2,1)S(1)}, u32[]{:S(2)}, u32[]{:S(2)}) collective-permute-start(bf16[144,768]{1,0:T(8,128)(2,1)S(1)} %get-tuple-element.114), channel_id=1, source_target_pairs={{0,4},{1,5},{2,6},{3,7},{4,0},{5,1},{6,2},{7,3},{8,12},{9,13},{10,... | collective-permute-start | bytes 663560 | tf_op jit(solution)/shard_map/ppermute | solution.py:409
  97.3 4.8 %collective-permute-done.19.arrived = bf16[144,768]{1,0:T(8,128)(2,1)S(1)} collective-permute-done((bf16[144,768]{1,0:T(8,128)(2,1)S(1)}, bf16[144,768]{1,0:T(8,128)(2,1)S(1)}, u32[]{:S(2)}, u32[]{:S(2)}) %collective-permute-start.19) | collective-permute-done | bytes 221216 | tf_op jit(solution)/shard_map/ppermute | solution.py:409
  102.2 1.6 %collective-permute-start.20 = (bf16[144,768]{1,0:T(8,128)(2,1)S(1)}, bf16[144,768]{1,0:T(8,128)(2,1)S(1)}, u32[]{:S(2)}, u32[]{:S(2)}) collective-permute-start(bf16[144,768]{1,0:T(8,128)(2,1)S(1)} %pass_on.3), channel_id=1, source_target_pairs={{0,2},{1,3},{2,0},{3,1},{4,6},{5,7},{6,4},{7,5},{8,10},{9,11},{10,... | collective-permute-start | bytes 663560 | tf_op jit(solution)/shard_map/ppermute | solution.py:409
  104.4 1.6 %collective-permute-start.18 = (bf16[128,768]{1,0:T(8,128)(2,1)S(1)}, bf16[128,768]{1,0:T(8,128)(2,1)S(1)}, u32[]{:S(2)}, u32[]{:S(2)}) collective-permute-start(bf16[128,768]{1,0:T(8,128)(2,1)S(1)} %pass_on.2), channel_id=1, source_target_pairs={{0,4},{1,5},{2,6},{3,7},{4,0},{5,1},{6,2},{7,3},{8,12},{9,13},{10,... | collective-permute-start | bytes 589832 | tf_op jit(solution)/shard_map/ppermute | solution.py:409
  106.0 4.3 %collective-permute-done.15.refs_0_ = bf16[128,768]{1,0:T(8,128)(2,1)S(1)} collective-permute-done((bf16[128,768]{1,0:T(8,128)(2,1)S(1)}, bf16[128,768]{1,0:T(8,128)(2,1)S(1)}, u32[]{:S(2)}, u32[]{:S(2)}) %collective-permute-start.15) | collective-permute-done | bytes 196640 | tf_op jit(solution)/shard_map/ppermute | solution.py:409
  110.7 1.6 %collective-permute-start.21 = (bf16[128,768]{1,0:T(8,128)(2,1)S(1)}, bf16[128,768]{1,0:T(8,128)(2,1)S(1)}, u32[]{:S(2)}, u32[]{:S(2)}) collective-permute-start(bf16[128,768]{1,0:T(8,128)(2,1)S(1)} %get-tuple-element.115.refs_0_), channel_id=1, source_target_pairs={{0,2},{1,3},{2,0},{3,1},{4,6},{5,7},{6,4},{7,5},{8,10},{9,11},{10,... | collective-permute-start | bytes 589832 | tf_op jit(solution)/shard_map/ppermute | solution.py:409
  114.8 3.6 %collective-permute-done.21.refs_0_ = bf16[128,768]{1,0:T(8,128)(2,1)S(1)} collective-permute-done((bf16[128,768]{1,0:T(8,128)(2,1)S(1)}, bf16[128,768]{1,0:T(8,128)(2,1)S(1)}, u32[]{:S(2)}, u32[]{:S(2)}) %collective-permute-start.21) | collective-permute-done | bytes 196640 | tf_op jit(solution)/shard_map/ppermute | solution.py:409
  118.4 1.6 %collective-permute-start.27 = (bf16[128,768]{1,0:T(8,128)(2,1)S(1)}, bf16[128,768]{1,0:T(8,128)(2,1)S(1)}, u32[]{:S(2)}, u32[]{:S(2)}) collective-permute-start(bf16[128,768]{1,0:T(8,128)(2,1)S(1)} %collective-permute-done.21.refs_0_), channel_id=1, source_target_pairs={{0,4},{1,5},{2,6},{3,7},{4,0},{5,1},{6,2},{7,3},{8,12},{9,13},{10,... | collective-permute-start | bytes 589832 | tf_op jit(solution)/shard_map/ppermute | solution.py:409
  121.5 1.7 %collective-permute-done.22.refs_1_ = bf16[144,768]{1,0:T(8,128)(2,1)S(1)} collective-permute-done((bf16[144,768]{1,0:T(8,128)(2,1)S(1)}, bf16[144,768]{1,0:T(8,128)(2,1)S(1)}, u32[]{:S(2)}, u32[]{:S(2)}) %collective-permute-start.22) | collective-permute-done | bytes 221216 | tf_op jit(solution)/shard_map/ppermute | solution.py:409
  123.7 1.8 %assemble.3 = (f32[2048,768]{1,0:T(8,128)}, f32[8,1,256]{2,1,0:T(1,128)}) custom-call(s32[2]{0:T(128)S(1)} %pad_add_fusion.ids, bf16[128,768]{1,0:T(8,128)(2,1)S(1)} %get-tuple-element.115.refs_0_, bf16[144,768]{1,0:T(8,128)(2,1)S(1)} %get-tuple-element.116.refs_1_, bf16[128,768]{1,0:T(8,128)(2,1)S(1)} %collective-permute-done.24.refs_2_, ...), custom_call_target="tpu_custom_call" | custom-call | tf_op jit(solution)/shard_map/assemble/pallas_call | solution.py:374
  125.5 2.6 %collective-permute-done.27.refs_0_ = bf16[128,768]{1,0:T(8,128)(2,1)S(1)} collective-permute-done((bf16[128,768]{1,0:T(8,128)(2,1)S(1)}, bf16[128,768]{1,0:T(8,128)(2,1)S(1)}, u32[]{:S(2)}, u32[]{:S(2)}) %collective-permute-start.27) | collective-permute-done | bytes 196640 | tf_op jit(solution)/shard_map/ppermute | solution.py:409
  130.2 2.3 %assemble.4 = (f32[2048,768]{1,0:T(8,128)}, f32[8,1,256]{2,1,0:T(1,128)}) custom-call(s32[2]{0:T(128)S(1)} %pad_add_fusion.ids, bf16[128,768]{1,0:T(8,128)(2,1)S(1)} %collective-permute-done.21.refs_0_, bf16[144,768]{1,0:T(8,128)(2,1)S(1)} %collective-permute-done.22.refs_1_, ...), custom_call_target="tpu_custom_call", output_to_operand_aliasing={{0}: (9, {}), {1}: (10, {})} | custom-call | tf_op jit(solution)/shard_map/assemble/pallas_call | solution.py:374
  132.6 1.8 %assemble.5 = (f32[2048,768]{1,0:T(8,128)}, f32[8,1,256]{2,1,0:T(1,128)}) custom-call(s32[2]{0:T(128)S(1)} %pad_add_fusion.ids, bf16[128,768]{1,0:T(8,128)(2,1)S(1)} %collective-permute-done.27.refs_0_, bf16[144,768]{1,0:T(8,128)(2,1)S(1)} %collective-permute-done.28.refs_1_, ...), custom_call_target="tpu_custom_call", output_to_operand_aliasing={{0}: (5, {}), {1}: (6, {})} | custom-call | tf_op jit(solution)/shard_map/assemble/pallas_call | solution.py:374
  (62 shorter events, 21.3 us)
Async XLA Ops:
  0.6 11.4 %collective-permute-start.3 = (bf16[512,768]{1,0:T(8,128)(2,1)}, bf16[512,768]{1,0:T(8,128)(2,1)S(1)}, u32[]{:S(2)}, u32[]{:S(2)}) collective-permute-start(bf16[512,768]{1,0:T(8,128)(2,1)} %refs_0_.1), channel_id=1, source_target_pairs={{0,1},{1,0},{2,3},{3,2},{4,5},{5,4},{6,7},{7,6},{8,9},{9,8},{10,11... | collective-permute-start | bytes 2359304 | tf_op jit(solution)/shard_map/ppermute | solution.py:415
  1.1 21.0 %collective-permute-start.2 = (bf16[512,768]{1,0:T(8,128)(2,1)}, bf16[512,768]{1,0:T(8,128)(2,1)S(1)}, u32[]{:S(2)}, u32[]{:S(2)}) collective-permute-start(bf16[512,768]{1,0:T(8,128)(2,1)} %refs_0_.1), channel_id=1, source_target_pairs={{8,0},{0,8},{24,16},{16,24},{9,1},{1,9},{25,17},{17,25},{10,2},{2,... | collective-permute-start | bytes 2359304 | tf_op jit(solution)/shard_map/ppermute | solution.py:433
  3.8 19.1 %collective-permute-start = (bf16[512,768]{1,0:T(8,128)(2,1)}, bf16[512,768]{1,0:T(8,128)(2,1)S(1)}, u32[]{:S(2)}, u32[]{:S(2)}) collective-permute-start(bf16[512,768]{1,0:T(8,128)(2,1)} %refs_0_.1), channel_id=1, source_target_pairs={{16,8},{8,16},{17,9},{9,17},{18,10},{10,18},{19,11},{11,19},{20,12... | collective-permute-start | bytes 2359304 | tf_op jit(solution)/shard_map/ppermute | solution.py:433
  22.1 4.6 %collective-permute-start.5 = (bf16[512,768]{1,0:T(8,128)(2,1)S(1)}, bf16[512,768]{1,0:T(8,128)(2,1)S(1)}, u32[]{:S(2)}, u32[]{:S(2)}) collective-permute-start(bf16[512,768]{1,0:T(8,128)(2,1)S(1)} %collective-permute-done.2.refs_0_), channel_id=1, source_target_pairs={{0,1},{1,0},{2,3},{3,2},{4,5},{5,4},{6,7},{7,6},{8,9},{9,8},{10,11... | collective-permute-start | bytes 2359304 | tf_op jit(solution)/shard_map/ppermute | solution.py:415
  22.1 6.5 %collective-permute-start.4 = (bf16[512,768]{1,0:T(8,128)(2,1)S(1)}, bf16[512,768]{1,0:T(8,128)(2,1)S(1)}, u32[]{:S(2)}, u32[]{:S(2)}) collective-permute-start(bf16[512,768]{1,0:T(8,128)(2,1)S(1)} %collective-permute-done.2.refs_0_), channel_id=1, source_target_pairs={{16,8},{8,16},{17,9},{9,17},{18,10},{10,18},{19,11},{11,19},{20,12... | collective-permute-start | bytes 2359304 | tf_op jit(solution)/shard_map/ppermute | solution.py:433
  22.9 23.7 %collective-permute-start.1 = (bf16[512,768]{1,0:T(8,128)(2,1)S(1)}, bf16[512,768]{1,0:T(8,128)(2,1)S(1)}, u32[]{:S(2)}, u32[]{:S(2)}) collective-permute-start(bf16[512,768]{1,0:T(8,128)(2,1)S(1)} %collective-permute-done.refs_0_), channel_id=1, source_target_pairs={{8,0},{16,24},{9,1},{17,25},{10,2},{18,26},{11,3},{19,27},{12,4},{... | collective-permute-start | bytes 2359304 | tf_op jit(solution)/shard_map/ppermute | solution.py:433
  24.2 28.2 %collective-permute-start.8 = (bf16[512,768]{1,0:T(8,128)(2,1)S(1)}, bf16[512,768]{1,0:T(8,128)(2,1)S(1)}, u32[]{:S(2)}, u32[]{:S(2)}) collective-permute-start(bf16[512,768]{1,0:T(8,128)(2,1)S(1)} %collective-permute-done.refs_0_), channel_id=1, source_target_pairs={{8,9},{9,8},{10,11},{11,10},{12,13},{13,12},{14,15},{15,14},{16,17... | collective-permute-start | bytes 2359304 | tf_op jit(solution)/shard_map/ppermute | solution.py:415
  46.6 5.8 %collective-permute-start.9 = (bf16[512,768]{1,0:T(8,128)(2,1)S(1)}, bf16[512,768]{1,0:T(8,128)(2,1)S(1)}, u32[]{:S(2)}, u32[]{:S(2)}) collective-permute-start(bf16[512,768]{1,0:T(8,128)(2,1)S(1)} %collective-permute-done.1.refs_1_), channel_id=1, source_target_pairs={{0,1},{1,0},{2,3},{3,2},{4,5},{5,4},{6,7},{7,6},{24,25},{25,24},{2... | collective-permute-start | bytes 2359304 | tf_op jit(solution)/shard_map/ppermute | solution.py:415
  48.5 21.8 %collective-permute-start.7 = (bf16[512,768]{1,0:T(8,128)(2,1)S(1)}, bf16[512,768]{1,0:T(8,128)(2,1)S(1)}, u32[]{:S(2)}, u32[]{:S(2)}) collective-permute-start(bf16[512,768]{1,0:T(8,128)(2,1)S(1)} %collective-permute-done.4.refs_0_), channel_id=1, source_target_pairs={{8,0},{16,24},{9,1},{17,25},{10,2},{18,26},{11,3},{19,27},{12,4},{... | collective-permute-start | bytes 2359304 | tf_op jit(solution)/shard_map/ppermute | solution.py:433
  49.8 24.3 %collective-permute-start.6 = (bf16[512,768]{1,0:T(8,128)(2,1)S(1)}, bf16[512,768]{1,0:T(8,128)(2,1)S(1)}, u32[]{:S(2)}, u32[]{:S(2)}) collective-permute-start(bf16[512,768]{1,0:T(8,128)(2,1)S(1)} %collective-permute-done.4.refs_0_), channel_id=1, source_target_pairs={{8,9},{9,8},{10,11},{11,10},{12,13},{13,12},{14,15},{15,14},{16,17... | collective-permute-start | bytes 2359304 | tf_op jit(solution)/shard_map/ppermute | solution.py:415
  70.4 4.2 %collective-permute-start.10 = (bf16[512,768]{1,0:T(8,128)(2,1)S(1)}, bf16[512,768]{1,0:T(8,128)(2,1)S(1)}, u32[]{:S(2)}, u32[]{:S(2)}) collective-permute-start(bf16[512,768]{1,0:T(8,128)(2,1)S(1)} %collective-permute-done.7.refs_1_), channel_id=1, source_target_pairs={{0,1},{1,0},{2,3},{3,2},{4,5},{5,4},{6,7},{7,6},{24,25},{25,24},{2... | collective-permute-start | bytes 2359304 | tf_op jit(solution)/shard_map/ppermute | solution.py:415
  77.7 5.6 %collective-permute-start.12 = (f32[8,1,512]{2,1,0:T(1,128)S(1)}, f32[8,1,512]{2,1,0:T(1,128)S(1)}, u32[]{:S(2)}, u32[]{:S(2)}) collective-permute-start(f32[8,1,512]{2,1,0:T(1,128)S(1)} %add.22.refs_0_), channel_id=1, source_target_pairs={{0,8},{8,16},{16,24},{24,0},{1,9},{9,17},{17,25},{25,1},{2,10},{10... | collective-permute-start | bytes 49160 | tf_op jit(solution)/shard_map/ppermute | solution.py:481
  77.7 5.5 %collective-permute-start.13 = (f32[8,1,512]{2,1,0:T(1,128)S(1)}, f32[8,1,512]{2,1,0:T(1,128)S(1)}, u32[]{:S(2)}, u32[]{:S(2)}) collective-permute-start(f32[8,1,512]{2,1,0:T(1,128)S(1)} %add.22.refs_0_), channel_id=1, source_target_pairs={{0,16},{8,24},{16,0},{24,8},{1,17},{9,25},{17,1},{25,9},{2,18},{10... | collective-permute-start | bytes 49160 | tf_op jit(solution)/shard_map/ppermute | solution.py:481
  80.2 3.7 %collective-permute-start.14 = (f32[8,1,512]{2,1,0:T(1,128)S(1)}, f32[8,1,512]{2,1,0:T(1,128)S(1)}, u32[]{:S(2)}, u32[]{:S(2)}) collective-permute-start(f32[8,1,512]{2,1,0:T(1,128)S(1)} %add.22.refs_0_), channel_id=1, source_target_pairs={{0,24},{8,0},{16,8},{24,16},{1,25},{9,1},{17,9},{25,17},{2,26},{10... | collective-permute-start | bytes 49160 | tf_op jit(solution)/shard_map/ppermute | solution.py:481
  93.7 8.4 %collective-permute-start.19 = (bf16[144,768]{1,0:T(8,128)(2,1)S(1)}, bf16[144,768]{1,0:T(8,128)(2,1)S(1)}, u32[]{:S(2)}, u32[]{:S(2)}) collective-permute-start(bf16[144,768]{1,0:T(8,128)(2,1)S(1)} %get-tuple-element.114), channel_id=1, source_target_pairs={{0,4},{1,5},{2,6},{3,7},{4,0},{5,1},{6,2},{7,3},{8,12},{9,13},{10,... | collective-permute-start | bytes 663560 | tf_op jit(solution)/shard_map/ppermute | solution.py:409
  95.3 9.0 %collective-permute-start.17 = (bf16[128,768]{1,0:T(8,128)(2,1)S(1)}, bf16[128,768]{1,0:T(8,128)(2,1)S(1)}, u32[]{:S(2)}, u32[]{:S(2)}) collective-permute-start(bf16[128,768]{1,0:T(8,128)(2,1)S(1)} %get-tuple-element.112), channel_id=1, source_target_pairs={{0,2},{1,3},{2,0},{3,1},{4,6},{5,7},{6,4},{7,5},{8,10},{9,11},{10,... | collective-permute-start | bytes 589832 | tf_op jit(solution)/shard_map/ppermute | solution.py:409
  96.8 13.5 %collective-permute-start.16 = (bf16[144,768]{1,0:T(8,128)(2,1)S(1)}, bf16[144,768]{1,0:T(8,128)(2,1)S(1)}, u32[]{:S(2)}, u32[]{:S(2)}) collective-permute-start(bf16[144,768]{1,0:T(8,128)(2,1)S(1)} %get-tuple-element.110), channel_id=1, source_target_pairs={{0,4},{1,5},{2,6},{3,7},{4,0},{5,1},{6,2},{7,3},{8,12},{9,13},{10,... | collective-permute-start | bytes 663560 | tf_op jit(solution)/shard_map/ppermute | solution.py:409
  102.2 8.1 %collective-permute-start.20 = (bf16[144,768]{1,0:T(8,128)(2,1)S(1)}, bf16[144,768]{1,0:T(8,128)(2,1)S(1)}, u32[]{:S(2)}, u32[]{:S(2)}) collective-permute-start(bf16[144,768]{1,0:T(8,128)(2,1)S(1)} %pass_on.3), channel_id=1, source_target_pairs={{0,2},{1,3},{2,0},{3,1},{4,6},{5,7},{6,4},{7,5},{8,10},{9,11},{10,... | collective-permute-start | bytes 663560 | tf_op jit(solution)/shard_map/ppermute | solution.py:409
  103.8 6.5 %collective-permute-start.15 = (bf16[128,768]{1,0:T(8,128)(2,1)S(1)}, bf16[128,768]{1,0:T(8,128)(2,1)S(1)}, u32[]{:S(2)}, u32[]{:S(2)}) collective-permute-start(bf16[128,768]{1,0:T(8,128)(2,1)S(1)} %get-tuple-element.109), channel_id=1, source_target_pairs={{0,2},{1,3},{2,0},{3,1},{4,6},{5,7},{6,4},{7,5},{8,10},{9,11},{10,... | collective-permute-start | bytes 589832 | tf_op jit(solution)/shard_map/ppermute | solution.py:409
  104.4 6.0 %collective-permute-start.18 = (bf16[128,768]{1,0:T(8,128)(2,1)S(1)}, bf16[128,768]{1,0:T(8,128)(2,1)S(1)}, u32[]{:S(2)}, u32[]{:S(2)}) collective-permute-start(bf16[128,768]{1,0:T(8,128)(2,1)S(1)} %pass_on.2), channel_id=1, source_target_pairs={{0,4},{1,5},{2,6},{3,7},{4,0},{5,1},{6,2},{7,3},{8,12},{9,13},{10,... | collective-permute-start | bytes 589832 | tf_op jit(solution)/shard_map/ppermute | solution.py:409
  110.6 3.7 %collective-permute-start.24 = (bf16[128,768]{1,0:T(8,128)(2,1)S(1)}, bf16[128,768]{1,0:T(8,128)(2,1)S(1)}, u32[]{:S(2)}, u32[]{:S(2)}) collective-permute-start(bf16[128,768]{1,0:T(8,128)(2,1)S(1)} %get-tuple-element.115.refs_0_), channel_id=1, source_target_pairs={{0,1},{1,0},{2,3},{3,2},{4,5},{5,4},{6,7},{7,6},{8,9},{9,8},{10,11... | collective-permute-start | bytes 589832 | tf_op jit(solution)/shard_map/ppermute | solution.py:409
  110.7 7.8 %collective-permute-start.21 = (bf16[128,768]{1,0:T(8,128)(2,1)S(1)}, bf16[128,768]{1,0:T(8,128)(2,1)S(1)}, u32[]{:S(2)}, u32[]{:S(2)}) collective-permute-start(bf16[128,768]{1,0:T(8,128)(2,1)S(1)} %get-tuple-element.115.refs_0_), channel_id=1, source_target_pairs={{0,2},{1,3},{2,0},{3,1},{4,6},{5,7},{6,4},{7,5},{8,10},{9,11},{10,... | collective-permute-start | bytes 589832 | tf_op jit(solution)/shard_map/ppermute | solution.py:409
  112.2 8.3 %collective-permute-start.26 = (bf16[144,768]{1,0:T(8,128)(2,1)S(1)}, bf16[144,768]{1,0:T(8,128)(2,1)S(1)}, u32[]{:S(2)}, u32[]{:S(2)}) collective-permute-start(bf16[144,768]{1,0:T(8,128)(2,1)S(1)} %get-tuple-element.116.refs_1_), channel_id=1, source_target_pairs={{0,4},{1,5},{2,6},{3,7},{4,0},{5,1},{6,2},{7,3},{8,12},{9,13},{10,... | collective-permute-start | bytes 663560 | tf_op jit(solution)/shard_map/ppermute | solution.py:409
  113.8 9.4 %collective-permute-start.22 = (bf16[144,768]{1,0:T(8,128)(2,1)S(1)}, bf16[144,768]{1,0:T(8,128)(2,1)S(1)}, u32[]{:S(2)}, u32[]{:S(2)}) collective-permute-start(bf16[144,768]{1,0:T(8,128)(2,1)S(1)} %get-tuple-element.116.refs_1_), channel_id=1, source_target_pairs={{0,2},{1,3},{2,0},{3,1},{4,6},{5,7},{6,4},{7,5},{8,10},{9,11},{10,... | collective-permute-start | bytes 663560 | tf_op jit(solution)/shard_map/ppermute | solution.py:409
  114.3 8.9 %collective-permute-start.25 = (bf16[144,768]{1,0:T(8,128)(2,1)S(1)}, bf16[144,768]{1,0:T(8,128)(2,1)S(1)}, u32[]{:S(2)}, u32[]{:S(2)}) collective-permute-start(bf16[144,768]{1,0:T(8,128)(2,1)S(1)} %get-tuple-element.116.refs_1_), channel_id=1, source_target_pairs={{0,1},{1,0},{2,3},{3,2},{4,5},{5,4},{6,7},{7,6},{8,9},{9,8},{10,11... | collective-permute-start | bytes 663560 | tf_op jit(solution)/shard_map/ppermute | solution.py:409
  114.3 11.1 %collective-permute-start.23 = (bf16[128,768]{1,0:T(8,128)(2,1)S(1)}, bf16[128,768]{1,0:T(8,128)(2,1)S(1)}, u32[]{:S(2)}, u32[]{:S(2)}) collective-permute-start(bf16[128,768]{1,0:T(8,128)(2,1)S(1)} %get-tuple-element.115.refs_0_), channel_id=1, source_target_pairs={{0,4},{1,5},{2,6},{3,7},{4,0},{5,1},{6,2},{7,3},{8,12},{9,13},{10,... | collective-permute-start | bytes 589832 | tf_op jit(solution)/shard_map/ppermute | solution.py:409
  118.4 9.7 %collective-permute-start.27 = (bf16[128,768]{1,0:T(8,128)(2,1)S(1)}, bf16[128,768]{1,0:T(8,128)(2,1)S(1)}, u32[]{:S(2)}, u32[]{:S(2)}) collective-permute-start(bf16[128,768]{1,0:T(8,128)(2,1)S(1)} %collective-permute-done.21.refs_0_), channel_id=1, source_target_pairs={{0,4},{1,5},{2,6},{3,7},{4,0},{5,1},{6,2},{7,3},{8,12},{9,13},{10,... | collective-permute-start | bytes 589832 | tf_op jit(solution)/shard_map/ppermute | solution.py:409
  120.5 9.1 %collective-permute-start.28 = (bf16[144,768]{1,0:T(8,128)(2,1)S(1)}, bf16[144,768]{1,0:T(8,128)(2,1)S(1)}, u32[]{:S(2)}, u32[]{:S(2)}) collective-permute-start(bf16[144,768]{1,0:T(8,128)(2,1)S(1)} %collective-permute-done.26.refs_3_), channel_id=1, source_target_pairs={{0,2},{1,3},{2,0},{3,1},{4,6},{5,7},{6,4},{7,5},{8,10},{9,11},{10,... | collective-permute-start | bytes 663560 | tf_op jit(solution)/shard_map/ppermute | solution.py:409
  123.2 6.5 %collective-permute-start.30 = (bf16[144,768]{1,0:T(8,128)(2,1)S(1)}, bf16[144,768]{1,0:T(8,128)(2,1)S(1)}, u32[]{:S(2)}, u32[]{:S(2)}) collective-permute-start(bf16[144,768]{1,0:T(8,128)(2,1)S(1)} %collective-permute-done.22.refs_1_), channel_id=1, source_target_pairs={{0,1},{1,0},{2,3},{3,2},{4,5},{5,4},{6,7},{7,6},{8,9},{9,8},{10,11... | collective-permute-start | bytes 663560 | tf_op jit(solution)/shard_map/ppermute | solution.py:409
  123.2 6.5 %collective-permute-start.32 = (bf16[144,768]{1,0:T(8,128)(2,1)S(1)}, bf16[144,768]{1,0:T(8,128)(2,1)S(1)}, u32[]{:S(2)}, u32[]{:S(2)}) collective-permute-start(bf16[144,768]{1,0:T(8,128)(2,1)S(1)} %collective-permute-done.26.refs_3_), channel_id=1, source_target_pairs={{0,1},{1,0},{2,3},{3,2},{4,5},{5,4},{6,7},{7,6},{8,9},{9,8},{10,11... | collective-permute-start | bytes 663560 | tf_op jit(solution)/shard_map/ppermute | solution.py:409
  129.6 2.9 %collective-permute-start.34 = (bf16[144,768]{1,0:T(8,128)(2,1)S(1)}, bf16[144,768]{1,0:T(8,128)(2,1)S(1)}, u32[]{:S(2)}, u32[]{:S(2)}) collective-permute-start(bf16[144,768]{1,0:T(8,128)(2,1)S(1)} %collective-permute-done.28.refs_1_), channel_id=1, source_target_pairs={{0,1},{1,0},{2,3},{3,2},{4,5},{5,4},{6,7},{7,6},{8,9},{9,8},{10,11... | collective-permute-start | bytes 663560 | tf_op jit(solution)/shard_map/ppermute | solution.py:409
  129.8 2.7 %collective-permute-start.33 = (bf16[128,768]{1,0:T(8,128)(2,1)S(1)}, bf16[128,768]{1,0:T(8,128)(2,1)S(1)}, u32[]{:S(2)}, u32[]{:S(2)}) collective-permute-start(bf16[128,768]{1,0:T(8,128)(2,1)S(1)} %collective-permute-done.27.refs_0_), channel_id=1, source_target_pairs={{0,1},{1,0},{2,3},{3,2},{4,5},{5,4},{6,7},{7,6},{8,9},{9,8},{10,11... | collective-permute-start | bytes 589832 | tf_op jit(solution)/shard_map/ppermute | solution.py:409
  (4 other events, 6.5 us)

commit v12 on v11

--- a/solution.py
+++ b/solution.py
@@ -541,15 +541,12 @@
         last_half, done = lax.optimization_barrier((second[1], done))
         far[1] = (2, (last_half, first[1]))
     swapped = [swap(halves) for _, halves in far[:-1]]
-    arrays, swapped, done = lax.optimization_barrier(
-        ([halves for _, halves in far], swapped, done)
-    )
-    swapped.append(swap(arrays[-1]))
-    placed = [(0, away, halves) for (away, _), halves in zip(far, arrays)]
-    placed += [(1, away, halves) for (away, _), halves in zip(far, swapped)]
-    last = [piece for piece in placed if piece[1] == n_owners - 1]
-    early = [piece for piece in placed if piece[1] != n_owners - 1]
-    done = assemble(ids, early, done, n_rows, factor)
+    *near, (corner_away, corner_halves) = far
+    placed = [(0, away, halves) for away, halves in near]
+    placed += [(1, away, halves) for (away, _), halves in zip(near, swapped)]
+    done = assemble(ids, placed, done, n_rows, factor)
+    corner_halves, done = lax.optimization_barrier((corner_halves, done))
+    last = [(0, corner_away, corner_halves), (1, corner_away, swap(corner_halves))]
     done = assemble(ids, last, done, n_rows, factor)
     result, weights = done
     return (result, weights.reshape(local_centroids))

time: 135 us -> 138 us (1.022)
  waiting for transfers between devices: 65.3 us -> 67.9 us
    ppermute x21, waiting for transfers between devices: 20.1 us -> 22.8 us  [exchange(): lax.ppermute(array, 'rows', [(i, i ^ distance) for i in range(n_rows)])]
  transfers between devices with their start and end apart: 35 -> 35, of which waited for: 14 -> 13; matrix products, arithmetic and copies ran while one was open for 3% -> 3% of each run, Pallas kernels for 13% -> 12%
where the time goes in v12:
time: 138 us
  waiting for transfers between devices  67.9 us (49%)
  starting transfers between devices  32.2 us (23%)
  Pallas kernels  30.8 us (22%)
  other arithmetic  4.31 us (3%)
    ppermute x5, waiting for transfers between devices, start_ready(): lax.ppermute(slots[source_slot][hold][0], 'blk', pairs)  42.4 us
    ppermute x21, waiting for transfers between devices, exchange(): lax.ppermute(array, 'rows', [(i, i ^ distance) for i in range(n_rows)])  22.8 us
    ppermute x21, starting transfers between devices, exchange(): lax.ppermute(array, 'rows', [(i, i ^ distance) for i in range(n_rows)])  15.9 us
    pallas_call x8, Pallas kernels, score_block(): pl.pallas_call(functools.partial(score_kernel, n_sources, choice), grid_s...  14.8 us
    pallas_call x1, Pallas kernels, sum_rows(): pl.pallas_call(functools.partial(sum_kernel, plan, len(totals), n_owners,...  9.8 us
    ppermute x5, starting transfers between devices, start_ready(): lax.ppermute(slots[source_slot][hold][0], 'blk', pairs)  6.63 us
    pallas_call x3, Pallas kernels, assemble(): pl.pallas_call(functools.partial(assemble_kernel, factor, spots, n_blocks...  5.87 us
    ppermute x6, starting transfers between devices, swap_cores(): return lax.ppermute(array, ('blk', 'rows'), pairs)  5.76 us
  transfers between devices with their start and end apart: 35, of which 13 were waited for; matrix products, arithmetic and copies ran while one was open for 3% of the time, Pallas kernels for 12%

profile of v12, /device:TPU:0, one launch (start us, length us, event | category | flops | bytes accessed | tf_op | source)
XLA Modules:
  0.0 137.6 jit_solution(13998901893483748744)
XLA Ops:
  1.1 2.7 %collective-permute-start.2 = (bf16[512,768]{1,0:T(8,128)(2,1)}, bf16[512,768]{1,0:T(8,128)(2,1)S(1)}, u32[]{:S(2)}, u32[]{:S(2)}) collective-permute-start(bf16[512,768]{1,0:T(8,128)(2,1)} %refs_0_.1), channel_id=1, source_target_pairs={{8,0},{0,8},{24,16},{16,24},{9,1},{1,9},{25,17},{17,25},{10,2},{2,... | collective-permute-start | bytes 2359304 | tf_op jit(solution)/shard_map/ppermute | solution.py:433
  5.3 1.8 %fusion = f32[1024]{0:T(1024)S(1)} fusion(bf16[2048,768]{1,0:T(8,128)(2,1)} %param.4, s32[]{:T(128)S(6)} %select_n.4), kind=kLoop, calls=%fused_computation.2 | loop fusion | flops 2358272 | bytes 1576964 | tf_op jit(solution)/shard_map/reduce_sum | solution.py:21
  7.1 1.7 %fusion.1.refs_1_.refs_2_ = bf16[1024,768]{1,0:T(8,128)(2,1)S(1)} fusion(f32[1024]{0:T(1024)S(1)} %add_rsqrt_fusion, bf16[2048,768]{1,0:T(8,128)(2,1)} %param.4, s32[]{:T(128)S(6)} %select_n.4), kind=kLoop, calls=%fused_computation.3 | loop fusion | flops 2359296 | bytes 3149828 | tf_op jit(solution)/shard_map/convert_element_type | solution.py:21
  10.2 1.8 %scores.8 = (f32[8,1024,512]{2,1,0:T(8,128)S(1)}, bf16[4096,768]{1,0:T(8,128)(2,1)S(1)}, f32[8,1,512]{2,1,0:T(1,128)S(1)}) custom-call(s32[2]{0:T(128)S(1)} %pad_add_fusion.ids, bf16[512,768]{1,0:T(8,128)(2,1)S(1)} %copy-done, bf16[1024,768]{1,0:T(8,128)(2,1)S(1)} %fusion.1.refs_1_.refs_2_, f32[1024,128]{1,0:T(8,128)S(1)} %broadcast_in_dim.2.refs_2_.refs_3_), custom_call_target="tpu_custom_call" | custom-call | flops 805306368 | bytes 7340032 | tf_op jit(solution)/shard_map/scores/pallas_call | solution.py:105
  12.0 1.8 %scores.9 = (f32[8,1024,512]{2,1,0:T(8,128)S(1)}, bf16[4096,768]{1,0:T(8,128)(2,1)S(1)}, f32[8,1,512]{2,1,0:T(1,128)S(1)}) custom-call(s32[2]{0:T(128)S(1)} %pad_add_fusion.ids, bf16[512,768]{1,0:T(8,128)(2,1)S(1)} %collective-permute-done.3.refs_0_, ...), custom_call_target="tpu_custom_call", output_to_operand_aliasing={{0}: (4, {}), {1}: (5, {}), {2}: (6, {})} | custom-call | flops 805306368 | bytes 7340032 | tf_op jit(solution)/shard_map/scores/pallas_call | solution.py:105
  13.9 8.3 %collective-permute-done.2.refs_0_ = bf16[512,768]{1,0:T(8,128)(2,1)S(1)} collective-permute-done((bf16[512,768]{1,0:T(8,128)(2,1)}, bf16[512,768]{1,0:T(8,128)(2,1)S(1)}, u32[]{:S(2)}, u32[]{:S(2)}) %collective-permute-start.2) | collective-permute-done | bytes 786464 | tf_op jit(solution)/shard_map/ppermute | solution.py:433
  24.9 1.8 %scores.10 = (f32[8,1024,512]{2,1,0:T(8,128)S(1)}, bf16[4096,768]{1,0:T(8,128)(2,1)S(1)}, f32[8,1,512]{2,1,0:T(1,128)S(1)}) custom-call(s32[2]{0:T(128)S(1)} %pad_add_fusion.ids, bf16[512,768]{1,0:T(8,128)(2,1)S(1)} %collective-permute-done.2.refs_0_, ...), custom_call_target="tpu_custom_call", output_to_operand_aliasing={{0}: (4, {}), {1}: (5, {}), {2}: (6, {})} | custom-call | flops 805306368 | bytes 7340032 | tf_op jit(solution)/shard_map/scores/pallas_call | solution.py:105
  26.7 1.8 %scores.11 = (f32[8,1024,512]{2,1,0:T(8,128)S(1)}, bf16[4096,768]{1,0:T(8,128)(2,1)S(1)}, f32[8,1,512]{2,1,0:T(1,128)S(1)}) custom-call(s32[2]{0:T(128)S(1)} %pad_add_fusion.ids, bf16[512,768]{1,0:T(8,128)(2,1)S(1)} %collective-permute-done.5.refs_0_, ...), custom_call_target="tpu_custom_call", output_to_operand_aliasing={{0}: (4, {}), {1}: (5, {}), {2}: (6, {})} | custom-call | flops 805306368 | bytes 7340032 | tf_op jit(solution)/shard_map/scores/pallas_call | solution.py:105
  28.6 18.0 %collective-permute-done.1.refs_1_ = bf16[512,768]{1,0:T(8,128)(2,1)S(1)} collective-permute-done((bf16[512,768]{1,0:T(8,128)(2,1)S(1)}, bf16[512,768]{1,0:T(8,128)(2,1)S(1)}, u32[]{:S(2)}, u32[]{:S(2)}) %collective-permute-start.1) | collective-permute-done | bytes 786464 | tf_op jit(solution)/shard_map/ppermute | solution.py:433
  46.6 1.9 %collective-permute-start.9 = (bf16[512,768]{1,0:T(8,128)(2,1)S(1)}, bf16[512,768]{1,0:T(8,128)(2,1)S(1)}, u32[]{:S(2)}, u32[]{:S(2)}) collective-permute-start(bf16[512,768]{1,0:T(8,128)(2,1)S(1)} %collective-permute-done.1.refs_1_), channel_id=1, source_target_pairs={{0,1},{1,0},{2,3},{3,2},{4,5},{5,4},{6,7},{7,6},{24,25},{25,24},{2... | collective-permute-start | bytes 2359304 | tf_op jit(solution)/shard_map/ppermute | solution.py:415
  50.5 1.8 %scores.12 = (f32[8,1024,512]{2,1,0:T(8,128)S(1)}, bf16[4096,768]{1,0:T(8,128)(2,1)S(1)}, f32[8,1,512]{2,1,0:T(1,128)S(1)}) custom-call(s32[2]{0:T(128)S(1)} %pad_add_fusion.ids, bf16[512,768]{1,0:T(8,128)(2,1)S(1)} %collective-permute-done.refs_0_, ...), custom_call_target="tpu_custom_call", output_to_operand_aliasing={{0}: (5, {}), {1}: (6, {}), {2}: (7, {})} | custom-call | flops 805306368 | bytes 7340032 | tf_op jit(solution)/shard_map/scores/pallas_call | solution.py:105
  52.4 1.8 %scores.13 = (f32[8,1024,512]{2,1,0:T(8,128)S(1)}, bf16[4096,768]{1,0:T(8,128)(2,1)S(1)}, f32[8,1,512]{2,1,0:T(1,128)S(1)}) custom-call(s32[2]{0:T(128)S(1)} %pad_add_fusion.ids, bf16[512,768]{1,0:T(8,128)(2,1)S(1)} %collective-permute-done.8.refs_0_, ...), custom_call_target="tpu_custom_call", output_to_operand_aliasing={{0}: (5, {}), {1}: (6, {}), {2}: (7, {})} | custom-call | flops 805306368 | bytes 7340032 | tf_op jit(solution)/shard_map/scores/pallas_call | solution.py:105
  54.3 16.1 %collective-permute-done.7.refs_1_ = bf16[512,768]{1,0:T(8,128)(2,1)S(1)} collective-permute-done((bf16[512,768]{1,0:T(8,128)(2,1)S(1)}, bf16[512,768]{1,0:T(8,128)(2,1)S(1)}, u32[]{:S(2)}, u32[]{:S(2)}) %collective-permute-start.7) | collective-permute-done | bytes 786464 | tf_op jit(solution)/shard_map/ppermute | solution.py:433
  70.4 1.9 %collective-permute-start.10 = (bf16[512,768]{1,0:T(8,128)(2,1)S(1)}, bf16[512,768]{1,0:T(8,128)(2,1)S(1)}, u32[]{:S(2)}, u32[]{:S(2)}) collective-permute-start(bf16[512,768]{1,0:T(8,128)(2,1)S(1)} %collective-permute-done.7.refs_1_), channel_id=1, source_target_pairs={{0,1},{1,0},{2,3},{3,2},{4,5},{5,4},{6,7},{7,6},{24,25},{25,24},{2... | collective-permute-start | bytes 2359304 | tf_op jit(solution)/shard_map/ppermute | solution.py:415
  72.3 1.8 %scores.14 = (f32[8,1024,512]{2,1,0:T(8,128)S(1)}, bf16[4096,768]{1,0:T(8,128)(2,1)S(1)}, f32[8,1,512]{2,1,0:T(1,128)S(1)}) custom-call(s32[2]{0:T(128)S(1)} %pad_add_fusion.ids, bf16[512,768]{1,0:T(8,128)(2,1)S(1)} %collective-permute-done.4.refs_0_, ...), custom_call_target="tpu_custom_call", output_to_operand_aliasing={{0}: (5, {}), {1}: (6, {}), {2}: (7, {})} | custom-call | flops 805306368 | bytes 7340032 | tf_op jit(solution)/shard_map/scores/pallas_call | solution.py:105
  74.5 1.8 %scores.15 = (f32[8,1024,512]{2,1,0:T(8,128)S(1)}, bf16[4096,768]{1,0:T(8,128)(2,1)S(1)}, f32[8,1,512]{2,1,0:T(1,128)S(1)}) custom-call(s32[2]{0:T(128)S(1)} %pad_add_fusion.ids, bf16[512,768]{1,0:T(8,128)(2,1)S(1)} %collective-permute-done.6.refs_0_, ...), custom_call_target="tpu_custom_call", output_to_operand_aliasing={{0}: (5, {}), {1}: (6, {}), {2}: (7, {})} | custom-call | flops 805306368 | bytes 7340032 | tf_op jit(solution)/shard_map/scores/pallas_call | solution.py:105
  77.7 2.4 %collective-permute-start.13 = (f32[8,1,512]{2,1,0:T(1,128)S(1)}, f32[8,1,512]{2,1,0:T(1,128)S(1)}, u32[]{:S(2)}, u32[]{:S(2)}) collective-permute-start(f32[8,1,512]{2,1,0:T(1,128)S(1)} %add.22.refs_0_), channel_id=1, source_target_pairs={{0,16},{8,24},{16,0},{24,8},{1,17},{9,25},{17,1},{25,9},{2,18},{10... | collective-permute-start | bytes 49160 | tf_op jit(solution)/shard_map/ppermute | solution.py:481
  81.5 1.7 %collective-permute-done.12.refs_1_ = f32[8,1,512]{2,1,0:T(1,128)S(1)} collective-permute-done((f32[8,1,512]{2,1,0:T(1,128)S(1)}, f32[8,1,512]{2,1,0:T(1,128)S(1)}, u32[]{:S(2)}, u32[]{:S(2)}) %collective-permute-start.12) | collective-permute-done | bytes 16416 | tf_op jit(solution)/shard_map/ppermute | solution.py:481
  83.9 9.8 %sums.1 = (bf16[128,768]{1,0:T(8,128)(2,1)S(1)}, f32[144,768]{1,0:T(8,128)S(1)}, f32[128,768]{1,0:T(8,128)S(1)}, bf16[144,768]{1,0:T(8,128)(2,1)S(1)}, bf16[128,...) custom-call(s32[2]{0:T(128)S(1)} %pad_add_fusion.ids, ...), custom_call_target="tpu_custom_call" | custom-call | flops 6442450944 | bytes 26214400 | tf_op jit(solution)/shard_map/sums/pallas_call | solution.py:267
  93.7 1.6 %collective-permute-start.19 = (bf16[144,768]{1,0:T(8,128)(2,1)S(1)}, bf16[144,768]{1,0:T(8,128)(2,1)S(1)}, u32[]{:S(2)}, u32[]{:S(2)}) collective-permute-start(bf16[144,768]{1,0:T(8,128)(2,1)S(1)} %get-tuple-element.106), channel_id=1, source_target_pairs={{0,4},{1,5},{2,6},{3,7},{4,0},{5,1},{6,2},{7,3},{8,12},{9,13},{10,... | collective-permute-start | bytes 663560 | tf_op jit(solution)/shard_map/ppermute | solution.py:409
  97.3 4.8 %collective-permute-done.19.arrived = bf16[144,768]{1,0:T(8,128)(2,1)S(1)} collective-permute-done((bf16[144,768]{1,0:T(8,128)(2,1)S(1)}, bf16[144,768]{1,0:T(8,128)(2,1)S(1)}, u32[]{:S(2)}, u32[]{:S(2)}) %collective-permute-start.19) | collective-permute-done | bytes 221216 | tf_op jit(solution)/shard_map/ppermute | solution.py:409
  102.2 1.6 %collective-permute-start.20 = (bf16[144,768]{1,0:T(8,128)(2,1)S(1)}, bf16[144,768]{1,0:T(8,128)(2,1)S(1)}, u32[]{:S(2)}, u32[]{:S(2)}) collective-permute-start(bf16[144,768]{1,0:T(8,128)(2,1)S(1)} %pass_on.3), channel_id=1, source_target_pairs={{0,2},{1,3},{2,0},{3,1},{4,6},{5,7},{6,4},{7,5},{8,10},{9,11},{10,... | collective-permute-start | bytes 663560 | tf_op jit(solution)/shard_map/ppermute | solution.py:409
  104.4 1.6 %collective-permute-start.18 = (bf16[128,768]{1,0:T(8,128)(2,1)S(1)}, bf16[128,768]{1,0:T(8,128)(2,1)S(1)}, u32[]{:S(2)}, u32[]{:S(2)}) collective-permute-start(bf16[128,768]{1,0:T(8,128)(2,1)S(1)} %pass_on.2), channel_id=1, source_target_pairs={{0,4},{1,5},{2,6},{3,7},{4,0},{5,1},{6,2},{7,3},{8,12},{9,13},{10,... | collective-permute-start | bytes 589832 | tf_op jit(solution)/shard_map/ppermute | solution.py:409
  106.0 4.3 %collective-permute-done.15.refs_0_ = bf16[128,768]{1,0:T(8,128)(2,1)S(1)} collective-permute-done((bf16[128,768]{1,0:T(8,128)(2,1)S(1)}, bf16[128,768]{1,0:T(8,128)(2,1)S(1)}, u32[]{:S(2)}, u32[]{:S(2)}) %collective-permute-start.15) | collective-permute-done | bytes 196640 | tf_op jit(solution)/shard_map/ppermute | solution.py:409
  110.7 1.6 %collective-permute-start.21 = (bf16[128,768]{1,0:T(8,128)(2,1)S(1)}, bf16[128,768]{1,0:T(8,128)(2,1)S(1)}, u32[]{:S(2)}, u32[]{:S(2)}) collective-permute-start(bf16[128,768]{1,0:T(8,128)(2,1)S(1)} %get-tuple-element.107.refs_0_), channel_id=1, source_target_pairs={{0,2},{1,3},{2,0},{3,1},{4,6},{5,7},{6,4},{7,5},{8,10},{9,11},{10,... | collective-permute-start | bytes 589832 | tf_op jit(solution)/shard_map/ppermute | solution.py:409
  114.8 3.6 %collective-permute-done.21.refs_0_ = bf16[128,768]{1,0:T(8,128)(2,1)S(1)} collective-permute-done((bf16[128,768]{1,0:T(8,128)(2,1)S(1)}, bf16[128,768]{1,0:T(8,128)(2,1)S(1)}, u32[]{:S(2)}, u32[]{:S(2)}) %collective-permute-start.21) | collective-permute-done | bytes 196640 | tf_op jit(solution)/shard_map/ppermute | solution.py:409
  118.4 4.3 %collective-permute-done.25.refs_1_ = bf16[144,768]{1,0:T(8,128)(2,1)S(1)} collective-permute-done((bf16[144,768]{1,0:T(8,128)(2,1)S(1)}, bf16[144,768]{1,0:T(8,128)(2,1)S(1)}, u32[]{:S(2)}, u32[]{:S(2)}) %collective-permute-start.25) | collective-permute-done | bytes 221216 | tf_op jit(solution)/shard_map/ppermute | solution.py:409
  124.8 1.8 %assemble.3 = (f32[2048,768]{1,0:T(8,128)}, f32[8,1,256]{2,1,0:T(1,128)}) custom-call(s32[2]{0:T(128)S(1)} %pad_add_fusion.ids, bf16[128,768]{1,0:T(8,128)(2,1)S(1)} %get-tuple-element.107.refs_0_, bf16[144,768]{1,0:T(8,128)(2,1)S(1)} %get-tuple-element.108.refs_1_, bf16[128,768]{1,0:T(8,128)(2,1)S(1)} %collective-permute-done.27.refs_2_, ...), custom_call_target="tpu_custom_call" | custom-call | tf_op jit(solution)/shard_map/assemble/pallas_call | solution.py:374
  126.6 1.6 %collective-permute-start.22 = (bf16[128,768]{1,0:T(8,128)(2,1)S(1)}, bf16[128,768]{1,0:T(8,128)(2,1)S(1)}, u32[]{:S(2)}, u32[]{:S(2)}) collective-permute-start(bf16[128,768]{1,0:T(8,128)(2,1)S(1)} %collective-permute-done.21.refs_0_), channel_id=1, source_target_pairs={{0,4},{1,5},{2,6},{3,7},{4,0},{5,1},{6,2},{7,3},{8,12},{9,13},{10,... | collective-permute-start | bytes 589832 | tf_op jit(solution)/shard_map/ppermute | solution.py:409
  128.2 2.3 %assemble.4 = (f32[2048,768]{1,0:T(8,128)}, f32[8,1,256]{2,1,0:T(1,128)}) custom-call(s32[2]{0:T(128)S(1)} %pad_add_fusion.ids, bf16[128,768]{1,0:T(8,128)(2,1)S(1)} %collective-permute-done.21.refs_0_, bf16[144,768]{1,0:T(8,128)(2,1)S(1)} %collective-permute-done.25.refs_1_, ...), custom_call_target="tpu_custom_call", output_to_operand_aliasing={{0}: (9, {}), {1}: (10, {})} | custom-call | tf_op jit(solution)/shard_map/assemble/pallas_call | solution.py:374
  130.6 3.4 %collective-permute-done.22.refs_0_ = bf16[128,768]{1,0:T(8,128)(2,1)S(1)} collective-permute-done((bf16[128,768]{1,0:T(8,128)(2,1)S(1)}, bf16[128,768]{1,0:T(8,128)(2,1)S(1)}, u32[]{:S(2)}, u32[]{:S(2)}) %collective-permute-start.22) | collective-permute-done | bytes 196640 | tf_op jit(solution)/shard_map/ppermute | solution.py:409
  135.7 1.8 %assemble.5 = (f32[2048,768]{1,0:T(8,128)}, f32[8,1,256]{2,1,0:T(1,128)}) custom-call(s32[2]{0:T(128)S(1)} %pad_add_fusion.ids, bf16[128,768]{1,0:T(8,128)(2,1)S(1)} %collective-permute-done.22.refs_0_, bf16[144,768]{1,0:T(8,128)(2,1)S(1)} %collective-permute-done.24.refs_1_, ...), custom_call_target="tpu_custom_call", output_to_operand_aliasing={{0}: (5, {}), {1}: (6, {})} | custom-call | tf_op jit(solution)/shard_map/assemble/pallas_call | solution.py:374
  (62 shorter events, 21.1 us)
Async XLA Ops:
  0.6 11.4 %collective-permute-start.3 = (bf16[512,768]{1,0:T(8,128)(2,1)}, bf16[512,768]{1,0:T(8,128)(2,1)S(1)}, u32[]{:S(2)}, u32[]{:S(2)}) collective-permute-start(bf16[512,768]{1,0:T(8,128)(2,1)} %refs_0_.1), channel_id=1, source_target_pairs={{0,1},{1,0},{2,3},{3,2},{4,5},{5,4},{6,7},{7,6},{8,9},{9,8},{10,11... | collective-permute-start | bytes 2359304 | tf_op jit(solution)/shard_map/ppermute | solution.py:415
  1.1 21.0 %collective-permute-start.2 = (bf16[512,768]{1,0:T(8,128)(2,1)}, bf16[512,768]{1,0:T(8,128)(2,1)S(1)}, u32[]{:S(2)}, u32[]{:S(2)}) collective-permute-start(bf16[512,768]{1,0:T(8,128)(2,1)} %refs_0_.1), channel_id=1, source_target_pairs={{8,0},{0,8},{24,16},{16,24},{9,1},{1,9},{25,17},{17,25},{10,2},{2,... | collective-permute-start | bytes 2359304 | tf_op jit(solution)/shard_map/ppermute | solution.py:433
  3.8 19.1 %collective-permute-start = (bf16[512,768]{1,0:T(8,128)(2,1)}, bf16[512,768]{1,0:T(8,128)(2,1)S(1)}, u32[]{:S(2)}, u32[]{:S(2)}) collective-permute-start(bf16[512,768]{1,0:T(8,128)(2,1)} %refs_0_.1), channel_id=1, source_target_pairs={{16,8},{8,16},{17,9},{9,17},{18,10},{10,18},{19,11},{11,19},{20,12... | collective-permute-start | bytes 2359304 | tf_op jit(solution)/shard_map/ppermute | solution.py:433
  22.1 4.6 %collective-permute-start.5 = (bf16[512,768]{1,0:T(8,128)(2,1)S(1)}, bf16[512,768]{1,0:T(8,128)(2,1)S(1)}, u32[]{:S(2)}, u32[]{:S(2)}) collective-permute-start(bf16[512,768]{1,0:T(8,128)(2,1)S(1)} %collective-permute-done.2.refs_0_), channel_id=1, source_target_pairs={{0,1},{1,0},{2,3},{3,2},{4,5},{5,4},{6,7},{7,6},{8,9},{9,8},{10,11... | collective-permute-start | bytes 2359304 | tf_op jit(solution)/shard_map/ppermute | solution.py:415
  22.1 6.5 %collective-permute-start.4 = (bf16[512,768]{1,0:T(8,128)(2,1)S(1)}, bf16[512,768]{1,0:T(8,128)(2,1)S(1)}, u32[]{:S(2)}, u32[]{:S(2)}) collective-permute-start(bf16[512,768]{1,0:T(8,128)(2,1)S(1)} %collective-permute-done.2.refs_0_), channel_id=1, source_target_pairs={{16,8},{8,16},{17,9},{9,17},{18,10},{10,18},{19,11},{11,19},{20,12... | collective-permute-start | bytes 2359304 | tf_op jit(solution)/shard_map/ppermute | solution.py:433
  22.9 23.7 %collective-permute-start.1 = (bf16[512,768]{1,0:T(8,128)(2,1)S(1)}, bf16[512,768]{1,0:T(8,128)(2,1)S(1)}, u32[]{:S(2)}, u32[]{:S(2)}) collective-permute-start(bf16[512,768]{1,0:T(8,128)(2,1)S(1)} %collective-permute-done.refs_0_), channel_id=1, source_target_pairs={{8,0},{16,24},{9,1},{17,25},{10,2},{18,26},{11,3},{19,27},{12,4},{... | collective-permute-start | bytes 2359304 | tf_op jit(solution)/shard_map/ppermute | solution.py:433
  24.2 28.2 %collective-permute-start.8 = (bf16[512,768]{1,0:T(8,128)(2,1)S(1)}, bf16[512,768]{1,0:T(8,128)(2,1)S(1)}, u32[]{:S(2)}, u32[]{:S(2)}) collective-permute-start(bf16[512,768]{1,0:T(8,128)(2,1)S(1)} %collective-permute-done.refs_0_), channel_id=1, source_target_pairs={{8,9},{9,8},{10,11},{11,10},{12,13},{13,12},{14,15},{15,14},{16,17... | collective-permute-start | bytes 2359304 | tf_op jit(solution)/shard_map/ppermute | solution.py:415
  46.6 5.8 %collective-permute-start.9 = (bf16[512,768]{1,0:T(8,128)(2,1)S(1)}, bf16[512,768]{1,0:T(8,128)(2,1)S(1)}, u32[]{:S(2)}, u32[]{:S(2)}) collective-permute-start(bf16[512,768]{1,0:T(8,128)(2,1)S(1)} %collective-permute-done.1.refs_1_), channel_id=1, source_target_pairs={{0,1},{1,0},{2,3},{3,2},{4,5},{5,4},{6,7},{7,6},{24,25},{25,24},{2... | collective-permute-start | bytes 2359304 | tf_op jit(solution)/shard_map/ppermute | solution.py:415
  48.5 21.8 %collective-permute-start.7 = (bf16[512,768]{1,0:T(8,128)(2,1)S(1)}, bf16[512,768]{1,0:T(8,128)(2,1)S(1)}, u32[]{:S(2)}, u32[]{:S(2)}) collective-permute-start(bf16[512,768]{1,0:T(8,128)(2,1)S(1)} %collective-permute-done.4.refs_0_), channel_id=1, source_target_pairs={{8,0},{16,24},{9,1},{17,25},{10,2},{18,26},{11,3},{19,27},{12,4},{... | collective-permute-start | bytes 2359304 | tf_op jit(solution)/shard_map/ppermute | solution.py:433
  49.8 24.3 %collective-permute-start.6 = (bf16[512,768]{1,0:T(8,128)(2,1)S(1)}, bf16[512,768]{1,0:T(8,128)(2,1)S(1)}, u32[]{:S(2)}, u32[]{:S(2)}) collective-permute-start(bf16[512,768]{1,0:T(8,128)(2,1)S(1)} %collective-permute-done.4.refs_0_), channel_id=1, source_target_pairs={{8,9},{9,8},{10,11},{11,10},{12,13},{13,12},{14,15},{15,14},{16,17... | collective-permute-start | bytes 2359304 | tf_op jit(solution)/shard_map/ppermute | solution.py:415
  70.4 4.2 %collective-permute-start.10 = (bf16[512,768]{1,0:T(8,128)(2,1)S(1)}, bf16[512,768]{1,0:T(8,128)(2,1)S(1)}, u32[]{:S(2)}, u32[]{:S(2)}) collective-permute-start(bf16[512,768]{1,0:T(8,128)(2,1)S(1)} %collective-permute-done.7.refs_1_), channel_id=1, source_target_pairs={{0,1},{1,0},{2,3},{3,2},{4,5},{5,4},{6,7},{7,6},{24,25},{25,24},{2... | collective-permute-start | bytes 2359304 | tf_op jit(solution)/shard_map/ppermute | solution.py:415
  77.7 5.6 %collective-permute-start.12 = (f32[8,1,512]{2,1,0:T(1,128)S(1)}, f32[8,1,512]{2,1,0:T(1,128)S(1)}, u32[]{:S(2)}, u32[]{:S(2)}) collective-permute-start(f32[8,1,512]{2,1,0:T(1,128)S(1)} %add.22.refs_0_), channel_id=1, source_target_pairs={{0,8},{8,16},{16,24},{24,0},{1,9},{9,17},{17,25},{25,1},{2,10},{10... | collective-permute-start | bytes 49160 | tf_op jit(solution)/shard_map/ppermute | solution.py:481
  77.7 5.5 %collective-permute-start.13 = (f32[8,1,512]{2,1,0:T(1,128)S(1)}, f32[8,1,512]{2,1,0:T(1,128)S(1)}, u32[]{:S(2)}, u32[]{:S(2)}) collective-permute-start(f32[8,1,512]{2,1,0:T(1,128)S(1)} %add.22.refs_0_), channel_id=1, source_target_pairs={{0,16},{8,24},{16,0},{24,8},{1,17},{9,25},{17,1},{25,9},{2,18},{10... | collective-permute-start | bytes 49160 | tf_op jit(solution)/shard_map/ppermute | solution.py:481
  80.2 3.7 %collective-permute-start.14 = (f32[8,1,512]{2,1,0:T(1,128)S(1)}, f32[8,1,512]{2,1,0:T(1,128)S(1)}, u32[]{:S(2)}, u32[]{:S(2)}) collective-permute-start(f32[8,1,512]{2,1,0:T(1,128)S(1)} %add.22.refs_0_), channel_id=1, source_target_pairs={{0,24},{8,0},{16,8},{24,16},{1,25},{9,1},{17,9},{25,17},{2,26},{10... | collective-permute-start | bytes 49160 | tf_op jit(solution)/shard_map/ppermute | solution.py:481
  93.7 8.4 %collective-permute-start.19 = (bf16[144,768]{1,0:T(8,128)(2,1)S(1)}, bf16[144,768]{1,0:T(8,128)(2,1)S(1)}, u32[]{:S(2)}, u32[]{:S(2)}) collective-permute-start(bf16[144,768]{1,0:T(8,128)(2,1)S(1)} %get-tuple-element.106), channel_id=1, source_target_pairs={{0,4},{1,5},{2,6},{3,7},{4,0},{5,1},{6,2},{7,3},{8,12},{9,13},{10,... | collective-permute-start | bytes 663560 | tf_op jit(solution)/shard_map/ppermute | solution.py:409
  95.3 9.0 %collective-permute-start.17 = (bf16[128,768]{1,0:T(8,128)(2,1)S(1)}, bf16[128,768]{1,0:T(8,128)(2,1)S(1)}, u32[]{:S(2)}, u32[]{:S(2)}) collective-permute-start(bf16[128,768]{1,0:T(8,128)(2,1)S(1)} %get-tuple-element.104), channel_id=1, source_target_pairs={{0,2},{1,3},{2,0},{3,1},{4,6},{5,7},{6,4},{7,5},{8,10},{9,11},{10,... | collective-permute-start | bytes 589832 | tf_op jit(solution)/shard_map/ppermute | solution.py:409
  96.8 13.5 %collective-permute-start.16 = (bf16[144,768]{1,0:T(8,128)(2,1)S(1)}, bf16[144,768]{1,0:T(8,128)(2,1)S(1)}, u32[]{:S(2)}, u32[]{:S(2)}) collective-permute-start(bf16[144,768]{1,0:T(8,128)(2,1)S(1)} %get-tuple-element.102), channel_id=1, source_target_pairs={{0,4},{1,5},{2,6},{3,7},{4,0},{5,1},{6,2},{7,3},{8,12},{9,13},{10,... | collective-permute-start | bytes 663560 | tf_op jit(solution)/shard_map/ppermute | solution.py:409
  102.2 8.1 %collective-permute-start.20 = (bf16[144,768]{1,0:T(8,128)(2,1)S(1)}, bf16[144,768]{1,0:T(8,128)(2,1)S(1)}, u32[]{:S(2)}, u32[]{:S(2)}) collective-permute-start(bf16[144,768]{1,0:T(8,128)(2,1)S(1)} %pass_on.3), channel_id=1, source_target_pairs={{0,2},{1,3},{2,0},{3,1},{4,6},{5,7},{6,4},{7,5},{8,10},{9,11},{10,... | collective-permute-start | bytes 663560 | tf_op jit(solution)/shard_map/ppermute | solution.py:409
  103.8 6.5 %collective-permute-start.15 = (bf16[128,768]{1,0:T(8,128)(2,1)S(1)}, bf16[128,768]{1,0:T(8,128)(2,1)S(1)}, u32[]{:S(2)}, u32[]{:S(2)}) collective-permute-start(bf16[128,768]{1,0:T(8,128)(2,1)S(1)} %get-tuple-element.101), channel_id=1, source_target_pairs={{0,2},{1,3},{2,0},{3,1},{4,6},{5,7},{6,4},{7,5},{8,10},{9,11},{10,... | collective-permute-start | bytes 589832 | tf_op jit(solution)/shard_map/ppermute | solution.py:409
  104.4 6.0 %collective-permute-start.18 = (bf16[128,768]{1,0:T(8,128)(2,1)S(1)}, bf16[128,768]{1,0:T(8,128)(2,1)S(1)}, u32[]{:S(2)}, u32[]{:S(2)}) collective-permute-start(bf16[128,768]{1,0:T(8,128)(2,1)S(1)} %pass_on.2), channel_id=1, source_target_pairs={{0,4},{1,5},{2,6},{3,7},{4,0},{5,1},{6,2},{7,3},{8,12},{9,13},{10,... | collective-permute-start | bytes 589832 | tf_op jit(solution)/shard_map/ppermute | solution.py:409
  110.6 3.7 %collective-permute-start.27 = (bf16[128,768]{1,0:T(8,128)(2,1)S(1)}, bf16[128,768]{1,0:T(8,128)(2,1)S(1)}, u32[]{:S(2)}, u32[]{:S(2)}) collective-permute-start(bf16[128,768]{1,0:T(8,128)(2,1)S(1)} %get-tuple-element.107.refs_0_), channel_id=1, source_target_pairs={{0,1},{1,0},{2,3},{3,2},{4,5},{5,4},{6,7},{7,6},{8,9},{9,8},{10,11... | collective-permute-start | bytes 589832 | tf_op jit(solution)/shard_map/ppermute | solution.py:409
  110.7 7.8 %collective-permute-start.21 = (bf16[128,768]{1,0:T(8,128)(2,1)S(1)}, bf16[128,768]{1,0:T(8,128)(2,1)S(1)}, u32[]{:S(2)}, u32[]{:S(2)}) collective-permute-start(bf16[128,768]{1,0:T(8,128)(2,1)S(1)} %get-tuple-element.107.refs_0_), channel_id=1, source_target_pairs={{0,2},{1,3},{2,0},{3,1},{4,6},{5,7},{6,4},{7,5},{8,10},{9,11},{10,... | collective-permute-start | bytes 589832 | tf_op jit(solution)/shard_map/ppermute | solution.py:409
  112.2 10.5 %collective-permute-start.25 = (bf16[144,768]{1,0:T(8,128)(2,1)S(1)}, bf16[144,768]{1,0:T(8,128)(2,1)S(1)}, u32[]{:S(2)}, u32[]{:S(2)}) collective-permute-start(bf16[144,768]{1,0:T(8,128)(2,1)S(1)} %get-tuple-element.108.refs_1_), channel_id=1, source_target_pairs={{0,2},{1,3},{2,0},{3,1},{4,6},{5,7},{6,4},{7,5},{8,10},{9,11},{10,... | collective-permute-start | bytes 663560 | tf_op jit(solution)/shard_map/ppermute | solution.py:409
  112.8 10.0 %collective-permute-start.23 = (bf16[144,768]{1,0:T(8,128)(2,1)S(1)}, bf16[144,768]{1,0:T(8,128)(2,1)S(1)}, u32[]{:S(2)}, u32[]{:S(2)}) collective-permute-start(bf16[144,768]{1,0:T(8,128)(2,1)S(1)} %get-tuple-element.108.refs_1_), channel_id=1, source_target_pairs={{0,4},{1,5},{2,6},{3,7},{4,0},{5,1},{6,2},{7,3},{8,12},{9,13},{10,... | collective-permute-start | bytes 663560 | tf_op jit(solution)/shard_map/ppermute | solution.py:409
  114.3 8.9 %collective-permute-start.28 = (bf16[144,768]{1,0:T(8,128)(2,1)S(1)}, bf16[144,768]{1,0:T(8,128)(2,1)S(1)}, u32[]{:S(2)}, u32[]{:S(2)}) collective-permute-start(bf16[144,768]{1,0:T(8,128)(2,1)S(1)} %get-tuple-element.108.refs_1_), channel_id=1, source_target_pairs={{0,1},{1,0},{2,3},{3,2},{4,5},{5,4},{6,7},{7,6},{8,9},{9,8},{10,11... | collective-permute-start | bytes 663560 | tf_op jit(solution)/shard_map/ppermute | solution.py:409
  114.3 12.2 %collective-permute-start.26 = (bf16[128,768]{1,0:T(8,128)(2,1)S(1)}, bf16[128,768]{1,0:T(8,128)(2,1)S(1)}, u32[]{:S(2)}, u32[]{:S(2)}) collective-permute-start(bf16[128,768]{1,0:T(8,128)(2,1)S(1)} %get-tuple-element.107.refs_0_), channel_id=1, source_target_pairs={{0,4},{1,5},{2,6},{3,7},{4,0},{5,1},{6,2},{7,3},{8,12},{9,13},{10,... | collective-permute-start | bytes 589832 | tf_op jit(solution)/shard_map/ppermute | solution.py:409
  118.4 8.2 %collective-permute-start.29 = (bf16[128,768]{1,0:T(8,128)(2,1)S(1)}, bf16[128,768]{1,0:T(8,128)(2,1)S(1)}, u32[]{:S(2)}, u32[]{:S(2)}) collective-permute-start(bf16[128,768]{1,0:T(8,128)(2,1)S(1)} %collective-permute-done.21.refs_0_), channel_id=1, source_target_pairs={{0,1},{1,0},{2,3},{3,2},{4,5},{5,4},{6,7},{7,6},{8,9},{9,8},{10,11... | collective-permute-start | bytes 589832 | tf_op jit(solution)/shard_map/ppermute | solution.py:409
  122.7 5.5 %collective-permute-start.30 = (bf16[144,768]{1,0:T(8,128)(2,1)S(1)}, bf16[144,768]{1,0:T(8,128)(2,1)S(1)}, u32[]{:S(2)}, u32[]{:S(2)}) collective-permute-start(bf16[144,768]{1,0:T(8,128)(2,1)S(1)} %collective-permute-done.25.refs_1_), channel_id=1, source_target_pairs={{0,1},{1,0},{2,3},{3,2},{4,5},{5,4},{6,7},{7,6},{8,9},{9,8},{10,11... | collective-permute-start | bytes 663560 | tf_op jit(solution)/shard_map/ppermute | solution.py:409
  122.7 5.5 %collective-permute-start.32 = (bf16[144,768]{1,0:T(8,128)(2,1)S(1)}, bf16[144,768]{1,0:T(8,128)(2,1)S(1)}, u32[]{:S(2)}, u32[]{:S(2)}) collective-permute-start(bf16[144,768]{1,0:T(8,128)(2,1)S(1)} %collective-permute-done.23.refs_3_), channel_id=1, source_target_pairs={{0,1},{1,0},{2,3},{3,2},{4,5},{5,4},{6,7},{7,6},{8,9},{9,8},{10,11... | collective-permute-start | bytes 663560 | tf_op jit(solution)/shard_map/ppermute | solution.py:409
  123.2 10.7 %collective-permute-start.24 = (bf16[144,768]{1,0:T(8,128)(2,1)S(1)}, bf16[144,768]{1,0:T(8,128)(2,1)S(1)}, u32[]{:S(2)}, u32[]{:S(2)}) collective-permute-start(bf16[144,768]{1,0:T(8,128)(2,1)S(1)} %collective-permute-done.23.refs_3_), channel_id=1, source_target_pairs={{0,2},{1,3},{2,0},{3,1},{4,6},{5,7},{6,4},{7,5},{8,10},{9,11},{10,... | collective-permute-start | bytes 663560 | tf_op jit(solution)/shard_map/ppermute | solution.py:409
  126.6 7.3 %collective-permute-start.22 = (bf16[128,768]{1,0:T(8,128)(2,1)S(1)}, bf16[128,768]{1,0:T(8,128)(2,1)S(1)}, u32[]{:S(2)}, u32[]{:S(2)}) collective-permute-start(bf16[128,768]{1,0:T(8,128)(2,1)S(1)} %collective-permute-done.21.refs_0_), channel_id=1, source_target_pairs={{0,4},{1,5},{2,6},{3,7},{4,0},{5,1},{6,2},{7,3},{8,12},{9,13},{10,... | collective-permute-start | bytes 589832 | tf_op jit(solution)/shard_map/ppermute | solution.py:409
  133.9 1.8 %collective-permute-start.34 = (bf16[144,768]{1,0:T(8,128)(2,1)S(1)}, bf16[144,768]{1,0:T(8,128)(2,1)S(1)}, u32[]{:S(2)}, u32[]{:S(2)}) collective-permute-start(bf16[144,768]{1,0:T(8,128)(2,1)S(1)} %collective-permute-done.24.refs_1_), channel_id=1, source_target_pairs={{0,1},{1,0},{2,3},{3,2},{4,5},{5,4},{6,7},{7,6},{8,9},{9,8},{10,11... | collective-permute-start | bytes 663560 | tf_op jit(solution)/shard_map/ppermute | solution.py:409
  (4 other events, 5.8 us)
